TPU v7x, 32 devices: a whole 2x2x4 slice. The times are simulated.
32 devices in a mesh: gr: 4 (over z), gc: 8 (over y, x, core).
Axes of the slice: x: 2, y: 2, z: 4, core: 2. Of those that a mesh axis runs over, the one named last changes fastest.
Arguments:
- embeddings: bfloat16 [8192, 768], P(('gr', 'gc'))
- cluster_ids: int32 [8192], P(('gr', 'gc')), may hold values from 0 to 3, as said below
Outputs:
- neighbour_sum: float32 [8192, 768], P(('gr', 'gc'))
- density: float32 [8192], P(('gr', 'gc'))
Inputs may be any that keep to these rules, and one draw needn't show every extreme that they name: `cluster_ids`: each device's 256 rows hold exactly 64 rows of every cluster.
All inputs are finite; a program needn't handle non-finite values.
Results may differ from a plain program's by a relative error of at most 0.0017.
Values may be sent and summed in bfloat16 or wider, within the bound.
No kernel may reach another device: no remote copies, remote signals or barrier semaphores. Data moves between devices by JAX's collectives and lax.ppermute only.
A program may use at most 128 MiB of HBM per device.

v0:
```python
import functools
import math

import jax
import jax.numpy as jnp
from jax import lax
from jax.experimental import pallas as pl
from jax.experimental.pallas import tpu as pltpu
from jax.sharding import PartitionSpec as P

beta_scale = 16.0
LANES = 128
EXTRA = 8
TOP = 14.0
VMEM = pl.BlockSpec(memory_space=pltpu.VMEM)
HBM = pl.BlockSpec(memory_space=pltpu.HBM)
SMEM = pl.BlockSpec(memory_space=pltpu.SMEM)
GRANT = pltpu.CompilerParams(vmem_limit_bytes=40 * 1024 * 1024)


def in_hbm(array):
    return pltpu.with_memory_space_constraint(array, pltpu.HBM)


def diagonal(count):
    first = lax.broadcasted_iota(jnp.int32, (count, count), 0)
    second = lax.broadcasted_iota(jnp.int32, (count, count), 1)
    return first == second


def as_row(column):
    return jnp.sum(
        jnp.where(diagonal(column.shape[0]), column, jnp.zeros_like(column)),
        axis=0,
        keepdims=True,
    )


def as_column(row):
    return jnp.sum(
        jnp.where(diagonal(row.shape[1]), row, jnp.zeros_like(row)),
        axis=1,
        keepdims=True,
    )


def placement(own, ids, groups):
    count = ids.shape[1]
    first = lax.broadcasted_iota(jnp.int32, (count, count), 0)
    second = lax.broadcasted_iota(jnp.int32, (count, count), 1)
    earlier = jnp.where((as_column(ids) == ids) & (first < second), 1, 0)
    rank = jnp.sum(earlier, axis=0, keepdims=True)
    slot = (ids ^ own) * (count // groups) + rank
    return jnp.where(first == slot, 1.0, 0.0)


def sort_kernel(own_ref, ids_hbm, rows_hbm, *refs):
    chosen_ref, *out_refs = refs[:-4]
    ids_ref, rows_ref, ids_sem, rows_sem = refs[-4:]
    groups = len(out_refs)
    ids_copy = pltpu.make_async_copy(ids_hbm, ids_ref, ids_sem)
    rows_copy = pltpu.make_async_copy(rows_hbm, rows_ref, rows_sem)
    ids_copy.start()
    rows_copy.start()
    ids_copy.wait()
    chosen = placement(own_ref[0], ids_ref[...], groups).astype(jnp.bfloat16)
    chosen_ref[...] = chosen
    rows_copy.wait()
    ordered = jnp.dot(chosen, rows_ref[...], preferred_element_type=jnp.float32)
    ordered = ordered.astype(jnp.bfloat16)
    size = ordered.shape[0] // groups
    for k, out_ref in enumerate(out_refs):
        out_ref[...] = ordered[k * size : (k + 1) * size, :]


def inverse_norms(rows):
    wide = rows.astype(jnp.float32)
    return lax.rsqrt(jnp.sum(wide * wide, axis=1, keepdims=True) + 1e-06)


def add_columns(rows, col_refs, total, dens):
    count = rows.shape[0]
    scale = inverse_norms(rows) * (beta_scale * math.log2(math.e))
    blocks = [
        (col_ref, start)
        for col_ref in col_refs
        for start in range(0, col_ref.shape[0], count)
    ]
    for col_ref, start in blocks:
        cols = col_ref[start : min(start + count, col_ref.shape[0]), :]
        size = cols.shape[0]
        col_inv = as_row(inverse_norms(cols))
        raw = lax.dot_general(
            rows, cols, (((1,), (1,)), ((), ())), preferred_element_type=jnp.float32
        )
        weight = jnp.exp2(raw * scale * col_inv - beta_scale * math.log2(math.e))
        whole = size - size % LANES
        for lane in range(0, whole, LANES):
            dens += weight[:, lane : lane + LANES]
        if whole < size:
            part = jnp.sum(weight[:, whole:], axis=1, keepdims=True)
            dens += jnp.where(lax.broadcasted_iota(jnp.int32, dens.shape, 1) == 0, part, 0.0)
        coef = (weight * col_inv).astype(jnp.bfloat16)
        total += jnp.dot(coef, cols, preferred_element_type=jnp.float32)
    return total, dens


def first_kernel(rows_ref, *refs):
    col_refs, (total_ref, dens_ref) = refs[:-2], refs[-2:]
    total = jnp.zeros(total_ref.shape, jnp.float32)
    dens = jnp.zeros(dens_ref.shape, jnp.float32)
    total, dens = add_columns(rows_ref[...], col_refs, total, dens)
    total_ref[...] = total
    dens_ref[...] = dens


def middle_kernel(rows_ref, total_ref, dens_ref, *refs):
    col_refs, (total_out, dens_out) = refs[:-2], refs[-2:]
    total, dens = add_columns(rows_ref[...], col_refs, total_ref[...], dens_ref[...])
    total_out[...] = total
    dens_out[...] = dens


def exponent(value):
    return jnp.floor(jnp.log2(jnp.maximum(value, 1e-30)))


def last_kernel(groups, rows_ref, total_ref, dens_ref, *refs):
    col_refs, out_refs = refs[:-groups], refs[-groups:]
    padded, width = out_refs[0].shape
    size = padded - EXTRA
    total, dens = add_columns(rows_ref[...], col_refs, total_ref[...], dens_ref[...])
    dens = jnp.sum(dens, axis=1, keepdims=True)
    power = exponent(jnp.max(jnp.abs(total), axis=1, keepdims=True))
    total = total * jnp.exp2(TOP - power)
    dens_power = exponent(dens)
    part = dens * jnp.exp2(-dens_power)
    aside = [power, dens_power]
    for k in range(3):
        piece = part.astype(jnp.bfloat16).astype(jnp.float32)
        aside.append(piece * 2.0 ** (8 * k))
        part = part - piece
    for k, out_ref in enumerate(out_refs[::-1]):
        rows = slice(k * size, (k + 1) * size)
        out_ref[:size, :] = total[rows, :]
        out_ref[size:, :] = jnp.zeros((EXTRA, width), jnp.float32)
        for line, column in enumerate(aside):
            out_ref[size + line : size + line + 1, :size] = as_row(column[rows, :])


def restore_kernel(chosen_ref, *refs):
    part_refs, (total_ref, dens_ref) = refs[:-2], refs[-2:]
    groups = len(part_refs)
    size = part_refs[0].shape[0] - EXTRA
    chosen = chosen_ref[...]
    sums, dens = [], []
    for part_ref in part_refs[::-1]:
        power, dens_power, *pieces = [
            as_column(part_ref[size + line : size + line + 1, :size])
            for line in range(5)
        ]
        sums.append(part_ref[:size, :] * jnp.exp2(power - TOP))
        part = sum(piece * 2.0 ** (-8 * j) for j, piece in enumerate(pieces))
        dens.append(part * jnp.exp2(dens_power))
    dens_ref[...] = jnp.sum(
        chosen.astype(jnp.float32) * jnp.concatenate(dens, axis=0), axis=0, keepdims=True
    )
    rest = jnp.concatenate(sums, axis=0)
    back = jnp.zeros(rest.shape, jnp.float32)
    for _ in range(2):
        piece = rest.astype(jnp.bfloat16)
        rest = rest - piece.astype(jnp.float32)
        back += lax.dot_general(
            chosen, piece, (((0,), (0,)), ((), ())), preferred_element_type=jnp.float32
        )
    total_ref[...] = back


def on_device(n_gr, n_gc, embeddings, cluster_ids):
    count, width = embeddings.shape
    size = count // n_gr
    own = lax.axis_index("gr").astype(jnp.int32).reshape(1)
    ids = cluster_ids.reshape(1, count)

    chosen, *parts = pl.pallas_call(
        sort_kernel,
        out_shape=[jax.ShapeDtypeStruct((count, count), jnp.bfloat16)]
        + [jax.ShapeDtypeStruct((size, width), jnp.bfloat16)] * n_gr,
        in_specs=[SMEM, HBM, HBM],
        out_specs=[VMEM] * (1 + n_gr),
        scratch_shapes=[
            pltpu.VMEM((1, count), jnp.int32),
            pltpu.VMEM((count, width), embeddings.dtype),
            pltpu.SemaphoreType.DMA,
            pltpu.SemaphoreType.DMA,
        ],
        compiler_params=GRANT,
        name="sort_rows",
    )(own, in_hbm(ids), in_hbm(embeddings))

    def along_gr(part, bits):
        return lax.ppermute(part, "gr", [(i, i ^ bits) for i in range(n_gr)])

    def along_gc(block, bits):
        return lax.ppermute(block, "gc", [(i, i ^ bits) for i in range(n_gc)])

    def other_core(block):
        return along_gc(block, 1)

    def cost(*blocks):
        pairs = count * sum(block.shape[0] for block in blocks)
        return pl.CostEstimate(
            flops=4 * pairs * width,
            bytes_accessed=0,
            transcendentals=pairs,
        )

    held = [parts[0]] + [along_gr(parts[k], k) for k in range(1, n_gr)]
    half = n_gr // 2
    chunks = []
    for pieces in (held[:half], held[half:]):
        block = jnp.concatenate(pieces, axis=0)
        near = [block] + [along_gc(block, k) for k in range(2, n_gc, 2)]
        chunks.append(jnp.concatenate(near, axis=0))
    rows = jnp.concatenate(held, axis=0)
    chunks[0], rows = lax.optimization_barrier((chunks[0], rows))
    early = [chunks[0], other_core(chunks[0])]

    total, dens = pl.pallas_call(
        first_kernel,
        out_shape=[
            jax.ShapeDtypeStruct((count, width), jnp.float32),
            jax.ShapeDtypeStruct((count, LANES), jnp.float32),
        ],
        in_specs=[VMEM] * (1 + len(early)),
        out_specs=[VMEM] * 2,
        compiler_params=GRANT,
        cost_estimate=cost(*early),
        name="early_sums",
    )(rows, *early)
    total, dens = pl.pallas_call(
        middle_kernel,
        out_shape=[
            jax.ShapeDtypeStruct((count, width), jnp.float32),
            jax.ShapeDtypeStruct((count, LANES), jnp.float32),
        ],
        in_specs=[VMEM] * 4,
        out_specs=[VMEM] * 2,
        compiler_params=GRANT,
        cost_estimate=cost(chunks[1]),
        name="middle_sums",
    )(rows, total, dens, chunks[1])
    late = [other_core(chunks[1])]
    sums = pl.pallas_call(
        functools.partial(last_kernel, n_gr),
        out_shape=[jax.ShapeDtypeStruct((size + EXTRA, width), jnp.float32)] * n_gr,
        in_specs=[VMEM] * (3 + len(late)),
        out_specs=[VMEM] * n_gr,
        compiler_params=GRANT,
        cost_estimate=cost(*late),
        name="last_sums",
    )(rows, total, dens, *late)[::-1]

    sent = [part.astype(jnp.float16) for part in sums]
    back = [None] * n_gr
    back[0] = sent[0]
    for k in sorted(range(1, n_gr), reverse=True):
        back[k] = along_gr(sent[k], k)
    back = [part.astype(jnp.float32) for part in back]
    neighbour_sum, density = pl.pallas_call(
        restore_kernel,
        out_shape=[
            jax.ShapeDtypeStruct((count, width), jnp.float32),
            jax.ShapeDtypeStruct((1, count), jnp.float32),
        ],
        in_specs=[VMEM] * (1 + n_gr),
        out_specs=[VMEM, VMEM],
        compiler_params=GRANT,
        name="restore_rows",
    )(chosen, *back[::-1])
    return (neighbour_sum, density.reshape(count))


def solution(mesh):
    in_specs = (P(("gr", "gc"), None), P(("gr", "gc")))
    out_specs = (P(("gr", "gc"), None), P(("gr", "gc")))
    return jax.shard_map(
        functools.partial(on_device, mesh.shape["gr"], mesh.shape["gc"]),
        mesh=mesh,
        in_specs=in_specs,
        out_specs=out_specs,
        check_vma=False,
    )
```

profile of v0, /device:TPU:0, one launch (start us, length us, event | category | flops | bytes accessed | tf_op | source)
XLA Modules:
  0.0 47.0 jit_solution(2114019849969679239)
XLA Ops:
  0.6 1.3 %sort_rows.1 = (bf16[256,256]{1,0:T(8,128)(2,1)S(1)}, bf16[64,768]{1,0:T(8,128)(2,1)S(1)}, bf16[64,768]{1,0:T(8,128)(2,1)S(1)}, bf16[64,768]{1,0:T(8,128)(2,1)S(1)}, bf16[64,768]{1,0:T(8,128)(2,1)S(1)}) custom-call(s32[1]{0:T(128)} %bitcast.own_ref, s32[1,256]{1,0:T(1,128)} %bitcast.3, bf16[256,768]{1,0:T(8,128)(2,1)} %rows_hbm.1), custom_call_target="tpu_custom_call" | custom-call | tf_op jit(solution)/shard_map/sort_rows/pallas_call | solution.py:185
  1.9 3.1 %collective-permute-start = (bf16[64,768]{1,0:T(8,128)(2,1)S(1)}, bf16[64,768]{1,0:T(8,128)(2,1)S(1)}, u32[]{:S(2)}, u32[]{:S(2)}) collective-permute-start(bf16[64,768]{1,0:T(8,128)(2,1)S(1)} %get-tuple-element.21), channel_id=1, source_target_pairs={{0,8},{8,0},{16,24},{24,16},{1,9},{9,1},{17,25},{25,17},{2,10},{10... | collective-permute-start | bytes 294920 | tf_op jit(solution)/shard_map/ppermute | solution.py:202
  5.0 2.5 %collective-permute-start.5 = (bf16[64,768]{1,0:T(8,128)(2,1)S(1)}, bf16[64,768]{1,0:T(8,128)(2,1)S(1)}, u32[]{:S(2)}, u32[]{:S(2)}) collective-permute-start(bf16[64,768]{1,0:T(8,128)(2,1)S(1)} %get-tuple-element.23), channel_id=1, source_target_pairs={{0,24},{8,16},{16,8},{24,0},{1,25},{9,17},{17,9},{25,1},{2,26},{10... | collective-permute-start | bytes 294920 | tf_op jit(solution)/shard_map/ppermute | solution.py:202
  7.5 0.1 collective-permute-start.4
  7.6 0.2 collective-permute-done
  7.8 1.8 %collective-permute-start.1 = (bf16[128,768]{1,0:T(8,128)(2,1)S(1)}, bf16[128,768]{1,0:T(8,128)(2,1)S(1)}, u32[]{:S(2)}, u32[]{:S(2)}) collective-permute-start(bf16[128,768]{1,0:T(8,128)(2,1)S(1)} %get-tuple-element.40), channel_id=1, source_target_pairs={{0,2},{1,3},{2,0},{3,1},{4,6},{5,7},{6,4},{7,5},{8,10},{9,11},{10,... | collective-permute-start | bytes 589832 | tf_op jit(solution)/shard_map/ppermute | solution.py:205
  9.6 1.5 %collective-permute-start.2 = (bf16[128,768]{1,0:T(8,128)(2,1)S(1)}, bf16[128,768]{1,0:T(8,128)(2,1)S(1)}, u32[]{:S(2)}, u32[]{:S(2)}) collective-permute-start(bf16[128,768]{1,0:T(8,128)(2,1)S(1)} %get-tuple-element.40), channel_id=1, source_target_pairs={{0,4},{1,5},{2,6},{3,7},{4,0},{5,1},{6,2},{7,3},{8,12},{9,13},{10,... | collective-permute-start | bytes 589832 | tf_op jit(solution)/shard_map/ppermute | solution.py:205
  11.2 0.2 collective-permute-start.3
  11.4 5.1 %collective-permute-done.4 = bf16[64,768]{1,0:T(8,128)(2,1)S(1)} collective-permute-done((bf16[64,768]{1,0:T(8,128)(2,1)S(1)}, bf16[64,768]{1,0:T(8,128)(2,1)S(1)}, u32[]{:S(2)}, u32[]{:S(2)}) %collective-permute-start.4) | collective-permute-done | bytes 98336 | tf_op jit(solution)/shard_map/ppermute | solution.py:202
  16.5 0.0 collective-permute-done.5
  16.5 1.6 %collective-permute-start.7 = (bf16[128,768]{1,0:T(8,128)(2,1)S(1)}, bf16[128,768]{1,0:T(8,128)(2,1)S(1)}, u32[]{:S(2)}, u32[]{:S(2)}) collective-permute-start(bf16[128,768]{1,0:T(8,128)(2,1)S(1)} %get-tuple-element.36), channel_id=1, source_target_pairs={{0,2},{1,3},{2,0},{3,1},{4,6},{5,7},{6,4},{7,5},{8,10},{9,11},{10,... | collective-permute-start | bytes 589832 | tf_op jit(solution)/shard_map/ppermute | solution.py:205
  18.1 1.5 %collective-permute-start.8 = (bf16[128,768]{1,0:T(8,128)(2,1)S(1)}, bf16[128,768]{1,0:T(8,128)(2,1)S(1)}, u32[]{:S(2)}, u32[]{:S(2)}) collective-permute-start(bf16[128,768]{1,0:T(8,128)(2,1)S(1)} %get-tuple-element.36), channel_id=1, source_target_pairs={{0,4},{1,5},{2,6},{3,7},{4,0},{5,1},{6,2},{7,3},{8,12},{9,13},{10,... | collective-permute-start | bytes 589832 | tf_op jit(solution)/shard_map/ppermute | solution.py:205
  19.6 0.0 collective-permute-done.1
  19.6 0.5 %collective-permute-start.9 = (bf16[128,768]{1,0:T(8,128)(2,1)S(1)}, bf16[128,768]{1,0:T(8,128)(2,1)S(1)}, u32[]{:S(2)}, u32[]{:S(2)}) collective-permute-start(bf16[128,768]{1,0:T(8,128)(2,1)S(1)} %get-tuple-element.36), channel_id=1, source_target_pairs={{0,6},{1,7},{2,4},{3,5},{4,2},{5,3},{6,0},{7,1},{8,14},{9,15},{10,... | collective-permute-start | bytes 589832 | tf_op jit(solution)/shard_map/ppermute | solution.py:205
  20.2 0.0 collective-permute-done.2
  20.2 0.0 collective-permute-done.3
  20.2 0.1 collective-permute-start.6
  20.3 4.1 %collective-permute-done.7 = bf16[128,768]{1,0:T(8,128)(2,1)S(1)} collective-permute-done((bf16[128,768]{1,0:T(8,128)(2,1)S(1)}, bf16[128,768]{1,0:T(8,128)(2,1)S(1)}, u32[]{:S(2)}, u32[]{:S(2)}) %collective-permute-start.7) | collective-permute-done | bytes 196640 | tf_op jit(solution)/shard_map/ppermute | solution.py:205
  24.4 4.0 %collective-permute-done.8 = bf16[128,768]{1,0:T(8,128)(2,1)S(1)} collective-permute-done((bf16[128,768]{1,0:T(8,128)(2,1)S(1)}, bf16[128,768]{1,0:T(8,128)(2,1)S(1)}, u32[]{:S(2)}, u32[]{:S(2)}) %collective-permute-start.8) | collective-permute-done | bytes 196640 | tf_op jit(solution)/shard_map/ppermute | solution.py:205
  28.4 0.0 collective-permute-done.9
  28.4 0.1 collective-permute-start.10
  28.5 0.0 collective-permute-done.6.refs_1_
  28.5 1.7 %early_sums.1 = (f32[256,768]{1,0:T(8,128)S(1)}, f32[256,128]{1,0:T(8,128)S(1)}) custom-call(bf16[256,768]{1,0:T(8,128)(2,1)S(1)} %pad_maximum_fusion.rows_ref, bf16[512,768]{1,0:T(8,128)(2,1)S(1)} %constant_dynamic-update-slice_fusion.2.refs_0_, bf16[512,768]{1,0:T(8,128)(2,1)S(1)} %collective-permute-done.6.refs_1_), custom_call_target="tpu_custom_call" | custom-call | flops 805306368 | tf_op jit(solution)/shard_map/early_sums/pallas_call | solution.py:229
  30.2 1.0 %middle_sums.1 = (f32[256,768]{1,0:T(8,128)S(1)}, f32[256,128]{1,0:T(8,128)S(1)}) custom-call(bf16[256,768]{1,0:T(8,128)(2,1)S(1)} %pad_maximum_fusion.rows_ref, f32[256,768]{1,0:T(8,128)S(1)} %get-tuple-element.26.total_ref, f32[256,128]{1,0:T(8,128)S(1)} %get-tuple-element.27.dens_ref, bf16[512,768]{1,0:T(8,128)(2,1)S(1)} %constant_dynamic-update-slice_fusion.9.refs_0_), custom_call_target="tpu_custom_call" | custom-call | flops 402653184 | tf_op jit(solution)/shard_map/middle_sums/pallas_call | solution.py:241
  31.2 1.2 %last_sums.1 = (f32[72,768]{1,0:T(8,128)S(1)}, f32[72,768]{1,0:T(8,128)S(1)}, f32[72,768]{1,0:T(8,128)S(1)}, f32[72,768]{1,0:T(8,128)S(1)}) custom-call(bf16[256,768]{1,0:T(8,128)(2,1)S(1)} %pad_maximum_fusion.rows_ref, f32[256,768]{1,0:T(8,128)S(1)} %get-tuple-element.28.total_ref, f32[256,128]{1,0:T(8,128)S(1)} %get-tuple-element.29.dens_ref, ...), custom_call_target="tpu_custom_call" | custom-call | flops 402653184 | tf_op jit(solution)/shard_map/last_sums/pallas_call | solution.py:254
  32.4 3.1 %collective-permute-start.11 = (f16[72,768]{1,0:T(8,128)(2,1)S(1)}, f16[72,768]{1,0:T(8,128)(2,1)S(1)}, u32[]{:S(2)}, u32[]{:S(2)}) collective-permute-start(f16[72,768]{1,0:T(8,128)(2,1)S(1)} %convert_element_type.24), channel_id=1, source_target_pairs={{0,24},{8,16},{16,8},{24,0},{1,25},{9,17},{17,9},{25,1},{2,26},{10... | collective-permute-start | bytes 331784 | tf_op jit(solution)/shard_map/ppermute | solution.py:202
  35.5 0.1 collective-permute-start.12
  35.6 1.4 %collective-permute-start.13 = (f16[72,768]{1,0:T(8,128)(2,1)S(1)}, f16[72,768]{1,0:T(8,128)(2,1)S(1)}, u32[]{:S(2)}, u32[]{:S(2)}) collective-permute-start(f16[72,768]{1,0:T(8,128)(2,1)S(1)} %convert_element_type.28), channel_id=1, source_target_pairs={{0,8},{8,0},{16,24},{24,16},{1,9},{9,1},{17,25},{25,17},{2,10},{10... | collective-permute-start | bytes 331784 | tf_op jit(solution)/shard_map/ppermute | solution.py:202
  37.1 3.2 %collective-permute-done.11 = f16[72,768]{1,0:T(8,128)(2,1)S(1)} collective-permute-done((f16[72,768]{1,0:T(8,128)(2,1)S(1)}, f16[72,768]{1,0:T(8,128)(2,1)S(1)}, u32[]{:S(2)}, u32[]{:S(2)}) %collective-permute-start.11) | collective-permute-done | bytes 110624 | tf_op jit(solution)/shard_map/ppermute | solution.py:202
  40.3 5.2 %collective-permute-done.12 = f16[72,768]{1,0:T(8,128)(2,1)S(1)} collective-permute-done((f16[72,768]{1,0:T(8,128)(2,1)S(1)}, f16[72,768]{1,0:T(8,128)(2,1)S(1)}, u32[]{:S(2)}, u32[]{:S(2)}) %collective-permute-start.12) | collective-permute-done | bytes 110624 | tf_op jit(solution)/shard_map/ppermute | solution.py:202
  45.5 0.0 collective-permute-done.13
  45.5 1.4 %restore_rows.1 = (f32[256,768]{1,0:T(8,128)}, f32[1,256]{1,0:T(1,128)}) custom-call(bf16[256,256]{1,0:T(8,128)(2,1)S(1)} %get-tuple-element.19.chosen_ref, f32[72,768]{1,0:T(8,128)S(1)} %convert_element_type.25.refs_0_, f32[72,768]{1,0:T(8,128)S(1)} %convert_element_type.27.refs_1_, f32[72,768]{1,0:T(8,128)S(1)} %convert_element_type.29.refs_2_, ...), custom_call_target="tpu_custom_call" | custom-call | tf_op jit(solution)/shard_map/restore_rows/pallas_call | solution.py:270
  (19 shorter events, 0.3 us)
Async XLA Ops:
  1.9 5.9 %collective-permute-start = (bf16[64,768]{1,0:T(8,128)(2,1)S(1)}, bf16[64,768]{1,0:T(8,128)(2,1)S(1)}, u32[]{:S(2)}, u32[]{:S(2)}) collective-permute-start(bf16[64,768]{1,0:T(8,128)(2,1)S(1)} %get-tuple-element.21), channel_id=1, source_target_pairs={{0,8},{8,0},{16,24},{24,16},{1,9},{9,1},{17,25},{25,17},{2,10},{10... | collective-permute-start | bytes 294920 | tf_op jit(solution)/shard_map/ppermute | solution.py:202
  5.0 11.4 %collective-permute-start.5 = (bf16[64,768]{1,0:T(8,128)(2,1)S(1)}, bf16[64,768]{1,0:T(8,128)(2,1)S(1)}, u32[]{:S(2)}, u32[]{:S(2)}) collective-permute-start(bf16[64,768]{1,0:T(8,128)(2,1)S(1)} %get-tuple-element.23), channel_id=1, source_target_pairs={{0,24},{8,16},{16,8},{24,0},{1,25},{9,17},{17,9},{25,1},{2,26},{10... | collective-permute-start | bytes 294920 | tf_op jit(solution)/shard_map/ppermute | solution.py:202
  7.5 8.9 %collective-permute-start.4 = (bf16[64,768]{1,0:T(8,128)(2,1)S(1)}, bf16[64,768]{1,0:T(8,128)(2,1)S(1)}, u32[]{:S(2)}, u32[]{:S(2)}) collective-permute-start(bf16[64,768]{1,0:T(8,128)(2,1)S(1)} %get-tuple-element.22), channel_id=1, source_target_pairs={{0,16},{8,24},{16,0},{24,8},{1,17},{9,25},{17,1},{25,9},{2,18},{10... | collective-permute-start | bytes 294920 | tf_op jit(solution)/shard_map/ppermute | solution.py:202
  7.8 11.8 %collective-permute-start.1 = (bf16[128,768]{1,0:T(8,128)(2,1)S(1)}, bf16[128,768]{1,0:T(8,128)(2,1)S(1)}, u32[]{:S(2)}, u32[]{:S(2)}) collective-permute-start(bf16[128,768]{1,0:T(8,128)(2,1)S(1)} %get-tuple-element.40), channel_id=1, source_target_pairs={{0,2},{1,3},{2,0},{3,1},{4,6},{5,7},{6,4},{7,5},{8,10},{9,11},{10,... | collective-permute-start | bytes 589832 | tf_op jit(solution)/shard_map/ppermute | solution.py:205
  9.6 10.5 %collective-permute-start.2 = (bf16[128,768]{1,0:T(8,128)(2,1)S(1)}, bf16[128,768]{1,0:T(8,128)(2,1)S(1)}, u32[]{:S(2)}, u32[]{:S(2)}) collective-permute-start(bf16[128,768]{1,0:T(8,128)(2,1)S(1)} %get-tuple-element.40), channel_id=1, source_target_pairs={{0,4},{1,5},{2,6},{3,7},{4,0},{5,1},{6,2},{7,3},{8,12},{9,13},{10,... | collective-permute-start | bytes 589832 | tf_op jit(solution)/shard_map/ppermute | solution.py:205
  11.2 9.1 %collective-permute-start.3 = (bf16[128,768]{1,0:T(8,128)(2,1)S(1)}, bf16[128,768]{1,0:T(8,128)(2,1)S(1)}, u32[]{:S(2)}, u32[]{:S(2)}) collective-permute-start(bf16[128,768]{1,0:T(8,128)(2,1)S(1)} %get-tuple-element.40), channel_id=1, source_target_pairs={{0,6},{1,7},{2,4},{3,5},{4,2},{5,3},{6,0},{7,1},{8,14},{9,15},{10,... | collective-permute-start | bytes 589832 | tf_op jit(solution)/shard_map/ppermute | solution.py:205
  16.5 7.9 %collective-permute-start.7 = (bf16[128,768]{1,0:T(8,128)(2,1)S(1)}, bf16[128,768]{1,0:T(8,128)(2,1)S(1)}, u32[]{:S(2)}, u32[]{:S(2)}) collective-permute-start(bf16[128,768]{1,0:T(8,128)(2,1)S(1)} %get-tuple-element.36), channel_id=1, source_target_pairs={{0,2},{1,3},{2,0},{3,1},{4,6},{5,7},{6,4},{7,5},{8,10},{9,11},{10,... | collective-permute-start | bytes 589832 | tf_op jit(solution)/shard_map/ppermute | solution.py:205
  18.1 10.3 %collective-permute-start.8 = (bf16[128,768]{1,0:T(8,128)(2,1)S(1)}, bf16[128,768]{1,0:T(8,128)(2,1)S(1)}, u32[]{:S(2)}, u32[]{:S(2)}) collective-permute-start(bf16[128,768]{1,0:T(8,128)(2,1)S(1)} %get-tuple-element.36), channel_id=1, source_target_pairs={{0,4},{1,5},{2,6},{3,7},{4,0},{5,1},{6,2},{7,3},{8,12},{9,13},{10,... | collective-permute-start | bytes 589832 | tf_op jit(solution)/shard_map/ppermute | solution.py:205
  19.6 8.8 %collective-permute-start.9 = (bf16[128,768]{1,0:T(8,128)(2,1)S(1)}, bf16[128,768]{1,0:T(8,128)(2,1)S(1)}, u32[]{:S(2)}, u32[]{:S(2)}) collective-permute-start(bf16[128,768]{1,0:T(8,128)(2,1)S(1)} %get-tuple-element.36), channel_id=1, source_target_pairs={{0,6},{1,7},{2,4},{3,5},{4,2},{5,3},{6,0},{7,1},{8,14},{9,15},{10,... | collective-permute-start | bytes 589832 | tf_op jit(solution)/shard_map/ppermute | solution.py:205
  20.2 8.3 %collective-permute-start.6 = (bf16[512,768]{1,0:T(8,128)(2,1)S(1)}, bf16[512,768]{1,0:T(8,128)(2,1)S(1)}, u32[]{:S(2)}, u32[]{:S(2)}) collective-permute-start(bf16[512,768]{1,0:T(8,128)(2,1)S(1)} %constant_dynamic-update-slice_fusion.2.refs_0_), channel_id=1, source_target_pairs={{0,1},{1,0},{2,3},{3,2},{4,5},{5,4},{6,7},{7,6},{8,9},{9,8},{10,11... | collective-permute-start | bytes 2359304 | tf_op jit(solution)/shard_map/ppermute | solution.py:205
  28.4 2.8 %collective-permute-start.10 = (bf16[512,768]{1,0:T(8,128)(2,1)S(1)}, bf16[512,768]{1,0:T(8,128)(2,1)S(1)}, u32[]{:S(2)}, u32[]{:S(2)}) collective-permute-start(bf16[512,768]{1,0:T(8,128)(2,1)S(1)} %constant_dynamic-update-slice_fusion.9.refs_0_), channel_id=1, source_target_pairs={{0,1},{1,0},{2,3},{3,2},{4,5},{5,4},{6,7},{7,6},{8,9},{9,8},{10,11... | collective-permute-start | bytes 2359304 | tf_op jit(solution)/shard_map/ppermute | solution.py:205
  32.4 7.8 %collective-permute-start.11 = (f16[72,768]{1,0:T(8,128)(2,1)S(1)}, f16[72,768]{1,0:T(8,128)(2,1)S(1)}, u32[]{:S(2)}, u32[]{:S(2)}) collective-permute-start(f16[72,768]{1,0:T(8,128)(2,1)S(1)} %convert_element_type.24), channel_id=1, source_target_pairs={{0,24},{8,16},{16,8},{24,0},{1,25},{9,17},{17,9},{25,1},{2,26},{10... | collective-permute-start | bytes 331784 | tf_op jit(solution)/shard_map/ppermute | solution.py:202
  35.5 9.9 %collective-permute-start.12 = (f16[72,768]{1,0:T(8,128)(2,1)S(1)}, f16[72,768]{1,0:T(8,128)(2,1)S(1)}, u32[]{:S(2)}, u32[]{:S(2)}) collective-permute-start(f16[72,768]{1,0:T(8,128)(2,1)S(1)} %convert_element_type.26), channel_id=1, source_target_pairs={{0,16},{8,24},{16,0},{24,8},{1,17},{9,25},{17,1},{25,9},{2,18},{10... | collective-permute-start | bytes 331784 | tf_op jit(solution)/shard_map/ppermute | solution.py:202
  35.6 9.9 %collective-permute-start.13 = (f16[72,768]{1,0:T(8,128)(2,1)S(1)}, f16[72,768]{1,0:T(8,128)(2,1)S(1)}, u32[]{:S(2)}, u32[]{:S(2)}) collective-permute-start(f16[72,768]{1,0:T(8,128)(2,1)S(1)} %convert_element_type.28), channel_id=1, source_target_pairs={{0,8},{8,0},{16,24},{24,16},{1,9},{9,1},{17,25},{25,17},{2,10},{10... | collective-permute-start | bytes 331784 | tf_op jit(solution)/shard_map/ppermute | solution.py:202
where the time goes:
time: 47.1 us; the launch traced here: 47 us
  waiting for transfers between devices  21.7 us (46%)
  starting transfers between devices  17.6 us (37%)
  Pallas kernels  6.6 us (14%)
  between operations  0.85 us (2%)
    ppermute x6, waiting for transfers between devices, along_gr(): return lax.ppermute(part, 'gr', [(i, i ^ bits) for i in range(n_gr)])  13.6 us
    ppermute x6, starting transfers between devices, along_gr(): return lax.ppermute(part, 'gr', [(i, i ^ bits) for i in range(n_gr)])  10.3 us
    ppermute x8, waiting for transfers between devices, along_gc(): return lax.ppermute(block, 'gc', [(i, i ^ bits) for i in range(n_gc)])  8.05 us
    ppermute x8, starting transfers between devices, along_gc(): return lax.ppermute(block, 'gc', [(i, i ^ bits) for i in range(n_gc)])  7.31 us
    pallas_call x1, Pallas kernels, on_device(): pl.pallas_call(first_kernel, out_shape=[jax.ShapeDtypeStruct((count, widt...  1.7 us
    pallas_call x1, Pallas kernels, on_device(): pl.pallas_call(restore_kernel, out_shape=[jax.ShapeDtypeStruct((count, wi...  1.45 us
    pallas_call x1, Pallas kernels, on_device(): pl.pallas_call(sort_kernel, out_shape=[jax.ShapeDtypeStruct((count, count...  1.3 us
    pallas_call x1, Pallas kernels, on_device(): pl.pallas_call(functools.partial(last_kernel, n_gr), out_shape=[jax.Shape...  1.15 us
  transfers between devices with their start and end apart: 14, of which 6 were waited for; matrix products, arithmetic and copies ran while one was open for 1% of the time, Pallas kernels for 6%

commit v1 on v0

--- a/solution.py
+++ b/solution.py
@@ -105,20 +105,20 @@
     return total, dens
 
 
-def first_kernel(rows_ref, *refs):
-    col_refs, (total_ref, dens_ref) = refs[:-2], refs[-2:]
-    total = jnp.zeros(total_ref.shape, jnp.float32)
-    dens = jnp.zeros(dens_ref.shape, jnp.float32)
+def add_kernel(n_blocks, rows_ref, *refs):
+    col_refs, sum_refs, (total_ref, dens_ref) = (
+        refs[:n_blocks],
+        refs[n_blocks:-2],
+        refs[-2:],
+    )
+    if sum_refs:
+        total, dens = (ref[...] for ref in sum_refs)
+    else:
+        total = jnp.zeros(total_ref.shape, jnp.float32)
+        dens = jnp.zeros(dens_ref.shape, jnp.float32)
     total, dens = add_columns(rows_ref[...], col_refs, total, dens)
     total_ref[...] = total
     dens_ref[...] = dens
-
-
-def middle_kernel(rows_ref, total_ref, dens_ref, *refs):
-    col_refs, (total_out, dens_out) = refs[:-2], refs[-2:]
-    total, dens = add_columns(rows_ref[...], col_refs, total_ref[...], dens_ref[...])
-    total_out[...] = total
-    dens_out[...] = dens
 
 
 def exponent(value):
@@ -217,40 +217,41 @@
 
     held = [parts[0]] + [along_gr(parts[k], k) for k in range(1, n_gr)]
     half = n_gr // 2
-    chunks = []
-    for pieces in (held[:half], held[half:]):
-        block = jnp.concatenate(pieces, axis=0)
-        near = [block] + [along_gc(block, k) for k in range(2, n_gc, 2)]
-        chunks.append(jnp.concatenate(near, axis=0))
+    early = jnp.concatenate(held[:half], axis=0)
+    late = jnp.concatenate(held[half:], axis=0)
+    first = [early] + [along_gc(early, k) for k in range(2, n_gc, 2)]
+    second = [late] + [along_gc(late, k) for k in range(2, n_gc, 2)]
+    if n_gc == 8:
+        direct = early.shape[0] // 2
+        split = (direct + early.shape[0]) // 2
+        first[3] = along_gc(early[:direct], 6)
+        second[1] = along_gc(jnp.concatenate([late, first[2][split:]], axis=0), 2)
+        second[2] = along_gc(jnp.concatenate([late, first[1][direct:split]], axis=0), 4)
+    first = jnp.concatenate(first, axis=0)
     rows = jnp.concatenate(held, axis=0)
-    chunks[0], rows = lax.optimization_barrier((chunks[0], rows))
-    early = [chunks[0], other_core(chunks[0])]
-
-    total, dens = pl.pallas_call(
-        first_kernel,
-        out_shape=[
-            jax.ShapeDtypeStruct((count, width), jnp.float32),
-            jax.ShapeDtypeStruct((count, LANES), jnp.float32),
-        ],
-        in_specs=[VMEM] * (1 + len(early)),
-        out_specs=[VMEM] * 2,
-        compiler_params=GRANT,
-        cost_estimate=cost(*early),
-        name="early_sums",
-    )(rows, *early)
-    total, dens = pl.pallas_call(
-        middle_kernel,
-        out_shape=[
-            jax.ShapeDtypeStruct((count, width), jnp.float32),
-            jax.ShapeDtypeStruct((count, LANES), jnp.float32),
-        ],
-        in_specs=[VMEM] * 4,
-        out_specs=[VMEM] * 2,
-        compiler_params=GRANT,
-        cost_estimate=cost(chunks[1]),
-        name="middle_sums",
-    )(rows, total, dens, chunks[1])
-    late = [other_core(chunks[1])]
+    middle = len(second) // 2
+    second, third = (
+        jnp.concatenate(second[:middle], axis=0),
+        jnp.concatenate(second[middle:], axis=0),
+    )
+
+    def add_sums(sums, name, *blocks):
+        return pl.pallas_call(
+            functools.partial(add_kernel, len(blocks)),
+            out_shape=[
+                jax.ShapeDtypeStruct((count, width), jnp.float32),
+                jax.ShapeDtypeStruct((count, LANES), jnp.float32),
+            ],
+            in_specs=[VMEM] * (1 + len(blocks) + len(sums)),
+            out_specs=[VMEM] * 2,
+            compiler_params=GRANT,
+            cost_estimate=cost(*blocks),
+            name=name,
+        )(rows, *blocks, *sums)
+
+    total, dens = add_sums([], "early_sums", first, other_core(first))
+    total, dens = add_sums([total, dens], "middle_sums", second, third)
+    late = [other_core(second), other_core(third)]
     sums = pl.pallas_call(
         functools.partial(last_kernel, n_gr),
         out_shape=[jax.ShapeDtypeStruct((size + EXTRA, width), jnp.float32)] * n_gr,

time: 47.1 us -> 50.6 us (1.074)
  starting transfers between devices: 17.6 us -> 21.3 us
  waiting for transfers between devices: 21.7 us -> 20.6 us
  Pallas kernels: 6.6 us -> 7.38 us
    ppermute x8 -> x9, starting transfers between devices: 7.31 us -> 11 us  [along_gc(): return lax.ppermute(block, 'gc', [(i, i ^ bits) for i in range(n_gc)])]
    ppermute x6, waiting for transfers between devices: 13.6 us -> 10.6 us  [along_gr(): return lax.ppermute(part, 'gr', [(i, i ^ bits) for i in range(n_gr)])]
    ppermute x8 -> x9, waiting for transfers between devices: 8.05 us -> 10 us  [along_gc(): return lax.ppermute(block, 'gc', [(i, i ^ bits) for i in range(n_gc)])]
  transfers between devices with their start and end apart: 14 -> 15, of which waited for: 6 -> 7; matrix products, arithmetic and copies ran while one was open for 1% -> 1% of each run, Pallas kernels for 6% -> 6%
where the time goes in v1:
time: 50.6 us; the launch traced here: 50.5 us
  starting transfers between devices  21.3 us (42%)
  waiting for transfers between devices  20.6 us (41%)
  Pallas kernels  7.38 us (15%)
  between operations  0.83 us (2%)
    ppermute x9, starting transfers between devices, along_gc(): return lax.ppermute(block, 'gc', [(i, i ^ bits) for i in range(n_gc)])  11 us
    ppermute x6, waiting for transfers between devices, along_gr(): return lax.ppermute(part, 'gr', [(i, i ^ bits) for i in range(n_gr)])  10.6 us
    ppermute x6, starting transfers between devices, along_gr(): return lax.ppermute(part, 'gr', [(i, i ^ bits) for i in range(n_gr)])  10.3 us
    ppermute x9, waiting for transfers between devices, along_gc(): return lax.ppermute(block, 'gc', [(i, i ^ bits) for i in range(n_gc)])  10 us
    pallas_call x2, Pallas kernels, add_sums(): pl.pallas_call(functools.partial(add_kernel, len(blocks)), out_shape=[jax...  3.09 us
    pallas_call x1, Pallas kernels, on_device(): pl.pallas_call(functools.partial(last_kernel, n_gr), out_shape=[jax.Shape...  1.55 us
    pallas_call x1, Pallas kernels, on_device(): pl.pallas_call(restore_kernel, out_shape=[jax.ShapeDtypeStruct((count, wi...  1.44 us
    pallas_call x1, Pallas kernels, on_device(): pl.pallas_call(sort_kernel, out_shape=[jax.ShapeDtypeStruct((count, count...  1.3 us
  transfers between devices with their start and end apart: 15, of which 7 were waited for; matrix products, arithmetic and copies ran while one was open for 1% of the time, Pallas kernels for 6%

profile of v1, /device:TPU:0, one launch (start us, length us, event | category | flops | bytes accessed | tf_op | source)
XLA Modules:
  0.0 50.5 jit_solution(7385745298181265324)
XLA Ops:
  0.6 1.3 %sort_rows.1 = (bf16[256,256]{1,0:T(8,128)(2,1)S(1)}, bf16[64,768]{1,0:T(8,128)(2,1)S(1)}, bf16[64,768]{1,0:T(8,128)(2,1)S(1)}, bf16[64,768]{1,0:T(8,128)(2,1)S(1)}, bf16[64,768]{1,0:T(8,128)(2,1)S(1)}) custom-call(s32[1]{0:T(128)} %bitcast.own_ref, s32[1,256]{1,0:T(1,128)} %bitcast.3, bf16[256,768]{1,0:T(8,128)(2,1)} %rows_hbm.1), custom_call_target="tpu_custom_call" | custom-call | tf_op jit(solution)/shard_map/sort_rows/pallas_call | solution.py:185
  1.9 4.1 %collective-permute-start.1 = (bf16[64,768]{1,0:T(8,128)(2,1)S(1)}, bf16[64,768]{1,0:T(8,128)(2,1)S(1)}, u32[]{:S(2)}, u32[]{:S(2)}) collective-permute-start(bf16[64,768]{1,0:T(8,128)(2,1)S(1)} %get-tuple-element.20), channel_id=1, source_target_pairs={{0,16},{8,24},{16,0},{24,8},{1,17},{9,25},{17,1},{25,9},{2,18},{10... | collective-permute-start | bytes 294920 | tf_op jit(solution)/shard_map/ppermute | solution.py:202
  6.0 1.6 %collective-permute-start = (bf16[64,768]{1,0:T(8,128)(2,1)S(1)}, bf16[64,768]{1,0:T(8,128)(2,1)S(1)}, u32[]{:S(2)}, u32[]{:S(2)}) collective-permute-start(bf16[64,768]{1,0:T(8,128)(2,1)S(1)} %get-tuple-element.19), channel_id=1, source_target_pairs={{0,8},{8,0},{16,24},{24,16},{1,9},{9,1},{17,25},{25,17},{2,10},{10... | collective-permute-start | bytes 294920 | tf_op jit(solution)/shard_map/ppermute | solution.py:202
  7.6 0.0 collective-permute-start.2
  7.6 2.7 %collective-permute-start.8 = (bf16[64,768]{1,0:T(8,128)(2,1)S(1)}, bf16[64,768]{1,0:T(8,128)(2,1)S(1)}, u32[]{:S(2)}, u32[]{:S(2)}) collective-permute-start(bf16[64,768]{1,0:T(8,128)(2,1)S(1)} %get-tuple-element.18), channel_id=1, source_target_pairs={{0,6},{1,7},{2,4},{3,5},{4,2},{5,3},{6,0},{7,1},{8,14},{9,15},{10,... | collective-permute-start | bytes 294920 | tf_op jit(solution)/shard_map/ppermute | solution.py:205
  10.3 0.9 %collective-permute-done = bf16[64,768]{1,0:T(8,128)(2,1)S(1)} collective-permute-done((bf16[64,768]{1,0:T(8,128)(2,1)S(1)}, bf16[64,768]{1,0:T(8,128)(2,1)S(1)}, u32[]{:S(2)}, u32[]{:S(2)}) %collective-permute-start) | collective-permute-done | bytes 98336 | tf_op jit(solution)/shard_map/ppermute | solution.py:202
  11.2 1.6 %collective-permute-start.5 = (bf16[128,768]{1,0:T(8,128)(2,1)S(1)}, bf16[128,768]{1,0:T(8,128)(2,1)S(1)}, u32[]{:S(2)}, u32[]{:S(2)}) collective-permute-start(bf16[128,768]{1,0:T(8,128)(2,1)S(1)} %get-tuple-element.35), channel_id=1, source_target_pairs={{0,2},{1,3},{2,0},{3,1},{4,6},{5,7},{6,4},{7,5},{8,10},{9,11},{10,... | collective-permute-start | bytes 589832 | tf_op jit(solution)/shard_map/ppermute | solution.py:205
  12.8 1.5 %collective-permute-start.3 = (bf16[128,768]{1,0:T(8,128)(2,1)S(1)}, bf16[128,768]{1,0:T(8,128)(2,1)S(1)}, u32[]{:S(2)}, u32[]{:S(2)}) collective-permute-start(bf16[128,768]{1,0:T(8,128)(2,1)S(1)} %get-tuple-element.35), channel_id=1, source_target_pairs={{0,4},{1,5},{2,6},{3,7},{4,0},{5,1},{6,2},{7,3},{8,12},{9,13},{10,... | collective-permute-start | bytes 589832 | tf_op jit(solution)/shard_map/ppermute | solution.py:205
  14.3 0.0 collective-permute-done.1
  14.3 0.0 collective-permute-done.2
  14.3 2.4 %collective-permute-start.7 = (bf16[128,768]{1,0:T(8,128)(2,1)S(1)}, bf16[128,768]{1,0:T(8,128)(2,1)S(1)}, u32[]{:S(2)}, u32[]{:S(2)}) collective-permute-start(bf16[128,768]{1,0:T(8,128)(2,1)S(1)} %pad_maximum_fusion.3), channel_id=1, source_target_pairs={{0,6},{1,7},{2,4},{3,5},{4,2},{5,3},{6,0},{7,1},{8,14},{9,15},{10,... | collective-permute-start | bytes 589832 | tf_op jit(solution)/shard_map/ppermute | solution.py:205
  16.7 1.5 %collective-permute-done.5 = bf16[128,768]{1,0:T(8,128)(2,1)S(1)} collective-permute-done((bf16[128,768]{1,0:T(8,128)(2,1)S(1)}, bf16[128,768]{1,0:T(8,128)(2,1)S(1)}, u32[]{:S(2)}, u32[]{:S(2)}) %collective-permute-start.5) | collective-permute-done | bytes 196640 | tf_op jit(solution)/shard_map/ppermute | solution.py:205
  18.2 4.6 %collective-permute-done.3 = bf16[128,768]{1,0:T(8,128)(2,1)S(1)} collective-permute-done((bf16[128,768]{1,0:T(8,128)(2,1)S(1)}, bf16[128,768]{1,0:T(8,128)(2,1)S(1)}, u32[]{:S(2)}, u32[]{:S(2)}) %collective-permute-start.3) | collective-permute-done | bytes 196640 | tf_op jit(solution)/shard_map/ppermute | solution.py:205
  22.9 0.1 collective-permute-start.4
  22.9 2.2 %collective-permute-start.6 = (bf16[160,768]{1,0:T(8,128)(2,1)S(1)}, bf16[160,768]{1,0:T(8,128)(2,1)S(1)}, u32[]{:S(2)}, u32[]{:S(2)}) collective-permute-start(bf16[160,768]{1,0:T(8,128)(2,1)S(1)} %get-tuple-element.32), channel_id=1, source_target_pairs={{0,4},{1,5},{2,6},{3,7},{4,0},{5,1},{6,2},{7,3},{8,12},{9,13},{10,... | collective-permute-start | bytes 737288 | tf_op jit(solution)/shard_map/ppermute | solution.py:205
  25.2 0.1 collective-permute-start.9
  25.3 3.8 %collective-permute-done.4 = bf16[160,768]{1,0:T(8,128)(2,1)S(1)} collective-permute-done((bf16[160,768]{1,0:T(8,128)(2,1)S(1)}, bf16[160,768]{1,0:T(8,128)(2,1)S(1)}, u32[]{:S(2)}, u32[]{:S(2)}) %collective-permute-start.4) | collective-permute-done | bytes 245792 | tf_op jit(solution)/shard_map/ppermute | solution.py:205
  29.1 0.1 collective-permute-start.10
  29.2 0.1 collective-permute-done.6
  29.3 0.0 collective-permute-done.7
  29.3 0.5 %collective-permute-start.11 = (bf16[288,768]{1,0:T(8,128)(2,1)S(1)}, bf16[288,768]{1,0:T(8,128)(2,1)S(1)}, u32[]{:S(2)}, u32[]{:S(2)}) collective-permute-start(bf16[288,768]{1,0:T(8,128)(2,1)S(1)} %constant_dynamic-update-slice_fusion.9.refs_1_), channel_id=1, source_target_pairs={{0,1},{1,0},{2,3},{3,2},{4,5},{5,4},{6,7},{7,6},{8,9},{9,8},{10,11... | collective-permute-start | bytes 1327112 | tf_op jit(solution)/shard_map/ppermute | solution.py:205
  29.9 1.7 %early_sums.1 = (f32[256,768]{1,0:T(8,128)S(1)}, f32[256,128]{1,0:T(8,128)S(1)}) custom-call(bf16[256,768]{1,0:T(8,128)(2,1)S(1)} %get-tuple-element.41.rows_ref, bf16[448,768]{1,0:T(8,128)(2,1)S(1)} %constant_dynamic-update-slice_fusion.11.refs_0_, bf16[448,768]{1,0:T(8,128)(2,1)S(1)} %collective-permute-done.9.refs_1_), custom_call_target="tpu_custom_call" | custom-call | flops 704643072 | tf_op jit(solution)/shard_map/early_sums/pallas_call | solution.py:239
  31.6 1.4 %middle_sums.1 = (f32[256,768]{1,0:T(8,128)S(1)}, f32[256,128]{1,0:T(8,128)S(1)}) custom-call(bf16[256,768]{1,0:T(8,128)(2,1)S(1)} %get-tuple-element.41.rows_ref, bf16[288,768]{1,0:T(8,128)(2,1)S(1)} %constant_dynamic-update-slice_fusion.6.refs_0_, bf16[288,768]{1,0:T(8,128)(2,1)S(1)} %constant_dynamic-update-slice_fusion.9.refs_1_, ...), custom_call_target="tpu_custom_call" | custom-call | flops 452984832 | tf_op jit(solution)/shard_map/middle_sums/pallas_call | solution.py:239
  33.0 0.0 collective-permute-done.10.refs_0_
  33.0 0.0 collective-permute-done.11.refs_1_
  33.0 1.5 %last_sums.1 = (f32[72,768]{1,0:T(8,128)S(1)}, f32[72,768]{1,0:T(8,128)S(1)}, f32[72,768]{1,0:T(8,128)S(1)}, f32[72,768]{1,0:T(8,128)S(1)}) custom-call(bf16[256,768]{1,0:T(8,128)(2,1)S(1)} %get-tuple-element.41.rows_ref, f32[256,768]{1,0:T(8,128)S(1)} %get-tuple-element.24.total_ref, f32[256,128]{1,0:T(8,128)S(1)} %get-tuple-element.25.dens_ref, ...), custom_call_target="tpu_custom_call" | custom-call | flops 452984832 | tf_op jit(solution)/shard_map/last_sums/pallas_call | solution.py:255
  34.6 3.6 %collective-permute-start.12 = (f16[72,768]{1,0:T(8,128)(2,1)S(1)}, f16[72,768]{1,0:T(8,128)(2,1)S(1)}, u32[]{:S(2)}, u32[]{:S(2)}) collective-permute-start(f16[72,768]{1,0:T(8,128)(2,1)S(1)} %convert_element_type.24), channel_id=1, source_target_pairs={{0,24},{8,16},{16,8},{24,0},{1,25},{9,17},{17,9},{25,1},{2,26},{10... | collective-permute-start | bytes 331784 | tf_op jit(solution)/shard_map/ppermute | solution.py:202
  38.2 0.8 %collective-permute-start.13 = (f16[72,768]{1,0:T(8,128)(2,1)S(1)}, f16[72,768]{1,0:T(8,128)(2,1)S(1)}, u32[]{:S(2)}, u32[]{:S(2)}) collective-permute-start(f16[72,768]{1,0:T(8,128)(2,1)S(1)} %convert_element_type.26), channel_id=1, source_target_pairs={{0,16},{8,24},{16,0},{24,8},{1,17},{9,25},{17,1},{25,9},{2,18},{10... | collective-permute-start | bytes 331784 | tf_op jit(solution)/shard_map/ppermute | solution.py:202
  39.0 0.2 collective-permute-start.14
  39.2 3.2 %collective-permute-done.12 = f16[72,768]{1,0:T(8,128)(2,1)S(1)} collective-permute-done((f16[72,768]{1,0:T(8,128)(2,1)S(1)}, f16[72,768]{1,0:T(8,128)(2,1)S(1)}, u32[]{:S(2)}, u32[]{:S(2)}) %collective-permute-start.12) | collective-permute-done | bytes 110624 | tf_op jit(solution)/shard_map/ppermute | solution.py:202
  42.4 6.6 %collective-permute-done.13 = f16[72,768]{1,0:T(8,128)(2,1)S(1)} collective-permute-done((f16[72,768]{1,0:T(8,128)(2,1)S(1)}, f16[72,768]{1,0:T(8,128)(2,1)S(1)}, u32[]{:S(2)}, u32[]{:S(2)}) %collective-permute-start.13) | collective-permute-done | bytes 110624 | tf_op jit(solution)/shard_map/ppermute | solution.py:202
  49.0 1.4 %restore_rows.1 = (f32[256,768]{1,0:T(8,128)}, f32[1,256]{1,0:T(1,128)}) custom-call(bf16[256,256]{1,0:T(8,128)(2,1)S(1)} %get-tuple-element.17.chosen_ref, f32[72,768]{1,0:T(8,128)S(1)} %convert_element_type.25.refs_0_, f32[72,768]{1,0:T(8,128)S(1)} %convert_element_type.27.refs_1_, f32[72,768]{1,0:T(8,128)S(1)} %convert_element_type.29.refs_2_, ...), custom_call_target="tpu_custom_call" | custom-call | tf_op jit(solution)/shard_map/restore_rows/pallas_call | solution.py:271
  (24 shorter events, 0.3 us)
Async XLA Ops:
  1.9 12.3 %collective-permute-start.1 = (bf16[64,768]{1,0:T(8,128)(2,1)S(1)}, bf16[64,768]{1,0:T(8,128)(2,1)S(1)}, u32[]{:S(2)}, u32[]{:S(2)}) collective-permute-start(bf16[64,768]{1,0:T(8,128)(2,1)S(1)} %get-tuple-element.20), channel_id=1, source_target_pairs={{0,16},{8,24},{16,0},{24,8},{1,17},{9,25},{17,1},{25,9},{2,18},{10... | collective-permute-start | bytes 294920 | tf_op jit(solution)/shard_map/ppermute | solution.py:202
  6.0 5.1 %collective-permute-start = (bf16[64,768]{1,0:T(8,128)(2,1)S(1)}, bf16[64,768]{1,0:T(8,128)(2,1)S(1)}, u32[]{:S(2)}, u32[]{:S(2)}) collective-permute-start(bf16[64,768]{1,0:T(8,128)(2,1)S(1)} %get-tuple-element.19), channel_id=1, source_target_pairs={{0,8},{8,0},{16,24},{24,16},{1,9},{9,1},{17,25},{25,17},{2,10},{10... | collective-permute-start | bytes 294920 | tf_op jit(solution)/shard_map/ppermute | solution.py:202
  7.6 6.7 %collective-permute-start.2 = (bf16[64,768]{1,0:T(8,128)(2,1)S(1)}, bf16[64,768]{1,0:T(8,128)(2,1)S(1)}, u32[]{:S(2)}, u32[]{:S(2)}) collective-permute-start(bf16[64,768]{1,0:T(8,128)(2,1)S(1)} %get-tuple-element.21), channel_id=1, source_target_pairs={{0,24},{8,16},{16,8},{24,0},{1,25},{9,17},{17,9},{25,1},{2,26},{10... | collective-permute-start | bytes 294920 | tf_op jit(solution)/shard_map/ppermute | solution.py:202
  7.6 17.5 %collective-permute-start.8 = (bf16[64,768]{1,0:T(8,128)(2,1)S(1)}, bf16[64,768]{1,0:T(8,128)(2,1)S(1)}, u32[]{:S(2)}, u32[]{:S(2)}) collective-permute-start(bf16[64,768]{1,0:T(8,128)(2,1)S(1)} %get-tuple-element.18), channel_id=1, source_target_pairs={{0,6},{1,7},{2,4},{3,5},{4,2},{5,3},{6,0},{7,1},{8,14},{9,15},{10,... | collective-permute-start | bytes 294920 | tf_op jit(solution)/shard_map/ppermute | solution.py:205
  11.2 7.0 %collective-permute-start.5 = (bf16[128,768]{1,0:T(8,128)(2,1)S(1)}, bf16[128,768]{1,0:T(8,128)(2,1)S(1)}, u32[]{:S(2)}, u32[]{:S(2)}) collective-permute-start(bf16[128,768]{1,0:T(8,128)(2,1)S(1)} %get-tuple-element.35), channel_id=1, source_target_pairs={{0,2},{1,3},{2,0},{3,1},{4,6},{5,7},{6,4},{7,5},{8,10},{9,11},{10,... | collective-permute-start | bytes 589832 | tf_op jit(solution)/shard_map/ppermute | solution.py:205
  12.8 10.1 %collective-permute-start.3 = (bf16[128,768]{1,0:T(8,128)(2,1)S(1)}, bf16[128,768]{1,0:T(8,128)(2,1)S(1)}, u32[]{:S(2)}, u32[]{:S(2)}) collective-permute-start(bf16[128,768]{1,0:T(8,128)(2,1)S(1)} %get-tuple-element.35), channel_id=1, source_target_pairs={{0,4},{1,5},{2,6},{3,7},{4,0},{5,1},{6,2},{7,3},{8,12},{9,13},{10,... | collective-permute-start | bytes 589832 | tf_op jit(solution)/shard_map/ppermute | solution.py:205
  14.3 15.0 %collective-permute-start.7 = (bf16[128,768]{1,0:T(8,128)(2,1)S(1)}, bf16[128,768]{1,0:T(8,128)(2,1)S(1)}, u32[]{:S(2)}, u32[]{:S(2)}) collective-permute-start(bf16[128,768]{1,0:T(8,128)(2,1)S(1)} %pad_maximum_fusion.3), channel_id=1, source_target_pairs={{0,6},{1,7},{2,4},{3,5},{4,2},{5,3},{6,0},{7,1},{8,14},{9,15},{10,... | collective-permute-start | bytes 589832 | tf_op jit(solution)/shard_map/ppermute | solution.py:205
  22.9 6.3 %collective-permute-start.4 = (bf16[160,768]{1,0:T(8,128)(2,1)S(1)}, bf16[160,768]{1,0:T(8,128)(2,1)S(1)}, u32[]{:S(2)}, u32[]{:S(2)}) collective-permute-start(bf16[160,768]{1,0:T(8,128)(2,1)S(1)} %get-tuple-element.33), channel_id=1, source_target_pairs={{0,2},{1,3},{2,0},{3,1},{4,6},{5,7},{6,4},{7,5},{8,10},{9,11},{10,... | collective-permute-start | bytes 737288 | tf_op jit(solution)/shard_map/ppermute | solution.py:205
  22.9 6.3 %collective-permute-start.6 = (bf16[160,768]{1,0:T(8,128)(2,1)S(1)}, bf16[160,768]{1,0:T(8,128)(2,1)S(1)}, u32[]{:S(2)}, u32[]{:S(2)}) collective-permute-start(bf16[160,768]{1,0:T(8,128)(2,1)S(1)} %get-tuple-element.32), channel_id=1, source_target_pairs={{0,4},{1,5},{2,6},{3,7},{4,0},{5,1},{6,2},{7,3},{8,12},{9,13},{10,... | collective-permute-start | bytes 737288 | tf_op jit(solution)/shard_map/ppermute | solution.py:205
  25.2 4.7 %collective-permute-start.9 = (bf16[448,768]{1,0:T(8,128)(2,1)S(1)}, bf16[448,768]{1,0:T(8,128)(2,1)S(1)}, u32[]{:S(2)}, u32[]{:S(2)}) collective-permute-start(bf16[448,768]{1,0:T(8,128)(2,1)S(1)} %constant_dynamic-update-slice_fusion.11.refs_0_), channel_id=1, source_target_pairs={{0,1},{1,0},{2,3},{3,2},{4,5},{5,4},{6,7},{7,6},{8,9},{9,8},{10,11... | collective-permute-start | bytes 2064392 | tf_op jit(solution)/shard_map/ppermute | solution.py:205
  29.1 3.8 %collective-permute-start.10 = (bf16[288,768]{1,0:T(8,128)(2,1)S(1)}, bf16[288,768]{1,0:T(8,128)(2,1)S(1)}, u32[]{:S(2)}, u32[]{:S(2)}) collective-permute-start(bf16[288,768]{1,0:T(8,128)(2,1)S(1)} %constant_dynamic-update-slice_fusion.6.refs_0_), channel_id=1, source_target_pairs={{0,1},{1,0},{2,3},{3,2},{4,5},{5,4},{6,7},{7,6},{8,9},{9,8},{10,11... | collective-permute-start | bytes 1327112 | tf_op jit(solution)/shard_map/ppermute | solution.py:205
  29.3 3.6 %collective-permute-start.11 = (bf16[288,768]{1,0:T(8,128)(2,1)S(1)}, bf16[288,768]{1,0:T(8,128)(2,1)S(1)}, u32[]{:S(2)}, u32[]{:S(2)}) collective-permute-start(bf16[288,768]{1,0:T(8,128)(2,1)S(1)} %constant_dynamic-update-slice_fusion.9.refs_1_), channel_id=1, source_target_pairs={{0,1},{1,0},{2,3},{3,2},{4,5},{5,4},{6,7},{7,6},{8,9},{9,8},{10,11... | collective-permute-start | bytes 1327112 | tf_op jit(solution)/shard_map/ppermute | solution.py:205
  34.6 7.8 %collective-permute-start.12 = (f16[72,768]{1,0:T(8,128)(2,1)S(1)}, f16[72,768]{1,0:T(8,128)(2,1)S(1)}, u32[]{:S(2)}, u32[]{:S(2)}) collective-permute-start(f16[72,768]{1,0:T(8,128)(2,1)S(1)} %convert_element_type.24), channel_id=1, source_target_pairs={{0,24},{8,16},{16,8},{24,0},{1,25},{9,17},{17,9},{25,1},{2,26},{10... | collective-permute-start | bytes 331784 | tf_op jit(solution)/shard_map/ppermute | solution.py:202
  38.2 10.8 %collective-permute-start.13 = (f16[72,768]{1,0:T(8,128)(2,1)S(1)}, f16[72,768]{1,0:T(8,128)(2,1)S(1)}, u32[]{:S(2)}, u32[]{:S(2)}) collective-permute-start(f16[72,768]{1,0:T(8,128)(2,1)S(1)} %convert_element_type.26), channel_id=1, source_target_pairs={{0,16},{8,24},{16,0},{24,8},{1,17},{9,25},{17,1},{25,9},{2,18},{10... | collective-permute-start | bytes 331784 | tf_op jit(solution)/shard_map/ppermute | solution.py:202
  39.0 10.0 %collective-permute-start.14 = (f16[72,768]{1,0:T(8,128)(2,1)S(1)}, f16[72,768]{1,0:T(8,128)(2,1)S(1)}, u32[]{:S(2)}, u32[]{:S(2)}) collective-permute-start(f16[72,768]{1,0:T(8,128)(2,1)S(1)} %convert_element_type.28), channel_id=1, source_target_pairs={{0,8},{8,0},{16,24},{24,16},{1,9},{9,1},{17,25},{25,17},{2,10},{10... | collective-permute-start | bytes 331784 | tf_op jit(solution)/shard_map/ppermute | solution.py:202

commit v2 on v1

--- a/solution.py
+++ b/solution.py
@@ -217,23 +217,21 @@
 
     held = [parts[0]] + [along_gr(parts[k], k) for k in range(1, n_gr)]
     half = n_gr // 2
+    sides = [k for k in range(2, n_gc, 2) if not k & (k - 1)]
+    corners = [k for k in range(2, n_gc, 2) if k & (k - 1)]
     early = jnp.concatenate(held[:half], axis=0)
     late = jnp.concatenate(held[half:], axis=0)
-    first = [early] + [along_gc(early, k) for k in range(2, n_gc, 2)]
-    second = [late] + [along_gc(late, k) for k in range(2, n_gc, 2)]
-    if n_gc == 8:
-        direct = early.shape[0] // 2
-        split = (direct + early.shape[0]) // 2
-        first[3] = along_gc(early[:direct], 6)
-        second[1] = along_gc(jnp.concatenate([late, first[2][split:]], axis=0), 2)
-        second[2] = along_gc(jnp.concatenate([late, first[1][direct:split]], axis=0), 4)
-    first = jnp.concatenate(first, axis=0)
+    rest = jnp.concatenate(held[1:half], axis=0)
+    filler = [along_gc(held[0], k) for k in corners]
+    filler, rest = lax.optimization_barrier((filler, rest))
+    first = [early] + [along_gc(early, k) for k in sides] + filler
+    rests = [along_gc(rest, k) for k in corners]
+    late_x = late_y = late_d = late
+    late_d, rests = lax.optimization_barrier((late, rests))
+    second = [late] + [along_gc(late_x, k) for k in sides[:1]] + [along_gc(late_y, k) for k in sides[1:]] + [along_gc(late_d, k) for k in corners]
+    first = jnp.concatenate(first + rests, axis=0)
     rows = jnp.concatenate(held, axis=0)
-    middle = len(second) // 2
-    second, third = (
-        jnp.concatenate(second[:middle], axis=0),
-        jnp.concatenate(second[middle:], axis=0),
-    )
+    second = jnp.concatenate(second, axis=0)
 
     def add_sums(sums, name, *blocks):
         return pl.pallas_call(
@@ -250,8 +248,8 @@
         )(rows, *blocks, *sums)
 
     total, dens = add_sums([], "early_sums", first, other_core(first))
-    total, dens = add_sums([total, dens], "middle_sums", second, third)
-    late = [other_core(second), other_core(third)]
+    total, dens = add_sums([total, dens], "middle_sums", second)
+    late = [other_core(second)]
     sums = pl.pallas_call(
         functools.partial(last_kernel, n_gr),
         out_shape=[jax.ShapeDtypeStruct((size + EXTRA, width), jnp.float32)] * n_gr,

time: 50.6 us -> 48.9 us (0.966)
  Pallas kernels: 7.38 us -> 6.59 us
  waiting for transfers between devices: 20.6 us -> 19.9 us
    ppermute x9, waiting for transfers between devices: 10 us -> 9.29 us  [along_gc(): return lax.ppermute(block, 'gc', [(i, i ^ bits) for i in range(n_gc)])]
where the time goes in v2:
time: 48.9 us; the launch traced here: 48.7 us
  starting transfers between devices  21.1 us (43%)
  waiting for transfers between devices  19.9 us (41%)
  Pallas kernels  6.59 us (13%)
  between operations  0.81 us (2%)
    ppermute x9, starting transfers between devices, along_gc(): return lax.ppermute(block, 'gc', [(i, i ^ bits) for i in range(n_gc)])  10.8 us
    ppermute x6, waiting for transfers between devices, along_gr(): return lax.ppermute(part, 'gr', [(i, i ^ bits) for i in range(n_gr)])  10.6 us
    ppermute x6, starting transfers between devices, along_gr(): return lax.ppermute(part, 'gr', [(i, i ^ bits) for i in range(n_gr)])  10.3 us
    ppermute x9, waiting for transfers between devices, along_gc(): return lax.ppermute(block, 'gc', [(i, i ^ bits) for i in range(n_gc)])  9.29 us
    pallas_call x2, Pallas kernels, add_sums(): pl.pallas_call(functools.partial(add_kernel, len(blocks)), out_shape=[jax...  2.7 us
    pallas_call x1, Pallas kernels, on_device(): pl.pallas_call(restore_kernel, out_shape=[jax.ShapeDtypeStruct((count, wi...  1.44 us
    pallas_call x1, Pallas kernels, on_device(): pl.pallas_call(sort_kernel, out_shape=[jax.ShapeDtypeStruct((count, count...  1.3 us
    pallas_call x1, Pallas kernels, on_device(): pl.pallas_call(functools.partial(last_kernel, n_gr), out_shape=[jax.Shape...  1.16 us
  transfers between devices with their start and end apart: 15, of which 7 were waited for; matrix products, arithmetic and copies ran while one was open for 1% of the time, Pallas kernels for 6%

profile of v2, /device:TPU:0, one launch (start us, length us, event | category | flops | bytes accessed | tf_op | source)
XLA Modules:
  0.0 48.7 jit_solution(9828445086689084449)
XLA Ops:
  0.6 1.3 %sort_rows.1 = (bf16[256,256]{1,0:T(8,128)(2,1)S(1)}, bf16[64,768]{1,0:T(8,128)(2,1)S(1)}, bf16[64,768]{1,0:T(8,128)(2,1)S(1)}, bf16[64,768]{1,0:T(8,128)(2,1)S(1)}, bf16[64,768]{1,0:T(8,128)(2,1)S(1)}) custom-call(s32[1]{0:T(128)} %bitcast.own_ref, s32[1,256]{1,0:T(1,128)} %bitcast.3, bf16[256,768]{1,0:T(8,128)(2,1)} %rows_hbm.1), custom_call_target="tpu_custom_call" | custom-call | tf_op jit(solution)/shard_map/sort_rows/pallas_call | solution.py:185
  1.9 4.1 %collective-permute-start.1 = (bf16[64,768]{1,0:T(8,128)(2,1)S(1)}, bf16[64,768]{1,0:T(8,128)(2,1)S(1)}, u32[]{:S(2)}, u32[]{:S(2)}) collective-permute-start(bf16[64,768]{1,0:T(8,128)(2,1)S(1)} %get-tuple-element.24), channel_id=1, source_target_pairs={{0,16},{8,24},{16,0},{24,8},{1,17},{9,25},{17,1},{25,9},{2,18},{10... | collective-permute-start | bytes 294920 | tf_op jit(solution)/shard_map/ppermute | solution.py:202
  6.0 1.6 %collective-permute-start = (bf16[64,768]{1,0:T(8,128)(2,1)S(1)}, bf16[64,768]{1,0:T(8,128)(2,1)S(1)}, u32[]{:S(2)}, u32[]{:S(2)}) collective-permute-start(bf16[64,768]{1,0:T(8,128)(2,1)S(1)} %get-tuple-element.23), channel_id=1, source_target_pairs={{0,8},{8,0},{16,24},{24,16},{1,9},{9,1},{17,25},{25,17},{2,10},{10... | collective-permute-start | bytes 294920 | tf_op jit(solution)/shard_map/ppermute | solution.py:202
  7.6 0.0 collective-permute-start.2
  7.6 2.7 %collective-permute-start.5 = (bf16[64,768]{1,0:T(8,128)(2,1)S(1)}, bf16[64,768]{1,0:T(8,128)(2,1)S(1)}, u32[]{:S(2)}, u32[]{:S(2)}) collective-permute-start(bf16[64,768]{1,0:T(8,128)(2,1)S(1)} %get-tuple-element.22), channel_id=1, source_target_pairs={{0,6},{1,7},{2,4},{3,5},{4,2},{5,3},{6,0},{7,1},{8,14},{9,15},{10,... | collective-permute-start | bytes 294920 | tf_op jit(solution)/shard_map/ppermute | solution.py:205
  10.3 0.9 %collective-permute-done = bf16[64,768]{1,0:T(8,128)(2,1)S(1)} collective-permute-done((bf16[64,768]{1,0:T(8,128)(2,1)S(1)}, bf16[64,768]{1,0:T(8,128)(2,1)S(1)}, u32[]{:S(2)}, u32[]{:S(2)}) %collective-permute-start) | collective-permute-done | bytes 98336 | tf_op jit(solution)/shard_map/ppermute | solution.py:202
  11.2 1.6 %collective-permute-start.8 = (bf16[128,768]{1,0:T(8,128)(2,1)S(1)}, bf16[128,768]{1,0:T(8,128)(2,1)S(1)}, u32[]{:S(2)}, u32[]{:S(2)}) collective-permute-start(bf16[128,768]{1,0:T(8,128)(2,1)S(1)} %get-tuple-element.40), channel_id=1, source_target_pairs={{0,2},{1,3},{2,0},{3,1},{4,6},{5,7},{6,4},{7,5},{8,10},{9,11},{10,... | collective-permute-start | bytes 589832 | tf_op jit(solution)/shard_map/ppermute | solution.py:205
  12.8 1.5 %collective-permute-start.9 = (bf16[128,768]{1,0:T(8,128)(2,1)S(1)}, bf16[128,768]{1,0:T(8,128)(2,1)S(1)}, u32[]{:S(2)}, u32[]{:S(2)}) collective-permute-start(bf16[128,768]{1,0:T(8,128)(2,1)S(1)} %get-tuple-element.40), channel_id=1, source_target_pairs={{0,4},{1,5},{2,6},{3,7},{4,0},{5,1},{6,2},{7,3},{8,12},{9,13},{10,... | collective-permute-start | bytes 589832 | tf_op jit(solution)/shard_map/ppermute | solution.py:205
  14.3 0.0 collective-permute-done.5
  14.3 2.6 %collective-permute-start.6 = (bf16[64,768]{1,0:T(8,128)(2,1)S(1)}, bf16[64,768]{1,0:T(8,128)(2,1)S(1)}, u32[]{:S(2)}, u32[]{:S(2)}) collective-permute-start(bf16[64,768]{1,0:T(8,128)(2,1)S(1)} %collective-permute-done), channel_id=1, source_target_pairs={{0,6},{1,7},{2,4},{3,5},{4,2},{5,3},{6,0},{7,1},{8,14},{9,15},{10,... | collective-permute-start | bytes 294920 | tf_op jit(solution)/shard_map/ppermute | solution.py:205
  16.9 0.0 collective-permute-done.1
  16.9 0.6 %collective-permute-start.3 = (bf16[128,768]{1,0:T(8,128)(2,1)S(1)}, bf16[128,768]{1,0:T(8,128)(2,1)S(1)}, u32[]{:S(2)}, u32[]{:S(2)}) collective-permute-start(bf16[128,768]{1,0:T(8,128)(2,1)S(1)} %get-tuple-element.27), channel_id=1, source_target_pairs={{0,2},{1,3},{2,0},{3,1},{4,6},{5,7},{6,4},{7,5},{8,10},{9,11},{10,... | collective-permute-start | bytes 589832 | tf_op jit(solution)/shard_map/ppermute | solution.py:205
  17.5 0.4 collective-permute-start.4
  17.9 4.3 %collective-permute-done.6 = bf16[64,768]{1,0:T(8,128)(2,1)S(1)} collective-permute-done((bf16[64,768]{1,0:T(8,128)(2,1)S(1)}, bf16[64,768]{1,0:T(8,128)(2,1)S(1)}, u32[]{:S(2)}, u32[]{:S(2)}) %collective-permute-start.6) | collective-permute-done | bytes 98336 | tf_op jit(solution)/shard_map/ppermute | solution.py:205
  22.2 1.4 %collective-permute-start.7 = (bf16[128,768]{1,0:T(8,128)(2,1)S(1)}, bf16[128,768]{1,0:T(8,128)(2,1)S(1)}, u32[]{:S(2)}, u32[]{:S(2)}) collective-permute-start(bf16[128,768]{1,0:T(8,128)(2,1)S(1)} %get-tuple-element.27), channel_id=1, source_target_pairs={{0,6},{1,7},{2,4},{3,5},{4,2},{5,3},{6,0},{7,1},{8,14},{9,15},{10,... | collective-permute-start | bytes 589832 | tf_op jit(solution)/shard_map/ppermute | solution.py:205
  23.6 0.0 collective-permute-done.8
  23.6 0.0 collective-permute-done.9
  23.7 0.1 collective-permute-start.10
  23.8 1.7 %collective-permute-done.3 = bf16[128,768]{1,0:T(8,128)(2,1)S(1)} collective-permute-done((bf16[128,768]{1,0:T(8,128)(2,1)S(1)}, bf16[128,768]{1,0:T(8,128)(2,1)S(1)}, u32[]{:S(2)}, u32[]{:S(2)}) %collective-permute-start.3) | collective-permute-done | bytes 196640 | tf_op jit(solution)/shard_map/ppermute | solution.py:205
  25.4 2.4 %collective-permute-done.4 = bf16[128,768]{1,0:T(8,128)(2,1)S(1)} collective-permute-done((bf16[128,768]{1,0:T(8,128)(2,1)S(1)}, bf16[128,768]{1,0:T(8,128)(2,1)S(1)}, u32[]{:S(2)}, u32[]{:S(2)}) %collective-permute-start.4) | collective-permute-done | bytes 196640 | tf_op jit(solution)/shard_map/ppermute | solution.py:205
  27.8 1.0 %collective-permute-done.7 = bf16[128,768]{1,0:T(8,128)(2,1)S(1)} collective-permute-done((bf16[128,768]{1,0:T(8,128)(2,1)S(1)}, bf16[128,768]{1,0:T(8,128)(2,1)S(1)}, u32[]{:S(2)}, u32[]{:S(2)}) %collective-permute-start.7) | collective-permute-done | bytes 196640 | tf_op jit(solution)/shard_map/ppermute | solution.py:205
  28.8 0.1 collective-permute-start.11
  28.9 0.0 collective-permute-done.10.refs_1_
  28.9 1.7 %early_sums.1 = (f32[256,768]{1,0:T(8,128)S(1)}, f32[256,128]{1,0:T(8,128)S(1)}) custom-call(bf16[256,768]{1,0:T(8,128)(2,1)S(1)} %get-tuple-element.48.rows_ref, bf16[512,768]{1,0:T(8,128)(2,1)S(1)} %constant_dynamic-update-slice_fusion.13.refs_0_, bf16[512,768]{1,0:T(8,128)(2,1)S(1)} %collective-permute-done.10.refs_1_), custom_call_target="tpu_custom_call" | custom-call | flops 805306368 | tf_op jit(solution)/shard_map/early_sums/pallas_call | solution.py:237
  30.6 1.0 %middle_sums.1 = (f32[256,768]{1,0:T(8,128)S(1)}, f32[256,128]{1,0:T(8,128)S(1)}) custom-call(bf16[256,768]{1,0:T(8,128)(2,1)S(1)} %get-tuple-element.48.rows_ref, bf16[512,768]{1,0:T(8,128)(2,1)S(1)} %constant_dynamic-update-slice_fusion.6.refs_0_, f32[256,768]{1,0:T(8,128)S(1)} %get-tuple-element.30.refs_1_, f32[256,128]{1,0:T(8,128)S(1)} %get-tuple-element.31.refs_2_), custom_call_target="tpu_custom_call" | custom-call | flops 402653184 | tf_op jit(solution)/shard_map/middle_sums/pallas_call | solution.py:237
  31.6 1.2 %last_sums.1 = (f32[72,768]{1,0:T(8,128)S(1)}, f32[72,768]{1,0:T(8,128)S(1)}, f32[72,768]{1,0:T(8,128)S(1)}, f32[72,768]{1,0:T(8,128)S(1)}) custom-call(bf16[256,768]{1,0:T(8,128)(2,1)S(1)} %get-tuple-element.48.rows_ref, f32[256,768]{1,0:T(8,128)S(1)} %get-tuple-element.32.total_ref, f32[256,128]{1,0:T(8,128)S(1)} %get-tuple-element.33.dens_ref, ...), custom_call_target="tpu_custom_call" | custom-call | flops 402653184 | tf_op jit(solution)/shard_map/last_sums/pallas_call | solution.py:253
  32.8 2.7 %collective-permute-start.12 = (f16[72,768]{1,0:T(8,128)(2,1)S(1)}, f16[72,768]{1,0:T(8,128)(2,1)S(1)}, u32[]{:S(2)}, u32[]{:S(2)}) collective-permute-start(f16[72,768]{1,0:T(8,128)(2,1)S(1)} %convert_element_type.24), channel_id=1, source_target_pairs={{0,24},{8,16},{16,8},{24,0},{1,25},{9,17},{17,9},{25,1},{2,26},{10... | collective-permute-start | bytes 331784 | tf_op jit(solution)/shard_map/ppermute | solution.py:202
  35.5 1.4 %collective-permute-start.13 = (f16[72,768]{1,0:T(8,128)(2,1)S(1)}, f16[72,768]{1,0:T(8,128)(2,1)S(1)}, u32[]{:S(2)}, u32[]{:S(2)}) collective-permute-start(f16[72,768]{1,0:T(8,128)(2,1)S(1)} %convert_element_type.26), channel_id=1, source_target_pairs={{0,16},{8,24},{16,0},{24,8},{1,17},{9,25},{17,1},{25,9},{2,18},{10... | collective-permute-start | bytes 331784 | tf_op jit(solution)/shard_map/ppermute | solution.py:202
  36.9 0.5 %collective-permute-start.14 = (f16[72,768]{1,0:T(8,128)(2,1)S(1)}, f16[72,768]{1,0:T(8,128)(2,1)S(1)}, u32[]{:S(2)}, u32[]{:S(2)}) collective-permute-start(f16[72,768]{1,0:T(8,128)(2,1)S(1)} %convert_element_type.28), channel_id=1, source_target_pairs={{0,8},{8,0},{16,24},{24,16},{1,9},{9,1},{17,25},{25,17},{2,10},{10... | collective-permute-start | bytes 331784 | tf_op jit(solution)/shard_map/ppermute | solution.py:202
  37.4 3.2 %collective-permute-done.12 = f16[72,768]{1,0:T(8,128)(2,1)S(1)} collective-permute-done((f16[72,768]{1,0:T(8,128)(2,1)S(1)}, f16[72,768]{1,0:T(8,128)(2,1)S(1)}, u32[]{:S(2)}, u32[]{:S(2)}) %collective-permute-start.12) | collective-permute-done | bytes 110624 | tf_op jit(solution)/shard_map/ppermute | solution.py:202
  40.6 6.6 %collective-permute-done.13 = f16[72,768]{1,0:T(8,128)(2,1)S(1)} collective-permute-done((f16[72,768]{1,0:T(8,128)(2,1)S(1)}, f16[72,768]{1,0:T(8,128)(2,1)S(1)}, u32[]{:S(2)}, u32[]{:S(2)}) %collective-permute-start.13) | collective-permute-done | bytes 110624 | tf_op jit(solution)/shard_map/ppermute | solution.py:202
  47.3 1.4 %restore_rows.1 = (f32[256,768]{1,0:T(8,128)}, f32[1,256]{1,0:T(1,128)}) custom-call(bf16[256,256]{1,0:T(8,128)(2,1)S(1)} %get-tuple-element.21.chosen_ref, f32[72,768]{1,0:T(8,128)S(1)} %convert_element_type.25.refs_0_, f32[72,768]{1,0:T(8,128)S(1)} %convert_element_type.27.refs_1_, f32[72,768]{1,0:T(8,128)S(1)} %convert_element_type.29.refs_2_, ...), custom_call_target="tpu_custom_call" | custom-call | tf_op jit(solution)/shard_map/restore_rows/pallas_call | solution.py:269
  (21 shorter events, 0.3 us)
Async XLA Ops:
  1.9 14.9 %collective-permute-start.1 = (bf16[64,768]{1,0:T(8,128)(2,1)S(1)}, bf16[64,768]{1,0:T(8,128)(2,1)S(1)}, u32[]{:S(2)}, u32[]{:S(2)}) collective-permute-start(bf16[64,768]{1,0:T(8,128)(2,1)S(1)} %get-tuple-element.24), channel_id=1, source_target_pairs={{0,16},{8,24},{16,0},{24,8},{1,17},{9,25},{17,1},{25,9},{2,18},{10... | collective-permute-start | bytes 294920 | tf_op jit(solution)/shard_map/ppermute | solution.py:202
  6.0 5.1 %collective-permute-start = (bf16[64,768]{1,0:T(8,128)(2,1)S(1)}, bf16[64,768]{1,0:T(8,128)(2,1)S(1)}, u32[]{:S(2)}, u32[]{:S(2)}) collective-permute-start(bf16[64,768]{1,0:T(8,128)(2,1)S(1)} %get-tuple-element.23), channel_id=1, source_target_pairs={{0,8},{8,0},{16,24},{24,16},{1,9},{9,1},{17,25},{25,17},{2,10},{10... | collective-permute-start | bytes 294920 | tf_op jit(solution)/shard_map/ppermute | solution.py:202
  7.6 9.3 %collective-permute-start.2 = (bf16[64,768]{1,0:T(8,128)(2,1)S(1)}, bf16[64,768]{1,0:T(8,128)(2,1)S(1)}, u32[]{:S(2)}, u32[]{:S(2)}) collective-permute-start(bf16[64,768]{1,0:T(8,128)(2,1)S(1)} %get-tuple-element.25), channel_id=1, source_target_pairs={{0,24},{8,16},{16,8},{24,0},{1,25},{9,17},{17,9},{25,1},{2,26},{10... | collective-permute-start | bytes 294920 | tf_op jit(solution)/shard_map/ppermute | solution.py:202
  7.6 6.7 %collective-permute-start.5 = (bf16[64,768]{1,0:T(8,128)(2,1)S(1)}, bf16[64,768]{1,0:T(8,128)(2,1)S(1)}, u32[]{:S(2)}, u32[]{:S(2)}) collective-permute-start(bf16[64,768]{1,0:T(8,128)(2,1)S(1)} %get-tuple-element.22), channel_id=1, source_target_pairs={{0,6},{1,7},{2,4},{3,5},{4,2},{5,3},{6,0},{7,1},{8,14},{9,15},{10,... | collective-permute-start | bytes 294920 | tf_op jit(solution)/shard_map/ppermute | solution.py:205
  11.2 12.4 %collective-permute-start.8 = (bf16[128,768]{1,0:T(8,128)(2,1)S(1)}, bf16[128,768]{1,0:T(8,128)(2,1)S(1)}, u32[]{:S(2)}, u32[]{:S(2)}) collective-permute-start(bf16[128,768]{1,0:T(8,128)(2,1)S(1)} %get-tuple-element.40), channel_id=1, source_target_pairs={{0,2},{1,3},{2,0},{3,1},{4,6},{5,7},{6,4},{7,5},{8,10},{9,11},{10,... | collective-permute-start | bytes 589832 | tf_op jit(solution)/shard_map/ppermute | solution.py:205
  12.8 10.9 %collective-permute-start.9 = (bf16[128,768]{1,0:T(8,128)(2,1)S(1)}, bf16[128,768]{1,0:T(8,128)(2,1)S(1)}, u32[]{:S(2)}, u32[]{:S(2)}) collective-permute-start(bf16[128,768]{1,0:T(8,128)(2,1)S(1)} %get-tuple-element.40), channel_id=1, source_target_pairs={{0,4},{1,5},{2,6},{3,7},{4,0},{5,1},{6,2},{7,3},{8,12},{9,13},{10,... | collective-permute-start | bytes 589832 | tf_op jit(solution)/shard_map/ppermute | solution.py:205
  14.3 7.9 %collective-permute-start.6 = (bf16[64,768]{1,0:T(8,128)(2,1)S(1)}, bf16[64,768]{1,0:T(8,128)(2,1)S(1)}, u32[]{:S(2)}, u32[]{:S(2)}) collective-permute-start(bf16[64,768]{1,0:T(8,128)(2,1)S(1)} %collective-permute-done), channel_id=1, source_target_pairs={{0,6},{1,7},{2,4},{3,5},{4,2},{5,3},{6,0},{7,1},{8,14},{9,15},{10,... | collective-permute-start | bytes 294920 | tf_op jit(solution)/shard_map/ppermute | solution.py:205
  16.9 8.5 %collective-permute-start.3 = (bf16[128,768]{1,0:T(8,128)(2,1)S(1)}, bf16[128,768]{1,0:T(8,128)(2,1)S(1)}, u32[]{:S(2)}, u32[]{:S(2)}) collective-permute-start(bf16[128,768]{1,0:T(8,128)(2,1)S(1)} %get-tuple-element.27), channel_id=1, source_target_pairs={{0,2},{1,3},{2,0},{3,1},{4,6},{5,7},{6,4},{7,5},{8,10},{9,11},{10,... | collective-permute-start | bytes 589832 | tf_op jit(solution)/shard_map/ppermute | solution.py:205
  17.5 10.3 %collective-permute-start.4 = (bf16[128,768]{1,0:T(8,128)(2,1)S(1)}, bf16[128,768]{1,0:T(8,128)(2,1)S(1)}, u32[]{:S(2)}, u32[]{:S(2)}) collective-permute-start(bf16[128,768]{1,0:T(8,128)(2,1)S(1)} %get-tuple-element.27), channel_id=1, source_target_pairs={{0,4},{1,5},{2,6},{3,7},{4,0},{5,1},{6,2},{7,3},{8,12},{9,13},{10,... | collective-permute-start | bytes 589832 | tf_op jit(solution)/shard_map/ppermute | solution.py:205
  22.2 6.6 %collective-permute-start.7 = (bf16[128,768]{1,0:T(8,128)(2,1)S(1)}, bf16[128,768]{1,0:T(8,128)(2,1)S(1)}, u32[]{:S(2)}, u32[]{:S(2)}) collective-permute-start(bf16[128,768]{1,0:T(8,128)(2,1)S(1)} %get-tuple-element.27), channel_id=1, source_target_pairs={{0,6},{1,7},{2,4},{3,5},{4,2},{5,3},{6,0},{7,1},{8,14},{9,15},{10,... | collective-permute-start | bytes 589832 | tf_op jit(solution)/shard_map/ppermute | solution.py:205
  23.7 5.2 %collective-permute-start.10 = (bf16[512,768]{1,0:T(8,128)(2,1)S(1)}, bf16[512,768]{1,0:T(8,128)(2,1)S(1)}, u32[]{:S(2)}, u32[]{:S(2)}) collective-permute-start(bf16[512,768]{1,0:T(8,128)(2,1)S(1)} %constant_dynamic-update-slice_fusion.13.refs_0_), channel_id=1, source_target_pairs={{0,1},{1,0},{2,3},{3,2},{4,5},{5,4},{6,7},{7,6},{8,9},{9,8},{10,11... | collective-permute-start | bytes 2359304 | tf_op jit(solution)/shard_map/ppermute | solution.py:205
  28.8 2.8 %collective-permute-start.11 = (bf16[512,768]{1,0:T(8,128)(2,1)S(1)}, bf16[512,768]{1,0:T(8,128)(2,1)S(1)}, u32[]{:S(2)}, u32[]{:S(2)}) collective-permute-start(bf16[512,768]{1,0:T(8,128)(2,1)S(1)} %constant_dynamic-update-slice_fusion.6.refs_0_), channel_id=1, source_target_pairs={{0,1},{1,0},{2,3},{3,2},{4,5},{5,4},{6,7},{7,6},{8,9},{9,8},{10,11... | collective-permute-start | bytes 2359304 | tf_op jit(solution)/shard_map/ppermute | solution.py:205
  32.8 7.8 %collective-permute-start.12 = (f16[72,768]{1,0:T(8,128)(2,1)S(1)}, f16[72,768]{1,0:T(8,128)(2,1)S(1)}, u32[]{:S(2)}, u32[]{:S(2)}) collective-permute-start(f16[72,768]{1,0:T(8,128)(2,1)S(1)} %convert_element_type.24), channel_id=1, source_target_pairs={{0,24},{8,16},{16,8},{24,0},{1,25},{9,17},{17,9},{25,1},{2,26},{10... | collective-permute-start | bytes 331784 | tf_op jit(solution)/shard_map/ppermute | solution.py:202
  35.5 11.7 %collective-permute-start.13 = (f16[72,768]{1,0:T(8,128)(2,1)S(1)}, f16[72,768]{1,0:T(8,128)(2,1)S(1)}, u32[]{:S(2)}, u32[]{:S(2)}) collective-permute-start(f16[72,768]{1,0:T(8,128)(2,1)S(1)} %convert_element_type.26), channel_id=1, source_target_pairs={{0,16},{8,24},{16,0},{24,8},{1,17},{9,25},{17,1},{25,9},{2,18},{10... | collective-permute-start | bytes 331784 | tf_op jit(solution)/shard_map/ppermute | solution.py:202
  36.9 10.3 %collective-permute-start.14 = (f16[72,768]{1,0:T(8,128)(2,1)S(1)}, f16[72,768]{1,0:T(8,128)(2,1)S(1)}, u32[]{:S(2)}, u32[]{:S(2)}) collective-permute-start(f16[72,768]{1,0:T(8,128)(2,1)S(1)} %convert_element_type.28), channel_id=1, source_target_pairs={{0,8},{8,0},{16,24},{24,16},{1,9},{9,1},{17,25},{25,17},{2,10},{10... | collective-permute-start | bytes 331784 | tf_op jit(solution)/shard_map/ppermute | solution.py:202

commit v3 on v0

--- a/solution.py
+++ b/solution.py
@@ -9,6 +9,8 @@
 from jax.sharding import PartitionSpec as P
 
 beta_scale = 16.0
+floor_weight = math.exp(-beta_scale)
+BLOCK = 256
 LANES = 128
 EXTRA = 8
 TOP = 14.0
@@ -73,50 +75,51 @@
         out_ref[...] = ordered[k * size : (k + 1) * size, :]
 
 
-def inverse_norms(rows):
-    wide = rows.astype(jnp.float32)
-    return lax.rsqrt(jnp.sum(wide * wide, axis=1, keepdims=True) + 1e-06)
-
-
-def add_columns(rows, col_refs, total, dens):
-    count = rows.shape[0]
-    scale = inverse_norms(rows) * (beta_scale * math.log2(math.e))
-    blocks = [
-        (col_ref, start)
-        for col_ref in col_refs
-        for start in range(0, col_ref.shape[0], count)
-    ]
-    for col_ref, start in blocks:
-        cols = col_ref[start : min(start + count, col_ref.shape[0]), :]
-        size = cols.shape[0]
-        col_inv = as_row(inverse_norms(cols))
-        raw = lax.dot_general(
-            rows, cols, (((1,), (1,)), ((), ())), preferred_element_type=jnp.float32
-        )
-        weight = jnp.exp2(raw * scale * col_inv - beta_scale * math.log2(math.e))
-        whole = size - size % LANES
-        for lane in range(0, whole, LANES):
-            dens += weight[:, lane : lane + LANES]
-        if whole < size:
-            part = jnp.sum(weight[:, whole:], axis=1, keepdims=True)
-            dens += jnp.where(lax.broadcasted_iota(jnp.int32, dens.shape, 1) == 0, part, 0.0)
-        coef = (weight * col_inv).astype(jnp.bfloat16)
-        total += jnp.dot(coef, cols, preferred_element_type=jnp.float32)
+def product(left, right, dims):
+    return lax.dot_general(
+        left, right, (dims, ((), ())), preferred_element_type=jnp.float32
+    )
+
+
+def add_columns(rows, scale, col_refs, total, dens):
+    for col_ref in col_refs:
+        for start in range(0, col_ref.shape[0], BLOCK):
+            cols = col_ref[start : min(start + BLOCK, col_ref.shape[0]), :]
+            size = cols.shape[0]
+            squares = jnp.where(diagonal(size), product(cols, cols, ((1,), (1,))), 0.0)
+            col_inv = lax.rsqrt(jnp.sum(squares, axis=0, keepdims=True) + 1e-06)
+            raw = product(rows, cols, ((1,), (1,)))
+            weight = jnp.exp2(raw * scale * col_inv)
+            whole = size - size % LANES
+            for lane in range(0, whole, LANES):
+                dens += weight[:, lane : lane + LANES]
+            if whole < size:
+                part = jnp.sum(weight[:, whole:], axis=1, keepdims=True)
+                lanes = lax.broadcasted_iota(jnp.int32, dens.shape, 1)
+                dens += jnp.where(lanes == 0, part, 0.0)
+            coef = (weight * (col_inv * floor_weight)).astype(jnp.bfloat16)
+            total += product(coef, cols, ((1,), (0,)))
     return total, dens
 
 
-def first_kernel(rows_ref, *refs):
-    col_refs, (total_ref, dens_ref) = refs[:-2], refs[-2:]
+def early_kernel(rows_ref, *refs):
+    col_refs, (scale_ref, total_ref, dens_ref) = refs[:-3], refs[-3:]
+    wide = rows_ref[...].astype(jnp.float32)
+    scale = lax.rsqrt(jnp.sum(wide * wide, axis=1, keepdims=True) + 1e-06)
+    scale = scale * (beta_scale * math.log2(math.e))
+    scale_ref[...] = jnp.broadcast_to(scale, scale_ref.shape)
     total = jnp.zeros(total_ref.shape, jnp.float32)
     dens = jnp.zeros(dens_ref.shape, jnp.float32)
-    total, dens = add_columns(rows_ref[...], col_refs, total, dens)
+    total, dens = add_columns(rows_ref[...], scale, col_refs, total, dens)
     total_ref[...] = total
     dens_ref[...] = dens
 
 
-def middle_kernel(rows_ref, total_ref, dens_ref, *refs):
+def middle_kernel(rows_ref, scale_ref, total_ref, dens_ref, *refs):
     col_refs, (total_out, dens_out) = refs[:-2], refs[-2:]
-    total, dens = add_columns(rows_ref[...], col_refs, total_ref[...], dens_ref[...])
+    total, dens = add_columns(
+        rows_ref[...], scale_ref[:, 0:1], col_refs, total_ref[...], dens_ref[...]
+    )
     total_out[...] = total
     dens_out[...] = dens
 
@@ -125,12 +128,14 @@
     return jnp.floor(jnp.log2(jnp.maximum(value, 1e-30)))
 
 
-def last_kernel(groups, rows_ref, total_ref, dens_ref, *refs):
+def last_kernel(groups, rows_ref, scale_ref, total_ref, dens_ref, *refs):
     col_refs, out_refs = refs[:-groups], refs[-groups:]
     padded, width = out_refs[0].shape
     size = padded - EXTRA
-    total, dens = add_columns(rows_ref[...], col_refs, total_ref[...], dens_ref[...])
-    dens = jnp.sum(dens, axis=1, keepdims=True)
+    total, dens = add_columns(
+        rows_ref[...], scale_ref[:, 0:1], col_refs, total_ref[...], dens_ref[...]
+    )
+    dens = jnp.sum(dens, axis=1, keepdims=True) * floor_weight
     power = exponent(jnp.max(jnp.abs(total), axis=1, keepdims=True))
     total = total * jnp.exp2(TOP - power)
     dens_power = exponent(dens)
@@ -204,9 +209,6 @@
     def along_gc(block, bits):
         return lax.ppermute(block, "gc", [(i, i ^ bits) for i in range(n_gc)])
 
-    def other_core(block):
-        return along_gc(block, 1)
-
     def cost(*blocks):
         pairs = count * sum(block.shape[0] for block in blocks)
         return pl.CostEstimate(
@@ -220,20 +222,22 @@
     chunks = []
     for pieces in (held[:half], held[half:]):
         block = jnp.concatenate(pieces, axis=0)
-        near = [block] + [along_gc(block, k) for k in range(2, n_gc, 2)]
-        chunks.append(jnp.concatenate(near, axis=0))
+        chunks.append([block] + [along_gc(block, k) for k in range(2, n_gc, 2)])
     rows = jnp.concatenate(held, axis=0)
-    chunks[0], rows = lax.optimization_barrier((chunks[0], rows))
-    early = [chunks[0], other_core(chunks[0])]
-
-    total, dens = pl.pallas_call(
-        first_kernel,
+    near = jnp.concatenate(chunks[0], axis=0)
+    near, rows = lax.optimization_barrier((near, rows))
+    late = jnp.concatenate(chunks[1], axis=0)
+    early = [near, along_gc(near, 1)]
+
+    scale, total, dens = pl.pallas_call(
+        early_kernel,
         out_shape=[
+            jax.ShapeDtypeStruct((count, LANES), jnp.float32),
             jax.ShapeDtypeStruct((count, width), jnp.float32),
             jax.ShapeDtypeStruct((count, LANES), jnp.float32),
         ],
-        in_specs=[VMEM] * (1 + len(early)),
-        out_specs=[VMEM] * 2,
+        in_specs=[VMEM] * 3,
+        out_specs=[VMEM] * 3,
         compiler_params=GRANT,
         cost_estimate=cost(*early),
         name="early_sums",
@@ -244,22 +248,22 @@
             jax.ShapeDtypeStruct((count, width), jnp.float32),
             jax.ShapeDtypeStruct((count, LANES), jnp.float32),
         ],
-        in_specs=[VMEM] * 4,
+        in_specs=[VMEM] * 5,
         out_specs=[VMEM] * 2,
         compiler_params=GRANT,
-        cost_estimate=cost(chunks[1]),
+        cost_estimate=cost(late),
         name="middle_sums",
-    )(rows, total, dens, chunks[1])
-    late = [other_core(chunks[1])]
+    )(rows, scale, total, dens, late)
+    late = along_gc(late, 1)
     sums = pl.pallas_call(
         functools.partial(last_kernel, n_gr),
         out_shape=[jax.ShapeDtypeStruct((size + EXTRA, width), jnp.float32)] * n_gr,
-        in_specs=[VMEM] * (3 + len(late)),
+        in_specs=[VMEM] * 5,
         out_specs=[VMEM] * n_gr,
         compiler_params=GRANT,
-        cost_estimate=cost(*late),
+        cost_estimate=cost(late),
         name="last_sums",
-    )(rows, total, dens, *late)[::-1]
+    )(rows, scale, total, dens, late)[::-1]
 
     sent = [part.astype(jnp.float16) for part in sums]
     back = [None] * n_gr

time: 47.1 us -> 47.6 us (1.011)
  Pallas kernels: 6.6 us -> 7.11 us
where the time goes in v3:
time: 47.6 us; the launch traced here: 47.5 us
  waiting for transfers between devices  21.7 us (46%)
  starting transfers between devices  17.6 us (37%)
  Pallas kernels  7.11 us (15%)
  between operations  0.85 us (2%)
    ppermute x6, waiting for transfers between devices, along_gr(): return lax.ppermute(part, 'gr', [(i, i ^ bits) for i in range(n_gr)])  13.6 us
    ppermute x6, starting transfers between devices, along_gr(): return lax.ppermute(part, 'gr', [(i, i ^ bits) for i in range(n_gr)])  10.3 us
    ppermute x8, waiting for transfers between devices, along_gc(): return lax.ppermute(block, 'gc', [(i, i ^ bits) for i in range(n_gc)])  8.05 us
    ppermute x8, starting transfers between devices, along_gc(): return lax.ppermute(block, 'gc', [(i, i ^ bits) for i in range(n_gc)])  7.31 us
    pallas_call x1, Pallas kernels, on_device(): pl.pallas_call(early_kernel, out_shape=[jax.ShapeDtypeStruct((count, LANE...  1.96 us
    pallas_call x1, Pallas kernels, on_device(): pl.pallas_call(restore_kernel, out_shape=[jax.ShapeDtypeStruct((count, wi...  1.44 us
    pallas_call x1, Pallas kernels, on_device(): pl.pallas_call(sort_kernel, out_shape=[jax.ShapeDtypeStruct((count, count...  1.3 us
    pallas_call x1, Pallas kernels, on_device(): pl.pallas_call(functools.partial(last_kernel, n_gr), out_shape=[jax.Shape...  1.28 us
  transfers between devices with their start and end apart: 14, of which 6 were waited for; matrix products, arithmetic and copies ran while one was open for 1% of the time, Pallas kernels for 6%

profile of v3, /device:TPU:0, one launch (start us, length us, event | category | flops | bytes accessed | tf_op | source)
XLA Modules:
  0.0 47.5 jit_solution(12510917091507792345)
XLA Ops:
  0.6 1.3 %sort_rows.1 = (bf16[256,256]{1,0:T(8,128)(2,1)S(1)}, bf16[64,768]{1,0:T(8,128)(2,1)S(1)}, bf16[64,768]{1,0:T(8,128)(2,1)S(1)}, bf16[64,768]{1,0:T(8,128)(2,1)S(1)}, bf16[64,768]{1,0:T(8,128)(2,1)S(1)}) custom-call(s32[1]{0:T(128)} %bitcast.own_ref, s32[1,256]{1,0:T(1,128)} %bitcast.3, bf16[256,768]{1,0:T(8,128)(2,1)} %rows_hbm.1), custom_call_target="tpu_custom_call" | custom-call | tf_op jit(solution)/shard_map/sort_rows/pallas_call | solution.py:190
  1.9 3.1 %collective-permute-start = (bf16[64,768]{1,0:T(8,128)(2,1)S(1)}, bf16[64,768]{1,0:T(8,128)(2,1)S(1)}, u32[]{:S(2)}, u32[]{:S(2)}) collective-permute-start(bf16[64,768]{1,0:T(8,128)(2,1)S(1)} %get-tuple-element.22), channel_id=1, source_target_pairs={{0,8},{8,0},{16,24},{24,16},{1,9},{9,1},{17,25},{25,17},{2,10},{10... | collective-permute-start | bytes 294920 | tf_op jit(solution)/shard_map/ppermute | solution.py:207
  5.0 2.5 %collective-permute-start.5 = (bf16[64,768]{1,0:T(8,128)(2,1)S(1)}, bf16[64,768]{1,0:T(8,128)(2,1)S(1)}, u32[]{:S(2)}, u32[]{:S(2)}) collective-permute-start(bf16[64,768]{1,0:T(8,128)(2,1)S(1)} %get-tuple-element.24), channel_id=1, source_target_pairs={{0,24},{8,16},{16,8},{24,0},{1,25},{9,17},{17,9},{25,1},{2,26},{10... | collective-permute-start | bytes 294920 | tf_op jit(solution)/shard_map/ppermute | solution.py:207
  7.5 0.1 collective-permute-start.4
  7.6 0.2 collective-permute-done
  7.8 1.8 %collective-permute-start.1 = (bf16[128,768]{1,0:T(8,128)(2,1)S(1)}, bf16[128,768]{1,0:T(8,128)(2,1)S(1)}, u32[]{:S(2)}, u32[]{:S(2)}) collective-permute-start(bf16[128,768]{1,0:T(8,128)(2,1)S(1)} %get-tuple-element.42), channel_id=1, source_target_pairs={{0,2},{1,3},{2,0},{3,1},{4,6},{5,7},{6,4},{7,5},{8,10},{9,11},{10,... | collective-permute-start | bytes 589832 | tf_op jit(solution)/shard_map/ppermute | solution.py:210
  9.6 1.5 %collective-permute-start.2 = (bf16[128,768]{1,0:T(8,128)(2,1)S(1)}, bf16[128,768]{1,0:T(8,128)(2,1)S(1)}, u32[]{:S(2)}, u32[]{:S(2)}) collective-permute-start(bf16[128,768]{1,0:T(8,128)(2,1)S(1)} %get-tuple-element.42), channel_id=1, source_target_pairs={{0,4},{1,5},{2,6},{3,7},{4,0},{5,1},{6,2},{7,3},{8,12},{9,13},{10,... | collective-permute-start | bytes 589832 | tf_op jit(solution)/shard_map/ppermute | solution.py:210
  11.2 0.2 collective-permute-start.3
  11.4 5.1 %collective-permute-done.4 = bf16[64,768]{1,0:T(8,128)(2,1)S(1)} collective-permute-done((bf16[64,768]{1,0:T(8,128)(2,1)S(1)}, bf16[64,768]{1,0:T(8,128)(2,1)S(1)}, u32[]{:S(2)}, u32[]{:S(2)}) %collective-permute-start.4) | collective-permute-done | bytes 98336 | tf_op jit(solution)/shard_map/ppermute | solution.py:207
  16.5 0.0 collective-permute-done.5
  16.5 1.6 %collective-permute-start.7 = (bf16[128,768]{1,0:T(8,128)(2,1)S(1)}, bf16[128,768]{1,0:T(8,128)(2,1)S(1)}, u32[]{:S(2)}, u32[]{:S(2)}) collective-permute-start(bf16[128,768]{1,0:T(8,128)(2,1)S(1)} %get-tuple-element.38), channel_id=1, source_target_pairs={{0,2},{1,3},{2,0},{3,1},{4,6},{5,7},{6,4},{7,5},{8,10},{9,11},{10,... | collective-permute-start | bytes 589832 | tf_op jit(solution)/shard_map/ppermute | solution.py:210
  18.1 1.5 %collective-permute-start.8 = (bf16[128,768]{1,0:T(8,128)(2,1)S(1)}, bf16[128,768]{1,0:T(8,128)(2,1)S(1)}, u32[]{:S(2)}, u32[]{:S(2)}) collective-permute-start(bf16[128,768]{1,0:T(8,128)(2,1)S(1)} %get-tuple-element.38), channel_id=1, source_target_pairs={{0,4},{1,5},{2,6},{3,7},{4,0},{5,1},{6,2},{7,3},{8,12},{9,13},{10,... | collective-permute-start | bytes 589832 | tf_op jit(solution)/shard_map/ppermute | solution.py:210
  19.6 0.0 collective-permute-done.1
  19.6 0.5 %collective-permute-start.9 = (bf16[128,768]{1,0:T(8,128)(2,1)S(1)}, bf16[128,768]{1,0:T(8,128)(2,1)S(1)}, u32[]{:S(2)}, u32[]{:S(2)}) collective-permute-start(bf16[128,768]{1,0:T(8,128)(2,1)S(1)} %get-tuple-element.38), channel_id=1, source_target_pairs={{0,6},{1,7},{2,4},{3,5},{4,2},{5,3},{6,0},{7,1},{8,14},{9,15},{10,... | collective-permute-start | bytes 589832 | tf_op jit(solution)/shard_map/ppermute | solution.py:210
  20.2 0.0 collective-permute-done.2
  20.2 0.0 collective-permute-done.3
  20.2 0.1 collective-permute-start.6
  20.3 4.1 %collective-permute-done.7 = bf16[128,768]{1,0:T(8,128)(2,1)S(1)} collective-permute-done((bf16[128,768]{1,0:T(8,128)(2,1)S(1)}, bf16[128,768]{1,0:T(8,128)(2,1)S(1)}, u32[]{:S(2)}, u32[]{:S(2)}) %collective-permute-start.7) | collective-permute-done | bytes 196640 | tf_op jit(solution)/shard_map/ppermute | solution.py:210
  24.4 4.0 %collective-permute-done.8 = bf16[128,768]{1,0:T(8,128)(2,1)S(1)} collective-permute-done((bf16[128,768]{1,0:T(8,128)(2,1)S(1)}, bf16[128,768]{1,0:T(8,128)(2,1)S(1)}, u32[]{:S(2)}, u32[]{:S(2)}) %collective-permute-start.8) | collective-permute-done | bytes 196640 | tf_op jit(solution)/shard_map/ppermute | solution.py:210
  28.4 0.0 collective-permute-done.9
  28.4 0.1 collective-permute-start.10
  28.5 2.0 %early_sums.1 = (f32[256,128]{1,0:T(8,128)S(1)}, f32[256,768]{1,0:T(8,128)S(1)}, f32[256,128]{1,0:T(8,128)S(1)}) custom-call(bf16[256,768]{1,0:T(8,128)(2,1)S(1)} %pad_maximum_fusion.rows_ref, bf16[512,768]{1,0:T(8,128)(2,1)S(1)} %constant_dynamic-update-slice_fusion.2.refs_0_, bf16[512,768]{1,0:T(8,128)(2,1)S(1)} %collective-permute-done.6.refs_1_), custom_call_target="tpu_custom_call" | custom-call | flops 805306368 | tf_op jit(solution)/shard_map/early_sums/pallas_call | solution.py:232
  30.5 1.1 %middle_sums.1 = (f32[256,768]{1,0:T(8,128)S(1)}, f32[256,128]{1,0:T(8,128)S(1)}) custom-call(bf16[256,768]{1,0:T(8,128)(2,1)S(1)} %pad_maximum_fusion.rows_ref, f32[256,128]{1,0:T(8,128)S(1)} %get-tuple-element.27.scale_ref, f32[256,768]{1,0:T(8,128)S(1)} %get-tuple-element.28.total_ref, f32[256,128]{1,0:T(8,128)S(1)} %get-tuple-element.29.dens_ref, ...), custom_call_target="tpu_custom_call" | custom-call | flops 402653184 | tf_op jit(solution)/shard_map/middle_sums/pallas_call | solution.py:245
  31.6 0.0 collective-permute-done.10.refs_0_
  31.6 1.3 %last_sums.1 = (f32[72,768]{1,0:T(8,128)S(1)}, f32[72,768]{1,0:T(8,128)S(1)}, f32[72,768]{1,0:T(8,128)S(1)}, f32[72,768]{1,0:T(8,128)S(1)}) custom-call(bf16[256,768]{1,0:T(8,128)(2,1)S(1)} %pad_maximum_fusion.rows_ref, f32[256,128]{1,0:T(8,128)S(1)} %get-tuple-element.27.scale_ref, f32[256,768]{1,0:T(8,128)S(1)} %get-tuple-element.30.total_ref, ...), custom_call_target="tpu_custom_call" | custom-call | flops 402653184 | tf_op jit(solution)/shard_map/last_sums/pallas_call | solution.py:258
  32.9 3.1 %collective-permute-start.11 = (f16[72,768]{1,0:T(8,128)(2,1)S(1)}, f16[72,768]{1,0:T(8,128)(2,1)S(1)}, u32[]{:S(2)}, u32[]{:S(2)}) collective-permute-start(f16[72,768]{1,0:T(8,128)(2,1)S(1)} %convert_element_type.24), channel_id=1, source_target_pairs={{0,24},{8,16},{16,8},{24,0},{1,25},{9,17},{17,9},{25,1},{2,26},{10... | collective-permute-start | bytes 331784 | tf_op jit(solution)/shard_map/ppermute | solution.py:207
  36.0 0.1 collective-permute-start.12
  36.1 1.4 %collective-permute-start.13 = (f16[72,768]{1,0:T(8,128)(2,1)S(1)}, f16[72,768]{1,0:T(8,128)(2,1)S(1)}, u32[]{:S(2)}, u32[]{:S(2)}) collective-permute-start(f16[72,768]{1,0:T(8,128)(2,1)S(1)} %convert_element_type.28), channel_id=1, source_target_pairs={{0,8},{8,0},{16,24},{24,16},{1,9},{9,1},{17,25},{25,17},{2,10},{10... | collective-permute-start | bytes 331784 | tf_op jit(solution)/shard_map/ppermute | solution.py:207
  37.6 3.2 %collective-permute-done.11 = f16[72,768]{1,0:T(8,128)(2,1)S(1)} collective-permute-done((f16[72,768]{1,0:T(8,128)(2,1)S(1)}, f16[72,768]{1,0:T(8,128)(2,1)S(1)}, u32[]{:S(2)}, u32[]{:S(2)}) %collective-permute-start.11) | collective-permute-done | bytes 110624 | tf_op jit(solution)/shard_map/ppermute | solution.py:207
  40.8 5.2 %collective-permute-done.12 = f16[72,768]{1,0:T(8,128)(2,1)S(1)} collective-permute-done((f16[72,768]{1,0:T(8,128)(2,1)S(1)}, f16[72,768]{1,0:T(8,128)(2,1)S(1)}, u32[]{:S(2)}, u32[]{:S(2)}) %collective-permute-start.12) | collective-permute-done | bytes 110624 | tf_op jit(solution)/shard_map/ppermute | solution.py:207
  46.0 0.0 collective-permute-done.13
  46.0 1.4 %restore_rows.1 = (f32[256,768]{1,0:T(8,128)}, f32[1,256]{1,0:T(1,128)}) custom-call(bf16[256,256]{1,0:T(8,128)(2,1)S(1)} %get-tuple-element.20.chosen_ref, f32[72,768]{1,0:T(8,128)S(1)} %convert_element_type.25.refs_0_, f32[72,768]{1,0:T(8,128)S(1)} %convert_element_type.27.refs_1_, f32[72,768]{1,0:T(8,128)S(1)} %convert_element_type.29.refs_2_, ...), custom_call_target="tpu_custom_call" | custom-call | tf_op jit(solution)/shard_map/restore_rows/pallas_call | solution.py:274
  (19 shorter events, 0.3 us)
Async XLA Ops:
  1.9 5.9 %collective-permute-start = (bf16[64,768]{1,0:T(8,128)(2,1)S(1)}, bf16[64,768]{1,0:T(8,128)(2,1)S(1)}, u32[]{:S(2)}, u32[]{:S(2)}) collective-permute-start(bf16[64,768]{1,0:T(8,128)(2,1)S(1)} %get-tuple-element.22), channel_id=1, source_target_pairs={{0,8},{8,0},{16,24},{24,16},{1,9},{9,1},{17,25},{25,17},{2,10},{10... | collective-permute-start | bytes 294920 | tf_op jit(solution)/shard_map/ppermute | solution.py:207
  5.0 11.4 %collective-permute-start.5 = (bf16[64,768]{1,0:T(8,128)(2,1)S(1)}, bf16[64,768]{1,0:T(8,128)(2,1)S(1)}, u32[]{:S(2)}, u32[]{:S(2)}) collective-permute-start(bf16[64,768]{1,0:T(8,128)(2,1)S(1)} %get-tuple-element.24), channel_id=1, source_target_pairs={{0,24},{8,16},{16,8},{24,0},{1,25},{9,17},{17,9},{25,1},{2,26},{10... | collective-permute-start | bytes 294920 | tf_op jit(solution)/shard_map/ppermute | solution.py:207
  7.5 8.9 %collective-permute-start.4 = (bf16[64,768]{1,0:T(8,128)(2,1)S(1)}, bf16[64,768]{1,0:T(8,128)(2,1)S(1)}, u32[]{:S(2)}, u32[]{:S(2)}) collective-permute-start(bf16[64,768]{1,0:T(8,128)(2,1)S(1)} %get-tuple-element.23), channel_id=1, source_target_pairs={{0,16},{8,24},{16,0},{24,8},{1,17},{9,25},{17,1},{25,9},{2,18},{10... | collective-permute-start | bytes 294920 | tf_op jit(solution)/shard_map/ppermute | solution.py:207
  7.8 11.8 %collective-permute-start.1 = (bf16[128,768]{1,0:T(8,128)(2,1)S(1)}, bf16[128,768]{1,0:T(8,128)(2,1)S(1)}, u32[]{:S(2)}, u32[]{:S(2)}) collective-permute-start(bf16[128,768]{1,0:T(8,128)(2,1)S(1)} %get-tuple-element.42), channel_id=1, source_target_pairs={{0,2},{1,3},{2,0},{3,1},{4,6},{5,7},{6,4},{7,5},{8,10},{9,11},{10,... | collective-permute-start | bytes 589832 | tf_op jit(solution)/shard_map/ppermute | solution.py:210
  9.6 10.5 %collective-permute-start.2 = (bf16[128,768]{1,0:T(8,128)(2,1)S(1)}, bf16[128,768]{1,0:T(8,128)(2,1)S(1)}, u32[]{:S(2)}, u32[]{:S(2)}) collective-permute-start(bf16[128,768]{1,0:T(8,128)(2,1)S(1)} %get-tuple-element.42), channel_id=1, source_target_pairs={{0,4},{1,5},{2,6},{3,7},{4,0},{5,1},{6,2},{7,3},{8,12},{9,13},{10,... | collective-permute-start | bytes 589832 | tf_op jit(solution)/shard_map/ppermute | solution.py:210
  11.2 9.1 %collective-permute-start.3 = (bf16[128,768]{1,0:T(8,128)(2,1)S(1)}, bf16[128,768]{1,0:T(8,128)(2,1)S(1)}, u32[]{:S(2)}, u32[]{:S(2)}) collective-permute-start(bf16[128,768]{1,0:T(8,128)(2,1)S(1)} %get-tuple-element.42), channel_id=1, source_target_pairs={{0,6},{1,7},{2,4},{3,5},{4,2},{5,3},{6,0},{7,1},{8,14},{9,15},{10,... | collective-permute-start | bytes 589832 | tf_op jit(solution)/shard_map/ppermute | solution.py:210
  16.5 7.9 %collective-permute-start.7 = (bf16[128,768]{1,0:T(8,128)(2,1)S(1)}, bf16[128,768]{1,0:T(8,128)(2,1)S(1)}, u32[]{:S(2)}, u32[]{:S(2)}) collective-permute-start(bf16[128,768]{1,0:T(8,128)(2,1)S(1)} %get-tuple-element.38), channel_id=1, source_target_pairs={{0,2},{1,3},{2,0},{3,1},{4,6},{5,7},{6,4},{7,5},{8,10},{9,11},{10,... | collective-permute-start | bytes 589832 | tf_op jit(solution)/shard_map/ppermute | solution.py:210
  18.1 10.3 %collective-permute-start.8 = (bf16[128,768]{1,0:T(8,128)(2,1)S(1)}, bf16[128,768]{1,0:T(8,128)(2,1)S(1)}, u32[]{:S(2)}, u32[]{:S(2)}) collective-permute-start(bf16[128,768]{1,0:T(8,128)(2,1)S(1)} %get-tuple-element.38), channel_id=1, source_target_pairs={{0,4},{1,5},{2,6},{3,7},{4,0},{5,1},{6,2},{7,3},{8,12},{9,13},{10,... | collective-permute-start | bytes 589832 | tf_op jit(solution)/shard_map/ppermute | solution.py:210
  19.6 8.8 %collective-permute-start.9 = (bf16[128,768]{1,0:T(8,128)(2,1)S(1)}, bf16[128,768]{1,0:T(8,128)(2,1)S(1)}, u32[]{:S(2)}, u32[]{:S(2)}) collective-permute-start(bf16[128,768]{1,0:T(8,128)(2,1)S(1)} %get-tuple-element.38), channel_id=1, source_target_pairs={{0,6},{1,7},{2,4},{3,5},{4,2},{5,3},{6,0},{7,1},{8,14},{9,15},{10,... | collective-permute-start | bytes 589832 | tf_op jit(solution)/shard_map/ppermute | solution.py:210
  20.2 8.3 %collective-permute-start.6 = (bf16[512,768]{1,0:T(8,128)(2,1)S(1)}, bf16[512,768]{1,0:T(8,128)(2,1)S(1)}, u32[]{:S(2)}, u32[]{:S(2)}) collective-permute-start(bf16[512,768]{1,0:T(8,128)(2,1)S(1)} %constant_dynamic-update-slice_fusion.2.refs_0_), channel_id=1, source_target_pairs={{0,1},{1,0},{2,3},{3,2},{4,5},{5,4},{6,7},{7,6},{8,9},{9,8},{10,11... | collective-permute-start | bytes 2359304 | tf_op jit(solution)/shard_map/ppermute | solution.py:210
  28.4 3.2 %collective-permute-start.10 = (bf16[512,768]{1,0:T(8,128)(2,1)S(1)}, bf16[512,768]{1,0:T(8,128)(2,1)S(1)}, u32[]{:S(2)}, u32[]{:S(2)}) collective-permute-start(bf16[512,768]{1,0:T(8,128)(2,1)S(1)} %constant_dynamic-update-slice_fusion.9.refs_0_), channel_id=1, source_target_pairs={{0,1},{1,0},{2,3},{3,2},{4,5},{5,4},{6,7},{7,6},{8,9},{9,8},{10,11... | collective-permute-start | bytes 2359304 | tf_op jit(solution)/shard_map/ppermute | solution.py:210
  32.9 7.8 %collective-permute-start.11 = (f16[72,768]{1,0:T(8,128)(2,1)S(1)}, f16[72,768]{1,0:T(8,128)(2,1)S(1)}, u32[]{:S(2)}, u32[]{:S(2)}) collective-permute-start(f16[72,768]{1,0:T(8,128)(2,1)S(1)} %convert_element_type.24), channel_id=1, source_target_pairs={{0,24},{8,16},{16,8},{24,0},{1,25},{9,17},{17,9},{25,1},{2,26},{10... | collective-permute-start | bytes 331784 | tf_op jit(solution)/shard_map/ppermute | solution.py:207
  36.0 9.9 %collective-permute-start.12 = (f16[72,768]{1,0:T(8,128)(2,1)S(1)}, f16[72,768]{1,0:T(8,128)(2,1)S(1)}, u32[]{:S(2)}, u32[]{:S(2)}) collective-permute-start(f16[72,768]{1,0:T(8,128)(2,1)S(1)} %convert_element_type.26), channel_id=1, source_target_pairs={{0,16},{8,24},{16,0},{24,8},{1,17},{9,25},{17,1},{25,9},{2,18},{10... | collective-permute-start | bytes 331784 | tf_op jit(solution)/shard_map/ppermute | solution.py:207
  36.1 9.9 %collective-permute-start.13 = (f16[72,768]{1,0:T(8,128)(2,1)S(1)}, f16[72,768]{1,0:T(8,128)(2,1)S(1)}, u32[]{:S(2)}, u32[]{:S(2)}) collective-permute-start(f16[72,768]{1,0:T(8,128)(2,1)S(1)} %convert_element_type.28), channel_id=1, source_target_pairs={{0,8},{8,0},{16,24},{24,16},{1,9},{9,1},{17,25},{25,17},{2,10},{10... | collective-permute-start | bytes 331784 | tf_op jit(solution)/shard_map/ppermute | solution.py:207

commit v4 on v0

--- a/solution.py
+++ b/solution.py
@@ -125,11 +125,12 @@
     return jnp.floor(jnp.log2(jnp.maximum(value, 1e-30)))
 
 
-def last_kernel(groups, rows_ref, total_ref, dens_ref, *refs):
-    col_refs, out_refs = refs[:-groups], refs[-groups:]
-    padded, width = out_refs[0].shape
-    size = padded - EXTRA
-    total, dens = add_columns(rows_ref[...], col_refs, total_ref[...], dens_ref[...])
+def last_kernel(half, rows_ref, total_ref, dens_ref, cols_ref, *out_refs):
+    groups = len(out_refs) - half
+    size = out_refs[half].shape[0]
+    total, dens = add_columns(
+        rows_ref[...], [cols_ref], total_ref[...], dens_ref[...]
+    )
     dens = jnp.sum(dens, axis=1, keepdims=True)
     power = exponent(jnp.max(jnp.abs(total), axis=1, keepdims=True))
     total = total * jnp.exp2(TOP - power)
@@ -140,26 +141,33 @@
         piece = part.astype(jnp.bfloat16).astype(jnp.float32)
         aside.append(piece * 2.0 ** (8 * k))
         part = part - piece
-    for k, out_ref in enumerate(out_refs[::-1]):
+    for k in range(groups):
         rows = slice(k * size, (k + 1) * size)
-        out_ref[:size, :] = total[rows, :]
-        out_ref[size:, :] = jnp.zeros((EXTRA, width), jnp.float32)
+        out_refs[k][:size, :] = total[rows, :]
+        if k < half:
+            aside_ref, top = out_refs[k], size
+            aside_ref[size:, :] = jnp.zeros((EXTRA, total.shape[1]), jnp.float32)
+        else:
+            aside_ref, top = out_refs[half + k], 0
+            aside_ref[...] = jnp.zeros(aside_ref.shape, jnp.float32)
         for line, column in enumerate(aside):
-            out_ref[size + line : size + line + 1, :size] = as_row(column[rows, :])
-
-
-def restore_kernel(chosen_ref, *refs):
-    part_refs, (total_ref, dens_ref) = refs[:-2], refs[-2:]
-    groups = len(part_refs)
-    size = part_refs[0].shape[0] - EXTRA
+            aside_ref[top + line : top + line + 1, :size] = as_row(column[rows, :])
+
+
+def restore_kernel(half, chosen_ref, *refs):
+    refs, (total_ref, dens_ref) = refs[:-2], refs[-2:]
+    groups = len(refs) - half
+    part_refs = refs[groups - 1 :: -1] + refs[: groups - 1 : -1]
+    size = part_refs[half].shape[0]
     chosen = chosen_ref[...]
     sums, dens = [], []
-    for part_ref in part_refs[::-1]:
+    for k in range(groups):
+        aside_ref, top = (part_refs[k], size) if k < half else (part_refs[half + k], 0)
         power, dens_power, *pieces = [
-            as_column(part_ref[size + line : size + line + 1, :size])
+            as_column(aside_ref[top + line : top + line + 1, :size])
             for line in range(5)
         ]
-        sums.append(part_ref[:size, :] * jnp.exp2(power - TOP))
+        sums.append(part_refs[k][:size, :] * jnp.exp2(power - TOP))
         part = sum(piece * 2.0 ** (-8 * j) for j, piece in enumerate(pieces))
         dens.append(part * jnp.exp2(dens_power))
     dens_ref[...] = jnp.sum(
@@ -252,32 +260,32 @@
     )(rows, total, dens, chunks[1])
     late = [other_core(chunks[1])]
     sums = pl.pallas_call(
-        functools.partial(last_kernel, n_gr),
-        out_shape=[jax.ShapeDtypeStruct((size + EXTRA, width), jnp.float32)] * n_gr,
-        in_specs=[VMEM] * (3 + len(late)),
-        out_specs=[VMEM] * n_gr,
+        functools.partial(last_kernel, half),
+        out_shape=[jax.ShapeDtypeStruct((size + EXTRA, width), jnp.float32)] * half
+        + [jax.ShapeDtypeStruct((size, width), jnp.float32)] * (n_gr - half)
+        + [jax.ShapeDtypeStruct((EXTRA, LANES), jnp.float32)] * (n_gr - half),
+        in_specs=[VMEM] * 4,
+        out_specs=[VMEM] * (2 * n_gr - half),
         compiler_params=GRANT,
         cost_estimate=cost(*late),
         name="last_sums",
-    )(rows, total, dens, *late)[::-1]
-
-    sent = [part.astype(jnp.float16) for part in sums]
-    back = [None] * n_gr
-    back[0] = sent[0]
-    for k in sorted(range(1, n_gr), reverse=True):
-        back[k] = along_gr(sent[k], k)
+    )(rows, total, dens, *late)
+
+    sent = [part.astype(jnp.float16) for part in sums[:n_gr]]
+    back = [sent[0]] + [along_gr(sent[k], k) for k in range(1, n_gr)]
     back = [part.astype(jnp.float32) for part in back]
+    back += [along_gr(sums[half + k], k) for k in range(half, n_gr)]
     neighbour_sum, density = pl.pallas_call(
-        restore_kernel,
+        functools.partial(restore_kernel, half),
         out_shape=[
             jax.ShapeDtypeStruct((count, width), jnp.float32),
             jax.ShapeDtypeStruct((1, count), jnp.float32),
         ],
-        in_specs=[VMEM] * (1 + n_gr),
+        in_specs=[VMEM] * (1 + len(back)),
         out_specs=[VMEM, VMEM],
         compiler_params=GRANT,
         name="restore_rows",
-    )(chosen, *back[::-1])
+    )(chosen, *back[n_gr - 1 :: -1], *back[:n_gr - 1 : -1])
     return (neighbour_sum, density.reshape(count))
 
 

time: 47.1 us -> 46.4 us (0.985)
  waiting for transfers between devices: 21.7 us -> 17.9 us
  starting transfers between devices: 17.6 us -> 20.6 us
    ppermute x6 -> x8, waiting for transfers between devices: 13.6 us -> 9.85 us  [along_gr(): return lax.ppermute(part, 'gr', [(i, i ^ bits) for i in range(n_gr)])]
    ppermute x6 -> x8, starting transfers between devices: 10.3 us -> 13.3 us  [along_gr(): return lax.ppermute(part, 'gr', [(i, i ^ bits) for i in range(n_gr)])]
  transfers between devices with their start and end apart: 14 -> 16, of which waited for: 6 -> 5; matrix products, arithmetic and copies ran while one was open for 1% -> 1% of each run, Pallas kernels for 6% -> 6%
where the time goes in v4:
time: 46.4 us; the launch traced here: 46.2 us
  starting transfers between devices  20.6 us (44%)
  waiting for transfers between devices  17.9 us (39%)
  Pallas kernels  6.6 us (14%)
  between operations  0.87 us (2%)
    ppermute x8, starting transfers between devices, along_gr(): return lax.ppermute(part, 'gr', [(i, i ^ bits) for i in range(n_gr)])  13.3 us
    ppermute x8, waiting for transfers between devices, along_gr(): return lax.ppermute(part, 'gr', [(i, i ^ bits) for i in range(n_gr)])  9.85 us
    ppermute x8, waiting for transfers between devices, along_gc(): return lax.ppermute(block, 'gc', [(i, i ^ bits) for i in range(n_gc)])  8.05 us
    ppermute x8, starting transfers between devices, along_gc(): return lax.ppermute(block, 'gc', [(i, i ^ bits) for i in range(n_gc)])  7.31 us
    pallas_call x1, Pallas kernels, on_device(): pl.pallas_call(first_kernel, out_shape=[jax.ShapeDtypeStruct((count, widt...  1.7 us
    pallas_call x1, Pallas kernels, on_device(): pl.pallas_call(functools.partial(restore_kernel, half), out_shape=[jax.Sh...  1.44 us
    pallas_call x1, Pallas kernels, on_device(): pl.pallas_call(sort_kernel, out_shape=[jax.ShapeDtypeStruct((count, count...  1.3 us
    pallas_call x1, Pallas kernels, on_device(): pl.pallas_call(functools.partial(last_kernel, half), out_shape=[jax.Shape...  1.16 us
  transfers between devices with their start and end apart: 16, of which 5 were waited for; matrix products, arithmetic and copies ran while one was open for 1% of the time, Pallas kernels for 6%

profile of v4, /device:TPU:0, one launch (start us, length us, event | category | flops | bytes accessed | tf_op | source)
XLA Modules:
  0.0 46.2 jit_solution(7119121475019703940)
XLA Ops:
  0.6 1.3 %sort_rows.1 = (bf16[256,256]{1,0:T(8,128)(2,1)S(1)}, bf16[64,768]{1,0:T(8,128)(2,1)S(1)}, bf16[64,768]{1,0:T(8,128)(2,1)S(1)}, bf16[64,768]{1,0:T(8,128)(2,1)S(1)}, bf16[64,768]{1,0:T(8,128)(2,1)S(1)}) custom-call(s32[1]{0:T(128)} %bitcast.own_ref, s32[1,256]{1,0:T(1,128)} %bitcast.3, bf16[256,768]{1,0:T(8,128)(2,1)} %rows_hbm.1), custom_call_target="tpu_custom_call" | custom-call | tf_op jit(solution)/shard_map/sort_rows/pallas_call | solution.py:193
  1.9 3.1 %collective-permute-start = (bf16[64,768]{1,0:T(8,128)(2,1)S(1)}, bf16[64,768]{1,0:T(8,128)(2,1)S(1)}, u32[]{:S(2)}, u32[]{:S(2)}) collective-permute-start(bf16[64,768]{1,0:T(8,128)(2,1)S(1)} %get-tuple-element.23), channel_id=1, source_target_pairs={{0,8},{8,0},{16,24},{24,16},{1,9},{9,1},{17,25},{25,17},{2,10},{10... | collective-permute-start | bytes 294920 | tf_op jit(solution)/shard_map/ppermute | solution.py:210
  5.0 2.5 %collective-permute-start.5 = (bf16[64,768]{1,0:T(8,128)(2,1)S(1)}, bf16[64,768]{1,0:T(8,128)(2,1)S(1)}, u32[]{:S(2)}, u32[]{:S(2)}) collective-permute-start(bf16[64,768]{1,0:T(8,128)(2,1)S(1)} %get-tuple-element.25), channel_id=1, source_target_pairs={{0,24},{8,16},{16,8},{24,0},{1,25},{9,17},{17,9},{25,1},{2,26},{10... | collective-permute-start | bytes 294920 | tf_op jit(solution)/shard_map/ppermute | solution.py:210
  7.5 0.1 collective-permute-start.4
  7.6 0.2 collective-permute-done
  7.8 1.8 %collective-permute-start.1 = (bf16[128,768]{1,0:T(8,128)(2,1)S(1)}, bf16[128,768]{1,0:T(8,128)(2,1)S(1)}, u32[]{:S(2)}, u32[]{:S(2)}) collective-permute-start(bf16[128,768]{1,0:T(8,128)(2,1)S(1)} %get-tuple-element.44), channel_id=1, source_target_pairs={{0,2},{1,3},{2,0},{3,1},{4,6},{5,7},{6,4},{7,5},{8,10},{9,11},{10,... | collective-permute-start | bytes 589832 | tf_op jit(solution)/shard_map/ppermute | solution.py:213
  9.6 1.5 %collective-permute-start.2 = (bf16[128,768]{1,0:T(8,128)(2,1)S(1)}, bf16[128,768]{1,0:T(8,128)(2,1)S(1)}, u32[]{:S(2)}, u32[]{:S(2)}) collective-permute-start(bf16[128,768]{1,0:T(8,128)(2,1)S(1)} %get-tuple-element.44), channel_id=1, source_target_pairs={{0,4},{1,5},{2,6},{3,7},{4,0},{5,1},{6,2},{7,3},{8,12},{9,13},{10,... | collective-permute-start | bytes 589832 | tf_op jit(solution)/shard_map/ppermute | solution.py:213
  11.2 0.2 collective-permute-start.3
  11.4 5.1 %collective-permute-done.4 = bf16[64,768]{1,0:T(8,128)(2,1)S(1)} collective-permute-done((bf16[64,768]{1,0:T(8,128)(2,1)S(1)}, bf16[64,768]{1,0:T(8,128)(2,1)S(1)}, u32[]{:S(2)}, u32[]{:S(2)}) %collective-permute-start.4) | collective-permute-done | bytes 98336 | tf_op jit(solution)/shard_map/ppermute | solution.py:210
  16.5 0.0 collective-permute-done.5
  16.5 1.6 %collective-permute-start.7 = (bf16[128,768]{1,0:T(8,128)(2,1)S(1)}, bf16[128,768]{1,0:T(8,128)(2,1)S(1)}, u32[]{:S(2)}, u32[]{:S(2)}) collective-permute-start(bf16[128,768]{1,0:T(8,128)(2,1)S(1)} %get-tuple-element.40), channel_id=1, source_target_pairs={{0,2},{1,3},{2,0},{3,1},{4,6},{5,7},{6,4},{7,5},{8,10},{9,11},{10,... | collective-permute-start | bytes 589832 | tf_op jit(solution)/shard_map/ppermute | solution.py:213
  18.1 1.5 %collective-permute-start.8 = (bf16[128,768]{1,0:T(8,128)(2,1)S(1)}, bf16[128,768]{1,0:T(8,128)(2,1)S(1)}, u32[]{:S(2)}, u32[]{:S(2)}) collective-permute-start(bf16[128,768]{1,0:T(8,128)(2,1)S(1)} %get-tuple-element.40), channel_id=1, source_target_pairs={{0,4},{1,5},{2,6},{3,7},{4,0},{5,1},{6,2},{7,3},{8,12},{9,13},{10,... | collective-permute-start | bytes 589832 | tf_op jit(solution)/shard_map/ppermute | solution.py:213
  19.6 0.5 %collective-permute-start.9 = (bf16[128,768]{1,0:T(8,128)(2,1)S(1)}, bf16[128,768]{1,0:T(8,128)(2,1)S(1)}, u32[]{:S(2)}, u32[]{:S(2)}) collective-permute-start(bf16[128,768]{1,0:T(8,128)(2,1)S(1)} %get-tuple-element.40), channel_id=1, source_target_pairs={{0,6},{1,7},{2,4},{3,5},{4,2},{5,3},{6,0},{7,1},{8,14},{9,15},{10,... | collective-permute-start | bytes 589832 | tf_op jit(solution)/shard_map/ppermute | solution.py:213
  20.2 0.0 collective-permute-done.2
  20.2 0.0 collective-permute-done.3
  20.2 0.1 collective-permute-start.6
  20.3 4.1 %collective-permute-done.7 = bf16[128,768]{1,0:T(8,128)(2,1)S(1)} collective-permute-done((bf16[128,768]{1,0:T(8,128)(2,1)S(1)}, bf16[128,768]{1,0:T(8,128)(2,1)S(1)}, u32[]{:S(2)}, u32[]{:S(2)}) %collective-permute-start.7) | collective-permute-done | bytes 196640 | tf_op jit(solution)/shard_map/ppermute | solution.py:213
  24.4 4.0 %collective-permute-done.8 = bf16[128,768]{1,0:T(8,128)(2,1)S(1)} collective-permute-done((bf16[128,768]{1,0:T(8,128)(2,1)S(1)}, bf16[128,768]{1,0:T(8,128)(2,1)S(1)}, u32[]{:S(2)}, u32[]{:S(2)}) %collective-permute-start.8) | collective-permute-done | bytes 196640 | tf_op jit(solution)/shard_map/ppermute | solution.py:213
  28.4 0.1 collective-permute-start.10
  28.5 0.0 collective-permute-done.6.refs_1_
  28.5 1.7 %early_sums.1 = (f32[256,768]{1,0:T(8,128)S(1)}, f32[256,128]{1,0:T(8,128)S(1)}) custom-call(bf16[256,768]{1,0:T(8,128)(2,1)S(1)} %pad_maximum_fusion.rows_ref, bf16[512,768]{1,0:T(8,128)(2,1)S(1)} %constant_dynamic-update-slice_fusion.2.refs_0_, bf16[512,768]{1,0:T(8,128)(2,1)S(1)} %collective-permute-done.6.refs_1_), custom_call_target="tpu_custom_call" | custom-call | flops 805306368 | tf_op jit(solution)/shard_map/early_sums/pallas_call | solution.py:237
  30.2 1.0 %middle_sums.1 = (f32[256,768]{1,0:T(8,128)S(1)}, f32[256,128]{1,0:T(8,128)S(1)}) custom-call(bf16[256,768]{1,0:T(8,128)(2,1)S(1)} %pad_maximum_fusion.rows_ref, f32[256,768]{1,0:T(8,128)S(1)} %get-tuple-element.28.total_ref, f32[256,128]{1,0:T(8,128)S(1)} %get-tuple-element.29.dens_ref, bf16[512,768]{1,0:T(8,128)(2,1)S(1)} %constant_dynamic-update-slice_fusion.9.refs_0_), custom_call_target="tpu_custom_call" | custom-call | flops 402653184 | tf_op jit(solution)/shard_map/middle_sums/pallas_call | solution.py:249
  31.2 0.0 collective-permute-done.10.cols_ref
  31.2 1.2 %last_sums.1 = (f32[72,768]{1,0:T(8,128)S(1)}, f32[72,768]{1,0:T(8,128)S(1)}, f32[64,768]{1,0:T(8,128)S(1)}, f32[64,768]{1,0:T(8,128)S(1)}, f32[8,128]{1,0:T(8,128)S(1)}, /*index=5*/f32[8,128]{1,0:T(8,128)S(1)}) custom-call(bf16[256,768]{1,0:T(8,128)(2,1)S(1)} %pad_maximum_fusion.rows_ref, f32[256,768]{1,0:T(8,128)S(1)} %get-tuple-element.30.total_ref, ...), custom_call_target="tpu_custom_call" | custom-call | flops 402653184 | tf_op jit(solution)/shard_map/last_sums/pallas_call | solution.py:262
  32.4 3.1 %collective-permute-start.11 = (f16[64,768]{1,0:T(8,128)(2,1)S(1)}, f16[64,768]{1,0:T(8,128)(2,1)S(1)}, u32[]{:S(2)}, u32[]{:S(2)}) collective-permute-start(f16[64,768]{1,0:T(8,128)(2,1)S(1)} %convert_element_type.24), channel_id=1, source_target_pairs={{0,24},{8,16},{16,8},{24,0},{1,25},{9,17},{17,9},{25,1},{2,26},{10... | collective-permute-start | bytes 294920 | tf_op jit(solution)/shard_map/ppermute | solution.py:210
  35.5 0.1 collective-permute-start.12
  35.6 1.4 %collective-permute-start.13 = (f16[72,768]{1,0:T(8,128)(2,1)S(1)}, f16[72,768]{1,0:T(8,128)(2,1)S(1)}, u32[]{:S(2)}, u32[]{:S(2)}) collective-permute-start(f16[72,768]{1,0:T(8,128)(2,1)S(1)} %convert_element_type.28), channel_id=1, source_target_pairs={{0,8},{8,0},{16,24},{24,16},{1,9},{9,1},{17,25},{25,17},{2,10},{10... | collective-permute-start | bytes 331784 | tf_op jit(solution)/shard_map/ppermute | solution.py:210
  37.0 3.0 %collective-permute-start.14 = (f32[8,128]{1,0:T(8,128)S(1)}, f32[8,128]{1,0:T(8,128)S(1)}, u32[]{:S(2)}, u32[]{:S(2)}) collective-permute-start(f32[8,128]{1,0:T(8,128)S(1)} %get-tuple-element.36), channel_id=1, source_target_pairs={{0,24},{8,16},{16,8},{24,0},{1,25},{9,17},{17,9},{25,1},{2,26},{10... | collective-permute-start | bytes 12296 | tf_op jit(solution)/shard_map/ppermute | solution.py:210
  40.1 0.0 collective-permute-start.15
  40.1 4.6 %collective-permute-done.12 = f16[64,768]{1,0:T(8,128)(2,1)S(1)} collective-permute-done((f16[64,768]{1,0:T(8,128)(2,1)S(1)}, f16[64,768]{1,0:T(8,128)(2,1)S(1)}, u32[]{:S(2)}, u32[]{:S(2)}) %collective-permute-start.12) | collective-permute-done | bytes 98336 | tf_op jit(solution)/shard_map/ppermute | solution.py:210
  44.8 0.0 collective-permute-done.15.refs_5_
  44.8 1.4 %restore_rows.1 = (f32[256,768]{1,0:T(8,128)}, f32[1,256]{1,0:T(1,128)}) custom-call(bf16[256,256]{1,0:T(8,128)(2,1)S(1)} %get-tuple-element.21.chosen_ref, f32[64,768]{1,0:T(8,128)S(1)} %convert_element_type.25.refs_0_, f32[64,768]{1,0:T(8,128)S(1)} %convert_element_type.27.refs_1_, f32[72,768]{1,0:T(8,128)S(1)} %convert_element_type.29.refs_2_, ...), custom_call_target="tpu_custom_call" | custom-call | tf_op jit(solution)/shard_map/restore_rows/pallas_call | solution.py:278
  (23 shorter events, 0.3 us)
Async XLA Ops:
  1.9 5.9 %collective-permute-start = (bf16[64,768]{1,0:T(8,128)(2,1)S(1)}, bf16[64,768]{1,0:T(8,128)(2,1)S(1)}, u32[]{:S(2)}, u32[]{:S(2)}) collective-permute-start(bf16[64,768]{1,0:T(8,128)(2,1)S(1)} %get-tuple-element.23), channel_id=1, source_target_pairs={{0,8},{8,0},{16,24},{24,16},{1,9},{9,1},{17,25},{25,17},{2,10},{10... | collective-permute-start | bytes 294920 | tf_op jit(solution)/shard_map/ppermute | solution.py:210
  5.0 11.4 %collective-permute-start.5 = (bf16[64,768]{1,0:T(8,128)(2,1)S(1)}, bf16[64,768]{1,0:T(8,128)(2,1)S(1)}, u32[]{:S(2)}, u32[]{:S(2)}) collective-permute-start(bf16[64,768]{1,0:T(8,128)(2,1)S(1)} %get-tuple-element.25), channel_id=1, source_target_pairs={{0,24},{8,16},{16,8},{24,0},{1,25},{9,17},{17,9},{25,1},{2,26},{10... | collective-permute-start | bytes 294920 | tf_op jit(solution)/shard_map/ppermute | solution.py:210
  7.5 8.9 %collective-permute-start.4 = (bf16[64,768]{1,0:T(8,128)(2,1)S(1)}, bf16[64,768]{1,0:T(8,128)(2,1)S(1)}, u32[]{:S(2)}, u32[]{:S(2)}) collective-permute-start(bf16[64,768]{1,0:T(8,128)(2,1)S(1)} %get-tuple-element.24), channel_id=1, source_target_pairs={{0,16},{8,24},{16,0},{24,8},{1,17},{9,25},{17,1},{25,9},{2,18},{10... | collective-permute-start | bytes 294920 | tf_op jit(solution)/shard_map/ppermute | solution.py:210
  7.8 11.8 %collective-permute-start.1 = (bf16[128,768]{1,0:T(8,128)(2,1)S(1)}, bf16[128,768]{1,0:T(8,128)(2,1)S(1)}, u32[]{:S(2)}, u32[]{:S(2)}) collective-permute-start(bf16[128,768]{1,0:T(8,128)(2,1)S(1)} %get-tuple-element.44), channel_id=1, source_target_pairs={{0,2},{1,3},{2,0},{3,1},{4,6},{5,7},{6,4},{7,5},{8,10},{9,11},{10,... | collective-permute-start | bytes 589832 | tf_op jit(solution)/shard_map/ppermute | solution.py:213
  9.6 10.5 %collective-permute-start.2 = (bf16[128,768]{1,0:T(8,128)(2,1)S(1)}, bf16[128,768]{1,0:T(8,128)(2,1)S(1)}, u32[]{:S(2)}, u32[]{:S(2)}) collective-permute-start(bf16[128,768]{1,0:T(8,128)(2,1)S(1)} %get-tuple-element.44), channel_id=1, source_target_pairs={{0,4},{1,5},{2,6},{3,7},{4,0},{5,1},{6,2},{7,3},{8,12},{9,13},{10,... | collective-permute-start | bytes 589832 | tf_op jit(solution)/shard_map/ppermute | solution.py:213
  11.2 9.1 %collective-permute-start.3 = (bf16[128,768]{1,0:T(8,128)(2,1)S(1)}, bf16[128,768]{1,0:T(8,128)(2,1)S(1)}, u32[]{:S(2)}, u32[]{:S(2)}) collective-permute-start(bf16[128,768]{1,0:T(8,128)(2,1)S(1)} %get-tuple-element.44), channel_id=1, source_target_pairs={{0,6},{1,7},{2,4},{3,5},{4,2},{5,3},{6,0},{7,1},{8,14},{9,15},{10,... | collective-permute-start | bytes 589832 | tf_op jit(solution)/shard_map/ppermute | solution.py:213
  16.5 7.9 %collective-permute-start.7 = (bf16[128,768]{1,0:T(8,128)(2,1)S(1)}, bf16[128,768]{1,0:T(8,128)(2,1)S(1)}, u32[]{:S(2)}, u32[]{:S(2)}) collective-permute-start(bf16[128,768]{1,0:T(8,128)(2,1)S(1)} %get-tuple-element.40), channel_id=1, source_target_pairs={{0,2},{1,3},{2,0},{3,1},{4,6},{5,7},{6,4},{7,5},{8,10},{9,11},{10,... | collective-permute-start | bytes 589832 | tf_op jit(solution)/shard_map/ppermute | solution.py:213
  18.1 10.3 %collective-permute-start.8 = (bf16[128,768]{1,0:T(8,128)(2,1)S(1)}, bf16[128,768]{1,0:T(8,128)(2,1)S(1)}, u32[]{:S(2)}, u32[]{:S(2)}) collective-permute-start(bf16[128,768]{1,0:T(8,128)(2,1)S(1)} %get-tuple-element.40), channel_id=1, source_target_pairs={{0,4},{1,5},{2,6},{3,7},{4,0},{5,1},{6,2},{7,3},{8,12},{9,13},{10,... | collective-permute-start | bytes 589832 | tf_op jit(solution)/shard_map/ppermute | solution.py:213
  19.6 8.8 %collective-permute-start.9 = (bf16[128,768]{1,0:T(8,128)(2,1)S(1)}, bf16[128,768]{1,0:T(8,128)(2,1)S(1)}, u32[]{:S(2)}, u32[]{:S(2)}) collective-permute-start(bf16[128,768]{1,0:T(8,128)(2,1)S(1)} %get-tuple-element.40), channel_id=1, source_target_pairs={{0,6},{1,7},{2,4},{3,5},{4,2},{5,3},{6,0},{7,1},{8,14},{9,15},{10,... | collective-permute-start | bytes 589832 | tf_op jit(solution)/shard_map/ppermute | solution.py:213
  20.2 8.3 %collective-permute-start.6 = (bf16[512,768]{1,0:T(8,128)(2,1)S(1)}, bf16[512,768]{1,0:T(8,128)(2,1)S(1)}, u32[]{:S(2)}, u32[]{:S(2)}) collective-permute-start(bf16[512,768]{1,0:T(8,128)(2,1)S(1)} %constant_dynamic-update-slice_fusion.2.refs_0_), channel_id=1, source_target_pairs={{0,1},{1,0},{2,3},{3,2},{4,5},{5,4},{6,7},{7,6},{8,9},{9,8},{10,11... | collective-permute-start | bytes 2359304 | tf_op jit(solution)/shard_map/ppermute | solution.py:213
  28.4 2.8 %collective-permute-start.10 = (bf16[512,768]{1,0:T(8,128)(2,1)S(1)}, bf16[512,768]{1,0:T(8,128)(2,1)S(1)}, u32[]{:S(2)}, u32[]{:S(2)}) collective-permute-start(bf16[512,768]{1,0:T(8,128)(2,1)S(1)} %constant_dynamic-update-slice_fusion.9.refs_0_), channel_id=1, source_target_pairs={{0,1},{1,0},{2,3},{3,2},{4,5},{5,4},{6,7},{7,6},{8,9},{9,8},{10,11... | collective-permute-start | bytes 2359304 | tf_op jit(solution)/shard_map/ppermute | solution.py:213
  32.4 7.7 %collective-permute-start.11 = (f16[64,768]{1,0:T(8,128)(2,1)S(1)}, f16[64,768]{1,0:T(8,128)(2,1)S(1)}, u32[]{:S(2)}, u32[]{:S(2)}) collective-permute-start(f16[64,768]{1,0:T(8,128)(2,1)S(1)} %convert_element_type.24), channel_id=1, source_target_pairs={{0,24},{8,16},{16,8},{24,0},{1,25},{9,17},{17,9},{25,1},{2,26},{10... | collective-permute-start | bytes 294920 | tf_op jit(solution)/shard_map/ppermute | solution.py:210
  35.5 9.2 %collective-permute-start.12 = (f16[64,768]{1,0:T(8,128)(2,1)S(1)}, f16[64,768]{1,0:T(8,128)(2,1)S(1)}, u32[]{:S(2)}, u32[]{:S(2)}) collective-permute-start(f16[64,768]{1,0:T(8,128)(2,1)S(1)} %convert_element_type.26), channel_id=1, source_target_pairs={{0,16},{8,24},{16,0},{24,8},{1,17},{9,25},{17,1},{25,9},{2,18},{10... | collective-permute-start | bytes 294920 | tf_op jit(solution)/shard_map/ppermute | solution.py:210
  35.6 9.1 %collective-permute-start.13 = (f16[72,768]{1,0:T(8,128)(2,1)S(1)}, f16[72,768]{1,0:T(8,128)(2,1)S(1)}, u32[]{:S(2)}, u32[]{:S(2)}) collective-permute-start(f16[72,768]{1,0:T(8,128)(2,1)S(1)} %convert_element_type.28), channel_id=1, source_target_pairs={{0,8},{8,0},{16,24},{24,16},{1,9},{9,1},{17,25},{25,17},{2,10},{10... | collective-permute-start | bytes 331784 | tf_op jit(solution)/shard_map/ppermute | solution.py:210
  37.0 7.7 %collective-permute-start.14 = (f32[8,128]{1,0:T(8,128)S(1)}, f32[8,128]{1,0:T(8,128)S(1)}, u32[]{:S(2)}, u32[]{:S(2)}) collective-permute-start(f32[8,128]{1,0:T(8,128)S(1)} %get-tuple-element.36), channel_id=1, source_target_pairs={{0,24},{8,16},{16,8},{24,0},{1,25},{9,17},{17,9},{25,1},{2,26},{10... | collective-permute-start | bytes 12296 | tf_op jit(solution)/shard_map/ppermute | solution.py:210
  40.1 4.7 %collective-permute-start.15 = (f32[8,128]{1,0:T(8,128)S(1)}, f32[8,128]{1,0:T(8,128)S(1)}, u32[]{:S(2)}, u32[]{:S(2)}) collective-permute-start(f32[8,128]{1,0:T(8,128)S(1)} %get-tuple-element.37), channel_id=1, source_target_pairs={{0,16},{8,24},{16,0},{24,8},{1,17},{9,25},{17,1},{25,9},{2,18},{10... | collective-permute-start | bytes 12296 | tf_op jit(solution)/shard_map/ppermute | solution.py:210

commit v5 on v4

--- a/solution.py
+++ b/solution.py
@@ -225,12 +225,17 @@
 
     held = [parts[0]] + [along_gr(parts[k], k) for k in range(1, n_gr)]
     half = n_gr // 2
-    chunks = []
-    for pieces in (held[:half], held[half:]):
-        block = jnp.concatenate(pieces, axis=0)
-        near = [block] + [along_gc(block, k) for k in range(2, n_gc, 2)]
-        chunks.append(jnp.concatenate(near, axis=0))
+    sides = [k for k in range(2, n_gc, 2) if not k & (k - 1)]
+    pair = jnp.concatenate(held[1:half], axis=0)
+    block = jnp.concatenate(held[:half], axis=0)
+    late = jnp.concatenate(held[half:], axis=0)
+    own_near = [along_gc(held[0], k) for k in sides]
+    own_near, pair = lax.optimization_barrier((own_near, pair))
+    pair_near = [along_gc(pair, k) for k in sides]
+    both_near = [along_gc(block, k) for k in range(2, n_gc, 2) if k not in sides]
     rows = jnp.concatenate(held, axis=0)
+    late_near = [along_gc(late, k) for k in range(2, n_gc, 2)]
+    chunks = [jnp.concatenate(both_near + pair_near + own_near + [block], axis=0), jnp.concatenate([late] + late_near, axis=0)]
     chunks[0], rows = lax.optimization_barrier((chunks[0], rows))
     early = [chunks[0], other_core(chunks[0])]
 

time: 46.4 us -> 47 us (1.013)
  starting transfers between devices: 20.6 us -> 23.2 us
  waiting for transfers between devices: 17.9 us -> 15.9 us
    ppermute x8 -> x10, starting transfers between devices: 7.31 us -> 10.3 us  [along_gc(): return lax.ppermute(block, 'gc', [(i, i ^ bits) for i in range(n_gc)])]
    ppermute x8, waiting for transfers between devices: 9.85 us -> 8.72 us  [along_gr(): return lax.ppermute(part, 'gr', [(i, i ^ bits) for i in range(n_gr)])]
    ppermute x8 -> x10, waiting for transfers between devices: 8.05 us -> 7.16 us  [along_gc(): return lax.ppermute(block, 'gc', [(i, i ^ bits) for i in range(n_gc)])]
  transfers between devices with their start and end apart: 16 -> 18, of which waited for: 5 -> 7; matrix products, arithmetic and copies ran while one was open for 1% -> 1% of each run, Pallas kernels for 6% -> 6%
where the time goes in v5:
time: 47 us; the launch traced here: 46.8 us
  starting transfers between devices  23.2 us (49%)
  waiting for transfers between devices  15.9 us (34%)
  Pallas kernels  6.6 us (14%)
  between operations  0.87 us (2%)
    ppermute x8, starting transfers between devices, along_gr(): return lax.ppermute(part, 'gr', [(i, i ^ bits) for i in range(n_gr)])  12.9 us
    ppermute x10, starting transfers between devices, along_gc(): return lax.ppermute(block, 'gc', [(i, i ^ bits) for i in range(n_gc)])  10.3 us
    ppermute x8, waiting for transfers between devices, along_gr(): return lax.ppermute(part, 'gr', [(i, i ^ bits) for i in range(n_gr)])  8.72 us
    ppermute x10, waiting for transfers between devices, along_gc(): return lax.ppermute(block, 'gc', [(i, i ^ bits) for i in range(n_gc)])  7.16 us
    pallas_call x1, Pallas kernels, on_device(): pl.pallas_call(first_kernel, out_shape=[jax.ShapeDtypeStruct((count, widt...  1.7 us
    pallas_call x1, Pallas kernels, on_device(): pl.pallas_call(functools.partial(restore_kernel, half), out_shape=[jax.Sh...  1.44 us
    pallas_call x1, Pallas kernels, on_device(): pl.pallas_call(sort_kernel, out_shape=[jax.ShapeDtypeStruct((count, count...  1.3 us
    pallas_call x1, Pallas kernels, on_device(): pl.pallas_call(functools.partial(last_kernel, half), out_shape=[jax.Shape...  1.16 us
  transfers between devices with their start and end apart: 18, of which 7 were waited for; matrix products, arithmetic and copies ran while one was open for 1% of the time, Pallas kernels for 6%

profile of v5, /device:TPU:0, one launch (start us, length us, event | category | flops | bytes accessed | tf_op | source)
XLA Modules:
  0.0 46.8 jit_solution(11421916233209230)
XLA Ops:
  0.6 1.3 %sort_rows.1 = (bf16[256,256]{1,0:T(8,128)(2,1)S(1)}, bf16[64,768]{1,0:T(8,128)(2,1)S(1)}, bf16[64,768]{1,0:T(8,128)(2,1)S(1)}, bf16[64,768]{1,0:T(8,128)(2,1)S(1)}, bf16[64,768]{1,0:T(8,128)(2,1)S(1)}) custom-call(s32[1]{0:T(128)} %bitcast.own_ref, s32[1,256]{1,0:T(1,128)} %bitcast.3, bf16[256,768]{1,0:T(8,128)(2,1)} %rows_hbm.1), custom_call_target="tpu_custom_call" | custom-call | tf_op jit(solution)/shard_map/sort_rows/pallas_call | solution.py:193
  1.9 3.1 %collective-permute-start = (bf16[64,768]{1,0:T(8,128)(2,1)S(1)}, bf16[64,768]{1,0:T(8,128)(2,1)S(1)}, u32[]{:S(2)}, u32[]{:S(2)}) collective-permute-start(bf16[64,768]{1,0:T(8,128)(2,1)S(1)} %get-tuple-element.26), channel_id=1, source_target_pairs={{0,8},{8,0},{16,24},{24,16},{1,9},{9,1},{17,25},{25,17},{2,10},{10... | collective-permute-start | bytes 294920 | tf_op jit(solution)/shard_map/ppermute | solution.py:210
  5.0 1.5 %collective-permute-start.2 = (bf16[64,768]{1,0:T(8,128)(2,1)S(1)}, bf16[64,768]{1,0:T(8,128)(2,1)S(1)}, u32[]{:S(2)}, u32[]{:S(2)}) collective-permute-start(bf16[64,768]{1,0:T(8,128)(2,1)S(1)} %get-tuple-element.25), channel_id=1, source_target_pairs={{0,2},{1,3},{2,0},{3,1},{4,6},{5,7},{6,4},{7,5},{8,10},{9,11},{10,... | collective-permute-start | bytes 294920 | tf_op jit(solution)/shard_map/ppermute | solution.py:213
  6.5 1.5 %collective-permute-start.3 = (bf16[64,768]{1,0:T(8,128)(2,1)S(1)}, bf16[64,768]{1,0:T(8,128)(2,1)S(1)}, u32[]{:S(2)}, u32[]{:S(2)}) collective-permute-start(bf16[64,768]{1,0:T(8,128)(2,1)S(1)} %get-tuple-element.25), channel_id=1, source_target_pairs={{0,4},{1,5},{2,6},{3,7},{4,0},{5,1},{6,2},{7,3},{8,12},{9,13},{10,... | collective-permute-start | bytes 294920 | tf_op jit(solution)/shard_map/ppermute | solution.py:213
  8.0 2.5 %collective-permute-start.7 = (bf16[64,768]{1,0:T(8,128)(2,1)S(1)}, bf16[64,768]{1,0:T(8,128)(2,1)S(1)}, u32[]{:S(2)}, u32[]{:S(2)}) collective-permute-start(bf16[64,768]{1,0:T(8,128)(2,1)S(1)} %get-tuple-element.31), channel_id=1, source_target_pairs={{0,24},{8,16},{16,8},{24,0},{1,25},{9,17},{17,9},{25,1},{2,26},{10... | collective-permute-start | bytes 294920 | tf_op jit(solution)/shard_map/ppermute | solution.py:210
  10.5 0.1 collective-permute-start.6
  10.6 0.5 %collective-permute-done.3 = bf16[64,768]{1,0:T(8,128)(2,1)S(1)} collective-permute-done((bf16[64,768]{1,0:T(8,128)(2,1)S(1)}, bf16[64,768]{1,0:T(8,128)(2,1)S(1)}, u32[]{:S(2)}, u32[]{:S(2)}) %collective-permute-start.3) | collective-permute-done | bytes 98336 | tf_op jit(solution)/shard_map/ppermute | solution.py:213
  11.1 0.5 %collective-permute-start.4 = (bf16[64,768]{1,0:T(8,128)(2,1)S(1)}, bf16[64,768]{1,0:T(8,128)(2,1)S(1)}, u32[]{:S(2)}, u32[]{:S(2)}) collective-permute-start(bf16[64,768]{1,0:T(8,128)(2,1)S(1)} %collective-permute-done), channel_id=1, source_target_pairs={{0,2},{1,3},{2,0},{3,1},{4,6},{5,7},{6,4},{7,5},{8,10},{9,11},{10,... | collective-permute-start | bytes 294920 | tf_op jit(solution)/shard_map/ppermute | solution.py:213
  11.7 1.5 %collective-permute-start.5 = (bf16[64,768]{1,0:T(8,128)(2,1)S(1)}, bf16[64,768]{1,0:T(8,128)(2,1)S(1)}, u32[]{:S(2)}, u32[]{:S(2)}) collective-permute-start(bf16[64,768]{1,0:T(8,128)(2,1)S(1)} %collective-permute-done), channel_id=1, source_target_pairs={{0,4},{1,5},{2,6},{3,7},{4,0},{5,1},{6,2},{7,3},{8,12},{9,13},{10,... | collective-permute-start | bytes 294920 | tf_op jit(solution)/shard_map/ppermute | solution.py:213
  13.2 1.5 %collective-permute-start.1 = (bf16[128,768]{1,0:T(8,128)(2,1)S(1)}, bf16[128,768]{1,0:T(8,128)(2,1)S(1)}, u32[]{:S(2)}, u32[]{:S(2)}) collective-permute-start(bf16[128,768]{1,0:T(8,128)(2,1)S(1)} %pad_maximum_fusion.1), channel_id=1, source_target_pairs={{0,6},{1,7},{2,4},{3,5},{4,2},{5,3},{6,0},{7,1},{8,14},{9,15},{10,... | collective-permute-start | bytes 589832 | tf_op jit(solution)/shard_map/ppermute | solution.py:213
  14.7 4.2 %collective-permute-done.6 = bf16[64,768]{1,0:T(8,128)(2,1)S(1)} collective-permute-done((bf16[64,768]{1,0:T(8,128)(2,1)S(1)}, bf16[64,768]{1,0:T(8,128)(2,1)S(1)}, u32[]{:S(2)}, u32[]{:S(2)}) %collective-permute-start.6) | collective-permute-done | bytes 98336 | tf_op jit(solution)/shard_map/ppermute | solution.py:210
  18.9 0.0 collective-permute-done.7
  19.0 0.6 %collective-permute-start.9 = (bf16[128,768]{1,0:T(8,128)(2,1)S(1)}, bf16[128,768]{1,0:T(8,128)(2,1)S(1)}, u32[]{:S(2)}, u32[]{:S(2)}) collective-permute-start(bf16[128,768]{1,0:T(8,128)(2,1)S(1)} %get-tuple-element.46), channel_id=1, source_target_pairs={{0,2},{1,3},{2,0},{3,1},{4,6},{5,7},{6,4},{7,5},{8,10},{9,11},{10,... | collective-permute-start | bytes 589832 | tf_op jit(solution)/shard_map/ppermute | solution.py:213
  19.6 0.7 %collective-permute-start.10 = (bf16[128,768]{1,0:T(8,128)(2,1)S(1)}, bf16[128,768]{1,0:T(8,128)(2,1)S(1)}, u32[]{:S(2)}, u32[]{:S(2)}) collective-permute-start(bf16[128,768]{1,0:T(8,128)(2,1)S(1)} %get-tuple-element.46), channel_id=1, source_target_pairs={{0,4},{1,5},{2,6},{3,7},{4,0},{5,1},{6,2},{7,3},{8,12},{9,13},{10,... | collective-permute-start | bytes 589832 | tf_op jit(solution)/shard_map/ppermute | solution.py:213
  20.3 0.0 collective-permute-done.1
  20.3 2.3 %collective-permute-start.11 = (bf16[128,768]{1,0:T(8,128)(2,1)S(1)}, bf16[128,768]{1,0:T(8,128)(2,1)S(1)}, u32[]{:S(2)}, u32[]{:S(2)}) collective-permute-start(bf16[128,768]{1,0:T(8,128)(2,1)S(1)} %get-tuple-element.46), channel_id=1, source_target_pairs={{0,6},{1,7},{2,4},{3,5},{4,2},{5,3},{6,0},{7,1},{8,14},{9,15},{10,... | collective-permute-start | bytes 589832 | tf_op jit(solution)/shard_map/ppermute | solution.py:213
  22.8 0.1 collective-permute-start.8
  22.8 4.0 %collective-permute-done.9 = bf16[128,768]{1,0:T(8,128)(2,1)S(1)} collective-permute-done((bf16[128,768]{1,0:T(8,128)(2,1)S(1)}, bf16[128,768]{1,0:T(8,128)(2,1)S(1)}, u32[]{:S(2)}, u32[]{:S(2)}) %collective-permute-start.9) | collective-permute-done | bytes 196640 | tf_op jit(solution)/shard_map/ppermute | solution.py:213
  26.9 2.6 %collective-permute-done.10 = bf16[128,768]{1,0:T(8,128)(2,1)S(1)} collective-permute-done((bf16[128,768]{1,0:T(8,128)(2,1)S(1)}, bf16[128,768]{1,0:T(8,128)(2,1)S(1)}, u32[]{:S(2)}, u32[]{:S(2)}) %collective-permute-start.10) | collective-permute-done | bytes 196640 | tf_op jit(solution)/shard_map/ppermute | solution.py:213
  29.5 0.1 collective-permute-start.12
  29.6 1.7 %early_sums.1 = (f32[256,768]{1,0:T(8,128)S(1)}, f32[256,128]{1,0:T(8,128)S(1)}) custom-call(bf16[256,768]{1,0:T(8,128)(2,1)S(1)} %pad_maximum_fusion.rows_ref, bf16[512,768]{1,0:T(8,128)(2,1)S(1)} %constant_dynamic-update-slice_fusion.refs_0_, bf16[512,768]{1,0:T(8,128)(2,1)S(1)} %collective-permute-done.8.refs_1_), custom_call_target="tpu_custom_call" | custom-call | flops 805306368 | tf_op jit(solution)/shard_map/early_sums/pallas_call | solution.py:242
  31.3 1.0 %middle_sums.1 = (f32[256,768]{1,0:T(8,128)S(1)}, f32[256,128]{1,0:T(8,128)S(1)}) custom-call(bf16[256,768]{1,0:T(8,128)(2,1)S(1)} %pad_maximum_fusion.rows_ref, f32[256,768]{1,0:T(8,128)S(1)} %get-tuple-element.34.total_ref, f32[256,128]{1,0:T(8,128)S(1)} %get-tuple-element.35.dens_ref, bf16[512,768]{1,0:T(8,128)(2,1)S(1)} %constant_dynamic-update-slice_fusion.9.refs_0_), custom_call_target="tpu_custom_call" | custom-call | flops 402653184 | tf_op jit(solution)/shard_map/middle_sums/pallas_call | solution.py:254
  32.4 1.2 %last_sums.1 = (f32[72,768]{1,0:T(8,128)S(1)}, f32[72,768]{1,0:T(8,128)S(1)}, f32[64,768]{1,0:T(8,128)S(1)}, f32[64,768]{1,0:T(8,128)S(1)}, f32[8,128]{1,0:T(8,128)S(1)}, /*index=5*/f32[8,128]{1,0:T(8,128)S(1)}) custom-call(bf16[256,768]{1,0:T(8,128)(2,1)S(1)} %pad_maximum_fusion.rows_ref, f32[256,768]{1,0:T(8,128)S(1)} %get-tuple-element.36.total_ref, ...), custom_call_target="tpu_custom_call" | custom-call | flops 402653184 | tf_op jit(solution)/shard_map/last_sums/pallas_call | solution.py:267
  33.5 2.7 %collective-permute-start.13 = (f16[64,768]{1,0:T(8,128)(2,1)S(1)}, f16[64,768]{1,0:T(8,128)(2,1)S(1)}, u32[]{:S(2)}, u32[]{:S(2)}) collective-permute-start(f16[64,768]{1,0:T(8,128)(2,1)S(1)} %convert_element_type.24), channel_id=1, source_target_pairs={{0,24},{8,16},{16,8},{24,0},{1,25},{9,17},{17,9},{25,1},{2,26},{10... | collective-permute-start | bytes 294920 | tf_op jit(solution)/shard_map/ppermute | solution.py:210
  36.2 0.1 collective-permute-start.14
  36.3 1.8 %collective-permute-start.15 = (f16[72,768]{1,0:T(8,128)(2,1)S(1)}, f16[72,768]{1,0:T(8,128)(2,1)S(1)}, u32[]{:S(2)}, u32[]{:S(2)}) collective-permute-start(f16[72,768]{1,0:T(8,128)(2,1)S(1)} %convert_element_type.28), channel_id=1, source_target_pairs={{0,8},{8,0},{16,24},{24,16},{1,9},{9,1},{17,25},{25,17},{2,10},{10... | collective-permute-start | bytes 331784 | tf_op jit(solution)/shard_map/ppermute | solution.py:210
  38.2 2.6 %collective-permute-start.16 = (f32[8,128]{1,0:T(8,128)S(1)}, f32[8,128]{1,0:T(8,128)S(1)}, u32[]{:S(2)}, u32[]{:S(2)}) collective-permute-start(f32[8,128]{1,0:T(8,128)S(1)} %get-tuple-element.42), channel_id=1, source_target_pairs={{0,24},{8,16},{16,8},{24,0},{1,25},{9,17},{17,9},{25,1},{2,26},{10... | collective-permute-start | bytes 12296 | tf_op jit(solution)/shard_map/ppermute | solution.py:210
  40.8 0.3 collective-permute-done.13
  41.1 4.0 %collective-permute-done.14 = f16[64,768]{1,0:T(8,128)(2,1)S(1)} collective-permute-done((f16[64,768]{1,0:T(8,128)(2,1)S(1)}, f16[64,768]{1,0:T(8,128)(2,1)S(1)}, u32[]{:S(2)}, u32[]{:S(2)}) %collective-permute-start.14) | collective-permute-done | bytes 98336 | tf_op jit(solution)/shard_map/ppermute | solution.py:210
  45.2 0.1 collective-permute-done.15
  45.3 0.0 collective-permute-done.17.refs_5_
  45.4 1.4 %restore_rows.1 = (f32[256,768]{1,0:T(8,128)}, f32[1,256]{1,0:T(1,128)}) custom-call(bf16[256,256]{1,0:T(8,128)(2,1)S(1)} %get-tuple-element.24.chosen_ref, f32[64,768]{1,0:T(8,128)S(1)} %convert_element_type.25.refs_0_, f32[64,768]{1,0:T(8,128)S(1)} %convert_element_type.27.refs_1_, f32[72,768]{1,0:T(8,128)S(1)} %convert_element_type.29.refs_2_, ...), custom_call_target="tpu_custom_call" | custom-call | tf_op jit(solution)/shard_map/restore_rows/pallas_call | solution.py:283
  (30 shorter events, 0.3 us)
Async XLA Ops:
  1.9 8.7 %collective-permute-start = (bf16[64,768]{1,0:T(8,128)(2,1)S(1)}, bf16[64,768]{1,0:T(8,128)(2,1)S(1)}, u32[]{:S(2)}, u32[]{:S(2)}) collective-permute-start(bf16[64,768]{1,0:T(8,128)(2,1)S(1)} %get-tuple-element.26), channel_id=1, source_target_pairs={{0,8},{8,0},{16,24},{24,16},{1,9},{9,1},{17,25},{25,17},{2,10},{10... | collective-permute-start | bytes 294920 | tf_op jit(solution)/shard_map/ppermute | solution.py:210
  5.0 5.6 %collective-permute-start.2 = (bf16[64,768]{1,0:T(8,128)(2,1)S(1)}, bf16[64,768]{1,0:T(8,128)(2,1)S(1)}, u32[]{:S(2)}, u32[]{:S(2)}) collective-permute-start(bf16[64,768]{1,0:T(8,128)(2,1)S(1)} %get-tuple-element.25), channel_id=1, source_target_pairs={{0,2},{1,3},{2,0},{3,1},{4,6},{5,7},{6,4},{7,5},{8,10},{9,11},{10,... | collective-permute-start | bytes 294920 | tf_op jit(solution)/shard_map/ppermute | solution.py:213
  6.5 4.6 %collective-permute-start.3 = (bf16[64,768]{1,0:T(8,128)(2,1)S(1)}, bf16[64,768]{1,0:T(8,128)(2,1)S(1)}, u32[]{:S(2)}, u32[]{:S(2)}) collective-permute-start(bf16[64,768]{1,0:T(8,128)(2,1)S(1)} %get-tuple-element.25), channel_id=1, source_target_pairs={{0,4},{1,5},{2,6},{3,7},{4,0},{5,1},{6,2},{7,3},{8,12},{9,13},{10,... | collective-permute-start | bytes 294920 | tf_op jit(solution)/shard_map/ppermute | solution.py:213
  8.0 10.9 %collective-permute-start.7 = (bf16[64,768]{1,0:T(8,128)(2,1)S(1)}, bf16[64,768]{1,0:T(8,128)(2,1)S(1)}, u32[]{:S(2)}, u32[]{:S(2)}) collective-permute-start(bf16[64,768]{1,0:T(8,128)(2,1)S(1)} %get-tuple-element.31), channel_id=1, source_target_pairs={{0,24},{8,16},{16,8},{24,0},{1,25},{9,17},{17,9},{25,1},{2,26},{10... | collective-permute-start | bytes 294920 | tf_op jit(solution)/shard_map/ppermute | solution.py:210
  10.5 8.4 %collective-permute-start.6 = (bf16[64,768]{1,0:T(8,128)(2,1)S(1)}, bf16[64,768]{1,0:T(8,128)(2,1)S(1)}, u32[]{:S(2)}, u32[]{:S(2)}) collective-permute-start(bf16[64,768]{1,0:T(8,128)(2,1)S(1)} %get-tuple-element.30), channel_id=1, source_target_pairs={{0,16},{8,24},{16,0},{24,8},{1,17},{9,25},{17,1},{25,9},{2,18},{10... | collective-permute-start | bytes 294920 | tf_op jit(solution)/shard_map/ppermute | solution.py:210
  11.1 11.5 %collective-permute-start.4 = (bf16[64,768]{1,0:T(8,128)(2,1)S(1)}, bf16[64,768]{1,0:T(8,128)(2,1)S(1)}, u32[]{:S(2)}, u32[]{:S(2)}) collective-permute-start(bf16[64,768]{1,0:T(8,128)(2,1)S(1)} %collective-permute-done), channel_id=1, source_target_pairs={{0,2},{1,3},{2,0},{3,1},{4,6},{5,7},{6,4},{7,5},{8,10},{9,11},{10,... | collective-permute-start | bytes 294920 | tf_op jit(solution)/shard_map/ppermute | solution.py:213
  11.7 11.0 %collective-permute-start.5 = (bf16[64,768]{1,0:T(8,128)(2,1)S(1)}, bf16[64,768]{1,0:T(8,128)(2,1)S(1)}, u32[]{:S(2)}, u32[]{:S(2)}) collective-permute-start(bf16[64,768]{1,0:T(8,128)(2,1)S(1)} %collective-permute-done), channel_id=1, source_target_pairs={{0,4},{1,5},{2,6},{3,7},{4,0},{5,1},{6,2},{7,3},{8,12},{9,13},{10,... | collective-permute-start | bytes 294920 | tf_op jit(solution)/shard_map/ppermute | solution.py:213
  13.2 7.1 %collective-permute-start.1 = (bf16[128,768]{1,0:T(8,128)(2,1)S(1)}, bf16[128,768]{1,0:T(8,128)(2,1)S(1)}, u32[]{:S(2)}, u32[]{:S(2)}) collective-permute-start(bf16[128,768]{1,0:T(8,128)(2,1)S(1)} %pad_maximum_fusion.1), channel_id=1, source_target_pairs={{0,6},{1,7},{2,4},{3,5},{4,2},{5,3},{6,0},{7,1},{8,14},{9,15},{10,... | collective-permute-start | bytes 589832 | tf_op jit(solution)/shard_map/ppermute | solution.py:213
  19.0 7.9 %collective-permute-start.9 = (bf16[128,768]{1,0:T(8,128)(2,1)S(1)}, bf16[128,768]{1,0:T(8,128)(2,1)S(1)}, u32[]{:S(2)}, u32[]{:S(2)}) collective-permute-start(bf16[128,768]{1,0:T(8,128)(2,1)S(1)} %get-tuple-element.46), channel_id=1, source_target_pairs={{0,2},{1,3},{2,0},{3,1},{4,6},{5,7},{6,4},{7,5},{8,10},{9,11},{10,... | collective-permute-start | bytes 589832 | tf_op jit(solution)/shard_map/ppermute | solution.py:213
  19.6 9.9 %collective-permute-start.10 = (bf16[128,768]{1,0:T(8,128)(2,1)S(1)}, bf16[128,768]{1,0:T(8,128)(2,1)S(1)}, u32[]{:S(2)}, u32[]{:S(2)}) collective-permute-start(bf16[128,768]{1,0:T(8,128)(2,1)S(1)} %get-tuple-element.46), channel_id=1, source_target_pairs={{0,4},{1,5},{2,6},{3,7},{4,0},{5,1},{6,2},{7,3},{8,12},{9,13},{10,... | collective-permute-start | bytes 589832 | tf_op jit(solution)/shard_map/ppermute | solution.py:213
  20.3 9.2 %collective-permute-start.11 = (bf16[128,768]{1,0:T(8,128)(2,1)S(1)}, bf16[128,768]{1,0:T(8,128)(2,1)S(1)}, u32[]{:S(2)}, u32[]{:S(2)}) collective-permute-start(bf16[128,768]{1,0:T(8,128)(2,1)S(1)} %get-tuple-element.46), channel_id=1, source_target_pairs={{0,6},{1,7},{2,4},{3,5},{4,2},{5,3},{6,0},{7,1},{8,14},{9,15},{10,... | collective-permute-start | bytes 589832 | tf_op jit(solution)/shard_map/ppermute | solution.py:213
  22.8 6.9 %collective-permute-start.8 = (bf16[512,768]{1,0:T(8,128)(2,1)S(1)}, bf16[512,768]{1,0:T(8,128)(2,1)S(1)}, u32[]{:S(2)}, u32[]{:S(2)}) collective-permute-start(bf16[512,768]{1,0:T(8,128)(2,1)S(1)} %constant_dynamic-update-slice_fusion.refs_0_), channel_id=1, source_target_pairs={{0,1},{1,0},{2,3},{3,2},{4,5},{5,4},{6,7},{7,6},{8,9},{9,8},{10,11... | collective-permute-start | bytes 2359304 | tf_op jit(solution)/shard_map/ppermute | solution.py:213
  29.5 2.8 %collective-permute-start.12 = (bf16[512,768]{1,0:T(8,128)(2,1)S(1)}, bf16[512,768]{1,0:T(8,128)(2,1)S(1)}, u32[]{:S(2)}, u32[]{:S(2)}) collective-permute-start(bf16[512,768]{1,0:T(8,128)(2,1)S(1)} %constant_dynamic-update-slice_fusion.9.refs_0_), channel_id=1, source_target_pairs={{0,1},{1,0},{2,3},{3,2},{4,5},{5,4},{6,7},{7,6},{8,9},{9,8},{10,11... | collective-permute-start | bytes 2359304 | tf_op jit(solution)/shard_map/ppermute | solution.py:213
  33.5 7.6 %collective-permute-start.13 = (f16[64,768]{1,0:T(8,128)(2,1)S(1)}, f16[64,768]{1,0:T(8,128)(2,1)S(1)}, u32[]{:S(2)}, u32[]{:S(2)}) collective-permute-start(f16[64,768]{1,0:T(8,128)(2,1)S(1)} %convert_element_type.24), channel_id=1, source_target_pairs={{0,24},{8,16},{16,8},{24,0},{1,25},{9,17},{17,9},{25,1},{2,26},{10... | collective-permute-start | bytes 294920 | tf_op jit(solution)/shard_map/ppermute | solution.py:210
  36.2 8.9 %collective-permute-start.14 = (f16[64,768]{1,0:T(8,128)(2,1)S(1)}, f16[64,768]{1,0:T(8,128)(2,1)S(1)}, u32[]{:S(2)}, u32[]{:S(2)}) collective-permute-start(f16[64,768]{1,0:T(8,128)(2,1)S(1)} %convert_element_type.26), channel_id=1, source_target_pairs={{0,16},{8,24},{16,0},{24,8},{1,17},{9,25},{17,1},{25,9},{2,18},{10... | collective-permute-start | bytes 294920 | tf_op jit(solution)/shard_map/ppermute | solution.py:210
  36.3 9.0 %collective-permute-start.15 = (f16[72,768]{1,0:T(8,128)(2,1)S(1)}, f16[72,768]{1,0:T(8,128)(2,1)S(1)}, u32[]{:S(2)}, u32[]{:S(2)}) collective-permute-start(f16[72,768]{1,0:T(8,128)(2,1)S(1)} %convert_element_type.28), channel_id=1, source_target_pairs={{0,8},{8,0},{16,24},{24,16},{1,9},{9,1},{17,25},{25,17},{2,10},{10... | collective-permute-start | bytes 331784 | tf_op jit(solution)/shard_map/ppermute | solution.py:210
  38.2 7.2 %collective-permute-start.16 = (f32[8,128]{1,0:T(8,128)S(1)}, f32[8,128]{1,0:T(8,128)S(1)}, u32[]{:S(2)}, u32[]{:S(2)}) collective-permute-start(f32[8,128]{1,0:T(8,128)S(1)} %get-tuple-element.42), channel_id=1, source_target_pairs={{0,24},{8,16},{16,8},{24,0},{1,25},{9,17},{17,9},{25,1},{2,26},{10... | collective-permute-start | bytes 12296 | tf_op jit(solution)/shard_map/ppermute | solution.py:210
  40.8 4.6 %collective-permute-start.17 = (f32[8,128]{1,0:T(8,128)S(1)}, f32[8,128]{1,0:T(8,128)S(1)}, u32[]{:S(2)}, u32[]{:S(2)}) collective-permute-start(f32[8,128]{1,0:T(8,128)S(1)} %get-tuple-element.43), channel_id=1, source_target_pairs={{0,16},{8,24},{16,0},{24,8},{1,17},{9,25},{17,1},{25,9},{2,18},{10... | collective-permute-start | bytes 12296 | tf_op jit(solution)/shard_map/ppermute | solution.py:210

commit v6 on v4

--- a/solution.py
+++ b/solution.py
@@ -225,10 +225,18 @@
 
     held = [parts[0]] + [along_gr(parts[k], k) for k in range(1, n_gr)]
     half = n_gr // 2
+    sides = [k for k in range(2, n_gc, 2) if not k & (k - 1)]
+    corners = [k for k in range(2, n_gc, 2) if k & (k - 1)]
+
+    def to_side(block, step):
+        pairs = [(i, i ^ sides[(step + i % 2) % len(sides)]) for i in range(n_gc)]
+        return lax.ppermute(block, "gc", pairs)
+
     chunks = []
     for pieces in (held[:half], held[half:]):
         block = jnp.concatenate(pieces, axis=0)
-        near = [block] + [along_gc(block, k) for k in range(2, n_gc, 2)]
+        near = [block] + [to_side(block, step) for step in range(len(sides))]
+        near += [along_gc(block, k) for k in corners]
         chunks.append(jnp.concatenate(near, axis=0))
     rows = jnp.concatenate(held, axis=0)
     chunks[0], rows = lax.optimization_barrier((chunks[0], rows))

time: 46.4 us -> 46.4 us (level)
    ppermute x8 -> x4, starting transfers between devices: 7.31 us -> 0.92 us  [along_gc(): return lax.ppermute(block, 'gc', [(i, i ^ bits) for i in range(n_gc)])]
    ppermute x0 -> x4, starting transfers between devices: none -> 6.4 us  [to_side(): return lax.ppermute(block, 'gc', pairs)]
    ppermute x8 -> x4, waiting for transfers between devices: 8.05 us -> 3.82 us  [along_gc(): return lax.ppermute(block, 'gc', [(i, i ^ bits) for i in range(n_gc)])]
    ppermute x0 -> x4, waiting for transfers between devices: none -> 4.18 us  [to_side(): return lax.ppermute(block, 'gc', pairs)]
  transfers between devices with their start and end apart: 16 -> 16, of which waited for: 5 -> 6; matrix products, arithmetic and copies ran while one was open for 1% -> 1% of each run, Pallas kernels for 6% -> 6%
where the time goes in v6:
time: 46.4 us; the launch traced here: 46.2 us
  starting transfers between devices  20.6 us (44%)
  waiting for transfers between devices  17.9 us (39%)
  Pallas kernels  6.58 us (14%)
  between operations  0.86 us (2%)
    ppermute x8, starting transfers between devices, along_gr(): return lax.ppermute(part, 'gr', [(i, i ^ bits) for i in range(n_gr)])  13.3 us
    ppermute x8, waiting for transfers between devices, along_gr(): return lax.ppermute(part, 'gr', [(i, i ^ bits) for i in range(n_gr)])  9.86 us
    ppermute x4, starting transfers between devices, to_side(): return lax.ppermute(block, 'gc', pairs)  6.4 us
    ppermute x4, waiting for transfers between devices, to_side(): return lax.ppermute(block, 'gc', pairs)  4.18 us
    ppermute x4, waiting for transfers between devices, along_gc(): return lax.ppermute(block, 'gc', [(i, i ^ bits) for i in range(n_gc)])  3.82 us
    pallas_call x1, Pallas kernels, on_device(): pl.pallas_call(first_kernel, out_shape=[jax.ShapeDtypeStruct((count, widt...  1.71 us
    pallas_call x1, Pallas kernels, on_device(): pl.pallas_call(functools.partial(restore_kernel, half), out_shape=[jax.Sh...  1.43 us
    pallas_call x1, Pallas kernels, on_device(): pl.pallas_call(sort_kernel, out_shape=[jax.ShapeDtypeStruct((count, count...  1.3 us
  transfers between devices with their start and end apart: 16, of which 6 were waited for; matrix products, arithmetic and copies ran while one was open for 1% of the time, Pallas kernels for 6%

profile of v6, /device:TPU:0, one launch (start us, length us, event | category | flops | bytes accessed | tf_op | source)
XLA Modules:
  0.0 46.2 jit_solution(13180946989356373233)
XLA Ops:
  0.6 1.3 %sort_rows.1 = (bf16[256,256]{1,0:T(8,128)(2,1)S(1)}, bf16[64,768]{1,0:T(8,128)(2,1)S(1)}, bf16[64,768]{1,0:T(8,128)(2,1)S(1)}, bf16[64,768]{1,0:T(8,128)(2,1)S(1)}, bf16[64,768]{1,0:T(8,128)(2,1)S(1)}) custom-call(s32[1]{0:T(128)} %bitcast.own_ref, s32[1,256]{1,0:T(1,128)} %bitcast.3, bf16[256,768]{1,0:T(8,128)(2,1)} %rows_hbm.1), custom_call_target="tpu_custom_call" | custom-call | tf_op jit(solution)/shard_map/sort_rows/pallas_call | solution.py:193
  1.9 3.1 %collective-permute-start = (bf16[64,768]{1,0:T(8,128)(2,1)S(1)}, bf16[64,768]{1,0:T(8,128)(2,1)S(1)}, u32[]{:S(2)}, u32[]{:S(2)}) collective-permute-start(bf16[64,768]{1,0:T(8,128)(2,1)S(1)} %get-tuple-element.23), channel_id=1, source_target_pairs={{0,8},{8,0},{16,24},{24,16},{1,9},{9,1},{17,25},{25,17},{2,10},{10... | collective-permute-start | bytes 294920 | tf_op jit(solution)/shard_map/ppermute | solution.py:210
  5.0 2.5 %collective-permute-start.5 = (bf16[64,768]{1,0:T(8,128)(2,1)S(1)}, bf16[64,768]{1,0:T(8,128)(2,1)S(1)}, u32[]{:S(2)}, u32[]{:S(2)}) collective-permute-start(bf16[64,768]{1,0:T(8,128)(2,1)S(1)} %get-tuple-element.25), channel_id=1, source_target_pairs={{0,24},{8,16},{16,8},{24,0},{1,25},{9,17},{17,9},{25,1},{2,26},{10... | collective-permute-start | bytes 294920 | tf_op jit(solution)/shard_map/ppermute | solution.py:210
  7.5 0.1 collective-permute-start.4
  7.6 0.2 collective-permute-done
  7.8 1.8 %collective-permute-start.1 = (bf16[128,768]{1,0:T(8,128)(2,1)S(1)}, bf16[128,768]{1,0:T(8,128)(2,1)S(1)}, u32[]{:S(2)}, u32[]{:S(2)}) collective-permute-start(bf16[128,768]{1,0:T(8,128)(2,1)S(1)} %get-tuple-element.44), channel_id=1, source_target_pairs={{0,2},{1,5},{2,0},{3,7},{4,6},{5,1},{6,4},{7,3},{8,10},{9,13},{10,... | collective-permute-start | bytes 589832 | tf_op jit(solution)/shard_map/ppermute | solution.py:233
  9.6 1.5 %collective-permute-start.2 = (bf16[128,768]{1,0:T(8,128)(2,1)S(1)}, bf16[128,768]{1,0:T(8,128)(2,1)S(1)}, u32[]{:S(2)}, u32[]{:S(2)}) collective-permute-start(bf16[128,768]{1,0:T(8,128)(2,1)S(1)} %get-tuple-element.44), channel_id=1, source_target_pairs={{0,4},{1,3},{2,6},{3,1},{4,0},{5,7},{6,2},{7,5},{8,12},{9,11},{10,... | collective-permute-start | bytes 589832 | tf_op jit(solution)/shard_map/ppermute | solution.py:233
  11.2 0.2 collective-permute-start.3
  11.4 5.1 %collective-permute-done.4 = bf16[64,768]{1,0:T(8,128)(2,1)S(1)} collective-permute-done((bf16[64,768]{1,0:T(8,128)(2,1)S(1)}, bf16[64,768]{1,0:T(8,128)(2,1)S(1)}, u32[]{:S(2)}, u32[]{:S(2)}) %collective-permute-start.4) | collective-permute-done | bytes 98336 | tf_op jit(solution)/shard_map/ppermute | solution.py:210
  16.5 0.0 collective-permute-done.5
  16.5 1.6 %collective-permute-start.7 = (bf16[128,768]{1,0:T(8,128)(2,1)S(1)}, bf16[128,768]{1,0:T(8,128)(2,1)S(1)}, u32[]{:S(2)}, u32[]{:S(2)}) collective-permute-start(bf16[128,768]{1,0:T(8,128)(2,1)S(1)} %get-tuple-element.40), channel_id=1, source_target_pairs={{0,2},{1,5},{2,0},{3,7},{4,6},{5,1},{6,4},{7,3},{8,10},{9,13},{10,... | collective-permute-start | bytes 589832 | tf_op jit(solution)/shard_map/ppermute | solution.py:233
  18.1 1.5 %collective-permute-start.8 = (bf16[128,768]{1,0:T(8,128)(2,1)S(1)}, bf16[128,768]{1,0:T(8,128)(2,1)S(1)}, u32[]{:S(2)}, u32[]{:S(2)}) collective-permute-start(bf16[128,768]{1,0:T(8,128)(2,1)S(1)} %get-tuple-element.40), channel_id=1, source_target_pairs={{0,4},{1,3},{2,6},{3,1},{4,0},{5,7},{6,2},{7,5},{8,12},{9,11},{10,... | collective-permute-start | bytes 589832 | tf_op jit(solution)/shard_map/ppermute | solution.py:233
  19.6 0.0 collective-permute-done.1
  19.6 0.5 %collective-permute-start.9 = (bf16[128,768]{1,0:T(8,128)(2,1)S(1)}, bf16[128,768]{1,0:T(8,128)(2,1)S(1)}, u32[]{:S(2)}, u32[]{:S(2)}) collective-permute-start(bf16[128,768]{1,0:T(8,128)(2,1)S(1)} %get-tuple-element.40), channel_id=1, source_target_pairs={{0,6},{1,7},{2,4},{3,5},{4,2},{5,3},{6,0},{7,1},{8,14},{9,15},{10,... | collective-permute-start | bytes 589832 | tf_op jit(solution)/shard_map/ppermute | solution.py:213
  20.2 0.0 collective-permute-done.2
  20.2 0.1 collective-permute-start.6
  20.3 4.0 %collective-permute-done.7 = bf16[128,768]{1,0:T(8,128)(2,1)S(1)} collective-permute-done((bf16[128,768]{1,0:T(8,128)(2,1)S(1)}, bf16[128,768]{1,0:T(8,128)(2,1)S(1)}, u32[]{:S(2)}, u32[]{:S(2)}) %collective-permute-start.7) | collective-permute-done | bytes 196640 | tf_op jit(solution)/shard_map/ppermute | solution.py:233
  24.4 0.2 collective-permute-done.8
  24.5 3.8 %collective-permute-done.9 = bf16[128,768]{1,0:T(8,128)(2,1)S(1)} collective-permute-done((bf16[128,768]{1,0:T(8,128)(2,1)S(1)}, bf16[128,768]{1,0:T(8,128)(2,1)S(1)}, u32[]{:S(2)}, u32[]{:S(2)}) %collective-permute-start.9) | collective-permute-done | bytes 196640 | tf_op jit(solution)/shard_map/ppermute | solution.py:213
  28.4 0.1 collective-permute-start.10
  28.5 0.0 collective-permute-done.6.refs_1_
  28.5 1.7 %early_sums.1 = (f32[256,768]{1,0:T(8,128)S(1)}, f32[256,128]{1,0:T(8,128)S(1)}) custom-call(bf16[256,768]{1,0:T(8,128)(2,1)S(1)} %pad_maximum_fusion.rows_ref, bf16[512,768]{1,0:T(8,128)(2,1)S(1)} %constant_dynamic-update-slice_fusion.2.refs_0_, bf16[512,768]{1,0:T(8,128)(2,1)S(1)} %collective-permute-done.6.refs_1_), custom_call_target="tpu_custom_call" | custom-call | flops 805306368 | tf_op jit(solution)/shard_map/early_sums/pallas_call | solution.py:245
  30.2 1.0 %middle_sums.1 = (f32[256,768]{1,0:T(8,128)S(1)}, f32[256,128]{1,0:T(8,128)S(1)}) custom-call(bf16[256,768]{1,0:T(8,128)(2,1)S(1)} %pad_maximum_fusion.rows_ref, f32[256,768]{1,0:T(8,128)S(1)} %get-tuple-element.28.total_ref, f32[256,128]{1,0:T(8,128)S(1)} %get-tuple-element.29.dens_ref, bf16[512,768]{1,0:T(8,128)(2,1)S(1)} %constant_dynamic-update-slice_fusion.9.refs_0_), custom_call_target="tpu_custom_call" | custom-call | flops 402653184 | tf_op jit(solution)/shard_map/middle_sums/pallas_call | solution.py:257
  31.2 1.2 %last_sums.1 = (f32[72,768]{1,0:T(8,128)S(1)}, f32[72,768]{1,0:T(8,128)S(1)}, f32[64,768]{1,0:T(8,128)S(1)}, f32[64,768]{1,0:T(8,128)S(1)}, f32[8,128]{1,0:T(8,128)S(1)}, /*index=5*/f32[8,128]{1,0:T(8,128)S(1)}) custom-call(bf16[256,768]{1,0:T(8,128)(2,1)S(1)} %pad_maximum_fusion.rows_ref, f32[256,768]{1,0:T(8,128)S(1)} %get-tuple-element.30.total_ref, ...), custom_call_target="tpu_custom_call" | custom-call | flops 402653184 | tf_op jit(solution)/shard_map/last_sums/pallas_call | solution.py:270
  32.4 3.1 %collective-permute-start.11 = (f16[64,768]{1,0:T(8,128)(2,1)S(1)}, f16[64,768]{1,0:T(8,128)(2,1)S(1)}, u32[]{:S(2)}, u32[]{:S(2)}) collective-permute-start(f16[64,768]{1,0:T(8,128)(2,1)S(1)} %convert_element_type.24), channel_id=1, source_target_pairs={{0,24},{8,16},{16,8},{24,0},{1,25},{9,17},{17,9},{25,1},{2,26},{10... | collective-permute-start | bytes 294920 | tf_op jit(solution)/shard_map/ppermute | solution.py:210
  35.5 0.1 collective-permute-start.12
  35.6 1.4 %collective-permute-start.13 = (f16[72,768]{1,0:T(8,128)(2,1)S(1)}, f16[72,768]{1,0:T(8,128)(2,1)S(1)}, u32[]{:S(2)}, u32[]{:S(2)}) collective-permute-start(f16[72,768]{1,0:T(8,128)(2,1)S(1)} %convert_element_type.28), channel_id=1, source_target_pairs={{0,8},{8,0},{16,24},{24,16},{1,9},{9,1},{17,25},{25,17},{2,10},{10... | collective-permute-start | bytes 331784 | tf_op jit(solution)/shard_map/ppermute | solution.py:210
  37.0 3.1 %collective-permute-start.14 = (f32[8,128]{1,0:T(8,128)S(1)}, f32[8,128]{1,0:T(8,128)S(1)}, u32[]{:S(2)}, u32[]{:S(2)}) collective-permute-start(f32[8,128]{1,0:T(8,128)S(1)} %get-tuple-element.36), channel_id=1, source_target_pairs={{0,24},{8,16},{16,8},{24,0},{1,25},{9,17},{17,9},{25,1},{2,26},{10... | collective-permute-start | bytes 12296 | tf_op jit(solution)/shard_map/ppermute | solution.py:210
  40.1 4.6 %collective-permute-done.12 = f16[64,768]{1,0:T(8,128)(2,1)S(1)} collective-permute-done((f16[64,768]{1,0:T(8,128)(2,1)S(1)}, f16[64,768]{1,0:T(8,128)(2,1)S(1)}, u32[]{:S(2)}, u32[]{:S(2)}) %collective-permute-start.12) | collective-permute-done | bytes 98336 | tf_op jit(solution)/shard_map/ppermute | solution.py:210
  44.7 0.0 collective-permute-done.13
  44.8 0.0 collective-permute-done.15.refs_5_
  44.8 1.4 %restore_rows.1 = (f32[256,768]{1,0:T(8,128)}, f32[1,256]{1,0:T(1,128)}) custom-call(bf16[256,256]{1,0:T(8,128)(2,1)S(1)} %get-tuple-element.21.chosen_ref, f32[64,768]{1,0:T(8,128)S(1)} %convert_element_type.25.refs_0_, f32[64,768]{1,0:T(8,128)S(1)} %convert_element_type.27.refs_1_, f32[72,768]{1,0:T(8,128)S(1)} %convert_element_type.29.refs_2_, ...), custom_call_target="tpu_custom_call" | custom-call | tf_op jit(solution)/shard_map/restore_rows/pallas_call | solution.py:286
  (23 shorter events, 0.3 us)
Async XLA Ops:
  1.9 5.9 %collective-permute-start = (bf16[64,768]{1,0:T(8,128)(2,1)S(1)}, bf16[64,768]{1,0:T(8,128)(2,1)S(1)}, u32[]{:S(2)}, u32[]{:S(2)}) collective-permute-start(bf16[64,768]{1,0:T(8,128)(2,1)S(1)} %get-tuple-element.23), channel_id=1, source_target_pairs={{0,8},{8,0},{16,24},{24,16},{1,9},{9,1},{17,25},{25,17},{2,10},{10... | collective-permute-start | bytes 294920 | tf_op jit(solution)/shard_map/ppermute | solution.py:210
  5.0 11.4 %collective-permute-start.5 = (bf16[64,768]{1,0:T(8,128)(2,1)S(1)}, bf16[64,768]{1,0:T(8,128)(2,1)S(1)}, u32[]{:S(2)}, u32[]{:S(2)}) collective-permute-start(bf16[64,768]{1,0:T(8,128)(2,1)S(1)} %get-tuple-element.25), channel_id=1, source_target_pairs={{0,24},{8,16},{16,8},{24,0},{1,25},{9,17},{17,9},{25,1},{2,26},{10... | collective-permute-start | bytes 294920 | tf_op jit(solution)/shard_map/ppermute | solution.py:210
  7.5 8.9 %collective-permute-start.4 = (bf16[64,768]{1,0:T(8,128)(2,1)S(1)}, bf16[64,768]{1,0:T(8,128)(2,1)S(1)}, u32[]{:S(2)}, u32[]{:S(2)}) collective-permute-start(bf16[64,768]{1,0:T(8,128)(2,1)S(1)} %get-tuple-element.24), channel_id=1, source_target_pairs={{0,16},{8,24},{16,0},{24,8},{1,17},{9,25},{17,1},{25,9},{2,18},{10... | collective-permute-start | bytes 294920 | tf_op jit(solution)/shard_map/ppermute | solution.py:210
  7.8 11.8 %collective-permute-start.1 = (bf16[128,768]{1,0:T(8,128)(2,1)S(1)}, bf16[128,768]{1,0:T(8,128)(2,1)S(1)}, u32[]{:S(2)}, u32[]{:S(2)}) collective-permute-start(bf16[128,768]{1,0:T(8,128)(2,1)S(1)} %get-tuple-element.44), channel_id=1, source_target_pairs={{0,2},{1,5},{2,0},{3,7},{4,6},{5,1},{6,4},{7,3},{8,10},{9,13},{10,... | collective-permute-start | bytes 589832 | tf_op jit(solution)/shard_map/ppermute | solution.py:233
  9.6 10.5 %collective-permute-start.2 = (bf16[128,768]{1,0:T(8,128)(2,1)S(1)}, bf16[128,768]{1,0:T(8,128)(2,1)S(1)}, u32[]{:S(2)}, u32[]{:S(2)}) collective-permute-start(bf16[128,768]{1,0:T(8,128)(2,1)S(1)} %get-tuple-element.44), channel_id=1, source_target_pairs={{0,4},{1,3},{2,6},{3,1},{4,0},{5,7},{6,2},{7,5},{8,12},{9,11},{10,... | collective-permute-start | bytes 589832 | tf_op jit(solution)/shard_map/ppermute | solution.py:233
  11.2 9.1 %collective-permute-start.3 = (bf16[128,768]{1,0:T(8,128)(2,1)S(1)}, bf16[128,768]{1,0:T(8,128)(2,1)S(1)}, u32[]{:S(2)}, u32[]{:S(2)}) collective-permute-start(bf16[128,768]{1,0:T(8,128)(2,1)S(1)} %get-tuple-element.44), channel_id=1, source_target_pairs={{0,6},{1,7},{2,4},{3,5},{4,2},{5,3},{6,0},{7,1},{8,14},{9,15},{10,... | collective-permute-start | bytes 589832 | tf_op jit(solution)/shard_map/ppermute | solution.py:213
  16.5 7.8 %collective-permute-start.7 = (bf16[128,768]{1,0:T(8,128)(2,1)S(1)}, bf16[128,768]{1,0:T(8,128)(2,1)S(1)}, u32[]{:S(2)}, u32[]{:S(2)}) collective-permute-start(bf16[128,768]{1,0:T(8,128)(2,1)S(1)} %get-tuple-element.40), channel_id=1, source_target_pairs={{0,2},{1,5},{2,0},{3,7},{4,6},{5,1},{6,4},{7,3},{8,10},{9,13},{10,... | collective-permute-start | bytes 589832 | tf_op jit(solution)/shard_map/ppermute | solution.py:233
  18.1 6.5 %collective-permute-start.8 = (bf16[128,768]{1,0:T(8,128)(2,1)S(1)}, bf16[128,768]{1,0:T(8,128)(2,1)S(1)}, u32[]{:S(2)}, u32[]{:S(2)}) collective-permute-start(bf16[128,768]{1,0:T(8,128)(2,1)S(1)} %get-tuple-element.40), channel_id=1, source_target_pairs={{0,4},{1,3},{2,6},{3,1},{4,0},{5,7},{6,2},{7,5},{8,12},{9,11},{10,... | collective-permute-start | bytes 589832 | tf_op jit(solution)/shard_map/ppermute | solution.py:233
  19.6 8.7 %collective-permute-start.9 = (bf16[128,768]{1,0:T(8,128)(2,1)S(1)}, bf16[128,768]{1,0:T(8,128)(2,1)S(1)}, u32[]{:S(2)}, u32[]{:S(2)}) collective-permute-start(bf16[128,768]{1,0:T(8,128)(2,1)S(1)} %get-tuple-element.40), channel_id=1, source_target_pairs={{0,6},{1,7},{2,4},{3,5},{4,2},{5,3},{6,0},{7,1},{8,14},{9,15},{10,... | collective-permute-start | bytes 589832 | tf_op jit(solution)/shard_map/ppermute | solution.py:213
  20.2 8.2 %collective-permute-start.6 = (bf16[512,768]{1,0:T(8,128)(2,1)S(1)}, bf16[512,768]{1,0:T(8,128)(2,1)S(1)}, u32[]{:S(2)}, u32[]{:S(2)}) collective-permute-start(bf16[512,768]{1,0:T(8,128)(2,1)S(1)} %constant_dynamic-update-slice_fusion.2.refs_0_), channel_id=1, source_target_pairs={{0,1},{1,0},{2,3},{3,2},{4,5},{5,4},{6,7},{7,6},{8,9},{9,8},{10,11... | collective-permute-start | bytes 2359304 | tf_op jit(solution)/shard_map/ppermute | solution.py:213
  28.4 2.8 %collective-permute-start.10 = (bf16[512,768]{1,0:T(8,128)(2,1)S(1)}, bf16[512,768]{1,0:T(8,128)(2,1)S(1)}, u32[]{:S(2)}, u32[]{:S(2)}) collective-permute-start(bf16[512,768]{1,0:T(8,128)(2,1)S(1)} %constant_dynamic-update-slice_fusion.9.refs_0_), channel_id=1, source_target_pairs={{0,1},{1,0},{2,3},{3,2},{4,5},{5,4},{6,7},{7,6},{8,9},{9,8},{10,11... | collective-permute-start | bytes 2359304 | tf_op jit(solution)/shard_map/ppermute | solution.py:213
  32.4 7.7 %collective-permute-start.11 = (f16[64,768]{1,0:T(8,128)(2,1)S(1)}, f16[64,768]{1,0:T(8,128)(2,1)S(1)}, u32[]{:S(2)}, u32[]{:S(2)}) collective-permute-start(f16[64,768]{1,0:T(8,128)(2,1)S(1)} %convert_element_type.24), channel_id=1, source_target_pairs={{0,24},{8,16},{16,8},{24,0},{1,25},{9,17},{17,9},{25,1},{2,26},{10... | collective-permute-start | bytes 294920 | tf_op jit(solution)/shard_map/ppermute | solution.py:210
  35.5 9.2 %collective-permute-start.12 = (f16[64,768]{1,0:T(8,128)(2,1)S(1)}, f16[64,768]{1,0:T(8,128)(2,1)S(1)}, u32[]{:S(2)}, u32[]{:S(2)}) collective-permute-start(f16[64,768]{1,0:T(8,128)(2,1)S(1)} %convert_element_type.26), channel_id=1, source_target_pairs={{0,16},{8,24},{16,0},{24,8},{1,17},{9,25},{17,1},{25,9},{2,18},{10... | collective-permute-start | bytes 294920 | tf_op jit(solution)/shard_map/ppermute | solution.py:210
  35.6 9.1 %collective-permute-start.13 = (f16[72,768]{1,0:T(8,128)(2,1)S(1)}, f16[72,768]{1,0:T(8,128)(2,1)S(1)}, u32[]{:S(2)}, u32[]{:S(2)}) collective-permute-start(f16[72,768]{1,0:T(8,128)(2,1)S(1)} %convert_element_type.28), channel_id=1, source_target_pairs={{0,8},{8,0},{16,24},{24,16},{1,9},{9,1},{17,25},{25,17},{2,10},{10... | collective-permute-start | bytes 331784 | tf_op jit(solution)/shard_map/ppermute | solution.py:210
  37.0 7.8 %collective-permute-start.14 = (f32[8,128]{1,0:T(8,128)S(1)}, f32[8,128]{1,0:T(8,128)S(1)}, u32[]{:S(2)}, u32[]{:S(2)}) collective-permute-start(f32[8,128]{1,0:T(8,128)S(1)} %get-tuple-element.36), channel_id=1, source_target_pairs={{0,24},{8,16},{16,8},{24,0},{1,25},{9,17},{17,9},{25,1},{2,26},{10... | collective-permute-start | bytes 12296 | tf_op jit(solution)/shard_map/ppermute | solution.py:210
  40.1 4.7 %collective-permute-start.15 = (f32[8,128]{1,0:T(8,128)S(1)}, f32[8,128]{1,0:T(8,128)S(1)}, u32[]{:S(2)}, u32[]{:S(2)}) collective-permute-start(f32[8,128]{1,0:T(8,128)S(1)} %get-tuple-element.37), channel_id=1, source_target_pairs={{0,16},{8,24},{16,0},{24,8},{1,17},{9,25},{17,1},{25,9},{2,18},{10... | collective-permute-start | bytes 12296 | tf_op jit(solution)/shard_map/ppermute | solution.py:210

commit v7 on v6

--- a/solution.py
+++ b/solution.py
@@ -232,14 +232,18 @@
         pairs = [(i, i ^ sides[(step + i % 2) % len(sides)]) for i in range(n_gc)]
         return lax.ppermute(block, "gc", pairs)
 
-    chunks = []
-    for pieces in (held[:half], held[half:]):
-        block = jnp.concatenate(pieces, axis=0)
-        near = [block] + [to_side(block, step) for step in range(len(sides))]
-        near += [along_gc(block, k) for k in corners]
-        chunks.append(jnp.concatenate(near, axis=0))
+    early = jnp.concatenate(held[:half], axis=0)
+    late = jnp.concatenate(held[half:], axis=0)
+    rest = jnp.concatenate(held[1:half], axis=0)
+    filler = [along_gc(held[0], k) for k in corners]
+    filler, rest = lax.optimization_barrier((filler, rest))
+    rest_corners = [along_gc(rest, k) for k in corners]
+    early_sides = [to_side(early, step) for step in range(len(sides))]
+    late_near = [to_side(late, 0)] + [along_gc(late, k) for k in corners]
+    rest_corners, late = lax.optimization_barrier((rest_corners, late))
+    late_near += [to_side(late, step) for step in range(1, len(sides))]
     rows = jnp.concatenate(held, axis=0)
-    chunks[0], rows = lax.optimization_barrier((chunks[0], rows))
+    chunks = [jnp.concatenate(early_sides + rest_corners + filler + [early], axis=0), jnp.concatenate([late] + late_near, axis=0)]
     early = [chunks[0], other_core(chunks[0])]
 
     total, dens = pl.pallas_call(

time: 46.4 us -> 47.5 us (1.024)
  starting transfers between devices: 20.6 us -> 23.4 us
  waiting for transfers between devices: 17.9 us -> 16.2 us
    ppermute x4 -> x5, starting transfers between devices: 0.92 us -> 6.68 us  [along_gc(): return lax.ppermute(block, 'gc', [(i, i ^ bits) for i in range(n_gc)])]
    ppermute x4, starting transfers between devices: 6.4 us -> 2.43 us  [to_side(): return lax.ppermute(block, 'gc', pairs)]
    ppermute x8, waiting for transfers between devices: 9.86 us -> 8.82 us  [along_gr(): return lax.ppermute(part, 'gr', [(i, i ^ bits) for i in range(n_gr)])]
    ppermute x8, starting transfers between devices: 13.3 us -> 14.3 us  [along_gr(): return lax.ppermute(part, 'gr', [(i, i ^ bits) for i in range(n_gr)])]
    ppermute x4 -> x5, waiting for transfers between devices: 3.82 us -> 3.4 us  [along_gc(): return lax.ppermute(block, 'gc', [(i, i ^ bits) for i in range(n_gc)])]
  transfers between devices with their start and end apart: 16 -> 17, of which waited for: 6 -> 6; matrix products, arithmetic and copies ran while one was open for 1% -> 1% of each run, Pallas kernels for 6% -> 6%
where the time goes in v7:
time: 47.5 us; the launch traced here: 47.3 us
  starting transfers between devices  23.4 us (49%)
  waiting for transfers between devices  16.2 us (34%)
  Pallas kernels  6.58 us (14%)
  between operations  0.9 us (2%)
    ppermute x8, starting transfers between devices, along_gr(): return lax.ppermute(part, 'gr', [(i, i ^ bits) for i in range(n_gr)])  14.3 us
    ppermute x8, waiting for transfers between devices, along_gr(): return lax.ppermute(part, 'gr', [(i, i ^ bits) for i in range(n_gr)])  8.82 us
    ppermute x5, starting transfers between devices, along_gc(): return lax.ppermute(block, 'gc', [(i, i ^ bits) for i in range(n_gc)])  6.68 us
    ppermute x4, waiting for transfers between devices, to_side(): return lax.ppermute(block, 'gc', pairs)  3.93 us
    ppermute x5, waiting for transfers between devices, along_gc(): return lax.ppermute(block, 'gc', [(i, i ^ bits) for i in range(n_gc)])  3.4 us
    ppermute x4, starting transfers between devices, to_side(): return lax.ppermute(block, 'gc', pairs)  2.43 us
    pallas_call x1, Pallas kernels, on_device(): pl.pallas_call(first_kernel, out_shape=[jax.ShapeDtypeStruct((count, widt...  1.71 us
    pallas_call x1, Pallas kernels, on_device(): pl.pallas_call(functools.partial(restore_kernel, half), out_shape=[jax.Sh...  1.44 us
  transfers between devices with their start and end apart: 17, of which 6 were waited for; matrix products, arithmetic and copies ran while one was open for 1% of the time, Pallas kernels for 6%

profile of v7, /device:TPU:0, one launch (start us, length us, event | category | flops | bytes accessed | tf_op | source)
XLA Modules:
  0.0 47.3 jit_solution(15540573520362152452)
XLA Ops:
  0.6 1.3 %sort_rows.1 = (bf16[256,256]{1,0:T(8,128)(2,1)S(1)}, bf16[64,768]{1,0:T(8,128)(2,1)S(1)}, bf16[64,768]{1,0:T(8,128)(2,1)S(1)}, bf16[64,768]{1,0:T(8,128)(2,1)S(1)}, bf16[64,768]{1,0:T(8,128)(2,1)S(1)}) custom-call(s32[1]{0:T(128)} %bitcast.own_ref, s32[1,256]{1,0:T(1,128)} %bitcast.3, bf16[256,768]{1,0:T(8,128)(2,1)} %rows_hbm.1), custom_call_target="tpu_custom_call" | custom-call | tf_op jit(solution)/shard_map/sort_rows/pallas_call | solution.py:193
  1.9 3.1 %collective-permute-start = (bf16[64,768]{1,0:T(8,128)(2,1)S(1)}, bf16[64,768]{1,0:T(8,128)(2,1)S(1)}, u32[]{:S(2)}, u32[]{:S(2)}) collective-permute-start(bf16[64,768]{1,0:T(8,128)(2,1)S(1)} %get-tuple-element.25), channel_id=1, source_target_pairs={{0,8},{8,0},{16,24},{24,16},{1,9},{9,1},{17,25},{25,17},{2,10},{10... | collective-permute-start | bytes 294920 | tf_op jit(solution)/shard_map/ppermute | solution.py:210
  5.0 2.4 %collective-permute-start.5 = (bf16[64,768]{1,0:T(8,128)(2,1)S(1)}, bf16[64,768]{1,0:T(8,128)(2,1)S(1)}, u32[]{:S(2)}, u32[]{:S(2)}) collective-permute-start(bf16[64,768]{1,0:T(8,128)(2,1)S(1)} %get-tuple-element.24), channel_id=1, source_target_pairs={{0,6},{1,7},{2,4},{3,5},{4,2},{5,3},{6,0},{7,1},{8,14},{9,15},{10,... | collective-permute-start | bytes 294920 | tf_op jit(solution)/shard_map/ppermute | solution.py:213
  7.5 2.6 %collective-permute-start.1 = (bf16[64,768]{1,0:T(8,128)(2,1)S(1)}, bf16[64,768]{1,0:T(8,128)(2,1)S(1)}, u32[]{:S(2)}, u32[]{:S(2)}) collective-permute-start(bf16[64,768]{1,0:T(8,128)(2,1)S(1)} %get-tuple-element.26), channel_id=1, source_target_pairs={{0,16},{8,24},{16,0},{24,8},{1,17},{9,25},{17,1},{25,9},{2,18},{10... | collective-permute-start | bytes 294920 | tf_op jit(solution)/shard_map/ppermute | solution.py:210
  10.1 0.2 collective-permute-start.2
  10.3 0.0 collective-permute-done
  10.3 0.6 %collective-permute-start.3 = (bf16[128,768]{1,0:T(8,128)(2,1)S(1)}, bf16[128,768]{1,0:T(8,128)(2,1)S(1)}, u32[]{:S(2)}, u32[]{:S(2)}) collective-permute-start(bf16[128,768]{1,0:T(8,128)(2,1)S(1)} %constant_dynamic-update-slice_fusion.4), channel_id=1, source_target_pairs={{0,2},{1,5},{2,0},{3,7},{4,6},{5,1},{6,4},{7,3},{8,10},{9,13},{10,... | collective-permute-start | bytes 589832 | tf_op jit(solution)/shard_map/ppermute | solution.py:233
  10.9 0.3 collective-permute-start.4
  11.2 2.7 %collective-permute-start.6 = (bf16[64,768]{1,0:T(8,128)(2,1)S(1)}, bf16[64,768]{1,0:T(8,128)(2,1)S(1)}, u32[]{:S(2)}, u32[]{:S(2)}) collective-permute-start(bf16[64,768]{1,0:T(8,128)(2,1)S(1)} %collective-permute-done), channel_id=1, source_target_pairs={{0,6},{1,7},{2,4},{3,5},{4,2},{5,3},{6,0},{7,1},{8,14},{9,15},{10,... | collective-permute-start | bytes 294920 | tf_op jit(solution)/shard_map/ppermute | solution.py:213
  13.9 3.4 %collective-permute-done.1 = bf16[64,768]{1,0:T(8,128)(2,1)S(1)} collective-permute-done((bf16[64,768]{1,0:T(8,128)(2,1)S(1)}, bf16[64,768]{1,0:T(8,128)(2,1)S(1)}, u32[]{:S(2)}, u32[]{:S(2)}) %collective-permute-start.1) | collective-permute-done | bytes 98336 | tf_op jit(solution)/shard_map/ppermute | solution.py:210
  17.3 0.8 %collective-permute-start.8 = (bf16[128,768]{1,0:T(8,128)(2,1)S(1)}, bf16[128,768]{1,0:T(8,128)(2,1)S(1)}, u32[]{:S(2)}, u32[]{:S(2)}) collective-permute-start(bf16[128,768]{1,0:T(8,128)(2,1)S(1)} %constant_dynamic-update-slice_fusion.6), channel_id=1, source_target_pairs={{0,2},{1,5},{2,0},{3,7},{4,6},{5,1},{6,4},{7,3},{8,10},{9,13},{10,... | collective-permute-start | bytes 589832 | tf_op jit(solution)/shard_map/ppermute | solution.py:233
  18.1 1.4 %collective-permute-start.9 = (bf16[128,768]{1,0:T(8,128)(2,1)S(1)}, bf16[128,768]{1,0:T(8,128)(2,1)S(1)}, u32[]{:S(2)}, u32[]{:S(2)}) collective-permute-start(bf16[128,768]{1,0:T(8,128)(2,1)S(1)} %constant_dynamic-update-slice_fusion.6), channel_id=1, source_target_pairs={{0,6},{1,7},{2,4},{3,5},{4,2},{5,3},{6,0},{7,1},{8,14},{9,15},{10,... | collective-permute-start | bytes 589832 | tf_op jit(solution)/shard_map/ppermute | solution.py:213
  19.5 0.6 %collective-permute-done.6 = bf16[64,768]{1,0:T(8,128)(2,1)S(1)} collective-permute-done((bf16[64,768]{1,0:T(8,128)(2,1)S(1)}, bf16[64,768]{1,0:T(8,128)(2,1)S(1)}, u32[]{:S(2)}, u32[]{:S(2)}) %collective-permute-start.6) | collective-permute-done | bytes 98336 | tf_op jit(solution)/shard_map/ppermute | solution.py:213
  20.1 0.8 %collective-permute-start.10 = (bf16[128,768]{1,0:T(8,128)(2,1)S(1)}, bf16[128,768]{1,0:T(8,128)(2,1)S(1)}, u32[]{:S(2)}, u32[]{:S(2)}) collective-permute-start(bf16[128,768]{1,0:T(8,128)(2,1)S(1)} %constant_dynamic-update-slice_fusion.6), channel_id=1, source_target_pairs={{0,4},{1,3},{2,6},{3,1},{4,0},{5,7},{6,2},{7,5},{8,12},{9,11},{10,... | collective-permute-start | bytes 589832 | tf_op jit(solution)/shard_map/ppermute | solution.py:233
  20.9 0.0 collective-permute-done.3
  20.9 0.0 collective-permute-done.4
  21.0 0.1 collective-permute-start.7
  21.1 3.9 %collective-permute-done.8 = bf16[128,768]{1,0:T(8,128)(2,1)S(1)} collective-permute-done((bf16[128,768]{1,0:T(8,128)(2,1)S(1)}, bf16[128,768]{1,0:T(8,128)(2,1)S(1)}, u32[]{:S(2)}, u32[]{:S(2)}) %collective-permute-start.8) | collective-permute-done | bytes 196640 | tf_op jit(solution)/shard_map/ppermute | solution.py:233
  25.0 2.8 %collective-permute-done.9 = bf16[128,768]{1,0:T(8,128)(2,1)S(1)} collective-permute-done((bf16[128,768]{1,0:T(8,128)(2,1)S(1)}, bf16[128,768]{1,0:T(8,128)(2,1)S(1)}, u32[]{:S(2)}, u32[]{:S(2)}) %collective-permute-start.9) | collective-permute-done | bytes 196640 | tf_op jit(solution)/shard_map/ppermute | solution.py:213
  27.9 0.1 collective-permute-start.11
  28.0 1.7 %early_sums.1 = (f32[256,768]{1,0:T(8,128)S(1)}, f32[256,128]{1,0:T(8,128)S(1)}) custom-call(bf16[256,768]{1,0:T(8,128)(2,1)S(1)} %constant_dynamic-update-slice_fusion.rows_ref, bf16[512,768]{1,0:T(8,128)(2,1)S(1)} %get-tuple-element.44.refs_0_, bf16[512,768]{1,0:T(8,128)(2,1)S(1)} %collective-permute-done.7.refs_1_), custom_call_target="tpu_custom_call" | custom-call | flops 805306368 | tf_op jit(solution)/shard_map/early_sums/pallas_call | solution.py:249
  29.7 1.0 %middle_sums.1 = (f32[256,768]{1,0:T(8,128)S(1)}, f32[256,128]{1,0:T(8,128)S(1)}) custom-call(bf16[256,768]{1,0:T(8,128)(2,1)S(1)} %constant_dynamic-update-slice_fusion.rows_ref, f32[256,768]{1,0:T(8,128)S(1)} %get-tuple-element.31.total_ref, f32[256,128]{1,0:T(8,128)S(1)} %get-tuple-element.32.dens_ref, ...), custom_call_target="tpu_custom_call" | custom-call | flops 402653184 | tf_op jit(solution)/shard_map/middle_sums/pallas_call | solution.py:261
  30.7 1.2 %last_sums.1 = (f32[72,768]{1,0:T(8,128)S(1)}, f32[72,768]{1,0:T(8,128)S(1)}, f32[64,768]{1,0:T(8,128)S(1)}, f32[64,768]{1,0:T(8,128)S(1)}, f32[8,128]{1,0:T(8,128)S(1)}, /*index=5*/f32[8,128]{1,0:T(8,128)S(1)}) custom-call(bf16[256,768]{1,0:T(8,128)(2,1)S(1)} %constant_dynamic-update-slice_fusion.rows_ref, f32[256,768]{1,0:T(8,128)S(1)} %get-tuple-element.34.total_ref, ...), custom_call_target="tpu_custom_call" | custom-call | flops 402653184 | tf_op jit(solution)/shard_map/last_sums/pallas_call | solution.py:274
  31.9 3.9 %collective-permute-start.12 = (f16[64,768]{1,0:T(8,128)(2,1)S(1)}, f16[64,768]{1,0:T(8,128)(2,1)S(1)}, u32[]{:S(2)}, u32[]{:S(2)}) collective-permute-start(f16[64,768]{1,0:T(8,128)(2,1)S(1)} %convert_element_type.24), channel_id=1, source_target_pairs={{0,24},{8,16},{16,8},{24,0},{1,25},{9,17},{17,9},{25,1},{2,26},{10... | collective-permute-start | bytes 294920 | tf_op jit(solution)/shard_map/ppermute | solution.py:210
  35.8 0.5 %collective-permute-start.13 = (f16[64,768]{1,0:T(8,128)(2,1)S(1)}, f16[64,768]{1,0:T(8,128)(2,1)S(1)}, u32[]{:S(2)}, u32[]{:S(2)}) collective-permute-start(f16[64,768]{1,0:T(8,128)(2,1)S(1)} %convert_element_type.26), channel_id=1, source_target_pairs={{0,16},{8,24},{16,0},{24,8},{1,17},{9,25},{17,1},{25,9},{2,18},{10... | collective-permute-start | bytes 294920 | tf_op jit(solution)/shard_map/ppermute | solution.py:210
  36.3 0.2 collective-permute-start.14
  36.5 3.8 %collective-permute-start.15 = (f32[8,128]{1,0:T(8,128)S(1)}, f32[8,128]{1,0:T(8,128)S(1)}, u32[]{:S(2)}, u32[]{:S(2)}) collective-permute-start(f32[8,128]{1,0:T(8,128)S(1)} %get-tuple-element.40), channel_id=1, source_target_pairs={{0,24},{8,16},{16,8},{24,0},{1,25},{9,17},{17,9},{25,1},{2,26},{10... | collective-permute-start | bytes 12296 | tf_op jit(solution)/shard_map/ppermute | solution.py:210
  40.4 0.0 collective-permute-done.12
  40.4 5.4 %collective-permute-done.13 = f16[64,768]{1,0:T(8,128)(2,1)S(1)} collective-permute-done((f16[64,768]{1,0:T(8,128)(2,1)S(1)}, f16[64,768]{1,0:T(8,128)(2,1)S(1)}, u32[]{:S(2)}, u32[]{:S(2)}) %collective-permute-start.13) | collective-permute-done | bytes 98336 | tf_op jit(solution)/shard_map/ppermute | solution.py:210
  45.8 0.0 collective-permute-done.15.refs_4_
  45.8 0.1 collective-permute-done.16.refs_5_
  45.9 1.4 %restore_rows.1 = (f32[256,768]{1,0:T(8,128)}, f32[1,256]{1,0:T(1,128)}) custom-call(bf16[256,256]{1,0:T(8,128)(2,1)S(1)} %get-tuple-element.23.chosen_ref, f32[64,768]{1,0:T(8,128)S(1)} %convert_element_type.25.refs_0_, f32[64,768]{1,0:T(8,128)S(1)} %convert_element_type.27.refs_1_, f32[72,768]{1,0:T(8,128)S(1)} %convert_element_type.29.refs_2_, ...), custom_call_target="tpu_custom_call" | custom-call | tf_op jit(solution)/shard_map/restore_rows/pallas_call | solution.py:290
  (30 shorter events, 0.3 us)
Async XLA Ops:
  1.9 8.4 %collective-permute-start = (bf16[64,768]{1,0:T(8,128)(2,1)S(1)}, bf16[64,768]{1,0:T(8,128)(2,1)S(1)}, u32[]{:S(2)}, u32[]{:S(2)}) collective-permute-start(bf16[64,768]{1,0:T(8,128)(2,1)S(1)} %get-tuple-element.25), channel_id=1, source_target_pairs={{0,8},{8,0},{16,24},{24,16},{1,9},{9,1},{17,25},{25,17},{2,10},{10... | collective-permute-start | bytes 294920 | tf_op jit(solution)/shard_map/ppermute | solution.py:210
  5.0 6.2 %collective-permute-start.5 = (bf16[64,768]{1,0:T(8,128)(2,1)S(1)}, bf16[64,768]{1,0:T(8,128)(2,1)S(1)}, u32[]{:S(2)}, u32[]{:S(2)}) collective-permute-start(bf16[64,768]{1,0:T(8,128)(2,1)S(1)} %get-tuple-element.24), channel_id=1, source_target_pairs={{0,6},{1,7},{2,4},{3,5},{4,2},{5,3},{6,0},{7,1},{8,14},{9,15},{10,... | collective-permute-start | bytes 294920 | tf_op jit(solution)/shard_map/ppermute | solution.py:213
  7.5 9.8 %collective-permute-start.1 = (bf16[64,768]{1,0:T(8,128)(2,1)S(1)}, bf16[64,768]{1,0:T(8,128)(2,1)S(1)}, u32[]{:S(2)}, u32[]{:S(2)}) collective-permute-start(bf16[64,768]{1,0:T(8,128)(2,1)S(1)} %get-tuple-element.26), channel_id=1, source_target_pairs={{0,16},{8,24},{16,0},{24,8},{1,17},{9,25},{17,1},{25,9},{2,18},{10... | collective-permute-start | bytes 294920 | tf_op jit(solution)/shard_map/ppermute | solution.py:210
  10.1 7.2 %collective-permute-start.2 = (bf16[64,768]{1,0:T(8,128)(2,1)S(1)}, bf16[64,768]{1,0:T(8,128)(2,1)S(1)}, u32[]{:S(2)}, u32[]{:S(2)}) collective-permute-start(bf16[64,768]{1,0:T(8,128)(2,1)S(1)} %get-tuple-element.27), channel_id=1, source_target_pairs={{0,24},{8,16},{16,8},{24,0},{1,25},{9,17},{17,9},{25,1},{2,26},{10... | collective-permute-start | bytes 294920 | tf_op jit(solution)/shard_map/ppermute | solution.py:210
  10.3 10.6 %collective-permute-start.3 = (bf16[128,768]{1,0:T(8,128)(2,1)S(1)}, bf16[128,768]{1,0:T(8,128)(2,1)S(1)}, u32[]{:S(2)}, u32[]{:S(2)}) collective-permute-start(bf16[128,768]{1,0:T(8,128)(2,1)S(1)} %constant_dynamic-update-slice_fusion.4), channel_id=1, source_target_pairs={{0,2},{1,5},{2,0},{3,7},{4,6},{5,1},{6,4},{7,3},{8,10},{9,13},{10,... | collective-permute-start | bytes 589832 | tf_op jit(solution)/shard_map/ppermute | solution.py:233
  10.9 10.0 %collective-permute-start.4 = (bf16[128,768]{1,0:T(8,128)(2,1)S(1)}, bf16[128,768]{1,0:T(8,128)(2,1)S(1)}, u32[]{:S(2)}, u32[]{:S(2)}) collective-permute-start(bf16[128,768]{1,0:T(8,128)(2,1)S(1)} %constant_dynamic-update-slice_fusion.4), channel_id=1, source_target_pairs={{0,4},{1,3},{2,6},{3,1},{4,0},{5,7},{6,2},{7,5},{8,12},{9,11},{10,... | collective-permute-start | bytes 589832 | tf_op jit(solution)/shard_map/ppermute | solution.py:233
  11.2 8.9 %collective-permute-start.6 = (bf16[64,768]{1,0:T(8,128)(2,1)S(1)}, bf16[64,768]{1,0:T(8,128)(2,1)S(1)}, u32[]{:S(2)}, u32[]{:S(2)}) collective-permute-start(bf16[64,768]{1,0:T(8,128)(2,1)S(1)} %collective-permute-done), channel_id=1, source_target_pairs={{0,6},{1,7},{2,4},{3,5},{4,2},{5,3},{6,0},{7,1},{8,14},{9,15},{10,... | collective-permute-start | bytes 294920 | tf_op jit(solution)/shard_map/ppermute | solution.py:213
  17.3 7.7 %collective-permute-start.8 = (bf16[128,768]{1,0:T(8,128)(2,1)S(1)}, bf16[128,768]{1,0:T(8,128)(2,1)S(1)}, u32[]{:S(2)}, u32[]{:S(2)}) collective-permute-start(bf16[128,768]{1,0:T(8,128)(2,1)S(1)} %constant_dynamic-update-slice_fusion.6), channel_id=1, source_target_pairs={{0,2},{1,5},{2,0},{3,7},{4,6},{5,1},{6,4},{7,3},{8,10},{9,13},{10,... | collective-permute-start | bytes 589832 | tf_op jit(solution)/shard_map/ppermute | solution.py:233
  18.1 9.8 %collective-permute-start.9 = (bf16[128,768]{1,0:T(8,128)(2,1)S(1)}, bf16[128,768]{1,0:T(8,128)(2,1)S(1)}, u32[]{:S(2)}, u32[]{:S(2)}) collective-permute-start(bf16[128,768]{1,0:T(8,128)(2,1)S(1)} %constant_dynamic-update-slice_fusion.6), channel_id=1, source_target_pairs={{0,6},{1,7},{2,4},{3,5},{4,2},{5,3},{6,0},{7,1},{8,14},{9,15},{10,... | collective-permute-start | bytes 589832 | tf_op jit(solution)/shard_map/ppermute | solution.py:213
  20.1 7.8 %collective-permute-start.10 = (bf16[128,768]{1,0:T(8,128)(2,1)S(1)}, bf16[128,768]{1,0:T(8,128)(2,1)S(1)}, u32[]{:S(2)}, u32[]{:S(2)}) collective-permute-start(bf16[128,768]{1,0:T(8,128)(2,1)S(1)} %constant_dynamic-update-slice_fusion.6), channel_id=1, source_target_pairs={{0,4},{1,3},{2,6},{3,1},{4,0},{5,7},{6,2},{7,5},{8,12},{9,11},{10,... | collective-permute-start | bytes 589832 | tf_op jit(solution)/shard_map/ppermute | solution.py:233
  21.0 7.0 %collective-permute-start.7 = (bf16[512,768]{1,0:T(8,128)(2,1)S(1)}, bf16[512,768]{1,0:T(8,128)(2,1)S(1)}, u32[]{:S(2)}, u32[]{:S(2)}) collective-permute-start(bf16[512,768]{1,0:T(8,128)(2,1)S(1)} %get-tuple-element.44.refs_0_), channel_id=1, source_target_pairs={{0,1},{1,0},{2,3},{3,2},{4,5},{5,4},{6,7},{7,6},{8,9},{9,8},{10,11... | collective-permute-start | bytes 2359304 | tf_op jit(solution)/shard_map/ppermute | solution.py:213
  27.9 2.8 %collective-permute-start.11 = (bf16[512,768]{1,0:T(8,128)(2,1)S(1)}, bf16[512,768]{1,0:T(8,128)(2,1)S(1)}, u32[]{:S(2)}, u32[]{:S(2)}) collective-permute-start(bf16[512,768]{1,0:T(8,128)(2,1)S(1)} %constant_dynamic-update-slice_fusion.14.refs_0_), channel_id=1, source_target_pairs={{0,1},{1,0},{2,3},{3,2},{4,5},{5,4},{6,7},{7,6},{8,9},{9,8},{10,11... | collective-permute-start | bytes 2359304 | tf_op jit(solution)/shard_map/ppermute | solution.py:213
  31.9 8.5 %collective-permute-start.12 = (f16[64,768]{1,0:T(8,128)(2,1)S(1)}, f16[64,768]{1,0:T(8,128)(2,1)S(1)}, u32[]{:S(2)}, u32[]{:S(2)}) collective-permute-start(f16[64,768]{1,0:T(8,128)(2,1)S(1)} %convert_element_type.24), channel_id=1, source_target_pairs={{0,24},{8,16},{16,8},{24,0},{1,25},{9,17},{17,9},{25,1},{2,26},{10... | collective-permute-start | bytes 294920 | tf_op jit(solution)/shard_map/ppermute | solution.py:210
  35.8 10.0 %collective-permute-start.13 = (f16[64,768]{1,0:T(8,128)(2,1)S(1)}, f16[64,768]{1,0:T(8,128)(2,1)S(1)}, u32[]{:S(2)}, u32[]{:S(2)}) collective-permute-start(f16[64,768]{1,0:T(8,128)(2,1)S(1)} %convert_element_type.26), channel_id=1, source_target_pairs={{0,16},{8,24},{16,0},{24,8},{1,17},{9,25},{17,1},{25,9},{2,18},{10... | collective-permute-start | bytes 294920 | tf_op jit(solution)/shard_map/ppermute | solution.py:210
  36.3 9.5 %collective-permute-start.14 = (f16[72,768]{1,0:T(8,128)(2,1)S(1)}, f16[72,768]{1,0:T(8,128)(2,1)S(1)}, u32[]{:S(2)}, u32[]{:S(2)}) collective-permute-start(f16[72,768]{1,0:T(8,128)(2,1)S(1)} %convert_element_type.28), channel_id=1, source_target_pairs={{0,8},{8,0},{16,24},{24,16},{1,9},{9,1},{17,25},{25,17},{2,10},{10... | collective-permute-start | bytes 331784 | tf_op jit(solution)/shard_map/ppermute | solution.py:210
  36.5 9.3 %collective-permute-start.15 = (f32[8,128]{1,0:T(8,128)S(1)}, f32[8,128]{1,0:T(8,128)S(1)}, u32[]{:S(2)}, u32[]{:S(2)}) collective-permute-start(f32[8,128]{1,0:T(8,128)S(1)} %get-tuple-element.40), channel_id=1, source_target_pairs={{0,24},{8,16},{16,8},{24,0},{1,25},{9,17},{17,9},{25,1},{2,26},{10... | collective-permute-start | bytes 12296 | tf_op jit(solution)/shard_map/ppermute | solution.py:210
  40.3 5.6 %collective-permute-start.16 = (f32[8,128]{1,0:T(8,128)S(1)}, f32[8,128]{1,0:T(8,128)S(1)}, u32[]{:S(2)}, u32[]{:S(2)}) collective-permute-start(f32[8,128]{1,0:T(8,128)S(1)} %get-tuple-element.41), channel_id=1, source_target_pairs={{0,16},{8,24},{16,0},{24,8},{1,17},{9,25},{17,1},{25,9},{2,18},{10... | collective-permute-start | bytes 12296 | tf_op jit(solution)/shard_map/ppermute | solution.py:210

commit v8 on v6

--- a/solution.py
+++ b/solution.py
@@ -235,8 +235,8 @@
     chunks = []
     for pieces in (held[:half], held[half:]):
         block = jnp.concatenate(pieces, axis=0)
-        near = [block] + [to_side(block, step) for step in range(len(sides))]
-        near += [along_gc(block, k) for k in corners]
+        near = [block] + [along_gc(block, k) for k in corners]
+        near += [to_side(block, step) for step in range(len(sides))]
         chunks.append(jnp.concatenate(near, axis=0))
     rows = jnp.concatenate(held, axis=0)
     chunks[0], rows = lax.optimization_barrier((chunks[0], rows))

time: 46.4 us -> 46 us (level)
    ppermute x4, starting transfers between devices: 0.92 us -> 5.41 us  [along_gc(): return lax.ppermute(block, 'gc', [(i, i ^ bits) for i in range(n_gc)])]
    ppermute x4, starting transfers between devices: 6.4 us -> 1.9 us  [to_side(): return lax.ppermute(block, 'gc', pairs)]
    ppermute x4, waiting for transfers between devices: 4.18 us -> 2.87 us  [to_side(): return lax.ppermute(block, 'gc', pairs)]
    ppermute x4, waiting for transfers between devices: 3.82 us -> 4.97 us  [along_gc(): return lax.ppermute(block, 'gc', [(i, i ^ bits) for i in range(n_gc)])]
where the time goes in v8:
time: 46 us; the launch traced here: 45.9 us
  starting transfers between devices  20.4 us (44%)
  waiting for transfers between devices  17.8 us (39%)
  Pallas kernels  6.59 us (14%)
  between operations  0.86 us (2%)
    ppermute x8, starting transfers between devices, along_gr(): return lax.ppermute(part, 'gr', [(i, i ^ bits) for i in range(n_gr)])  13.1 us
    ppermute x8, waiting for transfers between devices, along_gr(): return lax.ppermute(part, 'gr', [(i, i ^ bits) for i in range(n_gr)])  9.93 us
    ppermute x4, starting transfers between devices, along_gc(): return lax.ppermute(block, 'gc', [(i, i ^ bits) for i in range(n_gc)])  5.41 us
    ppermute x4, waiting for transfers between devices, along_gc(): return lax.ppermute(block, 'gc', [(i, i ^ bits) for i in range(n_gc)])  4.97 us
    ppermute x4, waiting for transfers between devices, to_side(): return lax.ppermute(block, 'gc', pairs)  2.87 us
    ppermute x4, starting transfers between devices, to_side(): return lax.ppermute(block, 'gc', pairs)  1.9 us
    pallas_call x1, Pallas kernels, on_device(): pl.pallas_call(first_kernel, out_shape=[jax.ShapeDtypeStruct((count, widt...  1.71 us
    pallas_call x1, Pallas kernels, on_device(): pl.pallas_call(functools.partial(restore_kernel, half), out_shape=[jax.Sh...  1.44 us
  transfers between devices with their start and end apart: 16, of which 6 were waited for; matrix products, arithmetic and copies ran while one was open for 1% of the time, Pallas kernels for 6%

profile of v8, /device:TPU:0, one launch (start us, length us, event | category | flops | bytes accessed | tf_op | source)
XLA Modules:
  0.0 45.9 jit_solution(3205613650655806232)
XLA Ops:
  0.6 1.3 %sort_rows.1 = (bf16[256,256]{1,0:T(8,128)(2,1)S(1)}, bf16[64,768]{1,0:T(8,128)(2,1)S(1)}, bf16[64,768]{1,0:T(8,128)(2,1)S(1)}, bf16[64,768]{1,0:T(8,128)(2,1)S(1)}, bf16[64,768]{1,0:T(8,128)(2,1)S(1)}) custom-call(s32[1]{0:T(128)} %bitcast.own_ref, s32[1,256]{1,0:T(1,128)} %bitcast.3, bf16[256,768]{1,0:T(8,128)(2,1)} %rows_hbm.1), custom_call_target="tpu_custom_call" | custom-call | tf_op jit(solution)/shard_map/sort_rows/pallas_call | solution.py:193
  1.9 3.1 %collective-permute-start = (bf16[64,768]{1,0:T(8,128)(2,1)S(1)}, bf16[64,768]{1,0:T(8,128)(2,1)S(1)}, u32[]{:S(2)}, u32[]{:S(2)}) collective-permute-start(bf16[64,768]{1,0:T(8,128)(2,1)S(1)} %get-tuple-element.23), channel_id=1, source_target_pairs={{0,8},{8,0},{16,24},{24,16},{1,9},{9,1},{17,25},{25,17},{2,10},{10... | collective-permute-start | bytes 294920 | tf_op jit(solution)/shard_map/ppermute | solution.py:210
  5.0 2.5 %collective-permute-start.5 = (bf16[64,768]{1,0:T(8,128)(2,1)S(1)}, bf16[64,768]{1,0:T(8,128)(2,1)S(1)}, u32[]{:S(2)}, u32[]{:S(2)}) collective-permute-start(bf16[64,768]{1,0:T(8,128)(2,1)S(1)} %get-tuple-element.25), channel_id=1, source_target_pairs={{0,24},{8,16},{16,8},{24,0},{1,25},{9,17},{17,9},{25,1},{2,26},{10... | collective-permute-start | bytes 294920 | tf_op jit(solution)/shard_map/ppermute | solution.py:210
  7.5 0.1 collective-permute-start.4
  7.6 0.2 collective-permute-done
  7.8 2.8 %collective-permute-start.1 = (bf16[128,768]{1,0:T(8,128)(2,1)S(1)}, bf16[128,768]{1,0:T(8,128)(2,1)S(1)}, u32[]{:S(2)}, u32[]{:S(2)}) collective-permute-start(bf16[128,768]{1,0:T(8,128)(2,1)S(1)} %get-tuple-element.44), channel_id=1, source_target_pairs={{0,6},{1,7},{2,4},{3,5},{4,2},{5,3},{6,0},{7,1},{8,14},{9,15},{10,... | collective-permute-start | bytes 589832 | tf_op jit(solution)/shard_map/ppermute | solution.py:213
  10.6 0.5 %collective-permute-start.2 = (bf16[128,768]{1,0:T(8,128)(2,1)S(1)}, bf16[128,768]{1,0:T(8,128)(2,1)S(1)}, u32[]{:S(2)}, u32[]{:S(2)}) collective-permute-start(bf16[128,768]{1,0:T(8,128)(2,1)S(1)} %get-tuple-element.44), channel_id=1, source_target_pairs={{0,2},{1,5},{2,0},{3,7},{4,6},{5,1},{6,4},{7,3},{8,10},{9,13},{10,... | collective-permute-start | bytes 589832 | tf_op jit(solution)/shard_map/ppermute | solution.py:233
  11.1 0.3 collective-permute-start.3
  11.4 5.1 %collective-permute-done.4 = bf16[64,768]{1,0:T(8,128)(2,1)S(1)} collective-permute-done((bf16[64,768]{1,0:T(8,128)(2,1)S(1)}, bf16[64,768]{1,0:T(8,128)(2,1)S(1)}, u32[]{:S(2)}, u32[]{:S(2)}) %collective-permute-start.4) | collective-permute-done | bytes 98336 | tf_op jit(solution)/shard_map/ppermute | solution.py:210
  16.5 0.0 collective-permute-done.5
  16.5 2.5 %collective-permute-start.7 = (bf16[128,768]{1,0:T(8,128)(2,1)S(1)}, bf16[128,768]{1,0:T(8,128)(2,1)S(1)}, u32[]{:S(2)}, u32[]{:S(2)}) collective-permute-start(bf16[128,768]{1,0:T(8,128)(2,1)S(1)} %get-tuple-element.40), channel_id=1, source_target_pairs={{0,6},{1,7},{2,4},{3,5},{4,2},{5,3},{6,0},{7,1},{8,14},{9,15},{10,... | collective-permute-start | bytes 589832 | tf_op jit(solution)/shard_map/ppermute | solution.py:213
  19.0 0.5 %collective-permute-start.8 = (bf16[128,768]{1,0:T(8,128)(2,1)S(1)}, bf16[128,768]{1,0:T(8,128)(2,1)S(1)}, u32[]{:S(2)}, u32[]{:S(2)}) collective-permute-start(bf16[128,768]{1,0:T(8,128)(2,1)S(1)} %get-tuple-element.40), channel_id=1, source_target_pairs={{0,2},{1,5},{2,0},{3,7},{4,6},{5,1},{6,4},{7,3},{8,10},{9,13},{10,... | collective-permute-start | bytes 589832 | tf_op jit(solution)/shard_map/ppermute | solution.py:233
  19.6 0.6 %collective-permute-start.9 = (bf16[128,768]{1,0:T(8,128)(2,1)S(1)}, bf16[128,768]{1,0:T(8,128)(2,1)S(1)}, u32[]{:S(2)}, u32[]{:S(2)}) collective-permute-start(bf16[128,768]{1,0:T(8,128)(2,1)S(1)} %get-tuple-element.40), channel_id=1, source_target_pairs={{0,4},{1,3},{2,6},{3,1},{4,0},{5,7},{6,2},{7,5},{8,12},{9,11},{10,... | collective-permute-start | bytes 589832 | tf_op jit(solution)/shard_map/ppermute | solution.py:233
  20.2 0.0 collective-permute-done.2
  20.2 0.0 collective-permute-done.3
  20.3 0.1 collective-permute-start.6
  20.3 5.0 %collective-permute-done.7 = bf16[128,768]{1,0:T(8,128)(2,1)S(1)} collective-permute-done((bf16[128,768]{1,0:T(8,128)(2,1)S(1)}, bf16[128,768]{1,0:T(8,128)(2,1)S(1)}, u32[]{:S(2)}, u32[]{:S(2)}) %collective-permute-start.7) | collective-permute-done | bytes 196640 | tf_op jit(solution)/shard_map/ppermute | solution.py:213
  25.3 2.9 %collective-permute-done.8 = bf16[128,768]{1,0:T(8,128)(2,1)S(1)} collective-permute-done((bf16[128,768]{1,0:T(8,128)(2,1)S(1)}, bf16[128,768]{1,0:T(8,128)(2,1)S(1)}, u32[]{:S(2)}, u32[]{:S(2)}) %collective-permute-start.8) | collective-permute-done | bytes 196640 | tf_op jit(solution)/shard_map/ppermute | solution.py:233
  28.2 0.1 collective-permute-start.10
  28.3 0.0 collective-permute-done.6.refs_1_
  28.3 1.7 %early_sums.1 = (f32[256,768]{1,0:T(8,128)S(1)}, f32[256,128]{1,0:T(8,128)S(1)}) custom-call(bf16[256,768]{1,0:T(8,128)(2,1)S(1)} %pad_maximum_fusion.rows_ref, bf16[512,768]{1,0:T(8,128)(2,1)S(1)} %constant_dynamic-update-slice_fusion.2.refs_0_, bf16[512,768]{1,0:T(8,128)(2,1)S(1)} %collective-permute-done.6.refs_1_), custom_call_target="tpu_custom_call" | custom-call | flops 805306368 | tf_op jit(solution)/shard_map/early_sums/pallas_call | solution.py:245
  30.0 1.0 %middle_sums.1 = (f32[256,768]{1,0:T(8,128)S(1)}, f32[256,128]{1,0:T(8,128)S(1)}) custom-call(bf16[256,768]{1,0:T(8,128)(2,1)S(1)} %pad_maximum_fusion.rows_ref, f32[256,768]{1,0:T(8,128)S(1)} %get-tuple-element.28.total_ref, f32[256,128]{1,0:T(8,128)S(1)} %get-tuple-element.29.dens_ref, bf16[512,768]{1,0:T(8,128)(2,1)S(1)} %constant_dynamic-update-slice_fusion.9.refs_0_), custom_call_target="tpu_custom_call" | custom-call | flops 402653184 | tf_op jit(solution)/shard_map/middle_sums/pallas_call | solution.py:257
  31.0 0.0 collective-permute-done.10.cols_ref
  31.0 1.2 %last_sums.1 = (f32[72,768]{1,0:T(8,128)S(1)}, f32[72,768]{1,0:T(8,128)S(1)}, f32[64,768]{1,0:T(8,128)S(1)}, f32[64,768]{1,0:T(8,128)S(1)}, f32[8,128]{1,0:T(8,128)S(1)}, /*index=5*/f32[8,128]{1,0:T(8,128)S(1)}) custom-call(bf16[256,768]{1,0:T(8,128)(2,1)S(1)} %pad_maximum_fusion.rows_ref, f32[256,768]{1,0:T(8,128)S(1)} %get-tuple-element.30.total_ref, ...), custom_call_target="tpu_custom_call" | custom-call | flops 402653184 | tf_op jit(solution)/shard_map/last_sums/pallas_call | solution.py:270
  32.2 2.9 %collective-permute-start.11 = (f16[64,768]{1,0:T(8,128)(2,1)S(1)}, f16[64,768]{1,0:T(8,128)(2,1)S(1)}, u32[]{:S(2)}, u32[]{:S(2)}) collective-permute-start(f16[64,768]{1,0:T(8,128)(2,1)S(1)} %convert_element_type.24), channel_id=1, source_target_pairs={{0,24},{8,16},{16,8},{24,0},{1,25},{9,17},{17,9},{25,1},{2,26},{10... | collective-permute-start | bytes 294920 | tf_op jit(solution)/shard_map/ppermute | solution.py:210
  35.1 0.1 collective-permute-start.12
  35.2 1.6 %collective-permute-start.13 = (f16[72,768]{1,0:T(8,128)(2,1)S(1)}, f16[72,768]{1,0:T(8,128)(2,1)S(1)}, u32[]{:S(2)}, u32[]{:S(2)}) collective-permute-start(f16[72,768]{1,0:T(8,128)(2,1)S(1)} %convert_element_type.28), channel_id=1, source_target_pairs={{0,8},{8,0},{16,24},{24,16},{1,9},{9,1},{17,25},{25,17},{2,10},{10... | collective-permute-start | bytes 331784 | tf_op jit(solution)/shard_map/ppermute | solution.py:210
  36.8 2.8 %collective-permute-start.14 = (f32[8,128]{1,0:T(8,128)S(1)}, f32[8,128]{1,0:T(8,128)S(1)}, u32[]{:S(2)}, u32[]{:S(2)}) collective-permute-start(f32[8,128]{1,0:T(8,128)S(1)} %get-tuple-element.36), channel_id=1, source_target_pairs={{0,24},{8,16},{16,8},{24,0},{1,25},{9,17},{17,9},{25,1},{2,26},{10... | collective-permute-start | bytes 12296 | tf_op jit(solution)/shard_map/ppermute | solution.py:210
  39.6 0.1 collective-permute-done.11
  39.8 4.6 %collective-permute-done.12 = f16[64,768]{1,0:T(8,128)(2,1)S(1)} collective-permute-done((f16[64,768]{1,0:T(8,128)(2,1)S(1)}, f16[64,768]{1,0:T(8,128)(2,1)S(1)}, u32[]{:S(2)}, u32[]{:S(2)}) %collective-permute-start.12) | collective-permute-done | bytes 98336 | tf_op jit(solution)/shard_map/ppermute | solution.py:210
  44.4 0.0 collective-permute-done.15.refs_5_
  44.4 1.4 %restore_rows.1 = (f32[256,768]{1,0:T(8,128)}, f32[1,256]{1,0:T(1,128)}) custom-call(bf16[256,256]{1,0:T(8,128)(2,1)S(1)} %get-tuple-element.21.chosen_ref, f32[64,768]{1,0:T(8,128)S(1)} %convert_element_type.25.refs_0_, f32[64,768]{1,0:T(8,128)S(1)} %convert_element_type.27.refs_1_, f32[72,768]{1,0:T(8,128)S(1)} %convert_element_type.29.refs_2_, ...), custom_call_target="tpu_custom_call" | custom-call | tf_op jit(solution)/shard_map/restore_rows/pallas_call | solution.py:286
  (23 shorter events, 0.3 us)
Async XLA Ops:
  1.9 5.9 %collective-permute-start = (bf16[64,768]{1,0:T(8,128)(2,1)S(1)}, bf16[64,768]{1,0:T(8,128)(2,1)S(1)}, u32[]{:S(2)}, u32[]{:S(2)}) collective-permute-start(bf16[64,768]{1,0:T(8,128)(2,1)S(1)} %get-tuple-element.23), channel_id=1, source_target_pairs={{0,8},{8,0},{16,24},{24,16},{1,9},{9,1},{17,25},{25,17},{2,10},{10... | collective-permute-start | bytes 294920 | tf_op jit(solution)/shard_map/ppermute | solution.py:210
  5.0 11.4 %collective-permute-start.5 = (bf16[64,768]{1,0:T(8,128)(2,1)S(1)}, bf16[64,768]{1,0:T(8,128)(2,1)S(1)}, u32[]{:S(2)}, u32[]{:S(2)}) collective-permute-start(bf16[64,768]{1,0:T(8,128)(2,1)S(1)} %get-tuple-element.25), channel_id=1, source_target_pairs={{0,24},{8,16},{16,8},{24,0},{1,25},{9,17},{17,9},{25,1},{2,26},{10... | collective-permute-start | bytes 294920 | tf_op jit(solution)/shard_map/ppermute | solution.py:210
  7.5 8.9 %collective-permute-start.4 = (bf16[64,768]{1,0:T(8,128)(2,1)S(1)}, bf16[64,768]{1,0:T(8,128)(2,1)S(1)}, u32[]{:S(2)}, u32[]{:S(2)}) collective-permute-start(bf16[64,768]{1,0:T(8,128)(2,1)S(1)} %get-tuple-element.24), channel_id=1, source_target_pairs={{0,16},{8,24},{16,0},{24,8},{1,17},{9,25},{17,1},{25,9},{2,18},{10... | collective-permute-start | bytes 294920 | tf_op jit(solution)/shard_map/ppermute | solution.py:210
  7.8 11.7 %collective-permute-start.1 = (bf16[128,768]{1,0:T(8,128)(2,1)S(1)}, bf16[128,768]{1,0:T(8,128)(2,1)S(1)}, u32[]{:S(2)}, u32[]{:S(2)}) collective-permute-start(bf16[128,768]{1,0:T(8,128)(2,1)S(1)} %get-tuple-element.44), channel_id=1, source_target_pairs={{0,6},{1,7},{2,4},{3,5},{4,2},{5,3},{6,0},{7,1},{8,14},{9,15},{10,... | collective-permute-start | bytes 589832 | tf_op jit(solution)/shard_map/ppermute | solution.py:213
  10.6 9.6 %collective-permute-start.2 = (bf16[128,768]{1,0:T(8,128)(2,1)S(1)}, bf16[128,768]{1,0:T(8,128)(2,1)S(1)}, u32[]{:S(2)}, u32[]{:S(2)}) collective-permute-start(bf16[128,768]{1,0:T(8,128)(2,1)S(1)} %get-tuple-element.44), channel_id=1, source_target_pairs={{0,2},{1,5},{2,0},{3,7},{4,6},{5,1},{6,4},{7,3},{8,10},{9,13},{10,... | collective-permute-start | bytes 589832 | tf_op jit(solution)/shard_map/ppermute | solution.py:233
  11.1 9.1 %collective-permute-start.3 = (bf16[128,768]{1,0:T(8,128)(2,1)S(1)}, bf16[128,768]{1,0:T(8,128)(2,1)S(1)}, u32[]{:S(2)}, u32[]{:S(2)}) collective-permute-start(bf16[128,768]{1,0:T(8,128)(2,1)S(1)} %get-tuple-element.44), channel_id=1, source_target_pairs={{0,4},{1,3},{2,6},{3,1},{4,0},{5,7},{6,2},{7,5},{8,12},{9,11},{10,... | collective-permute-start | bytes 589832 | tf_op jit(solution)/shard_map/ppermute | solution.py:233
  16.5 8.8 %collective-permute-start.7 = (bf16[128,768]{1,0:T(8,128)(2,1)S(1)}, bf16[128,768]{1,0:T(8,128)(2,1)S(1)}, u32[]{:S(2)}, u32[]{:S(2)}) collective-permute-start(bf16[128,768]{1,0:T(8,128)(2,1)S(1)} %get-tuple-element.40), channel_id=1, source_target_pairs={{0,6},{1,7},{2,4},{3,5},{4,2},{5,3},{6,0},{7,1},{8,14},{9,15},{10,... | collective-permute-start | bytes 589832 | tf_op jit(solution)/shard_map/ppermute | solution.py:213
  19.0 9.2 %collective-permute-start.8 = (bf16[128,768]{1,0:T(8,128)(2,1)S(1)}, bf16[128,768]{1,0:T(8,128)(2,1)S(1)}, u32[]{:S(2)}, u32[]{:S(2)}) collective-permute-start(bf16[128,768]{1,0:T(8,128)(2,1)S(1)} %get-tuple-element.40), channel_id=1, source_target_pairs={{0,2},{1,5},{2,0},{3,7},{4,6},{5,1},{6,4},{7,3},{8,10},{9,13},{10,... | collective-permute-start | bytes 589832 | tf_op jit(solution)/shard_map/ppermute | solution.py:233
  19.6 8.6 %collective-permute-start.9 = (bf16[128,768]{1,0:T(8,128)(2,1)S(1)}, bf16[128,768]{1,0:T(8,128)(2,1)S(1)}, u32[]{:S(2)}, u32[]{:S(2)}) collective-permute-start(bf16[128,768]{1,0:T(8,128)(2,1)S(1)} %get-tuple-element.40), channel_id=1, source_target_pairs={{0,4},{1,3},{2,6},{3,1},{4,0},{5,7},{6,2},{7,5},{8,12},{9,11},{10,... | collective-permute-start | bytes 589832 | tf_op jit(solution)/shard_map/ppermute | solution.py:233
  20.3 8.1 %collective-permute-start.6 = (bf16[512,768]{1,0:T(8,128)(2,1)S(1)}, bf16[512,768]{1,0:T(8,128)(2,1)S(1)}, u32[]{:S(2)}, u32[]{:S(2)}) collective-permute-start(bf16[512,768]{1,0:T(8,128)(2,1)S(1)} %constant_dynamic-update-slice_fusion.2.refs_0_), channel_id=1, source_target_pairs={{0,1},{1,0},{2,3},{3,2},{4,5},{5,4},{6,7},{7,6},{8,9},{9,8},{10,11... | collective-permute-start | bytes 2359304 | tf_op jit(solution)/shard_map/ppermute | solution.py:213
  28.2 2.8 %collective-permute-start.10 = (bf16[512,768]{1,0:T(8,128)(2,1)S(1)}, bf16[512,768]{1,0:T(8,128)(2,1)S(1)}, u32[]{:S(2)}, u32[]{:S(2)}) collective-permute-start(bf16[512,768]{1,0:T(8,128)(2,1)S(1)} %constant_dynamic-update-slice_fusion.9.refs_0_), channel_id=1, source_target_pairs={{0,1},{1,0},{2,3},{3,2},{4,5},{5,4},{6,7},{7,6},{8,9},{9,8},{10,11... | collective-permute-start | bytes 2359304 | tf_op jit(solution)/shard_map/ppermute | solution.py:213
  32.2 7.6 %collective-permute-start.11 = (f16[64,768]{1,0:T(8,128)(2,1)S(1)}, f16[64,768]{1,0:T(8,128)(2,1)S(1)}, u32[]{:S(2)}, u32[]{:S(2)}) collective-permute-start(f16[64,768]{1,0:T(8,128)(2,1)S(1)} %convert_element_type.24), channel_id=1, source_target_pairs={{0,24},{8,16},{16,8},{24,0},{1,25},{9,17},{17,9},{25,1},{2,26},{10... | collective-permute-start | bytes 294920 | tf_op jit(solution)/shard_map/ppermute | solution.py:210
  35.1 9.2 %collective-permute-start.12 = (f16[64,768]{1,0:T(8,128)(2,1)S(1)}, f16[64,768]{1,0:T(8,128)(2,1)S(1)}, u32[]{:S(2)}, u32[]{:S(2)}) collective-permute-start(f16[64,768]{1,0:T(8,128)(2,1)S(1)} %convert_element_type.26), channel_id=1, source_target_pairs={{0,16},{8,24},{16,0},{24,8},{1,17},{9,25},{17,1},{25,9},{2,18},{10... | collective-permute-start | bytes 294920 | tf_op jit(solution)/shard_map/ppermute | solution.py:210
  35.2 9.2 %collective-permute-start.13 = (f16[72,768]{1,0:T(8,128)(2,1)S(1)}, f16[72,768]{1,0:T(8,128)(2,1)S(1)}, u32[]{:S(2)}, u32[]{:S(2)}) collective-permute-start(f16[72,768]{1,0:T(8,128)(2,1)S(1)} %convert_element_type.28), channel_id=1, source_target_pairs={{0,8},{8,0},{16,24},{24,16},{1,9},{9,1},{17,25},{25,17},{2,10},{10... | collective-permute-start | bytes 331784 | tf_op jit(solution)/shard_map/ppermute | solution.py:210
  36.8 7.6 %collective-permute-start.14 = (f32[8,128]{1,0:T(8,128)S(1)}, f32[8,128]{1,0:T(8,128)S(1)}, u32[]{:S(2)}, u32[]{:S(2)}) collective-permute-start(f32[8,128]{1,0:T(8,128)S(1)} %get-tuple-element.36), channel_id=1, source_target_pairs={{0,24},{8,16},{16,8},{24,0},{1,25},{9,17},{17,9},{25,1},{2,26},{10... | collective-permute-start | bytes 12296 | tf_op jit(solution)/shard_map/ppermute | solution.py:210
  39.6 4.8 %collective-permute-start.15 = (f32[8,128]{1,0:T(8,128)S(1)}, f32[8,128]{1,0:T(8,128)S(1)}, u32[]{:S(2)}, u32[]{:S(2)}) collective-permute-start(f32[8,128]{1,0:T(8,128)S(1)} %get-tuple-element.37), channel_id=1, source_target_pairs={{0,16},{8,24},{16,0},{24,8},{1,17},{9,25},{17,1},{25,9},{2,18},{10... | collective-permute-start | bytes 12296 | tf_op jit(solution)/shard_map/ppermute | solution.py:210

commit v9 on v8

--- a/solution.py
+++ b/solution.py
@@ -12,6 +12,7 @@
 LANES = 128
 EXTRA = 8
 TOP = 14.0
+COPIES = 4
 VMEM = pl.BlockSpec(memory_space=pltpu.VMEM)
 HBM = pl.BlockSpec(memory_space=pltpu.HBM)
 SMEM = pl.BlockSpec(memory_space=pltpu.SMEM)
@@ -54,18 +55,28 @@
     return jnp.where(first == slot, 1.0, 0.0)
 
 
+def row_blocks(count):
+    size = count // COPIES
+    return [pl.ds(k * size, size) for k in range(COPIES)]
+
+
 def sort_kernel(own_ref, ids_hbm, rows_hbm, *refs):
     chosen_ref, *out_refs = refs[:-4]
     ids_ref, rows_ref, ids_sem, rows_sem = refs[-4:]
     groups = len(out_refs)
     ids_copy = pltpu.make_async_copy(ids_hbm, ids_ref, ids_sem)
-    rows_copy = pltpu.make_async_copy(rows_hbm, rows_ref, rows_sem)
     ids_copy.start()
-    rows_copy.start()
+    row_copies = []
+    for k, rows in enumerate(row_blocks(rows_hbm.shape[0])):
+        row_copies.append(
+            pltpu.make_async_copy(rows_hbm.at[rows], rows_ref.at[rows], rows_sem.at[k])
+        )
+        row_copies[-1].start()
     ids_copy.wait()
     chosen = placement(own_ref[0], ids_ref[...], groups).astype(jnp.bfloat16)
     chosen_ref[...] = chosen
-    rows_copy.wait()
+    for row_copy in row_copies:
+        row_copy.wait()
     ordered = jnp.dot(chosen, rows_ref[...], preferred_element_type=jnp.float32)
     ordered = ordered.astype(jnp.bfloat16)
     size = ordered.shape[0] // groups
@@ -154,12 +165,18 @@
             aside_ref[top + line : top + line + 1, :size] = as_row(column[rows, :])
 
 
-def restore_kernel(half, chosen_ref, *refs):
-    refs, (total_ref, dens_ref) = refs[:-2], refs[-2:]
+def turn_kernel(chosen_ref, turned_ref):
+    turned_ref[...] = chosen_ref[...].astype(jnp.float32).T.astype(jnp.bfloat16)
+
+
+def restore_kernel(half, chosen_ref, turned_ref, *refs):
+    refs, (total_hbm, dens_hbm, total_ref, dens_ref, total_sem, dens_sem) = (
+        refs[:-6],
+        refs[-6:],
+    )
     groups = len(refs) - half
     part_refs = refs[groups - 1 :: -1] + refs[: groups - 1 : -1]
     size = part_refs[half].shape[0]
-    chosen = chosen_ref[...]
     sums, dens = [], []
     for k in range(groups):
         aside_ref, top = (part_refs[k], size) if k < half else (part_refs[half + k], 0)
@@ -171,17 +188,28 @@
         part = sum(piece * 2.0 ** (-8 * j) for j, piece in enumerate(pieces))
         dens.append(part * jnp.exp2(dens_power))
     dens_ref[...] = jnp.sum(
-        chosen.astype(jnp.float32) * jnp.concatenate(dens, axis=0), axis=0, keepdims=True
-    )
+        chosen_ref[...].astype(jnp.float32) * jnp.concatenate(dens, axis=0),
+        axis=0,
+        keepdims=True,
+    )
+    copies = [pltpu.make_async_copy(dens_ref, dens_hbm, dens_sem)]
+    copies[0].start()
     rest = jnp.concatenate(sums, axis=0)
-    back = jnp.zeros(rest.shape, jnp.float32)
-    for _ in range(2):
-        piece = rest.astype(jnp.bfloat16)
-        rest = rest - piece.astype(jnp.float32)
-        back += lax.dot_general(
-            chosen, piece, (((0,), (0,)), ((), ())), preferred_element_type=jnp.float32
+    high = rest.astype(jnp.bfloat16)
+    low = (rest - high.astype(jnp.float32)).astype(jnp.bfloat16)
+    for k, rows in enumerate(row_blocks(total_ref.shape[0])):
+        turned = turned_ref[rows, :]
+        total_ref[rows, :] = jnp.dot(
+            turned, high, preferred_element_type=jnp.float32
+        ) + jnp.dot(turned, low, preferred_element_type=jnp.float32)
+        copies.append(
+            pltpu.make_async_copy(
+                total_ref.at[rows], total_hbm.at[rows], total_sem.at[k]
+            )
         )
-    total_ref[...] = back
+        copies[-1].start()
+    for copy in copies:
+        copy.wait()
 
 
 def on_device(n_gr, n_gc, embeddings, cluster_ids):
@@ -200,7 +228,7 @@
             pltpu.VMEM((1, count), jnp.int32),
             pltpu.VMEM((count, width), embeddings.dtype),
             pltpu.SemaphoreType.DMA,
-            pltpu.SemaphoreType.DMA,
+            pltpu.SemaphoreType.DMA((COPIES,)),
         ],
         compiler_params=GRANT,
         name="sort_rows",
@@ -282,18 +310,33 @@
     sent = [part.astype(jnp.float16) for part in sums[:n_gr]]
     back = [sent[0]] + [along_gr(sent[k], k) for k in range(1, n_gr)]
     back = [part.astype(jnp.float32) for part in back]
+    chosen, back[0] = lax.optimization_barrier((chosen, back[0]))
     back += [along_gr(sums[half + k], k) for k in range(half, n_gr)]
+    turned = pl.pallas_call(
+        turn_kernel,
+        out_shape=jax.ShapeDtypeStruct((count, count), jnp.bfloat16),
+        in_specs=[VMEM],
+        out_specs=VMEM,
+        compiler_params=GRANT,
+        name="turn_matrix",
+    )(chosen)
     neighbour_sum, density = pl.pallas_call(
         functools.partial(restore_kernel, half),
         out_shape=[
             jax.ShapeDtypeStruct((count, width), jnp.float32),
             jax.ShapeDtypeStruct((1, count), jnp.float32),
         ],
-        in_specs=[VMEM] * (1 + len(back)),
-        out_specs=[VMEM, VMEM],
+        in_specs=[VMEM] * (2 + len(back)),
+        out_specs=[HBM, HBM],
+        scratch_shapes=[
+            pltpu.VMEM((count, width), jnp.float32),
+            pltpu.VMEM((1, count), jnp.float32),
+            pltpu.SemaphoreType.DMA((COPIES,)),
+            pltpu.SemaphoreType.DMA,
+        ],
         compiler_params=GRANT,
         name="restore_rows",
-    )(chosen, *back[n_gr - 1 :: -1], *back[:n_gr - 1 : -1])
+    )(chosen, turned, *back[n_gr - 1 :: -1], *back[:n_gr - 1 : -1])
     return (neighbour_sum, density.reshape(count))
 
 

time: 46 us -> 46.2 us (level)
  transfers between devices with their start and end apart: 16 -> 16, of which waited for: 6 -> 5; matrix products, arithmetic and copies ran while one was open for 1% -> 1% of each run, Pallas kernels for 6% -> 6%
where the time goes in v9:
time: 46.2 us; the launch traced here: 46 us
  starting transfers between devices  20.4 us (44%)
  waiting for transfers between devices  17.7 us (38%)
  Pallas kernels  6.85 us (15%)
  between operations  0.86 us (2%)
    ppermute x8, starting transfers between devices, along_gr(): return lax.ppermute(part, 'gr', [(i, i ^ bits) for i in range(n_gr)])  13 us
    ppermute x8, waiting for transfers between devices, along_gr(): return lax.ppermute(part, 'gr', [(i, i ^ bits) for i in range(n_gr)])  9.82 us
    ppermute x4, starting transfers between devices, along_gc(): return lax.ppermute(block, 'gc', [(i, i ^ bits) for i in range(n_gc)])  5.41 us
    ppermute x4, waiting for transfers between devices, along_gc(): return lax.ppermute(block, 'gc', [(i, i ^ bits) for i in range(n_gc)])  4.97 us
    ppermute x4, waiting for transfers between devices, to_side(): return lax.ppermute(block, 'gc', pairs)  2.87 us
    ppermute x4, starting transfers between devices, to_side(): return lax.ppermute(block, 'gc', pairs)  1.9 us
    pallas_call x1, Pallas kernels, on_device(): pl.pallas_call(first_kernel, out_shape=[jax.ShapeDtypeStruct((count, widt...  1.71 us
    pallas_call x1, Pallas kernels, on_device(): pl.pallas_call(functools.partial(restore_kernel, half), out_shape=[jax.Sh...  1.53 us
  transfers between devices with their start and end apart: 16, of which 5 were waited for; matrix products, arithmetic and copies ran while one was open for 1% of the time, Pallas kernels for 6%

profile of v9, /device:TPU:0, one launch (start us, length us, event | category | flops | bytes accessed | tf_op | source)
XLA Modules:
  0.0 46.0 jit_solution(2613781577675310158)
XLA Ops:
  0.6 1.4 %sort_rows.1 = (bf16[256,256]{1,0:T(8,128)(2,1)S(1)}, bf16[64,768]{1,0:T(8,128)(2,1)S(1)}, bf16[64,768]{1,0:T(8,128)(2,1)S(1)}, bf16[64,768]{1,0:T(8,128)(2,1)S(1)}, bf16[64,768]{1,0:T(8,128)(2,1)S(1)}) custom-call(s32[1]{0:T(128)} %bitcast.own_ref, s32[1,256]{1,0:T(1,128)} %bitcast.3, bf16[256,768]{1,0:T(8,128)(2,1)} %rows_hbm.1), custom_call_target="tpu_custom_call" | custom-call | tf_op jit(solution)/shard_map/sort_rows/pallas_call | solution.py:221
  2.0 3.1 %collective-permute-start = (bf16[64,768]{1,0:T(8,128)(2,1)S(1)}, bf16[64,768]{1,0:T(8,128)(2,1)S(1)}, u32[]{:S(2)}, u32[]{:S(2)}) collective-permute-start(bf16[64,768]{1,0:T(8,128)(2,1)S(1)} %get-tuple-element.25), channel_id=1, source_target_pairs={{0,8},{8,0},{16,24},{24,16},{1,9},{9,1},{17,25},{25,17},{2,10},{10... | collective-permute-start | bytes 294920 | tf_op jit(solution)/shard_map/ppermute | solution.py:238
  5.1 2.5 %collective-permute-start.5 = (bf16[64,768]{1,0:T(8,128)(2,1)S(1)}, bf16[64,768]{1,0:T(8,128)(2,1)S(1)}, u32[]{:S(2)}, u32[]{:S(2)}) collective-permute-start(bf16[64,768]{1,0:T(8,128)(2,1)S(1)} %get-tuple-element.27), channel_id=1, source_target_pairs={{0,24},{8,16},{16,8},{24,0},{1,25},{9,17},{17,9},{25,1},{2,26},{10... | collective-permute-start | bytes 294920 | tf_op jit(solution)/shard_map/ppermute | solution.py:238
  7.6 0.1 collective-permute-start.4
  7.7 0.2 collective-permute-done
  7.9 2.8 %collective-permute-start.1 = (bf16[128,768]{1,0:T(8,128)(2,1)S(1)}, bf16[128,768]{1,0:T(8,128)(2,1)S(1)}, u32[]{:S(2)}, u32[]{:S(2)}) collective-permute-start(bf16[128,768]{1,0:T(8,128)(2,1)S(1)} %get-tuple-element.48), channel_id=1, source_target_pairs={{0,6},{1,7},{2,4},{3,5},{4,2},{5,3},{6,0},{7,1},{8,14},{9,15},{10,... | collective-permute-start | bytes 589832 | tf_op jit(solution)/shard_map/ppermute | solution.py:241
  10.7 0.5 %collective-permute-start.2 = (bf16[128,768]{1,0:T(8,128)(2,1)S(1)}, bf16[128,768]{1,0:T(8,128)(2,1)S(1)}, u32[]{:S(2)}, u32[]{:S(2)}) collective-permute-start(bf16[128,768]{1,0:T(8,128)(2,1)S(1)} %get-tuple-element.48), channel_id=1, source_target_pairs={{0,2},{1,5},{2,0},{3,7},{4,6},{5,1},{6,4},{7,3},{8,10},{9,13},{10,... | collective-permute-start | bytes 589832 | tf_op jit(solution)/shard_map/ppermute | solution.py:261
  11.2 0.3 collective-permute-start.3
  11.5 5.1 %collective-permute-done.4 = bf16[64,768]{1,0:T(8,128)(2,1)S(1)} collective-permute-done((bf16[64,768]{1,0:T(8,128)(2,1)S(1)}, bf16[64,768]{1,0:T(8,128)(2,1)S(1)}, u32[]{:S(2)}, u32[]{:S(2)}) %collective-permute-start.4) | collective-permute-done | bytes 98336 | tf_op jit(solution)/shard_map/ppermute | solution.py:238
  16.5 0.0 collective-permute-done.5
  16.6 2.5 %collective-permute-start.7 = (bf16[128,768]{1,0:T(8,128)(2,1)S(1)}, bf16[128,768]{1,0:T(8,128)(2,1)S(1)}, u32[]{:S(2)}, u32[]{:S(2)}) collective-permute-start(bf16[128,768]{1,0:T(8,128)(2,1)S(1)} %get-tuple-element.44), channel_id=1, source_target_pairs={{0,6},{1,7},{2,4},{3,5},{4,2},{5,3},{6,0},{7,1},{8,14},{9,15},{10,... | collective-permute-start | bytes 589832 | tf_op jit(solution)/shard_map/ppermute | solution.py:241
  19.1 0.5 %collective-permute-start.8 = (bf16[128,768]{1,0:T(8,128)(2,1)S(1)}, bf16[128,768]{1,0:T(8,128)(2,1)S(1)}, u32[]{:S(2)}, u32[]{:S(2)}) collective-permute-start(bf16[128,768]{1,0:T(8,128)(2,1)S(1)} %get-tuple-element.44), channel_id=1, source_target_pairs={{0,2},{1,5},{2,0},{3,7},{4,6},{5,1},{6,4},{7,3},{8,10},{9,13},{10,... | collective-permute-start | bytes 589832 | tf_op jit(solution)/shard_map/ppermute | solution.py:261
  19.7 0.6 %collective-permute-start.9 = (bf16[128,768]{1,0:T(8,128)(2,1)S(1)}, bf16[128,768]{1,0:T(8,128)(2,1)S(1)}, u32[]{:S(2)}, u32[]{:S(2)}) collective-permute-start(bf16[128,768]{1,0:T(8,128)(2,1)S(1)} %get-tuple-element.44), channel_id=1, source_target_pairs={{0,4},{1,3},{2,6},{3,1},{4,0},{5,7},{6,2},{7,5},{8,12},{9,11},{10,... | collective-permute-start | bytes 589832 | tf_op jit(solution)/shard_map/ppermute | solution.py:261
  20.2 0.0 collective-permute-done.2
  20.3 0.1 collective-permute-start.6
  20.4 5.0 %collective-permute-done.7 = bf16[128,768]{1,0:T(8,128)(2,1)S(1)} collective-permute-done((bf16[128,768]{1,0:T(8,128)(2,1)S(1)}, bf16[128,768]{1,0:T(8,128)(2,1)S(1)}, u32[]{:S(2)}, u32[]{:S(2)}) %collective-permute-start.7) | collective-permute-done | bytes 196640 | tf_op jit(solution)/shard_map/ppermute | solution.py:241
  25.4 2.9 %collective-permute-done.8 = bf16[128,768]{1,0:T(8,128)(2,1)S(1)} collective-permute-done((bf16[128,768]{1,0:T(8,128)(2,1)S(1)}, bf16[128,768]{1,0:T(8,128)(2,1)S(1)}, u32[]{:S(2)}, u32[]{:S(2)}) %collective-permute-start.8) | collective-permute-done | bytes 196640 | tf_op jit(solution)/shard_map/ppermute | solution.py:261
  28.3 0.0 collective-permute-done.9
  28.3 0.1 collective-permute-start.10
  28.4 0.0 collective-permute-done.6.refs_1_
  28.4 1.7 %early_sums.1 = (f32[256,768]{1,0:T(8,128)S(1)}, f32[256,128]{1,0:T(8,128)S(1)}) custom-call(bf16[256,768]{1,0:T(8,128)(2,1)S(1)} %pad_maximum_fusion.rows_ref, bf16[512,768]{1,0:T(8,128)(2,1)S(1)} %constant_dynamic-update-slice_fusion.2.refs_0_, bf16[512,768]{1,0:T(8,128)(2,1)S(1)} %collective-permute-done.6.refs_1_), custom_call_target="tpu_custom_call" | custom-call | flops 805306368 | tf_op jit(solution)/shard_map/early_sums/pallas_call | solution.py:273
  30.1 1.0 %middle_sums.1 = (f32[256,768]{1,0:T(8,128)S(1)}, f32[256,128]{1,0:T(8,128)S(1)}) custom-call(bf16[256,768]{1,0:T(8,128)(2,1)S(1)} %pad_maximum_fusion.rows_ref, f32[256,768]{1,0:T(8,128)S(1)} %get-tuple-element.30.total_ref, f32[256,128]{1,0:T(8,128)S(1)} %get-tuple-element.31.dens_ref, bf16[512,768]{1,0:T(8,128)(2,1)S(1)} %constant_dynamic-update-slice_fusion.9.refs_0_), custom_call_target="tpu_custom_call" | custom-call | flops 402653184 | tf_op jit(solution)/shard_map/middle_sums/pallas_call | solution.py:285
  31.1 1.2 %last_sums.1 = (f32[72,768]{1,0:T(8,128)S(1)}, f32[72,768]{1,0:T(8,128)S(1)}, f32[64,768]{1,0:T(8,128)S(1)}, f32[64,768]{1,0:T(8,128)S(1)}, f32[8,128]{1,0:T(8,128)S(1)}, /*index=5*/f32[8,128]{1,0:T(8,128)S(1)}) custom-call(bf16[256,768]{1,0:T(8,128)(2,1)S(1)} %pad_maximum_fusion.rows_ref, f32[256,768]{1,0:T(8,128)S(1)} %get-tuple-element.32.total_ref, ...), custom_call_target="tpu_custom_call" | custom-call | flops 402653184 | tf_op jit(solution)/shard_map/last_sums/pallas_call | solution.py:298
  32.3 2.9 %collective-permute-start.11 = (f16[64,768]{1,0:T(8,128)(2,1)S(1)}, f16[64,768]{1,0:T(8,128)(2,1)S(1)}, u32[]{:S(2)}, u32[]{:S(2)}) collective-permute-start(f16[64,768]{1,0:T(8,128)(2,1)S(1)} %convert_element_type.26), channel_id=1, source_target_pairs={{0,24},{8,16},{16,8},{24,0},{1,25},{9,17},{17,9},{25,1},{2,26},{10... | collective-permute-start | bytes 294920 | tf_op jit(solution)/shard_map/ppermute | solution.py:238
  35.1 0.1 collective-permute-start.12
  35.3 1.6 %collective-permute-start.13 = (f16[72,768]{1,0:T(8,128)(2,1)S(1)}, f16[72,768]{1,0:T(8,128)(2,1)S(1)}, u32[]{:S(2)}, u32[]{:S(2)}) collective-permute-start(f16[72,768]{1,0:T(8,128)(2,1)S(1)} %convert_element_type.30), channel_id=1, source_target_pairs={{0,8},{8,0},{16,24},{24,16},{1,9},{9,1},{17,25},{25,17},{2,10},{10... | collective-permute-start | bytes 331784 | tf_op jit(solution)/shard_map/ppermute | solution.py:238
  36.9 2.8 %collective-permute-start.14 = (f32[8,128]{1,0:T(8,128)S(1)}, f32[8,128]{1,0:T(8,128)S(1)}, u32[]{:S(2)}, u32[]{:S(2)}) collective-permute-start(f32[8,128]{1,0:T(8,128)S(1)} %get-tuple-element.40), channel_id=1, source_target_pairs={{0,24},{8,16},{16,8},{24,0},{1,25},{9,17},{17,9},{25,1},{2,26},{10... | collective-permute-start | bytes 12296 | tf_op jit(solution)/shard_map/ppermute | solution.py:238
  39.7 0.1 turn_matrix.1.turned_ref
  39.8 0.0 collective-permute-done.11
  39.9 4.5 %collective-permute-done.12 = f16[64,768]{1,0:T(8,128)(2,1)S(1)} collective-permute-done((f16[64,768]{1,0:T(8,128)(2,1)S(1)}, f16[64,768]{1,0:T(8,128)(2,1)S(1)}, u32[]{:S(2)}, u32[]{:S(2)}) %collective-permute-start.12) | collective-permute-done | bytes 98336 | tf_op jit(solution)/shard_map/ppermute | solution.py:238
  44.5 0.0 collective-permute-done.15.refs_5_
  44.5 1.5 %restore_rows.1 = (f32[256,768]{1,0:T(8,128)}, f32[1,256]{1,0:T(1,128)}) custom-call(bf16[256,256]{1,0:T(8,128)(2,1)S(1)} %get-tuple-element.35.chosen_ref, bf16[256,256]{1,0:T(8,128)(2,1)S(1)} %turn_matrix.1.turned_ref, f32[64,768]{1,0:T(8,128)S(1)} %convert_element_type.27.refs_0_, f32[64,768]{1,0:T(8,128)S(1)} %convert_element_type.29.refs_1_, ...), custom_call_target="tpu_custom_call" | custom-call | tf_op jit(solution)/shard_map/restore_rows/pallas_call | solution.py:323
  (24 shorter events, 0.3 us)
Async XLA Ops:
  2.0 5.9 %collective-permute-start = (bf16[64,768]{1,0:T(8,128)(2,1)S(1)}, bf16[64,768]{1,0:T(8,128)(2,1)S(1)}, u32[]{:S(2)}, u32[]{:S(2)}) collective-permute-start(bf16[64,768]{1,0:T(8,128)(2,1)S(1)} %get-tuple-element.25), channel_id=1, source_target_pairs={{0,8},{8,0},{16,24},{24,16},{1,9},{9,1},{17,25},{25,17},{2,10},{10... | collective-permute-start | bytes 294920 | tf_op jit(solution)/shard_map/ppermute | solution.py:238
  5.1 11.4 %collective-permute-start.5 = (bf16[64,768]{1,0:T(8,128)(2,1)S(1)}, bf16[64,768]{1,0:T(8,128)(2,1)S(1)}, u32[]{:S(2)}, u32[]{:S(2)}) collective-permute-start(bf16[64,768]{1,0:T(8,128)(2,1)S(1)} %get-tuple-element.27), channel_id=1, source_target_pairs={{0,24},{8,16},{16,8},{24,0},{1,25},{9,17},{17,9},{25,1},{2,26},{10... | collective-permute-start | bytes 294920 | tf_op jit(solution)/shard_map/ppermute | solution.py:238
  7.6 8.9 %collective-permute-start.4 = (bf16[64,768]{1,0:T(8,128)(2,1)S(1)}, bf16[64,768]{1,0:T(8,128)(2,1)S(1)}, u32[]{:S(2)}, u32[]{:S(2)}) collective-permute-start(bf16[64,768]{1,0:T(8,128)(2,1)S(1)} %get-tuple-element.26), channel_id=1, source_target_pairs={{0,16},{8,24},{16,0},{24,8},{1,17},{9,25},{17,1},{25,9},{2,18},{10... | collective-permute-start | bytes 294920 | tf_op jit(solution)/shard_map/ppermute | solution.py:238
  7.9 11.7 %collective-permute-start.1 = (bf16[128,768]{1,0:T(8,128)(2,1)S(1)}, bf16[128,768]{1,0:T(8,128)(2,1)S(1)}, u32[]{:S(2)}, u32[]{:S(2)}) collective-permute-start(bf16[128,768]{1,0:T(8,128)(2,1)S(1)} %get-tuple-element.48), channel_id=1, source_target_pairs={{0,6},{1,7},{2,4},{3,5},{4,2},{5,3},{6,0},{7,1},{8,14},{9,15},{10,... | collective-permute-start | bytes 589832 | tf_op jit(solution)/shard_map/ppermute | solution.py:241
  10.7 9.6 %collective-permute-start.2 = (bf16[128,768]{1,0:T(8,128)(2,1)S(1)}, bf16[128,768]{1,0:T(8,128)(2,1)S(1)}, u32[]{:S(2)}, u32[]{:S(2)}) collective-permute-start(bf16[128,768]{1,0:T(8,128)(2,1)S(1)} %get-tuple-element.48), channel_id=1, source_target_pairs={{0,2},{1,5},{2,0},{3,7},{4,6},{5,1},{6,4},{7,3},{8,10},{9,13},{10,... | collective-permute-start | bytes 589832 | tf_op jit(solution)/shard_map/ppermute | solution.py:261
  11.2 9.1 %collective-permute-start.3 = (bf16[128,768]{1,0:T(8,128)(2,1)S(1)}, bf16[128,768]{1,0:T(8,128)(2,1)S(1)}, u32[]{:S(2)}, u32[]{:S(2)}) collective-permute-start(bf16[128,768]{1,0:T(8,128)(2,1)S(1)} %get-tuple-element.48), channel_id=1, source_target_pairs={{0,4},{1,3},{2,6},{3,1},{4,0},{5,7},{6,2},{7,5},{8,12},{9,11},{10,... | collective-permute-start | bytes 589832 | tf_op jit(solution)/shard_map/ppermute | solution.py:261
  16.6 8.8 %collective-permute-start.7 = (bf16[128,768]{1,0:T(8,128)(2,1)S(1)}, bf16[128,768]{1,0:T(8,128)(2,1)S(1)}, u32[]{:S(2)}, u32[]{:S(2)}) collective-permute-start(bf16[128,768]{1,0:T(8,128)(2,1)S(1)} %get-tuple-element.44), channel_id=1, source_target_pairs={{0,6},{1,7},{2,4},{3,5},{4,2},{5,3},{6,0},{7,1},{8,14},{9,15},{10,... | collective-permute-start | bytes 589832 | tf_op jit(solution)/shard_map/ppermute | solution.py:241
  19.1 9.2 %collective-permute-start.8 = (bf16[128,768]{1,0:T(8,128)(2,1)S(1)}, bf16[128,768]{1,0:T(8,128)(2,1)S(1)}, u32[]{:S(2)}, u32[]{:S(2)}) collective-permute-start(bf16[128,768]{1,0:T(8,128)(2,1)S(1)} %get-tuple-element.44), channel_id=1, source_target_pairs={{0,2},{1,5},{2,0},{3,7},{4,6},{5,1},{6,4},{7,3},{8,10},{9,13},{10,... | collective-permute-start | bytes 589832 | tf_op jit(solution)/shard_map/ppermute | solution.py:261
  19.7 8.6 %collective-permute-start.9 = (bf16[128,768]{1,0:T(8,128)(2,1)S(1)}, bf16[128,768]{1,0:T(8,128)(2,1)S(1)}, u32[]{:S(2)}, u32[]{:S(2)}) collective-permute-start(bf16[128,768]{1,0:T(8,128)(2,1)S(1)} %get-tuple-element.44), channel_id=1, source_target_pairs={{0,4},{1,3},{2,6},{3,1},{4,0},{5,7},{6,2},{7,5},{8,12},{9,11},{10,... | collective-permute-start | bytes 589832 | tf_op jit(solution)/shard_map/ppermute | solution.py:261
  20.3 8.1 %collective-permute-start.6 = (bf16[512,768]{1,0:T(8,128)(2,1)S(1)}, bf16[512,768]{1,0:T(8,128)(2,1)S(1)}, u32[]{:S(2)}, u32[]{:S(2)}) collective-permute-start(bf16[512,768]{1,0:T(8,128)(2,1)S(1)} %constant_dynamic-update-slice_fusion.2.refs_0_), channel_id=1, source_target_pairs={{0,1},{1,0},{2,3},{3,2},{4,5},{5,4},{6,7},{7,6},{8,9},{9,8},{10,11... | collective-permute-start | bytes 2359304 | tf_op jit(solution)/shard_map/ppermute | solution.py:241
  28.3 2.8 %collective-permute-start.10 = (bf16[512,768]{1,0:T(8,128)(2,1)S(1)}, bf16[512,768]{1,0:T(8,128)(2,1)S(1)}, u32[]{:S(2)}, u32[]{:S(2)}) collective-permute-start(bf16[512,768]{1,0:T(8,128)(2,1)S(1)} %constant_dynamic-update-slice_fusion.9.refs_0_), channel_id=1, source_target_pairs={{0,1},{1,0},{2,3},{3,2},{4,5},{5,4},{6,7},{7,6},{8,9},{9,8},{10,11... | collective-permute-start | bytes 2359304 | tf_op jit(solution)/shard_map/ppermute | solution.py:241
  32.3 7.6 %collective-permute-start.11 = (f16[64,768]{1,0:T(8,128)(2,1)S(1)}, f16[64,768]{1,0:T(8,128)(2,1)S(1)}, u32[]{:S(2)}, u32[]{:S(2)}) collective-permute-start(f16[64,768]{1,0:T(8,128)(2,1)S(1)} %convert_element_type.26), channel_id=1, source_target_pairs={{0,24},{8,16},{16,8},{24,0},{1,25},{9,17},{17,9},{25,1},{2,26},{10... | collective-permute-start | bytes 294920 | tf_op jit(solution)/shard_map/ppermute | solution.py:238
  35.1 9.2 %collective-permute-start.12 = (f16[64,768]{1,0:T(8,128)(2,1)S(1)}, f16[64,768]{1,0:T(8,128)(2,1)S(1)}, u32[]{:S(2)}, u32[]{:S(2)}) collective-permute-start(f16[64,768]{1,0:T(8,128)(2,1)S(1)} %convert_element_type.28), channel_id=1, source_target_pairs={{0,16},{8,24},{16,0},{24,8},{1,17},{9,25},{17,1},{25,9},{2,18},{10... | collective-permute-start | bytes 294920 | tf_op jit(solution)/shard_map/ppermute | solution.py:238
  35.3 9.2 %collective-permute-start.13 = (f16[72,768]{1,0:T(8,128)(2,1)S(1)}, f16[72,768]{1,0:T(8,128)(2,1)S(1)}, u32[]{:S(2)}, u32[]{:S(2)}) collective-permute-start(f16[72,768]{1,0:T(8,128)(2,1)S(1)} %convert_element_type.30), channel_id=1, source_target_pairs={{0,8},{8,0},{16,24},{24,16},{1,9},{9,1},{17,25},{25,17},{2,10},{10... | collective-permute-start | bytes 331784 | tf_op jit(solution)/shard_map/ppermute | solution.py:238
  36.9 7.5 %collective-permute-start.14 = (f32[8,128]{1,0:T(8,128)S(1)}, f32[8,128]{1,0:T(8,128)S(1)}, u32[]{:S(2)}, u32[]{:S(2)}) collective-permute-start(f32[8,128]{1,0:T(8,128)S(1)} %get-tuple-element.40), channel_id=1, source_target_pairs={{0,24},{8,16},{16,8},{24,0},{1,25},{9,17},{17,9},{25,1},{2,26},{10... | collective-permute-start | bytes 12296 | tf_op jit(solution)/shard_map/ppermute | solution.py:238
  39.7 4.8 %collective-permute-start.15 = (f32[8,128]{1,0:T(8,128)S(1)}, f32[8,128]{1,0:T(8,128)S(1)}, u32[]{:S(2)}, u32[]{:S(2)}) collective-permute-start(f32[8,128]{1,0:T(8,128)S(1)} %get-tuple-element.41), channel_id=1, source_target_pairs={{0,16},{8,24},{16,0},{24,8},{1,17},{9,25},{17,1},{25,9},{2,18},{10... | collective-permute-start | bytes 12296 | tf_op jit(solution)/shard_map/ppermute | solution.py:238

commit v10 on v8

--- a/solution.py
+++ b/solution.py
@@ -9,6 +9,8 @@
 from jax.sharding import PartitionSpec as P
 
 beta_scale = 16.0
+floor_weight = math.exp(-beta_scale)
+BLOCK = 512
 LANES = 128
 EXTRA = 8
 TOP = 14.0
@@ -73,50 +75,48 @@
         out_ref[...] = ordered[k * size : (k + 1) * size, :]
 
 
-def inverse_norms(rows):
-    wide = rows.astype(jnp.float32)
-    return lax.rsqrt(jnp.sum(wide * wide, axis=1, keepdims=True) + 1e-06)
-
-
-def add_columns(rows, col_refs, total, dens):
-    count = rows.shape[0]
-    scale = inverse_norms(rows) * (beta_scale * math.log2(math.e))
-    blocks = [
-        (col_ref, start)
-        for col_ref in col_refs
-        for start in range(0, col_ref.shape[0], count)
-    ]
-    for col_ref, start in blocks:
-        cols = col_ref[start : min(start + count, col_ref.shape[0]), :]
-        size = cols.shape[0]
-        col_inv = as_row(inverse_norms(cols))
-        raw = lax.dot_general(
-            rows, cols, (((1,), (1,)), ((), ())), preferred_element_type=jnp.float32
-        )
-        weight = jnp.exp2(raw * scale * col_inv - beta_scale * math.log2(math.e))
-        whole = size - size % LANES
-        for lane in range(0, whole, LANES):
-            dens += weight[:, lane : lane + LANES]
-        if whole < size:
-            part = jnp.sum(weight[:, whole:], axis=1, keepdims=True)
-            dens += jnp.where(lax.broadcasted_iota(jnp.int32, dens.shape, 1) == 0, part, 0.0)
-        coef = (weight * col_inv).astype(jnp.bfloat16)
-        total += jnp.dot(coef, cols, preferred_element_type=jnp.float32)
+def folded_squares(rows):
+    total = 0.0
+    for lane in range(0, rows.shape[1], LANES):
+        wide = rows[:, lane : lane + LANES].astype(jnp.float32)
+        total += wide * wide
+    return total
+
+
+def add_columns(rows, scale, col_refs, total, dens):
+    for col_ref in col_refs:
+        for start in range(0, col_ref.shape[0], BLOCK):
+            cols = col_ref[start : min(start + BLOCK, col_ref.shape[0]), :]
+            squares = jnp.sum(folded_squares(cols).T, axis=0, keepdims=True)
+            col_inv = lax.rsqrt(squares + 1e-06)
+            raw = lax.dot_general(
+                rows, cols, (((1,), (1,)), ((), ())), preferred_element_type=jnp.float32
+            )
+            weight = jnp.exp2(raw * scale * col_inv)
+            for lane in range(0, cols.shape[0], LANES):
+                dens += weight[:, lane : lane + LANES]
+            coef = (weight * (col_inv * floor_weight)).astype(jnp.bfloat16)
+            total += jnp.dot(coef, cols, preferred_element_type=jnp.float32)
     return total, dens
 
 
-def first_kernel(rows_ref, *refs):
-    col_refs, (total_ref, dens_ref) = refs[:-2], refs[-2:]
+def early_kernel(rows_ref, *refs):
+    col_refs, (scale_ref, total_ref, dens_ref) = refs[:-3], refs[-3:]
+    squares = jnp.sum(folded_squares(rows_ref[...]), axis=1, keepdims=True)
+    scale = lax.rsqrt(squares + 1e-06) * (beta_scale * math.log2(math.e))
+    scale_ref[...] = jnp.broadcast_to(scale, scale_ref.shape)
     total = jnp.zeros(total_ref.shape, jnp.float32)
     dens = jnp.zeros(dens_ref.shape, jnp.float32)
-    total, dens = add_columns(rows_ref[...], col_refs, total, dens)
+    total, dens = add_columns(rows_ref[...], scale, col_refs, total, dens)
     total_ref[...] = total
     dens_ref[...] = dens
 
 
-def middle_kernel(rows_ref, total_ref, dens_ref, *refs):
+def middle_kernel(rows_ref, scale_ref, total_ref, dens_ref, *refs):
     col_refs, (total_out, dens_out) = refs[:-2], refs[-2:]
-    total, dens = add_columns(rows_ref[...], col_refs, total_ref[...], dens_ref[...])
+    total, dens = add_columns(
+        rows_ref[...], scale_ref[:, 0:1], col_refs, total_ref[...], dens_ref[...]
+    )
     total_out[...] = total
     dens_out[...] = dens
 
@@ -125,13 +125,13 @@
     return jnp.floor(jnp.log2(jnp.maximum(value, 1e-30)))
 
 
-def last_kernel(half, rows_ref, total_ref, dens_ref, cols_ref, *out_refs):
+def last_kernel(half, rows_ref, scale_ref, total_ref, dens_ref, cols_ref, *out_refs):
     groups = len(out_refs) - half
     size = out_refs[half].shape[0]
     total, dens = add_columns(
-        rows_ref[...], [cols_ref], total_ref[...], dens_ref[...]
-    )
-    dens = jnp.sum(dens, axis=1, keepdims=True)
+        rows_ref[...], scale_ref[:, 0:1], [cols_ref], total_ref[...], dens_ref[...]
+    )
+    dens = jnp.sum(dens, axis=1, keepdims=True) * floor_weight
     power = exponent(jnp.max(jnp.abs(total), axis=1, keepdims=True))
     total = total * jnp.exp2(TOP - power)
     dens_power = exponent(dens)
@@ -240,44 +240,33 @@
         chunks.append(jnp.concatenate(near, axis=0))
     rows = jnp.concatenate(held, axis=0)
     chunks[0], rows = lax.optimization_barrier((chunks[0], rows))
-    early = [chunks[0], other_core(chunks[0])]
-
-    total, dens = pl.pallas_call(
-        first_kernel,
+    early = [chunks[0], other_core(chunks[0]), chunks[1]]
+
+    scale, total, dens = pl.pallas_call(
+        early_kernel,
         out_shape=[
+            jax.ShapeDtypeStruct((count, LANES), jnp.float32),
             jax.ShapeDtypeStruct((count, width), jnp.float32),
             jax.ShapeDtypeStruct((count, LANES), jnp.float32),
         ],
         in_specs=[VMEM] * (1 + len(early)),
-        out_specs=[VMEM] * 2,
+        out_specs=[VMEM] * 3,
         compiler_params=GRANT,
         cost_estimate=cost(*early),
         name="early_sums",
     )(rows, *early)
-    total, dens = pl.pallas_call(
-        middle_kernel,
-        out_shape=[
-            jax.ShapeDtypeStruct((count, width), jnp.float32),
-            jax.ShapeDtypeStruct((count, LANES), jnp.float32),
-        ],
-        in_specs=[VMEM] * 4,
-        out_specs=[VMEM] * 2,
-        compiler_params=GRANT,
-        cost_estimate=cost(chunks[1]),
-        name="middle_sums",
-    )(rows, total, dens, chunks[1])
-    late = [other_core(chunks[1])]
+    late = other_core(chunks[1])
     sums = pl.pallas_call(
         functools.partial(last_kernel, half),
         out_shape=[jax.ShapeDtypeStruct((size + EXTRA, width), jnp.float32)] * half
         + [jax.ShapeDtypeStruct((size, width), jnp.float32)] * (n_gr - half)
         + [jax.ShapeDtypeStruct((EXTRA, LANES), jnp.float32)] * (n_gr - half),
-        in_specs=[VMEM] * 4,
+        in_specs=[VMEM] * 5,
         out_specs=[VMEM] * (2 * n_gr - half),
         compiler_params=GRANT,
-        cost_estimate=cost(*late),
+        cost_estimate=cost(late),
         name="last_sums",
-    )(rows, total, dens, *late)
+    )(rows, scale, total, dens, late)
 
     sent = [part.astype(jnp.float16) for part in sums[:n_gr]]
     back = [sent[0]] + [along_gr(sent[k], k) for k in range(1, n_gr)]

time: 46 us -> 45 us (0.978)
  Pallas kernels: 6.59 us -> 5.55 us
    pallas_call x2 -> x1, Pallas kernels: 2.69 us -> 1.95 us  [on_device(): pl.pallas_call(early_kernel, out_shape=[jax.ShapeDtypeStruct((count, LANE...]
  transfers between devices with their start and end apart: 16 -> 16, of which waited for: 6 -> 7; matrix products, arithmetic and copies ran while one was open for 1% -> 1% of each run, Pallas kernels for 6% -> 4%
where the time goes in v10:
time: 45 us; the launch traced here: 44.8 us
  starting transfers between devices  20.4 us (45%)
  waiting for transfers between devices  17.8 us (40%)
  Pallas kernels  5.55 us (12%)
  between operations  0.85 us (2%)
    ppermute x8, starting transfers between devices, along_gr(): return lax.ppermute(part, 'gr', [(i, i ^ bits) for i in range(n_gr)])  13.1 us
    ppermute x8, waiting for transfers between devices, along_gr(): return lax.ppermute(part, 'gr', [(i, i ^ bits) for i in range(n_gr)])  9.65 us
    ppermute x4, starting transfers between devices, along_gc(): return lax.ppermute(block, 'gc', [(i, i ^ bits) for i in range(n_gc)])  5.41 us
    ppermute x4, waiting for transfers between devices, along_gc(): return lax.ppermute(block, 'gc', [(i, i ^ bits) for i in range(n_gc)])  5.28 us
    ppermute x4, waiting for transfers between devices, to_side(): return lax.ppermute(block, 'gc', pairs)  2.87 us
    pallas_call x1, Pallas kernels, on_device(): pl.pallas_call(early_kernel, out_shape=[jax.ShapeDtypeStruct((count, LANE...  1.95 us
    ppermute x4, starting transfers between devices, to_side(): return lax.ppermute(block, 'gc', pairs)  1.9 us
    pallas_call x1, Pallas kernels, on_device(): pl.pallas_call(functools.partial(restore_kernel, half), out_shape=[jax.Sh...  1.44 us
  transfers between devices with their start and end apart: 16, of which 7 were waited for; matrix products, arithmetic and copies ran while one was open for 1% of the time, Pallas kernels for 4%

profile of v10, /device:TPU:0, one launch (start us, length us, event | category | flops | bytes accessed | tf_op | source)
XLA Modules:
  0.0 44.8 jit_solution(9941716812734183766)
XLA Ops:
  0.6 1.3 %sort_rows.1 = (bf16[256,256]{1,0:T(8,128)(2,1)S(1)}, bf16[64,768]{1,0:T(8,128)(2,1)S(1)}, bf16[64,768]{1,0:T(8,128)(2,1)S(1)}, bf16[64,768]{1,0:T(8,128)(2,1)S(1)}, bf16[64,768]{1,0:T(8,128)(2,1)S(1)}) custom-call(s32[1]{0:T(128)} %bitcast.own_ref, s32[1,256]{1,0:T(1,128)} %bitcast.3, bf16[256,768]{1,0:T(8,128)(2,1)} %rows_hbm.1), custom_call_target="tpu_custom_call" | custom-call | tf_op jit(solution)/shard_map/sort_rows/pallas_call | solution.py:193
  1.9 3.1 %collective-permute-start = (bf16[64,768]{1,0:T(8,128)(2,1)S(1)}, bf16[64,768]{1,0:T(8,128)(2,1)S(1)}, u32[]{:S(2)}, u32[]{:S(2)}) collective-permute-start(bf16[64,768]{1,0:T(8,128)(2,1)S(1)} %get-tuple-element.22), channel_id=1, source_target_pairs={{0,8},{8,0},{16,24},{24,16},{1,9},{9,1},{17,25},{25,17},{2,10},{10... | collective-permute-start | bytes 294920 | tf_op jit(solution)/shard_map/ppermute | solution.py:210
  5.0 2.5 %collective-permute-start.5 = (bf16[64,768]{1,0:T(8,128)(2,1)S(1)}, bf16[64,768]{1,0:T(8,128)(2,1)S(1)}, u32[]{:S(2)}, u32[]{:S(2)}) collective-permute-start(bf16[64,768]{1,0:T(8,128)(2,1)S(1)} %get-tuple-element.24), channel_id=1, source_target_pairs={{0,24},{8,16},{16,8},{24,0},{1,25},{9,17},{17,9},{25,1},{2,26},{10... | collective-permute-start | bytes 294920 | tf_op jit(solution)/shard_map/ppermute | solution.py:210
  7.5 0.1 collective-permute-start.4
  7.6 0.2 collective-permute-done
  7.8 2.8 %collective-permute-start.1 = (bf16[128,768]{1,0:T(8,128)(2,1)S(1)}, bf16[128,768]{1,0:T(8,128)(2,1)S(1)}, u32[]{:S(2)}, u32[]{:S(2)}) collective-permute-start(bf16[128,768]{1,0:T(8,128)(2,1)S(1)} %get-tuple-element.42), channel_id=1, source_target_pairs={{0,6},{1,7},{2,4},{3,5},{4,2},{5,3},{6,0},{7,1},{8,14},{9,15},{10,... | collective-permute-start | bytes 589832 | tf_op jit(solution)/shard_map/ppermute | solution.py:213
  10.6 0.5 %collective-permute-start.2 = (bf16[128,768]{1,0:T(8,128)(2,1)S(1)}, bf16[128,768]{1,0:T(8,128)(2,1)S(1)}, u32[]{:S(2)}, u32[]{:S(2)}) collective-permute-start(bf16[128,768]{1,0:T(8,128)(2,1)S(1)} %get-tuple-element.42), channel_id=1, source_target_pairs={{0,2},{1,5},{2,0},{3,7},{4,6},{5,1},{6,4},{7,3},{8,10},{9,13},{10,... | collective-permute-start | bytes 589832 | tf_op jit(solution)/shard_map/ppermute | solution.py:233
  11.1 0.3 collective-permute-start.3
  11.4 5.1 %collective-permute-done.4 = bf16[64,768]{1,0:T(8,128)(2,1)S(1)} collective-permute-done((bf16[64,768]{1,0:T(8,128)(2,1)S(1)}, bf16[64,768]{1,0:T(8,128)(2,1)S(1)}, u32[]{:S(2)}, u32[]{:S(2)}) %collective-permute-start.4) | collective-permute-done | bytes 98336 | tf_op jit(solution)/shard_map/ppermute | solution.py:210
  16.5 0.0 collective-permute-done.5
  16.5 2.5 %collective-permute-start.7 = (bf16[128,768]{1,0:T(8,128)(2,1)S(1)}, bf16[128,768]{1,0:T(8,128)(2,1)S(1)}, u32[]{:S(2)}, u32[]{:S(2)}) collective-permute-start(bf16[128,768]{1,0:T(8,128)(2,1)S(1)} %get-tuple-element.38), channel_id=1, source_target_pairs={{0,6},{1,7},{2,4},{3,5},{4,2},{5,3},{6,0},{7,1},{8,14},{9,15},{10,... | collective-permute-start | bytes 589832 | tf_op jit(solution)/shard_map/ppermute | solution.py:213
  19.0 0.5 %collective-permute-start.8 = (bf16[128,768]{1,0:T(8,128)(2,1)S(1)}, bf16[128,768]{1,0:T(8,128)(2,1)S(1)}, u32[]{:S(2)}, u32[]{:S(2)}) collective-permute-start(bf16[128,768]{1,0:T(8,128)(2,1)S(1)} %get-tuple-element.38), channel_id=1, source_target_pairs={{0,2},{1,5},{2,0},{3,7},{4,6},{5,1},{6,4},{7,3},{8,10},{9,13},{10,... | collective-permute-start | bytes 589832 | tf_op jit(solution)/shard_map/ppermute | solution.py:233
  19.6 0.6 %collective-permute-start.9 = (bf16[128,768]{1,0:T(8,128)(2,1)S(1)}, bf16[128,768]{1,0:T(8,128)(2,1)S(1)}, u32[]{:S(2)}, u32[]{:S(2)}) collective-permute-start(bf16[128,768]{1,0:T(8,128)(2,1)S(1)} %get-tuple-element.38), channel_id=1, source_target_pairs={{0,4},{1,3},{2,6},{3,1},{4,0},{5,7},{6,2},{7,5},{8,12},{9,11},{10,... | collective-permute-start | bytes 589832 | tf_op jit(solution)/shard_map/ppermute | solution.py:233
  20.2 0.0 collective-permute-done.2
  20.2 0.0 collective-permute-done.3
  20.2 0.1 collective-permute-start.6
  20.3 5.0 %collective-permute-done.7 = bf16[128,768]{1,0:T(8,128)(2,1)S(1)} collective-permute-done((bf16[128,768]{1,0:T(8,128)(2,1)S(1)}, bf16[128,768]{1,0:T(8,128)(2,1)S(1)}, u32[]{:S(2)}, u32[]{:S(2)}) %collective-permute-start.7) | collective-permute-done | bytes 196640 | tf_op jit(solution)/shard_map/ppermute | solution.py:213
  25.3 2.9 %collective-permute-done.8 = bf16[128,768]{1,0:T(8,128)(2,1)S(1)} collective-permute-done((bf16[128,768]{1,0:T(8,128)(2,1)S(1)}, bf16[128,768]{1,0:T(8,128)(2,1)S(1)}, u32[]{:S(2)}, u32[]{:S(2)}) %collective-permute-start.8) | collective-permute-done | bytes 196640 | tf_op jit(solution)/shard_map/ppermute | solution.py:233
  28.2 0.1 collective-permute-start.10
  28.3 0.0 collective-permute-done.6.refs_1_
  28.3 2.0 %early_sums.1 = (f32[256,128]{1,0:T(8,128)S(1)}, f32[256,768]{1,0:T(8,128)S(1)}, f32[256,128]{1,0:T(8,128)S(1)}) custom-call(bf16[256,768]{1,0:T(8,128)(2,1)S(1)} %pad_maximum_fusion.rows_ref, bf16[512,768]{1,0:T(8,128)(2,1)S(1)} %constant_dynamic-update-slice_fusion.2.refs_0_, bf16[512,768]{1,0:T(8,128)(2,1)S(1)} %collective-permute-done.6.refs_1_, ...), custom_call_target="tpu_custom_call" | custom-call | flops 1207959552 | tf_op jit(solution)/shard_map/early_sums/pallas_call | solution.py:245
  30.3 0.3 collective-permute-done.10.cols_ref
  30.6 0.9 %last_sums.1 = (f32[72,768]{1,0:T(8,128)S(1)}, f32[72,768]{1,0:T(8,128)S(1)}, f32[64,768]{1,0:T(8,128)S(1)}, f32[64,768]{1,0:T(8,128)S(1)}, f32[8,128]{1,0:T(8,128)S(1)}, /*index=5*/f32[8,128]{1,0:T(8,128)S(1)}) custom-call(bf16[256,768]{1,0:T(8,128)(2,1)S(1)} %pad_maximum_fusion.rows_ref, f32[256,128]{1,0:T(8,128)S(1)} %get-tuple-element.27.scale_ref, ...), custom_call_target="tpu_custom_call" | custom-call | flops 402653184 | tf_op jit(solution)/shard_map/last_sums/pallas_call | solution.py:259
  31.5 2.9 %collective-permute-start.11 = (f16[64,768]{1,0:T(8,128)(2,1)S(1)}, f16[64,768]{1,0:T(8,128)(2,1)S(1)}, u32[]{:S(2)}, u32[]{:S(2)}) collective-permute-start(f16[64,768]{1,0:T(8,128)(2,1)S(1)} %convert_element_type.24), channel_id=1, source_target_pairs={{0,24},{8,16},{16,8},{24,0},{1,25},{9,17},{17,9},{25,1},{2,26},{10... | collective-permute-start | bytes 294920 | tf_op jit(solution)/shard_map/ppermute | solution.py:210
  34.4 0.1 collective-permute-start.12
  34.5 1.6 %collective-permute-start.13 = (f16[72,768]{1,0:T(8,128)(2,1)S(1)}, f16[72,768]{1,0:T(8,128)(2,1)S(1)}, u32[]{:S(2)}, u32[]{:S(2)}) collective-permute-start(f16[72,768]{1,0:T(8,128)(2,1)S(1)} %convert_element_type.28), channel_id=1, source_target_pairs={{0,8},{8,0},{16,24},{24,16},{1,9},{9,1},{17,25},{25,17},{2,10},{10... | collective-permute-start | bytes 331784 | tf_op jit(solution)/shard_map/ppermute | solution.py:210
  36.1 2.8 %collective-permute-start.14 = (f32[8,128]{1,0:T(8,128)S(1)}, f32[8,128]{1,0:T(8,128)S(1)}, u32[]{:S(2)}, u32[]{:S(2)}) collective-permute-start(f32[8,128]{1,0:T(8,128)S(1)} %get-tuple-element.34), channel_id=1, source_target_pairs={{0,24},{8,16},{16,8},{24,0},{1,25},{9,17},{17,9},{25,1},{2,26},{10... | collective-permute-start | bytes 12296 | tf_op jit(solution)/shard_map/ppermute | solution.py:210
  38.9 0.0 collective-permute-start.15
  38.9 0.2 collective-permute-done.11
  39.1 4.2 %collective-permute-done.12 = f16[64,768]{1,0:T(8,128)(2,1)S(1)} collective-permute-done((f16[64,768]{1,0:T(8,128)(2,1)S(1)}, f16[64,768]{1,0:T(8,128)(2,1)S(1)}, u32[]{:S(2)}, u32[]{:S(2)}) %collective-permute-start.12) | collective-permute-done | bytes 98336 | tf_op jit(solution)/shard_map/ppermute | solution.py:210
  43.4 0.0 collective-permute-done.15.refs_5_
  43.4 1.4 %restore_rows.1 = (f32[256,768]{1,0:T(8,128)}, f32[1,256]{1,0:T(1,128)}) custom-call(bf16[256,256]{1,0:T(8,128)(2,1)S(1)} %get-tuple-element.20.chosen_ref, f32[64,768]{1,0:T(8,128)S(1)} %convert_element_type.25.refs_0_, f32[64,768]{1,0:T(8,128)S(1)} %convert_element_type.27.refs_1_, f32[72,768]{1,0:T(8,128)S(1)} %convert_element_type.29.refs_2_, ...), custom_call_target="tpu_custom_call" | custom-call | tf_op jit(solution)/shard_map/restore_rows/pallas_call | solution.py:275
  (22 shorter events, 0.3 us)
Async XLA Ops:
  1.9 5.9 %collective-permute-start = (bf16[64,768]{1,0:T(8,128)(2,1)S(1)}, bf16[64,768]{1,0:T(8,128)(2,1)S(1)}, u32[]{:S(2)}, u32[]{:S(2)}) collective-permute-start(bf16[64,768]{1,0:T(8,128)(2,1)S(1)} %get-tuple-element.22), channel_id=1, source_target_pairs={{0,8},{8,0},{16,24},{24,16},{1,9},{9,1},{17,25},{25,17},{2,10},{10... | collective-permute-start | bytes 294920 | tf_op jit(solution)/shard_map/ppermute | solution.py:210
  5.0 11.4 %collective-permute-start.5 = (bf16[64,768]{1,0:T(8,128)(2,1)S(1)}, bf16[64,768]{1,0:T(8,128)(2,1)S(1)}, u32[]{:S(2)}, u32[]{:S(2)}) collective-permute-start(bf16[64,768]{1,0:T(8,128)(2,1)S(1)} %get-tuple-element.24), channel_id=1, source_target_pairs={{0,24},{8,16},{16,8},{24,0},{1,25},{9,17},{17,9},{25,1},{2,26},{10... | collective-permute-start | bytes 294920 | tf_op jit(solution)/shard_map/ppermute | solution.py:210
  7.5 8.9 %collective-permute-start.4 = (bf16[64,768]{1,0:T(8,128)(2,1)S(1)}, bf16[64,768]{1,0:T(8,128)(2,1)S(1)}, u32[]{:S(2)}, u32[]{:S(2)}) collective-permute-start(bf16[64,768]{1,0:T(8,128)(2,1)S(1)} %get-tuple-element.23), channel_id=1, source_target_pairs={{0,16},{8,24},{16,0},{24,8},{1,17},{9,25},{17,1},{25,9},{2,18},{10... | collective-permute-start | bytes 294920 | tf_op jit(solution)/shard_map/ppermute | solution.py:210
  7.8 11.7 %collective-permute-start.1 = (bf16[128,768]{1,0:T(8,128)(2,1)S(1)}, bf16[128,768]{1,0:T(8,128)(2,1)S(1)}, u32[]{:S(2)}, u32[]{:S(2)}) collective-permute-start(bf16[128,768]{1,0:T(8,128)(2,1)S(1)} %get-tuple-element.42), channel_id=1, source_target_pairs={{0,6},{1,7},{2,4},{3,5},{4,2},{5,3},{6,0},{7,1},{8,14},{9,15},{10,... | collective-permute-start | bytes 589832 | tf_op jit(solution)/shard_map/ppermute | solution.py:213
  10.6 9.6 %collective-permute-start.2 = (bf16[128,768]{1,0:T(8,128)(2,1)S(1)}, bf16[128,768]{1,0:T(8,128)(2,1)S(1)}, u32[]{:S(2)}, u32[]{:S(2)}) collective-permute-start(bf16[128,768]{1,0:T(8,128)(2,1)S(1)} %get-tuple-element.42), channel_id=1, source_target_pairs={{0,2},{1,5},{2,0},{3,7},{4,6},{5,1},{6,4},{7,3},{8,10},{9,13},{10,... | collective-permute-start | bytes 589832 | tf_op jit(solution)/shard_map/ppermute | solution.py:233
  11.1 9.1 %collective-permute-start.3 = (bf16[128,768]{1,0:T(8,128)(2,1)S(1)}, bf16[128,768]{1,0:T(8,128)(2,1)S(1)}, u32[]{:S(2)}, u32[]{:S(2)}) collective-permute-start(bf16[128,768]{1,0:T(8,128)(2,1)S(1)} %get-tuple-element.42), channel_id=1, source_target_pairs={{0,4},{1,3},{2,6},{3,1},{4,0},{5,7},{6,2},{7,5},{8,12},{9,11},{10,... | collective-permute-start | bytes 589832 | tf_op jit(solution)/shard_map/ppermute | solution.py:233
  16.5 8.8 %collective-permute-start.7 = (bf16[128,768]{1,0:T(8,128)(2,1)S(1)}, bf16[128,768]{1,0:T(8,128)(2,1)S(1)}, u32[]{:S(2)}, u32[]{:S(2)}) collective-permute-start(bf16[128,768]{1,0:T(8,128)(2,1)S(1)} %get-tuple-element.38), channel_id=1, source_target_pairs={{0,6},{1,7},{2,4},{3,5},{4,2},{5,3},{6,0},{7,1},{8,14},{9,15},{10,... | collective-permute-start | bytes 589832 | tf_op jit(solution)/shard_map/ppermute | solution.py:213
  19.0 9.2 %collective-permute-start.8 = (bf16[128,768]{1,0:T(8,128)(2,1)S(1)}, bf16[128,768]{1,0:T(8,128)(2,1)S(1)}, u32[]{:S(2)}, u32[]{:S(2)}) collective-permute-start(bf16[128,768]{1,0:T(8,128)(2,1)S(1)} %get-tuple-element.38), channel_id=1, source_target_pairs={{0,2},{1,5},{2,0},{3,7},{4,6},{5,1},{6,4},{7,3},{8,10},{9,13},{10,... | collective-permute-start | bytes 589832 | tf_op jit(solution)/shard_map/ppermute | solution.py:233
  19.6 8.6 %collective-permute-start.9 = (bf16[128,768]{1,0:T(8,128)(2,1)S(1)}, bf16[128,768]{1,0:T(8,128)(2,1)S(1)}, u32[]{:S(2)}, u32[]{:S(2)}) collective-permute-start(bf16[128,768]{1,0:T(8,128)(2,1)S(1)} %get-tuple-element.38), channel_id=1, source_target_pairs={{0,4},{1,3},{2,6},{3,1},{4,0},{5,7},{6,2},{7,5},{8,12},{9,11},{10,... | collective-permute-start | bytes 589832 | tf_op jit(solution)/shard_map/ppermute | solution.py:233
  20.2 8.1 %collective-permute-start.6 = (bf16[512,768]{1,0:T(8,128)(2,1)S(1)}, bf16[512,768]{1,0:T(8,128)(2,1)S(1)}, u32[]{:S(2)}, u32[]{:S(2)}) collective-permute-start(bf16[512,768]{1,0:T(8,128)(2,1)S(1)} %constant_dynamic-update-slice_fusion.2.refs_0_), channel_id=1, source_target_pairs={{0,1},{1,0},{2,3},{3,2},{4,5},{5,4},{6,7},{7,6},{8,9},{9,8},{10,11... | collective-permute-start | bytes 2359304 | tf_op jit(solution)/shard_map/ppermute | solution.py:213
  28.2 2.4 %collective-permute-start.10 = (bf16[512,768]{1,0:T(8,128)(2,1)S(1)}, bf16[512,768]{1,0:T(8,128)(2,1)S(1)}, u32[]{:S(2)}, u32[]{:S(2)}) collective-permute-start(bf16[512,768]{1,0:T(8,128)(2,1)S(1)} %constant_dynamic-update-slice_fusion.9.refs_2_), channel_id=1, source_target_pairs={{0,1},{1,0},{2,3},{3,2},{4,5},{5,4},{6,7},{7,6},{8,9},{9,8},{10,11... | collective-permute-start | bytes 2359304 | tf_op jit(solution)/shard_map/ppermute | solution.py:213
  31.5 7.6 %collective-permute-start.11 = (f16[64,768]{1,0:T(8,128)(2,1)S(1)}, f16[64,768]{1,0:T(8,128)(2,1)S(1)}, u32[]{:S(2)}, u32[]{:S(2)}) collective-permute-start(f16[64,768]{1,0:T(8,128)(2,1)S(1)} %convert_element_type.24), channel_id=1, source_target_pairs={{0,24},{8,16},{16,8},{24,0},{1,25},{9,17},{17,9},{25,1},{2,26},{10... | collective-permute-start | bytes 294920 | tf_op jit(solution)/shard_map/ppermute | solution.py:210
  34.4 8.9 %collective-permute-start.12 = (f16[64,768]{1,0:T(8,128)(2,1)S(1)}, f16[64,768]{1,0:T(8,128)(2,1)S(1)}, u32[]{:S(2)}, u32[]{:S(2)}) collective-permute-start(f16[64,768]{1,0:T(8,128)(2,1)S(1)} %convert_element_type.26), channel_id=1, source_target_pairs={{0,16},{8,24},{16,0},{24,8},{1,17},{9,25},{17,1},{25,9},{2,18},{10... | collective-permute-start | bytes 294920 | tf_op jit(solution)/shard_map/ppermute | solution.py:210
  34.5 8.9 %collective-permute-start.13 = (f16[72,768]{1,0:T(8,128)(2,1)S(1)}, f16[72,768]{1,0:T(8,128)(2,1)S(1)}, u32[]{:S(2)}, u32[]{:S(2)}) collective-permute-start(f16[72,768]{1,0:T(8,128)(2,1)S(1)} %convert_element_type.28), channel_id=1, source_target_pairs={{0,8},{8,0},{16,24},{24,16},{1,9},{9,1},{17,25},{25,17},{2,10},{10... | collective-permute-start | bytes 331784 | tf_op jit(solution)/shard_map/ppermute | solution.py:210
  36.1 7.3 %collective-permute-start.14 = (f32[8,128]{1,0:T(8,128)S(1)}, f32[8,128]{1,0:T(8,128)S(1)}, u32[]{:S(2)}, u32[]{:S(2)}) collective-permute-start(f32[8,128]{1,0:T(8,128)S(1)} %get-tuple-element.34), channel_id=1, source_target_pairs={{0,24},{8,16},{16,8},{24,0},{1,25},{9,17},{17,9},{25,1},{2,26},{10... | collective-permute-start | bytes 12296 | tf_op jit(solution)/shard_map/ppermute | solution.py:210
  38.9 4.5 %collective-permute-start.15 = (f32[8,128]{1,0:T(8,128)S(1)}, f32[8,128]{1,0:T(8,128)S(1)}, u32[]{:S(2)}, u32[]{:S(2)}) collective-permute-start(f32[8,128]{1,0:T(8,128)S(1)} %get-tuple-element.35), channel_id=1, source_target_pairs={{0,16},{8,24},{16,0},{24,8},{1,17},{9,25},{17,1},{25,9},{2,18},{10... | collective-permute-start | bytes 12296 | tf_op jit(solution)/shard_map/ppermute | solution.py:210

commit v11 on v10

--- a/solution.py
+++ b/solution.py
@@ -141,45 +141,45 @@
         piece = part.astype(jnp.bfloat16).astype(jnp.float32)
         aside.append(piece * 2.0 ** (8 * k))
         part = part - piece
+    lanes = lax.broadcasted_iota(jnp.int32, (total.shape[0], LANES), 1)
+    table = jnp.zeros(lanes.shape, jnp.float32)
+    for line, column in enumerate(aside):
+        table = jnp.where(lanes == line, column, table)
     for k in range(groups):
         rows = slice(k * size, (k + 1) * size)
         out_refs[k][:size, :] = total[rows, :]
         if k < half:
             aside_ref, top = out_refs[k], size
-            aside_ref[size:, :] = jnp.zeros((EXTRA, total.shape[1]), jnp.float32)
         else:
             aside_ref, top = out_refs[half + k], 0
-            aside_ref[...] = jnp.zeros(aside_ref.shape, jnp.float32)
-        for line, column in enumerate(aside):
-            aside_ref[top + line : top + line + 1, :size] = as_row(column[rows, :])
-
-
-def restore_kernel(half, chosen_ref, *refs):
-    refs, (total_ref, dens_ref) = refs[:-2], refs[-2:]
-    groups = len(refs) - half
-    part_refs = refs[groups - 1 :: -1] + refs[: groups - 1 : -1]
-    size = part_refs[half].shape[0]
-    chosen = chosen_ref[...]
-    sums, dens = [], []
-    for k in range(groups):
-        aside_ref, top = (part_refs[k], size) if k < half else (part_refs[half + k], 0)
-        power, dens_power, *pieces = [
-            as_column(aside_ref[top + line : top + line + 1, :size])
-            for line in range(5)
-        ]
-        sums.append(part_refs[k][:size, :] * jnp.exp2(power - TOP))
-        part = sum(piece * 2.0 ** (-8 * j) for j, piece in enumerate(pieces))
-        dens.append(part * jnp.exp2(dens_power))
+        aside_ref[top:, :] = jnp.zeros((EXTRA, aside_ref.shape[1]), jnp.float32)
+        aside_ref[top:, :size] = table[rows, :].T[:EXTRA, :]
+
+
+def restore_kernel(groups, chosen_ref, *refs):
+    high_refs, low_refs, aside_refs, (total_ref, dens_ref) = (
+        refs[:groups],
+        refs[groups : 2 * groups],
+        refs[2 * groups : -2],
+        refs[-2:],
+    )
+    size = high_refs[0].shape[0]
+    scales, dens = [], []
+    for aside_ref in aside_refs[::-1]:
+        table = aside_ref[...].T[:size, :]
+        scales.append(jnp.exp2(table[:, 0:1] - TOP))
+        part = table[:, 2:3] + table[:, 3:4] * 2.0**-8 + table[:, 4:5] * 2.0**-16
+        dens.append(part * jnp.exp2(table[:, 1:2]))
+    chosen = chosen_ref[...].astype(jnp.float32)
     dens_ref[...] = jnp.sum(
-        chosen.astype(jnp.float32) * jnp.concatenate(dens, axis=0), axis=0, keepdims=True
-    )
-    rest = jnp.concatenate(sums, axis=0)
-    back = jnp.zeros(rest.shape, jnp.float32)
-    for _ in range(2):
-        piece = rest.astype(jnp.bfloat16)
-        rest = rest - piece.astype(jnp.float32)
+        chosen * jnp.concatenate(dens, axis=0), axis=0, keepdims=True
+    )
+    scaled = (chosen * jnp.concatenate(scales, axis=0)).astype(jnp.bfloat16)
+    back = 0.0
+    for part_refs in (high_refs, low_refs):
+        parts = jnp.concatenate([ref[...] for ref in part_refs[::-1]], axis=0)
         back += lax.dot_general(
-            chosen, piece, (((0,), (0,)), ((), ())), preferred_element_type=jnp.float32
+            scaled, parts, (((0,), (0,)), ((), ())), preferred_element_type=jnp.float32
         )
     total_ref[...] = back
 
@@ -270,19 +270,23 @@
 
     sent = [part.astype(jnp.float16) for part in sums[:n_gr]]
     back = [sent[0]] + [along_gr(sent[k], k) for k in range(1, n_gr)]
-    back = [part.astype(jnp.float32) for part in back]
-    back += [along_gr(sums[half + k], k) for k in range(half, n_gr)]
+    beside = [part[size:, :LANES].astype(jnp.float32) for part in back[:half]]
+    beside += [along_gr(sums[half + k], k) for k in range(half, n_gr)]
+    back = [part[:size].astype(jnp.float32) for part in back]
+    high = [lax.reduce_precision(part, 8, 7) for part in back]
+    low = [(part - top).astype(jnp.bfloat16) for part, top in zip(back, high)]
+    high = [part.astype(jnp.bfloat16) for part in high]
     neighbour_sum, density = pl.pallas_call(
-        functools.partial(restore_kernel, half),
+        functools.partial(restore_kernel, n_gr),
         out_shape=[
             jax.ShapeDtypeStruct((count, width), jnp.float32),
             jax.ShapeDtypeStruct((1, count), jnp.float32),
         ],
-        in_specs=[VMEM] * (1 + len(back)),
+        in_specs=[VMEM] * (1 + 3 * n_gr),
         out_specs=[VMEM, VMEM],
         compiler_params=GRANT,
         name="restore_rows",
-    )(chosen, *back[n_gr - 1 :: -1], *back[:n_gr - 1 : -1])
+    )(chosen, *high[::-1], *low[::-1], *beside[::-1])
     return (neighbour_sum, density.reshape(count))
 
 

time: 45 us -> 45.1 us (level)
  transfers between devices with their start and end apart: 16 -> 16, of which waited for: 7 -> 8; matrix products, arithmetic and copies ran while one was open for 1% -> 1% of each run, Pallas kernels for 4% -> 4%
where the time goes in v11:
time: 45.1 us; the launch traced here: 45 us
  starting transfers between devices  20.4 us (45%)
  waiting for transfers between devices  17.8 us (39%)
  Pallas kernels  5.65 us (13%)
  between operations  0.87 us (2%)
    ppermute x8, starting transfers between devices, along_gr(): return lax.ppermute(part, 'gr', [(i, i ^ bits) for i in range(n_gr)])  13.1 us
    ppermute x8, waiting for transfers between devices, along_gr(): return lax.ppermute(part, 'gr', [(i, i ^ bits) for i in range(n_gr)])  9.61 us
    ppermute x4, starting transfers between devices, along_gc(): return lax.ppermute(block, 'gc', [(i, i ^ bits) for i in range(n_gc)])  5.41 us
    ppermute x4, waiting for transfers between devices, along_gc(): return lax.ppermute(block, 'gc', [(i, i ^ bits) for i in range(n_gc)])  5.28 us
    ppermute x4, waiting for transfers between devices, to_side(): return lax.ppermute(block, 'gc', pairs)  2.87 us
    pallas_call x1, Pallas kernels, on_device(): pl.pallas_call(early_kernel, out_shape=[jax.ShapeDtypeStruct((count, LANE...  1.95 us
    ppermute x4, starting transfers between devices, to_side(): return lax.ppermute(block, 'gc', pairs)  1.9 us
    pallas_call x1, Pallas kernels, on_device(): pl.pallas_call(functools.partial(restore_kernel, n_gr), out_shape=[jax.Sh...  1.47 us
  transfers between devices with their start and end apart: 16, of which 8 were waited for; matrix products, arithmetic and copies ran while one was open for 1% of the time, Pallas kernels for 4%

profile of v11, /device:TPU:0, one launch (start us, length us, event | category | flops | bytes accessed | tf_op | source)
XLA Modules:
  0.0 45.0 jit_solution(9381336110484697516)
XLA Ops:
  0.6 1.3 %sort_rows.1 = (bf16[256,256]{1,0:T(8,128)(2,1)S(1)}, bf16[64,768]{1,0:T(8,128)(2,1)S(1)}, bf16[64,768]{1,0:T(8,128)(2,1)S(1)}, bf16[64,768]{1,0:T(8,128)(2,1)S(1)}, bf16[64,768]{1,0:T(8,128)(2,1)S(1)}) custom-call(s32[1]{0:T(128)} %bitcast.own_ref, s32[1,256]{1,0:T(1,128)} %bitcast.3, bf16[256,768]{1,0:T(8,128)(2,1)} %rows_hbm.1), custom_call_target="tpu_custom_call" | custom-call | tf_op jit(solution)/shard_map/sort_rows/pallas_call | solution.py:193
  1.9 3.1 %collective-permute-start = (bf16[64,768]{1,0:T(8,128)(2,1)S(1)}, bf16[64,768]{1,0:T(8,128)(2,1)S(1)}, u32[]{:S(2)}, u32[]{:S(2)}) collective-permute-start(bf16[64,768]{1,0:T(8,128)(2,1)S(1)} %get-tuple-element.22), channel_id=1, source_target_pairs={{0,8},{8,0},{16,24},{24,16},{1,9},{9,1},{17,25},{25,17},{2,10},{10... | collective-permute-start | bytes 294920 | tf_op jit(solution)/shard_map/ppermute | solution.py:210
  5.0 2.5 %collective-permute-start.5 = (bf16[64,768]{1,0:T(8,128)(2,1)S(1)}, bf16[64,768]{1,0:T(8,128)(2,1)S(1)}, u32[]{:S(2)}, u32[]{:S(2)}) collective-permute-start(bf16[64,768]{1,0:T(8,128)(2,1)S(1)} %get-tuple-element.24), channel_id=1, source_target_pairs={{0,24},{8,16},{16,8},{24,0},{1,25},{9,17},{17,9},{25,1},{2,26},{10... | collective-permute-start | bytes 294920 | tf_op jit(solution)/shard_map/ppermute | solution.py:210
  7.5 0.1 collective-permute-start.4
  7.6 0.2 collective-permute-done
  7.8 2.8 %collective-permute-start.1 = (bf16[128,768]{1,0:T(8,128)(2,1)S(1)}, bf16[128,768]{1,0:T(8,128)(2,1)S(1)}, u32[]{:S(2)}, u32[]{:S(2)}) collective-permute-start(bf16[128,768]{1,0:T(8,128)(2,1)S(1)} %get-tuple-element.50), channel_id=1, source_target_pairs={{0,6},{1,7},{2,4},{3,5},{4,2},{5,3},{6,0},{7,1},{8,14},{9,15},{10,... | collective-permute-start | bytes 589832 | tf_op jit(solution)/shard_map/ppermute | solution.py:213
  10.6 0.5 %collective-permute-start.2 = (bf16[128,768]{1,0:T(8,128)(2,1)S(1)}, bf16[128,768]{1,0:T(8,128)(2,1)S(1)}, u32[]{:S(2)}, u32[]{:S(2)}) collective-permute-start(bf16[128,768]{1,0:T(8,128)(2,1)S(1)} %get-tuple-element.50), channel_id=1, source_target_pairs={{0,2},{1,5},{2,0},{3,7},{4,6},{5,1},{6,4},{7,3},{8,10},{9,13},{10,... | collective-permute-start | bytes 589832 | tf_op jit(solution)/shard_map/ppermute | solution.py:233
  11.1 0.3 collective-permute-start.3
  11.4 5.1 %collective-permute-done.4 = bf16[64,768]{1,0:T(8,128)(2,1)S(1)} collective-permute-done((bf16[64,768]{1,0:T(8,128)(2,1)S(1)}, bf16[64,768]{1,0:T(8,128)(2,1)S(1)}, u32[]{:S(2)}, u32[]{:S(2)}) %collective-permute-start.4) | collective-permute-done | bytes 98336 | tf_op jit(solution)/shard_map/ppermute | solution.py:210
  16.5 2.5 %collective-permute-start.7 = (bf16[128,768]{1,0:T(8,128)(2,1)S(1)}, bf16[128,768]{1,0:T(8,128)(2,1)S(1)}, u32[]{:S(2)}, u32[]{:S(2)}) collective-permute-start(bf16[128,768]{1,0:T(8,128)(2,1)S(1)} %get-tuple-element.46), channel_id=1, source_target_pairs={{0,6},{1,7},{2,4},{3,5},{4,2},{5,3},{6,0},{7,1},{8,14},{9,15},{10,... | collective-permute-start | bytes 589832 | tf_op jit(solution)/shard_map/ppermute | solution.py:213
  19.0 0.5 %collective-permute-start.8 = (bf16[128,768]{1,0:T(8,128)(2,1)S(1)}, bf16[128,768]{1,0:T(8,128)(2,1)S(1)}, u32[]{:S(2)}, u32[]{:S(2)}) collective-permute-start(bf16[128,768]{1,0:T(8,128)(2,1)S(1)} %get-tuple-element.46), channel_id=1, source_target_pairs={{0,2},{1,5},{2,0},{3,7},{4,6},{5,1},{6,4},{7,3},{8,10},{9,13},{10,... | collective-permute-start | bytes 589832 | tf_op jit(solution)/shard_map/ppermute | solution.py:233
  19.6 0.0 collective-permute-done.1
  19.6 0.6 %collective-permute-start.9 = (bf16[128,768]{1,0:T(8,128)(2,1)S(1)}, bf16[128,768]{1,0:T(8,128)(2,1)S(1)}, u32[]{:S(2)}, u32[]{:S(2)}) collective-permute-start(bf16[128,768]{1,0:T(8,128)(2,1)S(1)} %get-tuple-element.46), channel_id=1, source_target_pairs={{0,4},{1,3},{2,6},{3,1},{4,0},{5,7},{6,2},{7,5},{8,12},{9,11},{10,... | collective-permute-start | bytes 589832 | tf_op jit(solution)/shard_map/ppermute | solution.py:233
  20.2 0.0 collective-permute-done.2
  20.2 0.1 collective-permute-start.6
  20.3 5.0 %collective-permute-done.7 = bf16[128,768]{1,0:T(8,128)(2,1)S(1)} collective-permute-done((bf16[128,768]{1,0:T(8,128)(2,1)S(1)}, bf16[128,768]{1,0:T(8,128)(2,1)S(1)}, u32[]{:S(2)}, u32[]{:S(2)}) %collective-permute-start.7) | collective-permute-done | bytes 196640 | tf_op jit(solution)/shard_map/ppermute | solution.py:213
  25.3 2.9 %collective-permute-done.8 = bf16[128,768]{1,0:T(8,128)(2,1)S(1)} collective-permute-done((bf16[128,768]{1,0:T(8,128)(2,1)S(1)}, bf16[128,768]{1,0:T(8,128)(2,1)S(1)}, u32[]{:S(2)}, u32[]{:S(2)}) %collective-permute-start.8) | collective-permute-done | bytes 196640 | tf_op jit(solution)/shard_map/ppermute | solution.py:233
  28.2 0.0 collective-permute-done.9
  28.2 0.1 collective-permute-start.10
  28.3 2.0 %early_sums.1 = (f32[256,128]{1,0:T(8,128)S(1)}, f32[256,768]{1,0:T(8,128)S(1)}, f32[256,128]{1,0:T(8,128)S(1)}) custom-call(bf16[256,768]{1,0:T(8,128)(2,1)S(1)} %pad_maximum_fusion.rows_ref, bf16[512,768]{1,0:T(8,128)(2,1)S(1)} %constant_dynamic-update-slice_fusion.2.refs_0_, bf16[512,768]{1,0:T(8,128)(2,1)S(1)} %collective-permute-done.6.refs_1_, ...), custom_call_target="tpu_custom_call" | custom-call | flops 1207959552 | tf_op jit(solution)/shard_map/early_sums/pallas_call | solution.py:245
  30.3 0.3 collective-permute-done.10.cols_ref
  30.6 0.9 %last_sums.1 = (f32[72,768]{1,0:T(8,128)S(1)}, f32[72,768]{1,0:T(8,128)S(1)}, f32[64,768]{1,0:T(8,128)S(1)}, f32[64,768]{1,0:T(8,128)S(1)}, f32[8,128]{1,0:T(8,128)S(1)}, /*index=5*/f32[8,128]{1,0:T(8,128)S(1)}) custom-call(bf16[256,768]{1,0:T(8,128)(2,1)S(1)} %pad_maximum_fusion.rows_ref, f32[256,128]{1,0:T(8,128)S(1)} %get-tuple-element.27.scale_ref, ...), custom_call_target="tpu_custom_call" | custom-call | flops 402653184 | tf_op jit(solution)/shard_map/last_sums/pallas_call | solution.py:259
  31.5 2.9 %collective-permute-start.11 = (f16[64,768]{1,0:T(8,128)(2,1)S(1)}, f16[64,768]{1,0:T(8,128)(2,1)S(1)}, u32[]{:S(2)}, u32[]{:S(2)}) collective-permute-start(f16[64,768]{1,0:T(8,128)(2,1)S(1)} %convert_element_type.54), channel_id=1, source_target_pairs={{0,24},{8,16},{16,8},{24,0},{1,25},{9,17},{17,9},{25,1},{2,26},{10... | collective-permute-start | bytes 294920 | tf_op jit(solution)/shard_map/ppermute | solution.py:210
  34.5 0.1 collective-permute-start.12
  34.6 1.6 %collective-permute-start.13 = (f16[72,768]{1,0:T(8,128)(2,1)S(1)}, f16[72,768]{1,0:T(8,128)(2,1)S(1)}, u32[]{:S(2)}, u32[]{:S(2)}) collective-permute-start(f16[72,768]{1,0:T(8,128)(2,1)S(1)} %convert_element_type.60), channel_id=1, source_target_pairs={{0,8},{8,0},{16,24},{24,16},{1,9},{9,1},{17,25},{25,17},{2,10},{10... | collective-permute-start | bytes 331784 | tf_op jit(solution)/shard_map/ppermute | solution.py:210
  36.2 2.8 %collective-permute-start.14 = (f32[8,128]{1,0:T(8,128)S(1)}, f32[8,128]{1,0:T(8,128)S(1)}, u32[]{:S(2)}, u32[]{:S(2)}) collective-permute-start(f32[8,128]{1,0:T(8,128)S(1)} %get-tuple-element.34), channel_id=1, source_target_pairs={{0,24},{8,16},{16,8},{24,0},{1,25},{9,17},{17,9},{25,1},{2,26},{10... | collective-permute-start | bytes 12296 | tf_op jit(solution)/shard_map/ppermute | solution.py:210
  39.0 0.0 collective-permute-start.15
  39.0 0.1 collective-permute-done.11
  39.2 4.2 %collective-permute-done.12 = f16[64,768]{1,0:T(8,128)(2,1)S(1)} collective-permute-done((f16[64,768]{1,0:T(8,128)(2,1)S(1)}, f16[64,768]{1,0:T(8,128)(2,1)S(1)}, u32[]{:S(2)}, u32[]{:S(2)}) %collective-permute-start.12) | collective-permute-done | bytes 98336 | tf_op jit(solution)/shard_map/ppermute | solution.py:210
  43.4 0.0 collective-permute-done.13
  43.5 0.1 collective-permute-done.15.refs_9_
  43.5 1.5 %restore_rows.1 = (f32[256,768]{1,0:T(8,128)}, f32[1,256]{1,0:T(1,128)}) custom-call(bf16[256,256]{1,0:T(8,128)(2,1)S(1)} %get-tuple-element.20.chosen_ref, bf16[64,768]{1,0:T(8,128)(2,1)S(1)} %get-tuple-element.45.refs_0_, bf16[64,768]{1,0:T(8,128)(2,1)S(1)} %get-tuple-element.43.refs_1_, bf16[64,768]{1,0:T(8,128)(2,1)S(1)} %get-tuple-element.41.refs_2_, ...), custom_call_target="tpu_custom_call" | custom-call | tf_op jit(solution)/shard_map/restore_rows/pallas_call | solution.py:279
  (25 shorter events, 0.4 us)
Async XLA Ops:
  1.9 5.9 %collective-permute-start = (bf16[64,768]{1,0:T(8,128)(2,1)S(1)}, bf16[64,768]{1,0:T(8,128)(2,1)S(1)}, u32[]{:S(2)}, u32[]{:S(2)}) collective-permute-start(bf16[64,768]{1,0:T(8,128)(2,1)S(1)} %get-tuple-element.22), channel_id=1, source_target_pairs={{0,8},{8,0},{16,24},{24,16},{1,9},{9,1},{17,25},{25,17},{2,10},{10... | collective-permute-start | bytes 294920 | tf_op jit(solution)/shard_map/ppermute | solution.py:210
  5.0 11.4 %collective-permute-start.5 = (bf16[64,768]{1,0:T(8,128)(2,1)S(1)}, bf16[64,768]{1,0:T(8,128)(2,1)S(1)}, u32[]{:S(2)}, u32[]{:S(2)}) collective-permute-start(bf16[64,768]{1,0:T(8,128)(2,1)S(1)} %get-tuple-element.24), channel_id=1, source_target_pairs={{0,24},{8,16},{16,8},{24,0},{1,25},{9,17},{17,9},{25,1},{2,26},{10... | collective-permute-start | bytes 294920 | tf_op jit(solution)/shard_map/ppermute | solution.py:210
  7.5 8.9 %collective-permute-start.4 = (bf16[64,768]{1,0:T(8,128)(2,1)S(1)}, bf16[64,768]{1,0:T(8,128)(2,1)S(1)}, u32[]{:S(2)}, u32[]{:S(2)}) collective-permute-start(bf16[64,768]{1,0:T(8,128)(2,1)S(1)} %get-tuple-element.23), channel_id=1, source_target_pairs={{0,16},{8,24},{16,0},{24,8},{1,17},{9,25},{17,1},{25,9},{2,18},{10... | collective-permute-start | bytes 294920 | tf_op jit(solution)/shard_map/ppermute | solution.py:210
  7.8 11.7 %collective-permute-start.1 = (bf16[128,768]{1,0:T(8,128)(2,1)S(1)}, bf16[128,768]{1,0:T(8,128)(2,1)S(1)}, u32[]{:S(2)}, u32[]{:S(2)}) collective-permute-start(bf16[128,768]{1,0:T(8,128)(2,1)S(1)} %get-tuple-element.50), channel_id=1, source_target_pairs={{0,6},{1,7},{2,4},{3,5},{4,2},{5,3},{6,0},{7,1},{8,14},{9,15},{10,... | collective-permute-start | bytes 589832 | tf_op jit(solution)/shard_map/ppermute | solution.py:213
  10.6 9.6 %collective-permute-start.2 = (bf16[128,768]{1,0:T(8,128)(2,1)S(1)}, bf16[128,768]{1,0:T(8,128)(2,1)S(1)}, u32[]{:S(2)}, u32[]{:S(2)}) collective-permute-start(bf16[128,768]{1,0:T(8,128)(2,1)S(1)} %get-tuple-element.50), channel_id=1, source_target_pairs={{0,2},{1,5},{2,0},{3,7},{4,6},{5,1},{6,4},{7,3},{8,10},{9,13},{10,... | collective-permute-start | bytes 589832 | tf_op jit(solution)/shard_map/ppermute | solution.py:233
  11.1 9.1 %collective-permute-start.3 = (bf16[128,768]{1,0:T(8,128)(2,1)S(1)}, bf16[128,768]{1,0:T(8,128)(2,1)S(1)}, u32[]{:S(2)}, u32[]{:S(2)}) collective-permute-start(bf16[128,768]{1,0:T(8,128)(2,1)S(1)} %get-tuple-element.50), channel_id=1, source_target_pairs={{0,4},{1,3},{2,6},{3,1},{4,0},{5,7},{6,2},{7,5},{8,12},{9,11},{10,... | collective-permute-start | bytes 589832 | tf_op jit(solution)/shard_map/ppermute | solution.py:233
  16.5 8.8 %collective-permute-start.7 = (bf16[128,768]{1,0:T(8,128)(2,1)S(1)}, bf16[128,768]{1,0:T(8,128)(2,1)S(1)}, u32[]{:S(2)}, u32[]{:S(2)}) collective-permute-start(bf16[128,768]{1,0:T(8,128)(2,1)S(1)} %get-tuple-element.46), channel_id=1, source_target_pairs={{0,6},{1,7},{2,4},{3,5},{4,2},{5,3},{6,0},{7,1},{8,14},{9,15},{10,... | collective-permute-start | bytes 589832 | tf_op jit(solution)/shard_map/ppermute | solution.py:213
  19.0 9.2 %collective-permute-start.8 = (bf16[128,768]{1,0:T(8,128)(2,1)S(1)}, bf16[128,768]{1,0:T(8,128)(2,1)S(1)}, u32[]{:S(2)}, u32[]{:S(2)}) collective-permute-start(bf16[128,768]{1,0:T(8,128)(2,1)S(1)} %get-tuple-element.46), channel_id=1, source_target_pairs={{0,2},{1,5},{2,0},{3,7},{4,6},{5,1},{6,4},{7,3},{8,10},{9,13},{10,... | collective-permute-start | bytes 589832 | tf_op jit(solution)/shard_map/ppermute | solution.py:233
  19.6 8.6 %collective-permute-start.9 = (bf16[128,768]{1,0:T(8,128)(2,1)S(1)}, bf16[128,768]{1,0:T(8,128)(2,1)S(1)}, u32[]{:S(2)}, u32[]{:S(2)}) collective-permute-start(bf16[128,768]{1,0:T(8,128)(2,1)S(1)} %get-tuple-element.46), channel_id=1, source_target_pairs={{0,4},{1,3},{2,6},{3,1},{4,0},{5,7},{6,2},{7,5},{8,12},{9,11},{10,... | collective-permute-start | bytes 589832 | tf_op jit(solution)/shard_map/ppermute | solution.py:233
  20.2 8.1 %collective-permute-start.6 = (bf16[512,768]{1,0:T(8,128)(2,1)S(1)}, bf16[512,768]{1,0:T(8,128)(2,1)S(1)}, u32[]{:S(2)}, u32[]{:S(2)}) collective-permute-start(bf16[512,768]{1,0:T(8,128)(2,1)S(1)} %constant_dynamic-update-slice_fusion.2.refs_0_), channel_id=1, source_target_pairs={{0,1},{1,0},{2,3},{3,2},{4,5},{5,4},{6,7},{7,6},{8,9},{9,8},{10,11... | collective-permute-start | bytes 2359304 | tf_op jit(solution)/shard_map/ppermute | solution.py:213
  28.2 2.4 %collective-permute-start.10 = (bf16[512,768]{1,0:T(8,128)(2,1)S(1)}, bf16[512,768]{1,0:T(8,128)(2,1)S(1)}, u32[]{:S(2)}, u32[]{:S(2)}) collective-permute-start(bf16[512,768]{1,0:T(8,128)(2,1)S(1)} %constant_dynamic-update-slice_fusion.9.refs_2_), channel_id=1, source_target_pairs={{0,1},{1,0},{2,3},{3,2},{4,5},{5,4},{6,7},{7,6},{8,9},{9,8},{10,11... | collective-permute-start | bytes 2359304 | tf_op jit(solution)/shard_map/ppermute | solution.py:213
  31.5 7.6 %collective-permute-start.11 = (f16[64,768]{1,0:T(8,128)(2,1)S(1)}, f16[64,768]{1,0:T(8,128)(2,1)S(1)}, u32[]{:S(2)}, u32[]{:S(2)}) collective-permute-start(f16[64,768]{1,0:T(8,128)(2,1)S(1)} %convert_element_type.54), channel_id=1, source_target_pairs={{0,24},{8,16},{16,8},{24,0},{1,25},{9,17},{17,9},{25,1},{2,26},{10... | collective-permute-start | bytes 294920 | tf_op jit(solution)/shard_map/ppermute | solution.py:210
  34.5 8.9 %collective-permute-start.12 = (f16[64,768]{1,0:T(8,128)(2,1)S(1)}, f16[64,768]{1,0:T(8,128)(2,1)S(1)}, u32[]{:S(2)}, u32[]{:S(2)}) collective-permute-start(f16[64,768]{1,0:T(8,128)(2,1)S(1)} %convert_element_type.57), channel_id=1, source_target_pairs={{0,16},{8,24},{16,0},{24,8},{1,17},{9,25},{17,1},{25,9},{2,18},{10... | collective-permute-start | bytes 294920 | tf_op jit(solution)/shard_map/ppermute | solution.py:210
  34.6 8.8 %collective-permute-start.13 = (f16[72,768]{1,0:T(8,128)(2,1)S(1)}, f16[72,768]{1,0:T(8,128)(2,1)S(1)}, u32[]{:S(2)}, u32[]{:S(2)}) collective-permute-start(f16[72,768]{1,0:T(8,128)(2,1)S(1)} %convert_element_type.60), channel_id=1, source_target_pairs={{0,8},{8,0},{16,24},{24,16},{1,9},{9,1},{17,25},{25,17},{2,10},{10... | collective-permute-start | bytes 331784 | tf_op jit(solution)/shard_map/ppermute | solution.py:210
  36.2 7.2 %collective-permute-start.14 = (f32[8,128]{1,0:T(8,128)S(1)}, f32[8,128]{1,0:T(8,128)S(1)}, u32[]{:S(2)}, u32[]{:S(2)}) collective-permute-start(f32[8,128]{1,0:T(8,128)S(1)} %get-tuple-element.34), channel_id=1, source_target_pairs={{0,24},{8,16},{16,8},{24,0},{1,25},{9,17},{17,9},{25,1},{2,26},{10... | collective-permute-start | bytes 12296 | tf_op jit(solution)/shard_map/ppermute | solution.py:210
  39.0 4.5 %collective-permute-start.15 = (f32[8,128]{1,0:T(8,128)S(1)}, f32[8,128]{1,0:T(8,128)S(1)}, u32[]{:S(2)}, u32[]{:S(2)}) collective-permute-start(f32[8,128]{1,0:T(8,128)S(1)} %get-tuple-element.35), channel_id=1, source_target_pairs={{0,16},{8,24},{16,0},{24,8},{1,17},{9,25},{17,1},{25,9},{2,18},{10... | collective-permute-start | bytes 12296 | tf_op jit(solution)/shard_map/ppermute | solution.py:210

commit v12 on v10

--- a/solution.py
+++ b/solution.py
@@ -157,7 +157,7 @@
 def restore_kernel(half, chosen_ref, *refs):
     refs, (total_ref, dens_ref) = refs[:-2], refs[-2:]
     groups = len(refs) - half
-    part_refs = refs[groups - 1 :: -1] + refs[: groups - 1 : -1]
+    part_refs = refs[:groups][::-1][:half] + refs[: groups - half] + refs[groups:]
     size = part_refs[half].shape[0]
     chosen = chosen_ref[...]
     sums, dens = [], []
@@ -272,6 +272,7 @@
     back = [sent[0]] + [along_gr(sent[k], k) for k in range(1, n_gr)]
     back = [part.astype(jnp.float32) for part in back]
     back += [along_gr(sums[half + k], k) for k in range(half, n_gr)]
+    order = [*range(half, n_gr), *range(half)[::-1]]
     neighbour_sum, density = pl.pallas_call(
         functools.partial(restore_kernel, half),
         out_shape=[
@@ -282,7 +283,7 @@
         out_specs=[VMEM, VMEM],
         compiler_params=GRANT,
         name="restore_rows",
-    )(chosen, *back[n_gr - 1 :: -1], *back[:n_gr - 1 : -1])
+    )(chosen, *[back[k] for k in order], *back[n_gr:])
     return (neighbour_sum, density.reshape(count))
 
 

time: 45 us -> 45.6 us (1.013)
  transfers between devices with their start and end apart: 16 -> 16, of which waited for: 7 -> 8; matrix products, arithmetic and copies ran while one was open for 1% -> 1% of each run, Pallas kernels for 4% -> 4%
where the time goes in v12:
time: 45.6 us; the launch traced here: 45.5 us
  starting transfers between devices  20.8 us (46%)
  waiting for transfers between devices  18 us (39%)
  Pallas kernels  5.56 us (12%)
  between operations  0.83 us (2%)
    ppermute x8, starting transfers between devices, along_gr(): return lax.ppermute(part, 'gr', [(i, i ^ bits) for i in range(n_gr)])  13.5 us
    ppermute x8, waiting for transfers between devices, along_gr(): return lax.ppermute(part, 'gr', [(i, i ^ bits) for i in range(n_gr)])  9.86 us
    ppermute x4, starting transfers between devices, along_gc(): return lax.ppermute(block, 'gc', [(i, i ^ bits) for i in range(n_gc)])  5.41 us
    ppermute x4, waiting for transfers between devices, along_gc(): return lax.ppermute(block, 'gc', [(i, i ^ bits) for i in range(n_gc)])  5.28 us
    ppermute x4, waiting for transfers between devices, to_side(): return lax.ppermute(block, 'gc', pairs)  2.87 us
    pallas_call x1, Pallas kernels, on_device(): pl.pallas_call(early_kernel, out_shape=[jax.ShapeDtypeStruct((count, LANE...  1.95 us
    ppermute x4, starting transfers between devices, to_side(): return lax.ppermute(block, 'gc', pairs)  1.9 us
    pallas_call x1, Pallas kernels, on_device(): pl.pallas_call(functools.partial(restore_kernel, half), out_shape=[jax.Sh...  1.45 us
  transfers between devices with their start and end apart: 16, of which 8 were waited for; matrix products, arithmetic and copies ran while one was open for 1% of the time, Pallas kernels for 4%

profile of v12, /device:TPU:0, one launch (start us, length us, event | category | flops | bytes accessed | tf_op | source)
XLA Modules:
  0.0 45.5 jit_solution(16811495617454334454)
XLA Ops:
  0.6 1.3 %sort_rows.1 = (bf16[256,256]{1,0:T(8,128)(2,1)S(1)}, bf16[64,768]{1,0:T(8,128)(2,1)S(1)}, bf16[64,768]{1,0:T(8,128)(2,1)S(1)}, bf16[64,768]{1,0:T(8,128)(2,1)S(1)}, bf16[64,768]{1,0:T(8,128)(2,1)S(1)}) custom-call(s32[1]{0:T(128)} %bitcast.own_ref, s32[1,256]{1,0:T(1,128)} %bitcast.3, bf16[256,768]{1,0:T(8,128)(2,1)} %rows_hbm.1), custom_call_target="tpu_custom_call" | custom-call | tf_op jit(solution)/shard_map/sort_rows/pallas_call | solution.py:193
  1.9 3.1 %collective-permute-start = (bf16[64,768]{1,0:T(8,128)(2,1)S(1)}, bf16[64,768]{1,0:T(8,128)(2,1)S(1)}, u32[]{:S(2)}, u32[]{:S(2)}) collective-permute-start(bf16[64,768]{1,0:T(8,128)(2,1)S(1)} %get-tuple-element.22), channel_id=1, source_target_pairs={{0,8},{8,0},{16,24},{24,16},{1,9},{9,1},{17,25},{25,17},{2,10},{10... | collective-permute-start | bytes 294920 | tf_op jit(solution)/shard_map/ppermute | solution.py:210
  5.0 2.5 %collective-permute-start.5 = (bf16[64,768]{1,0:T(8,128)(2,1)S(1)}, bf16[64,768]{1,0:T(8,128)(2,1)S(1)}, u32[]{:S(2)}, u32[]{:S(2)}) collective-permute-start(bf16[64,768]{1,0:T(8,128)(2,1)S(1)} %get-tuple-element.24), channel_id=1, source_target_pairs={{0,24},{8,16},{16,8},{24,0},{1,25},{9,17},{17,9},{25,1},{2,26},{10... | collective-permute-start | bytes 294920 | tf_op jit(solution)/shard_map/ppermute | solution.py:210
  7.5 0.1 collective-permute-start.4
  7.6 0.2 collective-permute-done
  7.8 2.8 %collective-permute-start.1 = (bf16[128,768]{1,0:T(8,128)(2,1)S(1)}, bf16[128,768]{1,0:T(8,128)(2,1)S(1)}, u32[]{:S(2)}, u32[]{:S(2)}) collective-permute-start(bf16[128,768]{1,0:T(8,128)(2,1)S(1)} %get-tuple-element.42), channel_id=1, source_target_pairs={{0,6},{1,7},{2,4},{3,5},{4,2},{5,3},{6,0},{7,1},{8,14},{9,15},{10,... | collective-permute-start | bytes 589832 | tf_op jit(solution)/shard_map/ppermute | solution.py:213
  10.6 0.5 %collective-permute-start.2 = (bf16[128,768]{1,0:T(8,128)(2,1)S(1)}, bf16[128,768]{1,0:T(8,128)(2,1)S(1)}, u32[]{:S(2)}, u32[]{:S(2)}) collective-permute-start(bf16[128,768]{1,0:T(8,128)(2,1)S(1)} %get-tuple-element.42), channel_id=1, source_target_pairs={{0,2},{1,5},{2,0},{3,7},{4,6},{5,1},{6,4},{7,3},{8,10},{9,13},{10,... | collective-permute-start | bytes 589832 | tf_op jit(solution)/shard_map/ppermute | solution.py:233
  11.1 0.3 collective-permute-start.3
  11.4 5.1 %collective-permute-done.4 = bf16[64,768]{1,0:T(8,128)(2,1)S(1)} collective-permute-done((bf16[64,768]{1,0:T(8,128)(2,1)S(1)}, bf16[64,768]{1,0:T(8,128)(2,1)S(1)}, u32[]{:S(2)}, u32[]{:S(2)}) %collective-permute-start.4) | collective-permute-done | bytes 98336 | tf_op jit(solution)/shard_map/ppermute | solution.py:210
  16.5 0.0 collective-permute-done.5
  16.5 2.5 %collective-permute-start.7 = (bf16[128,768]{1,0:T(8,128)(2,1)S(1)}, bf16[128,768]{1,0:T(8,128)(2,1)S(1)}, u32[]{:S(2)}, u32[]{:S(2)}) collective-permute-start(bf16[128,768]{1,0:T(8,128)(2,1)S(1)} %get-tuple-element.38), channel_id=1, source_target_pairs={{0,6},{1,7},{2,4},{3,5},{4,2},{5,3},{6,0},{7,1},{8,14},{9,15},{10,... | collective-permute-start | bytes 589832 | tf_op jit(solution)/shard_map/ppermute | solution.py:213
  19.0 0.5 %collective-permute-start.8 = (bf16[128,768]{1,0:T(8,128)(2,1)S(1)}, bf16[128,768]{1,0:T(8,128)(2,1)S(1)}, u32[]{:S(2)}, u32[]{:S(2)}) collective-permute-start(bf16[128,768]{1,0:T(8,128)(2,1)S(1)} %get-tuple-element.38), channel_id=1, source_target_pairs={{0,2},{1,5},{2,0},{3,7},{4,6},{5,1},{6,4},{7,3},{8,10},{9,13},{10,... | collective-permute-start | bytes 589832 | tf_op jit(solution)/shard_map/ppermute | solution.py:233
  19.6 0.0 collective-permute-done.1
  19.6 0.6 %collective-permute-start.9 = (bf16[128,768]{1,0:T(8,128)(2,1)S(1)}, bf16[128,768]{1,0:T(8,128)(2,1)S(1)}, u32[]{:S(2)}, u32[]{:S(2)}) collective-permute-start(bf16[128,768]{1,0:T(8,128)(2,1)S(1)} %get-tuple-element.38), channel_id=1, source_target_pairs={{0,4},{1,3},{2,6},{3,1},{4,0},{5,7},{6,2},{7,5},{8,12},{9,11},{10,... | collective-permute-start | bytes 589832 | tf_op jit(solution)/shard_map/ppermute | solution.py:233
  20.2 0.0 collective-permute-done.3
  20.2 0.1 collective-permute-start.6
  20.3 5.0 %collective-permute-done.7 = bf16[128,768]{1,0:T(8,128)(2,1)S(1)} collective-permute-done((bf16[128,768]{1,0:T(8,128)(2,1)S(1)}, bf16[128,768]{1,0:T(8,128)(2,1)S(1)}, u32[]{:S(2)}, u32[]{:S(2)}) %collective-permute-start.7) | collective-permute-done | bytes 196640 | tf_op jit(solution)/shard_map/ppermute | solution.py:213
  25.3 2.9 %collective-permute-done.8 = bf16[128,768]{1,0:T(8,128)(2,1)S(1)} collective-permute-done((bf16[128,768]{1,0:T(8,128)(2,1)S(1)}, bf16[128,768]{1,0:T(8,128)(2,1)S(1)}, u32[]{:S(2)}, u32[]{:S(2)}) %collective-permute-start.8) | collective-permute-done | bytes 196640 | tf_op jit(solution)/shard_map/ppermute | solution.py:233
  28.2 0.1 collective-permute-start.10
  28.3 0.0 collective-permute-done.6.refs_1_
  28.3 2.0 %early_sums.1 = (f32[256,128]{1,0:T(8,128)S(1)}, f32[256,768]{1,0:T(8,128)S(1)}, f32[256,128]{1,0:T(8,128)S(1)}) custom-call(bf16[256,768]{1,0:T(8,128)(2,1)S(1)} %pad_maximum_fusion.rows_ref, bf16[512,768]{1,0:T(8,128)(2,1)S(1)} %constant_dynamic-update-slice_fusion.2.refs_0_, bf16[512,768]{1,0:T(8,128)(2,1)S(1)} %collective-permute-done.6.refs_1_, ...), custom_call_target="tpu_custom_call" | custom-call | flops 1207959552 | tf_op jit(solution)/shard_map/early_sums/pallas_call | solution.py:245
  30.3 0.3 collective-permute-done.10.cols_ref
  30.6 0.9 %last_sums.1 = (f32[72,768]{1,0:T(8,128)S(1)}, f32[72,768]{1,0:T(8,128)S(1)}, f32[64,768]{1,0:T(8,128)S(1)}, f32[64,768]{1,0:T(8,128)S(1)}, f32[8,128]{1,0:T(8,128)S(1)}, /*index=5*/f32[8,128]{1,0:T(8,128)S(1)}) custom-call(bf16[256,768]{1,0:T(8,128)(2,1)S(1)} %pad_maximum_fusion.rows_ref, f32[256,128]{1,0:T(8,128)S(1)} %get-tuple-element.27.scale_ref, ...), custom_call_target="tpu_custom_call" | custom-call | flops 402653184 | tf_op jit(solution)/shard_map/last_sums/pallas_call | solution.py:259
  31.5 1.9 %collective-permute-start.11 = (f16[64,768]{1,0:T(8,128)(2,1)S(1)}, f16[64,768]{1,0:T(8,128)(2,1)S(1)}, u32[]{:S(2)}, u32[]{:S(2)}) collective-permute-start(f16[64,768]{1,0:T(8,128)(2,1)S(1)} %convert_element_type.24), channel_id=1, source_target_pairs={{0,16},{8,24},{16,0},{24,8},{1,17},{9,25},{17,1},{25,9},{2,18},{10... | collective-permute-start | bytes 294920 | tf_op jit(solution)/shard_map/ppermute | solution.py:210
  33.4 1.4 %collective-permute-start.12 = (f16[64,768]{1,0:T(8,128)(2,1)S(1)}, f16[64,768]{1,0:T(8,128)(2,1)S(1)}, u32[]{:S(2)}, u32[]{:S(2)}) collective-permute-start(f16[64,768]{1,0:T(8,128)(2,1)S(1)} %convert_element_type.26), channel_id=1, source_target_pairs={{0,24},{8,16},{16,8},{24,0},{1,25},{9,17},{17,9},{25,1},{2,26},{10... | collective-permute-start | bytes 294920 | tf_op jit(solution)/shard_map/ppermute | solution.py:210
  34.8 0.3 collective-permute-start.13
  35.2 2.8 %collective-permute-start.14 = (f32[8,128]{1,0:T(8,128)S(1)}, f32[8,128]{1,0:T(8,128)S(1)}, u32[]{:S(2)}, u32[]{:S(2)}) collective-permute-start(f32[8,128]{1,0:T(8,128)S(1)} %get-tuple-element.34), channel_id=1, source_target_pairs={{0,16},{8,24},{16,0},{24,8},{1,17},{9,25},{17,1},{25,9},{2,18},{10... | collective-permute-start | bytes 12296 | tf_op jit(solution)/shard_map/ppermute | solution.py:210
  37.9 1.4 %collective-permute-start.15 = (f32[8,128]{1,0:T(8,128)S(1)}, f32[8,128]{1,0:T(8,128)S(1)}, u32[]{:S(2)}, u32[]{:S(2)}) collective-permute-start(f32[8,128]{1,0:T(8,128)S(1)} %get-tuple-element.35), channel_id=1, source_target_pairs={{0,24},{8,16},{16,8},{24,0},{1,25},{9,17},{17,9},{25,1},{2,26},{10... | collective-permute-start | bytes 12296 | tf_op jit(solution)/shard_map/ppermute | solution.py:210
  39.3 2.7 %collective-permute-done.11 = f16[64,768]{1,0:T(8,128)(2,1)S(1)} collective-permute-done((f16[64,768]{1,0:T(8,128)(2,1)S(1)}, f16[64,768]{1,0:T(8,128)(2,1)S(1)}, u32[]{:S(2)}, u32[]{:S(2)}) %collective-permute-start.11) | collective-permute-done | bytes 98336 | tf_op jit(solution)/shard_map/ppermute | solution.py:210
  42.1 1.3 %collective-permute-done.13 = f16[72,768]{1,0:T(8,128)(2,1)S(1)} collective-permute-done((f16[72,768]{1,0:T(8,128)(2,1)S(1)}, f16[72,768]{1,0:T(8,128)(2,1)S(1)}, u32[]{:S(2)}, u32[]{:S(2)}) %collective-permute-start.13) | collective-permute-done | bytes 110624 | tf_op jit(solution)/shard_map/ppermute | solution.py:210
  43.4 0.6 %collective-permute-done.14.refs_4_ = f32[8,128]{1,0:T(8,128)S(1)} collective-permute-done((f32[8,128]{1,0:T(8,128)S(1)}, f32[8,128]{1,0:T(8,128)S(1)}, u32[]{:S(2)}, u32[]{:S(2)}) %collective-permute-start.14) | collective-permute-done | bytes 4128 | tf_op jit(solution)/shard_map/ppermute | solution.py:210
  44.0 1.4 %restore_rows.1 = (f32[256,768]{1,0:T(8,128)}, f32[1,256]{1,0:T(1,128)}) custom-call(bf16[256,256]{1,0:T(8,128)(2,1)S(1)} %get-tuple-element.20.chosen_ref, f32[64,768]{1,0:T(8,128)S(1)} %convert_element_type.25.refs_0_, f32[64,768]{1,0:T(8,128)S(1)} %convert_element_type.27.refs_1_, f32[72,768]{1,0:T(8,128)S(1)} %convert_element_type.29.refs_2_, ...), custom_call_target="tpu_custom_call" | custom-call | tf_op jit(solution)/shard_map/restore_rows/pallas_call | solution.py:276
  (22 shorter events, 0.3 us)
Async XLA Ops:
  1.9 5.9 %collective-permute-start = (bf16[64,768]{1,0:T(8,128)(2,1)S(1)}, bf16[64,768]{1,0:T(8,128)(2,1)S(1)}, u32[]{:S(2)}, u32[]{:S(2)}) collective-permute-start(bf16[64,768]{1,0:T(8,128)(2,1)S(1)} %get-tuple-element.22), channel_id=1, source_target_pairs={{0,8},{8,0},{16,24},{24,16},{1,9},{9,1},{17,25},{25,17},{2,10},{10... | collective-permute-start | bytes 294920 | tf_op jit(solution)/shard_map/ppermute | solution.py:210
  5.0 11.4 %collective-permute-start.5 = (bf16[64,768]{1,0:T(8,128)(2,1)S(1)}, bf16[64,768]{1,0:T(8,128)(2,1)S(1)}, u32[]{:S(2)}, u32[]{:S(2)}) collective-permute-start(bf16[64,768]{1,0:T(8,128)(2,1)S(1)} %get-tuple-element.24), channel_id=1, source_target_pairs={{0,24},{8,16},{16,8},{24,0},{1,25},{9,17},{17,9},{25,1},{2,26},{10... | collective-permute-start | bytes 294920 | tf_op jit(solution)/shard_map/ppermute | solution.py:210
  7.5 8.9 %collective-permute-start.4 = (bf16[64,768]{1,0:T(8,128)(2,1)S(1)}, bf16[64,768]{1,0:T(8,128)(2,1)S(1)}, u32[]{:S(2)}, u32[]{:S(2)}) collective-permute-start(bf16[64,768]{1,0:T(8,128)(2,1)S(1)} %get-tuple-element.23), channel_id=1, source_target_pairs={{0,16},{8,24},{16,0},{24,8},{1,17},{9,25},{17,1},{25,9},{2,18},{10... | collective-permute-start | bytes 294920 | tf_op jit(solution)/shard_map/ppermute | solution.py:210
  7.8 11.7 %collective-permute-start.1 = (bf16[128,768]{1,0:T(8,128)(2,1)S(1)}, bf16[128,768]{1,0:T(8,128)(2,1)S(1)}, u32[]{:S(2)}, u32[]{:S(2)}) collective-permute-start(bf16[128,768]{1,0:T(8,128)(2,1)S(1)} %get-tuple-element.42), channel_id=1, source_target_pairs={{0,6},{1,7},{2,4},{3,5},{4,2},{5,3},{6,0},{7,1},{8,14},{9,15},{10,... | collective-permute-start | bytes 589832 | tf_op jit(solution)/shard_map/ppermute | solution.py:213
  10.6 9.6 %collective-permute-start.2 = (bf16[128,768]{1,0:T(8,128)(2,1)S(1)}, bf16[128,768]{1,0:T(8,128)(2,1)S(1)}, u32[]{:S(2)}, u32[]{:S(2)}) collective-permute-start(bf16[128,768]{1,0:T(8,128)(2,1)S(1)} %get-tuple-element.42), channel_id=1, source_target_pairs={{0,2},{1,5},{2,0},{3,7},{4,6},{5,1},{6,4},{7,3},{8,10},{9,13},{10,... | collective-permute-start | bytes 589832 | tf_op jit(solution)/shard_map/ppermute | solution.py:233
  11.1 9.1 %collective-permute-start.3 = (bf16[128,768]{1,0:T(8,128)(2,1)S(1)}, bf16[128,768]{1,0:T(8,128)(2,1)S(1)}, u32[]{:S(2)}, u32[]{:S(2)}) collective-permute-start(bf16[128,768]{1,0:T(8,128)(2,1)S(1)} %get-tuple-element.42), channel_id=1, source_target_pairs={{0,4},{1,3},{2,6},{3,1},{4,0},{5,7},{6,2},{7,5},{8,12},{9,11},{10,... | collective-permute-start | bytes 589832 | tf_op jit(solution)/shard_map/ppermute | solution.py:233
  16.5 8.8 %collective-permute-start.7 = (bf16[128,768]{1,0:T(8,128)(2,1)S(1)}, bf16[128,768]{1,0:T(8,128)(2,1)S(1)}, u32[]{:S(2)}, u32[]{:S(2)}) collective-permute-start(bf16[128,768]{1,0:T(8,128)(2,1)S(1)} %get-tuple-element.38), channel_id=1, source_target_pairs={{0,6},{1,7},{2,4},{3,5},{4,2},{5,3},{6,0},{7,1},{8,14},{9,15},{10,... | collective-permute-start | bytes 589832 | tf_op jit(solution)/shard_map/ppermute | solution.py:213
  19.0 9.2 %collective-permute-start.8 = (bf16[128,768]{1,0:T(8,128)(2,1)S(1)}, bf16[128,768]{1,0:T(8,128)(2,1)S(1)}, u32[]{:S(2)}, u32[]{:S(2)}) collective-permute-start(bf16[128,768]{1,0:T(8,128)(2,1)S(1)} %get-tuple-element.38), channel_id=1, source_target_pairs={{0,2},{1,5},{2,0},{3,7},{4,6},{5,1},{6,4},{7,3},{8,10},{9,13},{10,... | collective-permute-start | bytes 589832 | tf_op jit(solution)/shard_map/ppermute | solution.py:233
  19.6 8.6 %collective-permute-start.9 = (bf16[128,768]{1,0:T(8,128)(2,1)S(1)}, bf16[128,768]{1,0:T(8,128)(2,1)S(1)}, u32[]{:S(2)}, u32[]{:S(2)}) collective-permute-start(bf16[128,768]{1,0:T(8,128)(2,1)S(1)} %get-tuple-element.38), channel_id=1, source_target_pairs={{0,4},{1,3},{2,6},{3,1},{4,0},{5,7},{6,2},{7,5},{8,12},{9,11},{10,... | collective-permute-start | bytes 589832 | tf_op jit(solution)/shard_map/ppermute | solution.py:233
  20.2 8.1 %collective-permute-start.6 = (bf16[512,768]{1,0:T(8,128)(2,1)S(1)}, bf16[512,768]{1,0:T(8,128)(2,1)S(1)}, u32[]{:S(2)}, u32[]{:S(2)}) collective-permute-start(bf16[512,768]{1,0:T(8,128)(2,1)S(1)} %constant_dynamic-update-slice_fusion.2.refs_0_), channel_id=1, source_target_pairs={{0,1},{1,0},{2,3},{3,2},{4,5},{5,4},{6,7},{7,6},{8,9},{9,8},{10,11... | collective-permute-start | bytes 2359304 | tf_op jit(solution)/shard_map/ppermute | solution.py:213
  28.2 2.4 %collective-permute-start.10 = (bf16[512,768]{1,0:T(8,128)(2,1)S(1)}, bf16[512,768]{1,0:T(8,128)(2,1)S(1)}, u32[]{:S(2)}, u32[]{:S(2)}) collective-permute-start(bf16[512,768]{1,0:T(8,128)(2,1)S(1)} %constant_dynamic-update-slice_fusion.9.refs_2_), channel_id=1, source_target_pairs={{0,1},{1,0},{2,3},{3,2},{4,5},{5,4},{6,7},{7,6},{8,9},{9,8},{10,11... | collective-permute-start | bytes 2359304 | tf_op jit(solution)/shard_map/ppermute | solution.py:213
  31.5 10.6 %collective-permute-start.11 = (f16[64,768]{1,0:T(8,128)(2,1)S(1)}, f16[64,768]{1,0:T(8,128)(2,1)S(1)}, u32[]{:S(2)}, u32[]{:S(2)}) collective-permute-start(f16[64,768]{1,0:T(8,128)(2,1)S(1)} %convert_element_type.24), channel_id=1, source_target_pairs={{0,16},{8,24},{16,0},{24,8},{1,17},{9,25},{17,1},{25,9},{2,18},{10... | collective-permute-start | bytes 294920 | tf_op jit(solution)/shard_map/ppermute | solution.py:210
  33.4 8.6 %collective-permute-start.12 = (f16[64,768]{1,0:T(8,128)(2,1)S(1)}, f16[64,768]{1,0:T(8,128)(2,1)S(1)}, u32[]{:S(2)}, u32[]{:S(2)}) collective-permute-start(f16[64,768]{1,0:T(8,128)(2,1)S(1)} %convert_element_type.26), channel_id=1, source_target_pairs={{0,24},{8,16},{16,8},{24,0},{1,25},{9,17},{17,9},{25,1},{2,26},{10... | collective-permute-start | bytes 294920 | tf_op jit(solution)/shard_map/ppermute | solution.py:210
  34.8 8.5 %collective-permute-start.13 = (f16[72,768]{1,0:T(8,128)(2,1)S(1)}, f16[72,768]{1,0:T(8,128)(2,1)S(1)}, u32[]{:S(2)}, u32[]{:S(2)}) collective-permute-start(f16[72,768]{1,0:T(8,128)(2,1)S(1)} %convert_element_type.28), channel_id=1, source_target_pairs={{0,8},{8,0},{16,24},{24,16},{1,9},{9,1},{17,25},{25,17},{2,10},{10... | collective-permute-start | bytes 331784 | tf_op jit(solution)/shard_map/ppermute | solution.py:210
  35.2 8.8 %collective-permute-start.14 = (f32[8,128]{1,0:T(8,128)S(1)}, f32[8,128]{1,0:T(8,128)S(1)}, u32[]{:S(2)}, u32[]{:S(2)}) collective-permute-start(f32[8,128]{1,0:T(8,128)S(1)} %get-tuple-element.34), channel_id=1, source_target_pairs={{0,16},{8,24},{16,0},{24,8},{1,17},{9,25},{17,1},{25,9},{2,18},{10... | collective-permute-start | bytes 12296 | tf_op jit(solution)/shard_map/ppermute | solution.py:210
  37.9 6.1 %collective-permute-start.15 = (f32[8,128]{1,0:T(8,128)S(1)}, f32[8,128]{1,0:T(8,128)S(1)}, u32[]{:S(2)}, u32[]{:S(2)}) collective-permute-start(f32[8,128]{1,0:T(8,128)S(1)} %get-tuple-element.35), channel_id=1, source_target_pairs={{0,24},{8,16},{16,8},{24,0},{1,25},{9,17},{17,9},{25,1},{2,26},{10... | collective-permute-start | bytes 12296 | tf_op jit(solution)/shard_map/ppermute | solution.py:210

commit v13 on v10

--- a/solution.py
+++ b/solution.py
@@ -232,14 +232,18 @@
         pairs = [(i, i ^ sides[(step + i % 2) % len(sides)]) for i in range(n_gc)]
         return lax.ppermute(block, "gc", pairs)
 
-    chunks = []
-    for pieces in (held[:half], held[half:]):
-        block = jnp.concatenate(pieces, axis=0)
-        near = [block] + [along_gc(block, k) for k in corners]
-        near += [to_side(block, step) for step in range(len(sides))]
-        chunks.append(jnp.concatenate(near, axis=0))
+    early = jnp.concatenate(held[:half], axis=0)
+    late = jnp.concatenate(held[half:], axis=0)
+    rest = jnp.concatenate(held[1:half], axis=0)
+    filler = [along_gc(held[0], k) for k in corners]
+    filler, rest = lax.optimization_barrier((filler, rest))
+    rest_corners = [along_gc(rest, k) for k in corners]
+    early_sides = [to_side(early, step) for step in range(len(sides))]
+    late_near = [along_gc(late, k) for k in corners] + [to_side(late, step) for step in range(1)]
+    rest_corners, late = lax.optimization_barrier((rest_corners, late))
+    late_near += [to_side(late, step) for step in range(1, len(sides))]
     rows = jnp.concatenate(held, axis=0)
-    chunks[0], rows = lax.optimization_barrier((chunks[0], rows))
+    chunks = [jnp.concatenate([early] + early_sides + filler + rest_corners, axis=0), jnp.concatenate(late_near + [late], axis=0)]
     early = [chunks[0], other_core(chunks[0]), chunks[1]]
 
     scale, total, dens = pl.pallas_call(

time: 45 us -> 46.6 us (1.036)
  starting transfers between devices: 20.4 us -> 23.8 us
  waiting for transfers between devices: 17.8 us -> 16 us
    ppermute x8, waiting for transfers between devices: 9.65 us -> 6.47 us  [along_gr(): return lax.ppermute(part, 'gr', [(i, i ^ bits) for i in range(n_gr)])]
    ppermute x4 -> x5, waiting for transfers between devices: 5.28 us -> 7.42 us  [along_gc(): return lax.ppermute(block, 'gc', [(i, i ^ bits) for i in range(n_gc)])]
    ppermute x4 -> x5, starting transfers between devices: 5.41 us -> 7.22 us  [along_gc(): return lax.ppermute(block, 'gc', [(i, i ^ bits) for i in range(n_gc)])]
    ppermute x4, starting transfers between devices: 1.9 us -> 3.66 us  [to_side(): return lax.ppermute(block, 'gc', pairs)]
    ppermute x4, waiting for transfers between devices: 2.87 us -> 2.07 us  [to_side(): return lax.ppermute(block, 'gc', pairs)]
  transfers between devices with their start and end apart: 16 -> 17, of which waited for: 7 -> 7; matrix products, arithmetic and copies ran while one was open for 1% -> 1% of each run, Pallas kernels for 4% -> 4%
where the time goes in v13:
time: 46.6 us; the launch traced here: 46.5 us
  starting transfers between devices  23.8 us (51%)
  waiting for transfers between devices  16 us (34%)
  Pallas kernels  5.59 us (12%)
  between operations  0.84 us (2%)
    ppermute x8, starting transfers between devices, along_gr(): return lax.ppermute(part, 'gr', [(i, i ^ bits) for i in range(n_gr)])  12.9 us
    ppermute x5, waiting for transfers between devices, along_gc(): return lax.ppermute(block, 'gc', [(i, i ^ bits) for i in range(n_gc)])  7.42 us
    ppermute x5, starting transfers between devices, along_gc(): return lax.ppermute(block, 'gc', [(i, i ^ bits) for i in range(n_gc)])  7.22 us
    ppermute x8, waiting for transfers between devices, along_gr(): return lax.ppermute(part, 'gr', [(i, i ^ bits) for i in range(n_gr)])  6.47 us
    ppermute x4, starting transfers between devices, to_side(): return lax.ppermute(block, 'gc', pairs)  3.66 us
    ppermute x4, waiting for transfers between devices, to_side(): return lax.ppermute(block, 'gc', pairs)  2.07 us
    pallas_call x1, Pallas kernels, on_device(): pl.pallas_call(early_kernel, out_shape=[jax.ShapeDtypeStruct((count, LANE...  1.97 us
    pallas_call x1, Pallas kernels, on_device(): pl.pallas_call(functools.partial(restore_kernel, half), out_shape=[jax.Sh...  1.44 us
  transfers between devices with their start and end apart: 17, of which 7 were waited for; matrix products, arithmetic and copies ran while one was open for 1% of the time, Pallas kernels for 4%

profile of v13, /device:TPU:0, one launch (start us, length us, event | category | flops | bytes accessed | tf_op | source)
XLA Modules:
  0.0 46.5 jit_solution(11985079053257557704)
XLA Ops:
  0.6 1.3 %sort_rows.1 = (bf16[256,256]{1,0:T(8,128)(2,1)S(1)}, bf16[64,768]{1,0:T(8,128)(2,1)S(1)}, bf16[64,768]{1,0:T(8,128)(2,1)S(1)}, bf16[64,768]{1,0:T(8,128)(2,1)S(1)}, bf16[64,768]{1,0:T(8,128)(2,1)S(1)}) custom-call(s32[1]{0:T(128)} %bitcast.own_ref, s32[1,256]{1,0:T(1,128)} %bitcast.3, bf16[256,768]{1,0:T(8,128)(2,1)} %rows_hbm.1), custom_call_target="tpu_custom_call" | custom-call | tf_op jit(solution)/shard_map/sort_rows/pallas_call | solution.py:193
  1.9 3.1 %collective-permute-start = (bf16[64,768]{1,0:T(8,128)(2,1)S(1)}, bf16[64,768]{1,0:T(8,128)(2,1)S(1)}, u32[]{:S(2)}, u32[]{:S(2)}) collective-permute-start(bf16[64,768]{1,0:T(8,128)(2,1)S(1)} %get-tuple-element.24), channel_id=1, source_target_pairs={{0,8},{8,0},{16,24},{24,16},{1,9},{9,1},{17,25},{25,17},{2,10},{10... | collective-permute-start | bytes 294920 | tf_op jit(solution)/shard_map/ppermute | solution.py:210
  5.0 2.6 %collective-permute-start.1 = (bf16[64,768]{1,0:T(8,128)(2,1)S(1)}, bf16[64,768]{1,0:T(8,128)(2,1)S(1)}, u32[]{:S(2)}, u32[]{:S(2)}) collective-permute-start(bf16[64,768]{1,0:T(8,128)(2,1)S(1)} %get-tuple-element.25), channel_id=1, source_target_pairs={{0,16},{8,24},{16,0},{24,8},{1,17},{9,25},{17,1},{25,9},{2,18},{10... | collective-permute-start | bytes 294920 | tf_op jit(solution)/shard_map/ppermute | solution.py:210
  7.6 2.7 %collective-permute-start.5 = (bf16[64,768]{1,0:T(8,128)(2,1)S(1)}, bf16[64,768]{1,0:T(8,128)(2,1)S(1)}, u32[]{:S(2)}, u32[]{:S(2)}) collective-permute-start(bf16[64,768]{1,0:T(8,128)(2,1)S(1)} %get-tuple-element.23), channel_id=1, source_target_pairs={{0,6},{1,7},{2,4},{3,5},{4,2},{5,3},{6,0},{7,1},{8,14},{9,15},{10,... | collective-permute-start | bytes 294920 | tf_op jit(solution)/shard_map/ppermute | solution.py:213
  10.3 0.0 collective-permute-done
  10.4 0.6 %collective-permute-start.3 = (bf16[128,768]{1,0:T(8,128)(2,1)S(1)}, bf16[128,768]{1,0:T(8,128)(2,1)S(1)}, u32[]{:S(2)}, u32[]{:S(2)}) collective-permute-start(bf16[128,768]{1,0:T(8,128)(2,1)S(1)} %get-tuple-element.46), channel_id=1, source_target_pairs={{0,2},{1,5},{2,0},{3,7},{4,6},{5,1},{6,4},{7,3},{8,10},{9,13},{10,... | collective-permute-start | bytes 589832 | tf_op jit(solution)/shard_map/ppermute | solution.py:233
  11.0 0.3 collective-permute-start.4
  11.2 2.3 %collective-permute-done.5 = bf16[64,768]{1,0:T(8,128)(2,1)S(1)} collective-permute-done((bf16[64,768]{1,0:T(8,128)(2,1)S(1)}, bf16[64,768]{1,0:T(8,128)(2,1)S(1)}, u32[]{:S(2)}, u32[]{:S(2)}) %collective-permute-start.5) | collective-permute-done | bytes 98336 | tf_op jit(solution)/shard_map/ppermute | solution.py:213
  13.5 3.4 %collective-permute-start.6 = (bf16[64,768]{1,0:T(8,128)(2,1)S(1)}, bf16[64,768]{1,0:T(8,128)(2,1)S(1)}, u32[]{:S(2)}, u32[]{:S(2)}) collective-permute-start(bf16[64,768]{1,0:T(8,128)(2,1)S(1)} %collective-permute-done), channel_id=1, source_target_pairs={{0,6},{1,7},{2,4},{3,5},{4,2},{5,3},{6,0},{7,1},{8,14},{9,15},{10,... | collective-permute-start | bytes 294920 | tf_op jit(solution)/shard_map/ppermute | solution.py:213
  16.9 0.0 collective-permute-done.2
  17.0 1.0 %collective-permute-start.8 = (bf16[128,768]{1,0:T(8,128)(2,1)S(1)}, bf16[128,768]{1,0:T(8,128)(2,1)S(1)}, u32[]{:S(2)}, u32[]{:S(2)}) collective-permute-start(bf16[128,768]{1,0:T(8,128)(2,1)S(1)} %get-tuple-element.30), channel_id=1, source_target_pairs={{0,6},{1,7},{2,4},{3,5},{4,2},{5,3},{6,0},{7,1},{8,14},{9,15},{10,... | collective-permute-start | bytes 589832 | tf_op jit(solution)/shard_map/ppermute | solution.py:213
  18.0 0.9 %collective-permute-start.9 = (bf16[128,768]{1,0:T(8,128)(2,1)S(1)}, bf16[128,768]{1,0:T(8,128)(2,1)S(1)}, u32[]{:S(2)}, u32[]{:S(2)}) collective-permute-start(bf16[128,768]{1,0:T(8,128)(2,1)S(1)} %get-tuple-element.30), channel_id=1, source_target_pairs={{0,2},{1,5},{2,0},{3,7},{4,6},{5,1},{6,4},{7,3},{8,10},{9,13},{10,... | collective-permute-start | bytes 589832 | tf_op jit(solution)/shard_map/ppermute | solution.py:233
  19.0 1.8 %collective-permute-done.6 = bf16[64,768]{1,0:T(8,128)(2,1)S(1)} collective-permute-done((bf16[64,768]{1,0:T(8,128)(2,1)S(1)}, bf16[64,768]{1,0:T(8,128)(2,1)S(1)}, u32[]{:S(2)}, u32[]{:S(2)}) %collective-permute-start.6) | collective-permute-done | bytes 98336 | tf_op jit(solution)/shard_map/ppermute | solution.py:213
  20.7 1.8 %collective-permute-start.10 = (bf16[128,768]{1,0:T(8,128)(2,1)S(1)}, bf16[128,768]{1,0:T(8,128)(2,1)S(1)}, u32[]{:S(2)}, u32[]{:S(2)}) collective-permute-start(bf16[128,768]{1,0:T(8,128)(2,1)S(1)} %get-tuple-element.30), channel_id=1, source_target_pairs={{0,4},{1,3},{2,6},{3,1},{4,0},{5,7},{6,2},{7,5},{8,12},{9,11},{10,... | collective-permute-start | bytes 589832 | tf_op jit(solution)/shard_map/ppermute | solution.py:233
  22.6 0.0 collective-permute-done.3
  22.7 0.1 collective-permute-start.7
  22.7 3.0 %collective-permute-done.8 = bf16[128,768]{1,0:T(8,128)(2,1)S(1)} collective-permute-done((bf16[128,768]{1,0:T(8,128)(2,1)S(1)}, bf16[128,768]{1,0:T(8,128)(2,1)S(1)}, u32[]{:S(2)}, u32[]{:S(2)}) %collective-permute-start.8) | collective-permute-done | bytes 196640 | tf_op jit(solution)/shard_map/ppermute | solution.py:213
  25.8 2.1 %collective-permute-done.9 = bf16[128,768]{1,0:T(8,128)(2,1)S(1)} collective-permute-done((bf16[128,768]{1,0:T(8,128)(2,1)S(1)}, bf16[128,768]{1,0:T(8,128)(2,1)S(1)}, u32[]{:S(2)}, u32[]{:S(2)}) %collective-permute-start.9) | collective-permute-done | bytes 196640 | tf_op jit(solution)/shard_map/ppermute | solution.py:233
  27.9 0.0 collective-permute-done.10
  27.9 0.1 collective-permute-start.11
  28.0 2.0 %early_sums.1 = (f32[256,128]{1,0:T(8,128)S(1)}, f32[256,768]{1,0:T(8,128)S(1)}, f32[256,128]{1,0:T(8,128)S(1)}) custom-call(bf16[256,768]{1,0:T(8,128)(2,1)S(1)} %get-tuple-element.43.rows_ref, bf16[512,768]{1,0:T(8,128)(2,1)S(1)} %constant_dynamic-update-slice_fusion.8.refs_0_, bf16[512,768]{1,0:T(8,128)(2,1)S(1)} %collective-permute-done.7.refs_1_, ...), custom_call_target="tpu_custom_call" | custom-call | flops 1207959552 | tf_op jit(solution)/shard_map/early_sums/pallas_call | solution.py:249
  30.0 0.3 collective-permute-done.11.cols_ref
  30.3 0.9 %last_sums.1 = (f32[72,768]{1,0:T(8,128)S(1)}, f32[72,768]{1,0:T(8,128)S(1)}, f32[64,768]{1,0:T(8,128)S(1)}, f32[64,768]{1,0:T(8,128)S(1)}, f32[8,128]{1,0:T(8,128)S(1)}, /*index=5*/f32[8,128]{1,0:T(8,128)S(1)}) custom-call(bf16[256,768]{1,0:T(8,128)(2,1)S(1)} %get-tuple-element.43.rows_ref, f32[256,128]{1,0:T(8,128)S(1)} %get-tuple-element.31.scale_ref, ...), custom_call_target="tpu_custom_call" | custom-call | flops 402653184 | tf_op jit(solution)/shard_map/last_sums/pallas_call | solution.py:263
  31.2 1.3 %collective-permute-start.14 = (f16[72,768]{1,0:T(8,128)(2,1)S(1)}, f16[72,768]{1,0:T(8,128)(2,1)S(1)}, u32[]{:S(2)}, u32[]{:S(2)}) collective-permute-start(f16[72,768]{1,0:T(8,128)(2,1)S(1)} %convert_element_type.28), channel_id=1, source_target_pairs={{0,8},{8,0},{16,24},{24,16},{1,9},{9,1},{17,25},{25,17},{2,10},{10... | collective-permute-start | bytes 331784 | tf_op jit(solution)/shard_map/ppermute | solution.py:210
  32.5 2.5 %collective-permute-start.12 = (f16[64,768]{1,0:T(8,128)(2,1)S(1)}, f16[64,768]{1,0:T(8,128)(2,1)S(1)}, u32[]{:S(2)}, u32[]{:S(2)}) collective-permute-start(f16[64,768]{1,0:T(8,128)(2,1)S(1)} %convert_element_type.24), channel_id=1, source_target_pairs={{0,24},{8,16},{16,8},{24,0},{1,25},{9,17},{17,9},{25,1},{2,26},{10... | collective-permute-start | bytes 294920 | tf_op jit(solution)/shard_map/ppermute | solution.py:210
  35.0 0.5 %collective-permute-start.13 = (f16[64,768]{1,0:T(8,128)(2,1)S(1)}, f16[64,768]{1,0:T(8,128)(2,1)S(1)}, u32[]{:S(2)}, u32[]{:S(2)}) collective-permute-start(f16[64,768]{1,0:T(8,128)(2,1)S(1)} %convert_element_type.26), channel_id=1, source_target_pairs={{0,16},{8,24},{16,0},{24,8},{1,17},{9,25},{17,1},{25,9},{2,18},{10... | collective-permute-start | bytes 294920 | tf_op jit(solution)/shard_map/ppermute | solution.py:210
  35.6 2.9 %collective-permute-start.15 = (f32[8,128]{1,0:T(8,128)S(1)}, f32[8,128]{1,0:T(8,128)S(1)}, u32[]{:S(2)}, u32[]{:S(2)}) collective-permute-start(f32[8,128]{1,0:T(8,128)S(1)} %get-tuple-element.38), channel_id=1, source_target_pairs={{0,24},{8,16},{16,8},{24,0},{1,25},{9,17},{17,9},{25,1},{2,26},{10... | collective-permute-start | bytes 12296 | tf_op jit(solution)/shard_map/ppermute | solution.py:210
  38.5 0.0 collective-permute-start.16
  38.5 2.5 %collective-permute-done.12 = f16[64,768]{1,0:T(8,128)(2,1)S(1)} collective-permute-done((f16[64,768]{1,0:T(8,128)(2,1)S(1)}, f16[64,768]{1,0:T(8,128)(2,1)S(1)}, u32[]{:S(2)}, u32[]{:S(2)}) %collective-permute-start.12) | collective-permute-done | bytes 98336 | tf_op jit(solution)/shard_map/ppermute | solution.py:210
  41.0 3.9 %collective-permute-done.13 = f16[64,768]{1,0:T(8,128)(2,1)S(1)} collective-permute-done((f16[64,768]{1,0:T(8,128)(2,1)S(1)}, f16[64,768]{1,0:T(8,128)(2,1)S(1)}, u32[]{:S(2)}, u32[]{:S(2)}) %collective-permute-start.13) | collective-permute-done | bytes 98336 | tf_op jit(solution)/shard_map/ppermute | solution.py:210
  45.0 0.0 collective-permute-done.16.refs_5_
  45.0 1.4 %restore_rows.1 = (f32[256,768]{1,0:T(8,128)}, f32[1,256]{1,0:T(1,128)}) custom-call(bf16[256,256]{1,0:T(8,128)(2,1)S(1)} %get-tuple-element.22.chosen_ref, f32[64,768]{1,0:T(8,128)S(1)} %convert_element_type.25.refs_0_, f32[64,768]{1,0:T(8,128)S(1)} %convert_element_type.27.refs_1_, f32[72,768]{1,0:T(8,128)S(1)} %convert_element_type.29.refs_2_, ...), custom_call_target="tpu_custom_call" | custom-call | tf_op jit(solution)/shard_map/restore_rows/pallas_call | solution.py:279
  (25 shorter events, 0.3 us)
Async XLA Ops:
  1.9 8.4 %collective-permute-start = (bf16[64,768]{1,0:T(8,128)(2,1)S(1)}, bf16[64,768]{1,0:T(8,128)(2,1)S(1)}, u32[]{:S(2)}, u32[]{:S(2)}) collective-permute-start(bf16[64,768]{1,0:T(8,128)(2,1)S(1)} %get-tuple-element.24), channel_id=1, source_target_pairs={{0,8},{8,0},{16,24},{24,16},{1,9},{9,1},{17,25},{25,17},{2,10},{10... | collective-permute-start | bytes 294920 | tf_op jit(solution)/shard_map/ppermute | solution.py:210
  5.0 11.9 %collective-permute-start.1 = (bf16[64,768]{1,0:T(8,128)(2,1)S(1)}, bf16[64,768]{1,0:T(8,128)(2,1)S(1)}, u32[]{:S(2)}, u32[]{:S(2)}) collective-permute-start(bf16[64,768]{1,0:T(8,128)(2,1)S(1)} %get-tuple-element.25), channel_id=1, source_target_pairs={{0,16},{8,24},{16,0},{24,8},{1,17},{9,25},{17,1},{25,9},{2,18},{10... | collective-permute-start | bytes 294920 | tf_op jit(solution)/shard_map/ppermute | solution.py:210
  7.6 9.3 %collective-permute-start.2 = (bf16[64,768]{1,0:T(8,128)(2,1)S(1)}, bf16[64,768]{1,0:T(8,128)(2,1)S(1)}, u32[]{:S(2)}, u32[]{:S(2)}) collective-permute-start(bf16[64,768]{1,0:T(8,128)(2,1)S(1)} %get-tuple-element.26), channel_id=1, source_target_pairs={{0,24},{8,16},{16,8},{24,0},{1,25},{9,17},{17,9},{25,1},{2,26},{10... | collective-permute-start | bytes 294920 | tf_op jit(solution)/shard_map/ppermute | solution.py:210
  7.6 5.9 %collective-permute-start.5 = (bf16[64,768]{1,0:T(8,128)(2,1)S(1)}, bf16[64,768]{1,0:T(8,128)(2,1)S(1)}, u32[]{:S(2)}, u32[]{:S(2)}) collective-permute-start(bf16[64,768]{1,0:T(8,128)(2,1)S(1)} %get-tuple-element.23), channel_id=1, source_target_pairs={{0,6},{1,7},{2,4},{3,5},{4,2},{5,3},{6,0},{7,1},{8,14},{9,15},{10,... | collective-permute-start | bytes 294920 | tf_op jit(solution)/shard_map/ppermute | solution.py:213
  10.4 12.2 %collective-permute-start.3 = (bf16[128,768]{1,0:T(8,128)(2,1)S(1)}, bf16[128,768]{1,0:T(8,128)(2,1)S(1)}, u32[]{:S(2)}, u32[]{:S(2)}) collective-permute-start(bf16[128,768]{1,0:T(8,128)(2,1)S(1)} %get-tuple-element.46), channel_id=1, source_target_pairs={{0,2},{1,5},{2,0},{3,7},{4,6},{5,1},{6,4},{7,3},{8,10},{9,13},{10,... | collective-permute-start | bytes 589832 | tf_op jit(solution)/shard_map/ppermute | solution.py:233
  11.0 11.6 %collective-permute-start.4 = (bf16[128,768]{1,0:T(8,128)(2,1)S(1)}, bf16[128,768]{1,0:T(8,128)(2,1)S(1)}, u32[]{:S(2)}, u32[]{:S(2)}) collective-permute-start(bf16[128,768]{1,0:T(8,128)(2,1)S(1)} %get-tuple-element.46), channel_id=1, source_target_pairs={{0,4},{1,3},{2,6},{3,1},{4,0},{5,7},{6,2},{7,5},{8,12},{9,11},{10,... | collective-permute-start | bytes 589832 | tf_op jit(solution)/shard_map/ppermute | solution.py:233
  13.5 7.2 %collective-permute-start.6 = (bf16[64,768]{1,0:T(8,128)(2,1)S(1)}, bf16[64,768]{1,0:T(8,128)(2,1)S(1)}, u32[]{:S(2)}, u32[]{:S(2)}) collective-permute-start(bf16[64,768]{1,0:T(8,128)(2,1)S(1)} %collective-permute-done), channel_id=1, source_target_pairs={{0,6},{1,7},{2,4},{3,5},{4,2},{5,3},{6,0},{7,1},{8,14},{9,15},{10,... | collective-permute-start | bytes 294920 | tf_op jit(solution)/shard_map/ppermute | solution.py:213
  17.0 8.8 %collective-permute-start.8 = (bf16[128,768]{1,0:T(8,128)(2,1)S(1)}, bf16[128,768]{1,0:T(8,128)(2,1)S(1)}, u32[]{:S(2)}, u32[]{:S(2)}) collective-permute-start(bf16[128,768]{1,0:T(8,128)(2,1)S(1)} %get-tuple-element.30), channel_id=1, source_target_pairs={{0,6},{1,7},{2,4},{3,5},{4,2},{5,3},{6,0},{7,1},{8,14},{9,15},{10,... | collective-permute-start | bytes 589832 | tf_op jit(solution)/shard_map/ppermute | solution.py:213
  18.0 9.8 %collective-permute-start.9 = (bf16[128,768]{1,0:T(8,128)(2,1)S(1)}, bf16[128,768]{1,0:T(8,128)(2,1)S(1)}, u32[]{:S(2)}, u32[]{:S(2)}) collective-permute-start(bf16[128,768]{1,0:T(8,128)(2,1)S(1)} %get-tuple-element.30), channel_id=1, source_target_pairs={{0,2},{1,5},{2,0},{3,7},{4,6},{5,1},{6,4},{7,3},{8,10},{9,13},{10,... | collective-permute-start | bytes 589832 | tf_op jit(solution)/shard_map/ppermute | solution.py:233
  20.7 7.2 %collective-permute-start.10 = (bf16[128,768]{1,0:T(8,128)(2,1)S(1)}, bf16[128,768]{1,0:T(8,128)(2,1)S(1)}, u32[]{:S(2)}, u32[]{:S(2)}) collective-permute-start(bf16[128,768]{1,0:T(8,128)(2,1)S(1)} %get-tuple-element.30), channel_id=1, source_target_pairs={{0,4},{1,3},{2,6},{3,1},{4,0},{5,7},{6,2},{7,5},{8,12},{9,11},{10,... | collective-permute-start | bytes 589832 | tf_op jit(solution)/shard_map/ppermute | solution.py:233
  22.7 5.4 %collective-permute-start.7 = (bf16[512,768]{1,0:T(8,128)(2,1)S(1)}, bf16[512,768]{1,0:T(8,128)(2,1)S(1)}, u32[]{:S(2)}, u32[]{:S(2)}) collective-permute-start(bf16[512,768]{1,0:T(8,128)(2,1)S(1)} %constant_dynamic-update-slice_fusion.8.refs_0_), channel_id=1, source_target_pairs={{0,1},{1,0},{2,3},{3,2},{4,5},{5,4},{6,7},{7,6},{8,9},{9,8},{10,11... | collective-permute-start | bytes 2359304 | tf_op jit(solution)/shard_map/ppermute | solution.py:213
  27.9 2.4 %collective-permute-start.11 = (bf16[512,768]{1,0:T(8,128)(2,1)S(1)}, bf16[512,768]{1,0:T(8,128)(2,1)S(1)}, u32[]{:S(2)}, u32[]{:S(2)}) collective-permute-start(bf16[512,768]{1,0:T(8,128)(2,1)S(1)} %constant_dynamic-update-slice_fusion.14.refs_2_), channel_id=1, source_target_pairs={{0,1},{1,0},{2,3},{3,2},{4,5},{5,4},{6,7},{7,6},{8,9},{9,8},{10,11... | collective-permute-start | bytes 2359304 | tf_op jit(solution)/shard_map/ppermute | solution.py:213
  31.2 13.8 %collective-permute-start.14 = (f16[72,768]{1,0:T(8,128)(2,1)S(1)}, f16[72,768]{1,0:T(8,128)(2,1)S(1)}, u32[]{:S(2)}, u32[]{:S(2)}) collective-permute-start(f16[72,768]{1,0:T(8,128)(2,1)S(1)} %convert_element_type.28), channel_id=1, source_target_pairs={{0,8},{8,0},{16,24},{24,16},{1,9},{9,1},{17,25},{25,17},{2,10},{10... | collective-permute-start | bytes 331784 | tf_op jit(solution)/shard_map/ppermute | solution.py:210
  32.5 8.5 %collective-permute-start.12 = (f16[64,768]{1,0:T(8,128)(2,1)S(1)}, f16[64,768]{1,0:T(8,128)(2,1)S(1)}, u32[]{:S(2)}, u32[]{:S(2)}) collective-permute-start(f16[64,768]{1,0:T(8,128)(2,1)S(1)} %convert_element_type.24), channel_id=1, source_target_pairs={{0,24},{8,16},{16,8},{24,0},{1,25},{9,17},{17,9},{25,1},{2,26},{10... | collective-permute-start | bytes 294920 | tf_op jit(solution)/shard_map/ppermute | solution.py:210
  35.0 9.9 %collective-permute-start.13 = (f16[64,768]{1,0:T(8,128)(2,1)S(1)}, f16[64,768]{1,0:T(8,128)(2,1)S(1)}, u32[]{:S(2)}, u32[]{:S(2)}) collective-permute-start(f16[64,768]{1,0:T(8,128)(2,1)S(1)} %convert_element_type.26), channel_id=1, source_target_pairs={{0,16},{8,24},{16,0},{24,8},{1,17},{9,25},{17,1},{25,9},{2,18},{10... | collective-permute-start | bytes 294920 | tf_op jit(solution)/shard_map/ppermute | solution.py:210
  35.6 9.4 %collective-permute-start.15 = (f32[8,128]{1,0:T(8,128)S(1)}, f32[8,128]{1,0:T(8,128)S(1)}, u32[]{:S(2)}, u32[]{:S(2)}) collective-permute-start(f32[8,128]{1,0:T(8,128)S(1)} %get-tuple-element.38), channel_id=1, source_target_pairs={{0,24},{8,16},{16,8},{24,0},{1,25},{9,17},{17,9},{25,1},{2,26},{10... | collective-permute-start | bytes 12296 | tf_op jit(solution)/shard_map/ppermute | solution.py:210
  38.5 6.6 %collective-permute-start.16 = (f32[8,128]{1,0:T(8,128)S(1)}, f32[8,128]{1,0:T(8,128)S(1)}, u32[]{:S(2)}, u32[]{:S(2)}) collective-permute-start(f32[8,128]{1,0:T(8,128)S(1)} %get-tuple-element.39), channel_id=1, source_target_pairs={{0,16},{8,24},{16,0},{24,8},{1,17},{9,25},{17,1},{25,9},{2,18},{10... | collective-permute-start | bytes 12296 | tf_op jit(solution)/shard_map/ppermute | solution.py:210

commit v14 on v10

--- a/solution.py
+++ b/solution.py
@@ -66,7 +66,11 @@
     rows_copy.start()
     ids_copy.wait()
     chosen = placement(own_ref[0], ids_ref[...], groups).astype(jnp.bfloat16)
-    chosen_ref[...] = chosen
+    size = chosen.shape[0] // groups
+    for k in range(groups):
+        chosen_ref[(groups - 1 - k) * size : (groups - k) * size, :] = chosen[
+            k * size : (k + 1) * size, :
+        ]
     rows_copy.wait()
     ordered = jnp.dot(chosen, rows_ref[...], preferred_element_type=jnp.float32)
     ordered = ordered.astype(jnp.bfloat16)
@@ -152,36 +156,6 @@
             aside_ref[...] = jnp.zeros(aside_ref.shape, jnp.float32)
         for line, column in enumerate(aside):
             aside_ref[top + line : top + line + 1, :size] = as_row(column[rows, :])
-
-
-def restore_kernel(half, chosen_ref, *refs):
-    refs, (total_ref, dens_ref) = refs[:-2], refs[-2:]
-    groups = len(refs) - half
-    part_refs = refs[groups - 1 :: -1] + refs[: groups - 1 : -1]
-    size = part_refs[half].shape[0]
-    chosen = chosen_ref[...]
-    sums, dens = [], []
-    for k in range(groups):
-        aside_ref, top = (part_refs[k], size) if k < half else (part_refs[half + k], 0)
-        power, dens_power, *pieces = [
-            as_column(aside_ref[top + line : top + line + 1, :size])
-            for line in range(5)
-        ]
-        sums.append(part_refs[k][:size, :] * jnp.exp2(power - TOP))
-        part = sum(piece * 2.0 ** (-8 * j) for j, piece in enumerate(pieces))
-        dens.append(part * jnp.exp2(dens_power))
-    dens_ref[...] = jnp.sum(
-        chosen.astype(jnp.float32) * jnp.concatenate(dens, axis=0), axis=0, keepdims=True
-    )
-    rest = jnp.concatenate(sums, axis=0)
-    back = jnp.zeros(rest.shape, jnp.float32)
-    for _ in range(2):
-        piece = rest.astype(jnp.bfloat16)
-        rest = rest - piece.astype(jnp.float32)
-        back += lax.dot_general(
-            chosen, piece, (((0,), (0,)), ((), ())), preferred_element_type=jnp.float32
-        )
-    total_ref[...] = back
 
 
 def on_device(n_gr, n_gc, embeddings, cluster_ids):
@@ -270,20 +244,28 @@
 
     sent = [part.astype(jnp.float16) for part in sums[:n_gr]]
     back = [sent[0]] + [along_gr(sent[k], k) for k in range(1, n_gr)]
-    back = [part.astype(jnp.float32) for part in back]
-    back += [along_gr(sums[half + k], k) for k in range(half, n_gr)]
-    neighbour_sum, density = pl.pallas_call(
-        functools.partial(restore_kernel, half),
-        out_shape=[
-            jax.ShapeDtypeStruct((count, width), jnp.float32),
-            jax.ShapeDtypeStruct((1, count), jnp.float32),
-        ],
-        in_specs=[VMEM] * (1 + len(back)),
-        out_specs=[VMEM, VMEM],
-        compiler_params=GRANT,
-        name="restore_rows",
-    )(chosen, *back[n_gr - 1 :: -1], *back[:n_gr - 1 : -1])
-    return (neighbour_sum, density.reshape(count))
+    asides = [along_gr(sums[half + k], k) for k in range(half, n_gr)]
+    far, asides = lax.optimization_barrier((back[half:][::-1], asides[::-1]))
+    back, asides = back[:half] + far[::-1], asides[::-1]
+    wide = [part[:size].astype(jnp.float32) for part in back[::-1]]
+    high = [lax.reduce_precision(part, 8, 7) for part in wide]
+    low = [(part - top).astype(jnp.bfloat16) for part, top in zip(wide, high)]
+    high = [part.astype(jnp.bfloat16) for part in high]
+    beside = [part[size:, :size].astype(jnp.float32) for part in back[:half]]
+    beside += [part[:, :size] for part in asides]
+    beside = jnp.concatenate(beside[::-1], axis=1)
+    scale = jnp.exp2(beside[0] - TOP).astype(jnp.bfloat16)
+    part = beside[2] + beside[3] * 2.0**-8 + beside[4] * 2.0**-16
+    dens = part * jnp.exp2(beside[1])
+    density = jnp.sum(chosen.astype(jnp.float32) * dens[:, None], axis=0)
+    scaled = chosen * scale[:, None]
+    neighbour_sum = lax.dot_general(
+        jnp.concatenate([scaled, scaled], axis=0),
+        jnp.concatenate(high + low, axis=0),
+        (((0,), (0,)), ((), ())),
+        preferred_element_type=jnp.float32,
+    )
+    return (neighbour_sum, density)
 
 
 def solution(mesh):

time: 45 us -> 46.7 us (1.038)
  Pallas kernels: 5.55 us -> 4.1 us
  matrix products: 0 us -> 1.27 us
  other arithmetic: 0.13 us -> 1.22 us
  starting transfers between devices: 20.4 us -> 21.2 us
    ppermute x4, waiting for transfers between devices: 2.87 us -> 6.47 us  [to_side(): return lax.ppermute(block, 'gc', pairs)]
    ppermute x4, waiting for transfers between devices: 5.28 us -> 2.04 us  [along_gc(): return lax.ppermute(block, 'gc', [(i, i ^ bits) for i in range(n_gc)])]
    pallas_call x1 -> x0, Pallas kernels: 1.44 us -> none  [on_device(): pl.pallas_call(functools.partial(restore_kernel, half), out_shape=[jax.Sh...]
    dot_general x0 -> x1, matrix products: none -> 1.27 us  [on_device(): lax.dot_general(jnp.concatenate([scaled, scaled], axis=0), jnp.concatenat...]
    ppermute x8, starting transfers between devices: 13.1 us -> 13.9 us  [along_gr(): return lax.ppermute(part, 'gr', [(i, i ^ bits) for i in range(n_gr)])]
    reduce_sum x0 -> x1, other arithmetic: none -> 0.68 us  [on_device(): density = jnp.sum(chosen.astype(jnp.float32) * dens[:, None], axis=0)]
  transfers between devices with their start and end apart: 16 -> 16, of which waited for: 7 -> 11; matrix products, arithmetic and copies ran while one was open for 1% -> 1% of each run, Pallas kernels for 4% -> 4%
where the time goes in v14:
time: 46.7 us; the launch traced here: 46.5 us
  starting transfers between devices  21.2 us (45%)
  waiting for transfers between devices  17.7 us (38%)
  Pallas kernels  4.1 us (9%)
  matrix products  1.27 us (3%)
  other arithmetic  1.22 us (3%)
  between operations  0.86 us (2%)
    ppermute x8, starting transfers between devices, along_gr(): return lax.ppermute(part, 'gr', [(i, i ^ bits) for i in range(n_gr)])  13.9 us
    ppermute x8, waiting for transfers between devices, along_gr(): return lax.ppermute(part, 'gr', [(i, i ^ bits) for i in range(n_gr)])  9.19 us
    ppermute x4, waiting for transfers between devices, to_side(): return lax.ppermute(block, 'gc', pairs)  6.47 us
    ppermute x4, starting transfers between devices, along_gc(): return lax.ppermute(block, 'gc', [(i, i ^ bits) for i in range(n_gc)])  5.41 us
    ppermute x4, waiting for transfers between devices, along_gc(): return lax.ppermute(block, 'gc', [(i, i ^ bits) for i in range(n_gc)])  2.04 us
    pallas_call x1, Pallas kernels, on_device(): pl.pallas_call(early_kernel, out_shape=[jax.ShapeDtypeStruct((count, LANE...  1.95 us
    ppermute x4, starting transfers between devices, to_side(): return lax.ppermute(block, 'gc', pairs)  1.9 us
    pallas_call x1, Pallas kernels, on_device(): pl.pallas_call(sort_kernel, out_shape=[jax.ShapeDtypeStruct((count, count...  1.3 us
  transfers between devices with their start and end apart: 16, of which 11 were waited for; matrix products, arithmetic and copies ran while one was open for 1% of the time, Pallas kernels for 4%

profile of v14, /device:TPU:0, one launch (start us, length us, event | category | flops | bytes accessed | tf_op | source)
XLA Modules:
  0.0 46.5 jit_solution(1563825231759570004)
XLA Ops:
  0.6 1.3 %sort_rows.1 = (bf16[256,256]{1,0:T(8,128)(2,1)S(1)}, bf16[64,768]{1,0:T(8,128)(2,1)S(1)}, bf16[64,768]{1,0:T(8,128)(2,1)S(1)}, bf16[64,768]{1,0:T(8,128)(2,1)S(1)}, bf16[64,768]{1,0:T(8,128)(2,1)S(1)}) custom-call(s32[1]{0:T(128)} %bitcast.own_ref, s32[1,256]{1,0:T(1,128)} %bitcast.11, bf16[256,768]{1,0:T(8,128)(2,1)} %rows_hbm.1), custom_call_target="tpu_custom_call" | custom-call | tf_op jit(solution)/shard_map/sort_rows/pallas_call | solution.py:167
  1.9 3.1 %collective-permute-start = (bf16[64,768]{1,0:T(8,128)(2,1)S(1)}, bf16[64,768]{1,0:T(8,128)(2,1)S(1)}, u32[]{:S(2)}, u32[]{:S(2)}) collective-permute-start(bf16[64,768]{1,0:T(8,128)(2,1)S(1)} %get-tuple-element.24), channel_id=1, source_target_pairs={{0,8},{8,0},{16,24},{24,16},{1,9},{9,1},{17,25},{25,17},{2,10},{10... | collective-permute-start | bytes 294920 | tf_op jit(solution)/shard_map/ppermute | solution.py:184
  5.0 2.6 %collective-permute-start.4 = (bf16[64,768]{1,0:T(8,128)(2,1)S(1)}, bf16[64,768]{1,0:T(8,128)(2,1)S(1)}, u32[]{:S(2)}, u32[]{:S(2)}) collective-permute-start(bf16[64,768]{1,0:T(8,128)(2,1)S(1)} %get-tuple-element.25), channel_id=1, source_target_pairs={{0,16},{8,24},{16,0},{24,8},{1,17},{9,25},{17,1},{25,9},{2,18},{10... | collective-permute-start | bytes 294920 | tf_op jit(solution)/shard_map/ppermute | solution.py:184
  7.6 0.2 collective-permute-done
  7.8 2.8 %collective-permute-start.1 = (bf16[128,768]{1,0:T(8,128)(2,1)S(1)}, bf16[128,768]{1,0:T(8,128)(2,1)S(1)}, u32[]{:S(2)}, u32[]{:S(2)}) collective-permute-start(bf16[128,768]{1,0:T(8,128)(2,1)S(1)} %get-tuple-element.46), channel_id=1, source_target_pairs={{0,6},{1,7},{2,4},{3,5},{4,2},{5,3},{6,0},{7,1},{8,14},{9,15},{10,... | collective-permute-start | bytes 589832 | tf_op jit(solution)/shard_map/ppermute | solution.py:187
  10.6 0.5 %collective-permute-start.2 = (bf16[128,768]{1,0:T(8,128)(2,1)S(1)}, bf16[128,768]{1,0:T(8,128)(2,1)S(1)}, u32[]{:S(2)}, u32[]{:S(2)}) collective-permute-start(bf16[128,768]{1,0:T(8,128)(2,1)S(1)} %get-tuple-element.46), channel_id=1, source_target_pairs={{0,2},{1,5},{2,0},{3,7},{4,6},{5,1},{6,4},{7,3},{8,10},{9,13},{10,... | collective-permute-start | bytes 589832 | tf_op jit(solution)/shard_map/ppermute | solution.py:207
  11.1 0.3 collective-permute-start.3
  11.4 4.1 %collective-permute-done.4 = bf16[64,768]{1,0:T(8,128)(2,1)S(1)} collective-permute-done((bf16[64,768]{1,0:T(8,128)(2,1)S(1)}, bf16[64,768]{1,0:T(8,128)(2,1)S(1)}, u32[]{:S(2)}, u32[]{:S(2)}) %collective-permute-start.4) | collective-permute-done | bytes 98336 | tf_op jit(solution)/shard_map/ppermute | solution.py:184
  15.5 2.5 %collective-permute-start.7 = (bf16[128,768]{1,0:T(8,128)(2,1)S(1)}, bf16[128,768]{1,0:T(8,128)(2,1)S(1)}, u32[]{:S(2)}, u32[]{:S(2)}) collective-permute-start(bf16[128,768]{1,0:T(8,128)(2,1)S(1)} %get-tuple-element.42), channel_id=1, source_target_pairs={{0,6},{1,7},{2,4},{3,5},{4,2},{5,3},{6,0},{7,1},{8,14},{9,15},{10,... | collective-permute-start | bytes 589832 | tf_op jit(solution)/shard_map/ppermute | solution.py:187
  18.0 0.5 %collective-permute-start.8 = (bf16[128,768]{1,0:T(8,128)(2,1)S(1)}, bf16[128,768]{1,0:T(8,128)(2,1)S(1)}, u32[]{:S(2)}, u32[]{:S(2)}) collective-permute-start(bf16[128,768]{1,0:T(8,128)(2,1)S(1)} %get-tuple-element.42), channel_id=1, source_target_pairs={{0,2},{1,5},{2,0},{3,7},{4,6},{5,1},{6,4},{7,3},{8,10},{9,13},{10,... | collective-permute-start | bytes 589832 | tf_op jit(solution)/shard_map/ppermute | solution.py:207
  18.6 0.6 %collective-permute-start.9 = (bf16[128,768]{1,0:T(8,128)(2,1)S(1)}, bf16[128,768]{1,0:T(8,128)(2,1)S(1)}, u32[]{:S(2)}, u32[]{:S(2)}) collective-permute-start(bf16[128,768]{1,0:T(8,128)(2,1)S(1)} %get-tuple-element.42), channel_id=1, source_target_pairs={{0,4},{1,3},{2,6},{3,1},{4,0},{5,7},{6,2},{7,5},{8,12},{9,11},{10,... | collective-permute-start | bytes 589832 | tf_op jit(solution)/shard_map/ppermute | solution.py:207
  19.2 1.8 %collective-permute-done.2 = bf16[128,768]{1,0:T(8,128)(2,1)S(1)} collective-permute-done((bf16[128,768]{1,0:T(8,128)(2,1)S(1)}, bf16[128,768]{1,0:T(8,128)(2,1)S(1)}, u32[]{:S(2)}, u32[]{:S(2)}) %collective-permute-start.2) | collective-permute-done | bytes 196640 | tf_op jit(solution)/shard_map/ppermute | solution.py:207
  21.0 2.3 %collective-permute-done.3 = bf16[128,768]{1,0:T(8,128)(2,1)S(1)} collective-permute-done((bf16[128,768]{1,0:T(8,128)(2,1)S(1)}, bf16[128,768]{1,0:T(8,128)(2,1)S(1)}, u32[]{:S(2)}, u32[]{:S(2)}) %collective-permute-start.3) | collective-permute-done | bytes 196640 | tf_op jit(solution)/shard_map/ppermute | solution.py:207
  23.3 0.1 collective-permute-start.6
  23.3 1.7 %collective-permute-done.7 = bf16[128,768]{1,0:T(8,128)(2,1)S(1)} collective-permute-done((bf16[128,768]{1,0:T(8,128)(2,1)S(1)}, bf16[128,768]{1,0:T(8,128)(2,1)S(1)}, u32[]{:S(2)}, u32[]{:S(2)}) %collective-permute-start.7) | collective-permute-done | bytes 196640 | tf_op jit(solution)/shard_map/ppermute | solution.py:187
  25.1 2.4 %collective-permute-done.8 = bf16[128,768]{1,0:T(8,128)(2,1)S(1)} collective-permute-done((bf16[128,768]{1,0:T(8,128)(2,1)S(1)}, bf16[128,768]{1,0:T(8,128)(2,1)S(1)}, u32[]{:S(2)}, u32[]{:S(2)}) %collective-permute-start.8) | collective-permute-done | bytes 196640 | tf_op jit(solution)/shard_map/ppermute | solution.py:207
  27.6 1.9 %early_sums.1 = (f32[256,128]{1,0:T(8,128)S(1)}, f32[256,768]{1,0:T(8,128)S(1)}, f32[256,128]{1,0:T(8,128)S(1)}) custom-call(bf16[256,768]{1,0:T(8,128)(2,1)S(1)} %pad_maximum_fusion.rows_ref, bf16[512,768]{1,0:T(8,128)(2,1)S(1)} %constant_dynamic-update-slice_fusion.2.refs_0_, bf16[512,768]{1,0:T(8,128)(2,1)S(1)} %collective-permute-done.6.refs_1_, ...), custom_call_target="tpu_custom_call" | custom-call | flops 1207959552 | tf_op jit(solution)/shard_map/early_sums/pallas_call | solution.py:219
  29.6 0.3 collective-permute-done.10.cols_ref
  29.9 0.9 %last_sums.1 = (f32[72,768]{1,0:T(8,128)S(1)}, f32[72,768]{1,0:T(8,128)S(1)}, f32[64,768]{1,0:T(8,128)S(1)}, f32[64,768]{1,0:T(8,128)S(1)}, f32[8,128]{1,0:T(8,128)S(1)}, /*index=5*/f32[8,128]{1,0:T(8,128)S(1)}) custom-call(bf16[256,768]{1,0:T(8,128)(2,1)S(1)} %pad_maximum_fusion.rows_ref, f32[256,128]{1,0:T(8,128)S(1)} %get-tuple-element.29.scale_ref, ...), custom_call_target="tpu_custom_call" | custom-call | flops 402653184 | tf_op jit(solution)/shard_map/last_sums/pallas_call | solution.py:233
  30.8 3.6 %collective-permute-start.11 = (f16[64,768]{1,0:T(8,128)(2,1)S(1)}, f16[64,768]{1,0:T(8,128)(2,1)S(1)}, u32[]{:S(2)}, u32[]{:S(2)}) collective-permute-start(f16[64,768]{1,0:T(8,128)(2,1)S(1)} %convert_element_type.67), channel_id=1, source_target_pairs={{0,24},{8,16},{16,8},{24,0},{1,25},{9,17},{17,9},{25,1},{2,26},{10... | collective-permute-start | bytes 294920 | tf_op jit(solution)/shard_map/ppermute | solution.py:184
  34.5 0.1 collective-permute-start.12
  34.5 1.8 %collective-permute-start.13 = (f32[8,128]{1,0:T(8,128)S(1)}, f32[8,128]{1,0:T(8,128)S(1)}, u32[]{:S(2)}, u32[]{:S(2)}) collective-permute-start(f32[8,128]{1,0:T(8,128)S(1)} %get-tuple-element.34), channel_id=1, source_target_pairs={{0,24},{8,16},{16,8},{24,0},{1,25},{9,17},{17,9},{25,1},{2,26},{10... | collective-permute-start | bytes 12296 | tf_op jit(solution)/shard_map/ppermute | solution.py:184
  36.3 1.1 %collective-permute-start.14 = (f32[8,128]{1,0:T(8,128)S(1)}, f32[8,128]{1,0:T(8,128)S(1)}, u32[]{:S(2)}, u32[]{:S(2)}) collective-permute-start(f32[8,128]{1,0:T(8,128)S(1)} %get-tuple-element.35), channel_id=1, source_target_pairs={{0,16},{8,24},{16,0},{24,8},{1,17},{9,25},{17,1},{25,9},{2,18},{10... | collective-permute-start | bytes 12296 | tf_op jit(solution)/shard_map/ppermute | solution.py:184
  37.5 1.6 %collective-permute-start.15 = (f16[72,768]{1,0:T(8,128)(2,1)S(1)}, f16[72,768]{1,0:T(8,128)(2,1)S(1)}, u32[]{:S(2)}, u32[]{:S(2)}) collective-permute-start(f16[72,768]{1,0:T(8,128)(2,1)S(1)} %convert_element_type.69), channel_id=1, source_target_pairs={{0,8},{8,0},{16,24},{24,16},{1,9},{9,1},{17,25},{25,17},{2,10},{10... | collective-permute-start | bytes 331784 | tf_op jit(solution)/shard_map/ppermute | solution.py:184
  39.1 1.0 %collective-permute-done.13 = f32[8,128]{1,0:T(8,128)S(1)} collective-permute-done((f32[8,128]{1,0:T(8,128)S(1)}, f32[8,128]{1,0:T(8,128)S(1)}, u32[]{:S(2)}, u32[]{:S(2)}) %collective-permute-start.13) | collective-permute-done | bytes 4128 | tf_op jit(solution)/shard_map/ppermute | solution.py:184
  40.1 3.2 %collective-permute-done.14 = f32[8,128]{1,0:T(8,128)S(1)} collective-permute-done((f32[8,128]{1,0:T(8,128)S(1)}, f32[8,128]{1,0:T(8,128)S(1)}, u32[]{:S(2)}, u32[]{:S(2)}) %collective-permute-start.14) | collective-permute-done | bytes 4128 | tf_op jit(solution)/shard_map/ppermute | solution.py:184
  43.3 0.8 %collective-permute-done.15 = f16[72,768]{1,0:T(8,128)(2,1)S(1)} collective-permute-done((f16[72,768]{1,0:T(8,128)(2,1)S(1)}, f16[72,768]{1,0:T(8,128)(2,1)S(1)}, u32[]{:S(2)}, u32[]{:S(2)}) %collective-permute-start.15) | collective-permute-done | bytes 110624 | tf_op jit(solution)/shard_map/ppermute | solution.py:184
  44.1 0.1 fusion.18
  44.2 0.1 convert_reduce_fusion
  44.3 0.7 %multiply_reduce_fusion = f32[256]{0:T(256)} fusion(bf16[256,256]{1,0:T(8,128)(2,1)S(1)} %get-tuple-element.22, f32[256]{0:T(256)S(1)} %bitcast.10), kind=kLoop, calls=%fused_computation.13 | loop fusion | flops 196352 | bytes 133120 | tf_op jit(solution)/shard_map/reduce_sum | solution.py:260
  45.0 0.1 broadcast_multiply_fusion
  45.3 1.3 %fusion = f32[256,768]{1,0:T(8,128)} fusion(bf16[512,768]{1,0:T(8,128)(2,1)S(1)} %fusion.8, bf16[256,256]{1,0:T(8,128)(2,1)S(1)} %broadcast_multiply_fusion), kind=kOutput, calls=%fused_computation.9 | convolution fusion | flops 201850880 | bytes 1703936 | tf_op jit(solution)/shard_map/dot_general | solution.py:262
  (33 shorter events, 0.5 us)
Async XLA Ops:
  1.9 5.9 %collective-permute-start = (bf16[64,768]{1,0:T(8,128)(2,1)S(1)}, bf16[64,768]{1,0:T(8,128)(2,1)S(1)}, u32[]{:S(2)}, u32[]{:S(2)}) collective-permute-start(bf16[64,768]{1,0:T(8,128)(2,1)S(1)} %get-tuple-element.24), channel_id=1, source_target_pairs={{0,8},{8,0},{16,24},{24,16},{1,9},{9,1},{17,25},{25,17},{2,10},{10... | collective-permute-start | bytes 294920 | tf_op jit(solution)/shard_map/ppermute | solution.py:184
  5.0 10.4 %collective-permute-start.4 = (bf16[64,768]{1,0:T(8,128)(2,1)S(1)}, bf16[64,768]{1,0:T(8,128)(2,1)S(1)}, u32[]{:S(2)}, u32[]{:S(2)}) collective-permute-start(bf16[64,768]{1,0:T(8,128)(2,1)S(1)} %get-tuple-element.25), channel_id=1, source_target_pairs={{0,16},{8,24},{16,0},{24,8},{1,17},{9,25},{17,1},{25,9},{2,18},{10... | collective-permute-start | bytes 294920 | tf_op jit(solution)/shard_map/ppermute | solution.py:184
  7.6 7.9 %collective-permute-start.5 = (bf16[64,768]{1,0:T(8,128)(2,1)S(1)}, bf16[64,768]{1,0:T(8,128)(2,1)S(1)}, u32[]{:S(2)}, u32[]{:S(2)}) collective-permute-start(bf16[64,768]{1,0:T(8,128)(2,1)S(1)} %get-tuple-element.26), channel_id=1, source_target_pairs={{0,24},{8,16},{16,8},{24,0},{1,25},{9,17},{17,9},{25,1},{2,26},{10... | collective-permute-start | bytes 294920 | tf_op jit(solution)/shard_map/ppermute | solution.py:184
  7.8 10.7 %collective-permute-start.1 = (bf16[128,768]{1,0:T(8,128)(2,1)S(1)}, bf16[128,768]{1,0:T(8,128)(2,1)S(1)}, u32[]{:S(2)}, u32[]{:S(2)}) collective-permute-start(bf16[128,768]{1,0:T(8,128)(2,1)S(1)} %get-tuple-element.46), channel_id=1, source_target_pairs={{0,6},{1,7},{2,4},{3,5},{4,2},{5,3},{6,0},{7,1},{8,14},{9,15},{10,... | collective-permute-start | bytes 589832 | tf_op jit(solution)/shard_map/ppermute | solution.py:187
  10.6 10.3 %collective-permute-start.2 = (bf16[128,768]{1,0:T(8,128)(2,1)S(1)}, bf16[128,768]{1,0:T(8,128)(2,1)S(1)}, u32[]{:S(2)}, u32[]{:S(2)}) collective-permute-start(bf16[128,768]{1,0:T(8,128)(2,1)S(1)} %get-tuple-element.46), channel_id=1, source_target_pairs={{0,2},{1,5},{2,0},{3,7},{4,6},{5,1},{6,4},{7,3},{8,10},{9,13},{10,... | collective-permute-start | bytes 589832 | tf_op jit(solution)/shard_map/ppermute | solution.py:207
  11.1 12.1 %collective-permute-start.3 = (bf16[128,768]{1,0:T(8,128)(2,1)S(1)}, bf16[128,768]{1,0:T(8,128)(2,1)S(1)}, u32[]{:S(2)}, u32[]{:S(2)}) collective-permute-start(bf16[128,768]{1,0:T(8,128)(2,1)S(1)} %get-tuple-element.46), channel_id=1, source_target_pairs={{0,4},{1,3},{2,6},{3,1},{4,0},{5,7},{6,2},{7,5},{8,12},{9,11},{10,... | collective-permute-start | bytes 589832 | tf_op jit(solution)/shard_map/ppermute | solution.py:207
  15.5 9.6 %collective-permute-start.7 = (bf16[128,768]{1,0:T(8,128)(2,1)S(1)}, bf16[128,768]{1,0:T(8,128)(2,1)S(1)}, u32[]{:S(2)}, u32[]{:S(2)}) collective-permute-start(bf16[128,768]{1,0:T(8,128)(2,1)S(1)} %get-tuple-element.42), channel_id=1, source_target_pairs={{0,6},{1,7},{2,4},{3,5},{4,2},{5,3},{6,0},{7,1},{8,14},{9,15},{10,... | collective-permute-start | bytes 589832 | tf_op jit(solution)/shard_map/ppermute | solution.py:187
  18.0 9.4 %collective-permute-start.8 = (bf16[128,768]{1,0:T(8,128)(2,1)S(1)}, bf16[128,768]{1,0:T(8,128)(2,1)S(1)}, u32[]{:S(2)}, u32[]{:S(2)}) collective-permute-start(bf16[128,768]{1,0:T(8,128)(2,1)S(1)} %get-tuple-element.42), channel_id=1, source_target_pairs={{0,2},{1,5},{2,0},{3,7},{4,6},{5,1},{6,4},{7,3},{8,10},{9,13},{10,... | collective-permute-start | bytes 589832 | tf_op jit(solution)/shard_map/ppermute | solution.py:207
  18.6 8.9 %collective-permute-start.9 = (bf16[128,768]{1,0:T(8,128)(2,1)S(1)}, bf16[128,768]{1,0:T(8,128)(2,1)S(1)}, u32[]{:S(2)}, u32[]{:S(2)}) collective-permute-start(bf16[128,768]{1,0:T(8,128)(2,1)S(1)} %get-tuple-element.42), channel_id=1, source_target_pairs={{0,4},{1,3},{2,6},{3,1},{4,0},{5,7},{6,2},{7,5},{8,12},{9,11},{10,... | collective-permute-start | bytes 589832 | tf_op jit(solution)/shard_map/ppermute | solution.py:207
  23.3 4.4 %collective-permute-start.6 = (bf16[512,768]{1,0:T(8,128)(2,1)S(1)}, bf16[512,768]{1,0:T(8,128)(2,1)S(1)}, u32[]{:S(2)}, u32[]{:S(2)}) collective-permute-start(bf16[512,768]{1,0:T(8,128)(2,1)S(1)} %constant_dynamic-update-slice_fusion.2.refs_0_), channel_id=1, source_target_pairs={{0,1},{1,0},{2,3},{3,2},{4,5},{5,4},{6,7},{7,6},{8,9},{9,8},{10,11... | collective-permute-start | bytes 2359304 | tf_op jit(solution)/shard_map/ppermute | solution.py:187
  27.6 2.4 %collective-permute-start.10 = (bf16[512,768]{1,0:T(8,128)(2,1)S(1)}, bf16[512,768]{1,0:T(8,128)(2,1)S(1)}, u32[]{:S(2)}, u32[]{:S(2)}) collective-permute-start(bf16[512,768]{1,0:T(8,128)(2,1)S(1)} %constant_dynamic-update-slice_fusion.9.refs_2_), channel_id=1, source_target_pairs={{0,1},{1,0},{2,3},{3,2},{4,5},{5,4},{6,7},{7,6},{8,9},{9,8},{10,11... | collective-permute-start | bytes 2359304 | tf_op jit(solution)/shard_map/ppermute | solution.py:187
  30.8 12.5 %collective-permute-start.11 = (f16[64,768]{1,0:T(8,128)(2,1)S(1)}, f16[64,768]{1,0:T(8,128)(2,1)S(1)}, u32[]{:S(2)}, u32[]{:S(2)}) collective-permute-start(f16[64,768]{1,0:T(8,128)(2,1)S(1)} %convert_element_type.67), channel_id=1, source_target_pairs={{0,24},{8,16},{16,8},{24,0},{1,25},{9,17},{17,9},{25,1},{2,26},{10... | collective-permute-start | bytes 294920 | tf_op jit(solution)/shard_map/ppermute | solution.py:184
  34.5 8.8 %collective-permute-start.12 = (f16[64,768]{1,0:T(8,128)(2,1)S(1)}, f16[64,768]{1,0:T(8,128)(2,1)S(1)}, u32[]{:S(2)}, u32[]{:S(2)}) collective-permute-start(f16[64,768]{1,0:T(8,128)(2,1)S(1)} %convert_element_type.68), channel_id=1, source_target_pairs={{0,16},{8,24},{16,0},{24,8},{1,17},{9,25},{17,1},{25,9},{2,18},{10... | collective-permute-start | bytes 294920 | tf_op jit(solution)/shard_map/ppermute | solution.py:184
  34.5 5.6 %collective-permute-start.13 = (f32[8,128]{1,0:T(8,128)S(1)}, f32[8,128]{1,0:T(8,128)S(1)}, u32[]{:S(2)}, u32[]{:S(2)}) collective-permute-start(f32[8,128]{1,0:T(8,128)S(1)} %get-tuple-element.34), channel_id=1, source_target_pairs={{0,24},{8,16},{16,8},{24,0},{1,25},{9,17},{17,9},{25,1},{2,26},{10... | collective-permute-start | bytes 12296 | tf_op jit(solution)/shard_map/ppermute | solution.py:184
  36.3 6.9 %collective-permute-start.14 = (f32[8,128]{1,0:T(8,128)S(1)}, f32[8,128]{1,0:T(8,128)S(1)}, u32[]{:S(2)}, u32[]{:S(2)}) collective-permute-start(f32[8,128]{1,0:T(8,128)S(1)} %get-tuple-element.35), channel_id=1, source_target_pairs={{0,16},{8,24},{16,0},{24,8},{1,17},{9,25},{17,1},{25,9},{2,18},{10... | collective-permute-start | bytes 12296 | tf_op jit(solution)/shard_map/ppermute | solution.py:184
  37.5 6.6 %collective-permute-start.15 = (f16[72,768]{1,0:T(8,128)(2,1)S(1)}, f16[72,768]{1,0:T(8,128)(2,1)S(1)}, u32[]{:S(2)}, u32[]{:S(2)}) collective-permute-start(f16[72,768]{1,0:T(8,128)(2,1)S(1)} %convert_element_type.69), channel_id=1, source_target_pairs={{0,8},{8,0},{16,24},{24,16},{1,9},{9,1},{17,25},{25,17},{2,10},{10... | collective-permute-start | bytes 331784 | tf_op jit(solution)/shard_map/ppermute | solution.py:184

commit v15 on v10

--- a/solution.py
+++ b/solution.py
@@ -125,11 +125,16 @@
     return jnp.floor(jnp.log2(jnp.maximum(value, 1e-30)))
 
 
-def last_kernel(half, rows_ref, scale_ref, total_ref, dens_ref, cols_ref, *out_refs):
-    groups = len(out_refs) - half
-    size = out_refs[half].shape[0]
+def last_kernel(first, padded, rows_ref, scale_ref, total_ref, dens_ref, cols_ref, *out_refs):
+    groups = len(out_refs) if padded else len(out_refs) // 2
+    size = out_refs[0].shape[0] - (EXTRA if padded else 0)
+    mine = slice(first, first + groups * size)
     total, dens = add_columns(
-        rows_ref[...], scale_ref[:, 0:1], [cols_ref], total_ref[...], dens_ref[...]
+        rows_ref[mine, :],
+        scale_ref[mine, 0:1],
+        [cols_ref],
+        total_ref[mine, :],
+        dens_ref[mine, :],
     )
     dens = jnp.sum(dens, axis=1, keepdims=True) * floor_weight
     power = exponent(jnp.max(jnp.abs(total), axis=1, keepdims=True))
@@ -144,12 +149,11 @@
     for k in range(groups):
         rows = slice(k * size, (k + 1) * size)
         out_refs[k][:size, :] = total[rows, :]
-        if k < half:
+        if padded:
             aside_ref, top = out_refs[k], size
-            aside_ref[size:, :] = jnp.zeros((EXTRA, total.shape[1]), jnp.float32)
         else:
-            aside_ref, top = out_refs[half + k], 0
-            aside_ref[...] = jnp.zeros(aside_ref.shape, jnp.float32)
+            aside_ref, top = out_refs[groups + k], 0
+        aside_ref[top:, :] = jnp.zeros((EXTRA, aside_ref.shape[1]), jnp.float32)
         for line, column in enumerate(aside):
             aside_ref[top + line : top + line + 1, :size] = as_row(column[rows, :])
 
@@ -256,17 +260,22 @@
         name="early_sums",
     )(rows, *early)
     late = other_core(chunks[1])
-    sums = pl.pallas_call(
-        functools.partial(last_kernel, half),
-        out_shape=[jax.ShapeDtypeStruct((size + EXTRA, width), jnp.float32)] * half
-        + [jax.ShapeDtypeStruct((size, width), jnp.float32)] * (n_gr - half)
-        + [jax.ShapeDtypeStruct((EXTRA, LANES), jnp.float32)] * (n_gr - half),
-        in_specs=[VMEM] * 5,
-        out_specs=[VMEM] * (2 * n_gr - half),
-        compiler_params=GRANT,
-        cost_estimate=cost(late),
-        name="last_sums",
-    )(rows, scale, total, dens, late)
+    def last_sums(first, padded, out_shape, name):
+        return pl.pallas_call(
+            functools.partial(last_kernel, first, padded),
+            out_shape=out_shape,
+            in_specs=[VMEM] * 5,
+            out_specs=[VMEM] * len(out_shape),
+            compiler_params=GRANT,
+            cost_estimate=cost(late),
+            name=name,
+        )(rows, scale, total, dens, late)
+
+    beside = jax.ShapeDtypeStruct((EXTRA, LANES), jnp.float32)
+    piece = jax.ShapeDtypeStruct((size, width), jnp.float32)
+    longer = jax.ShapeDtypeStruct((size + EXTRA, width), jnp.float32)
+    far = last_sums(half * size, False, [piece] * (n_gr - half) + [beside] * (n_gr - half), "far_sums")
+    sums = [*last_sums(0, True, [longer] * half, "near_sums"), *far]
 
     sent = [part.astype(jnp.float16) for part in sums[:n_gr]]
     back = [sent[0]] + [along_gr(sent[k], k) for k in range(1, n_gr)]

time: 45 us -> 45.6 us (1.013)
  Pallas kernels: 5.55 us -> 6.17 us
    pallas_call x1 -> x2, Pallas kernels: 0.87 us -> 1.47 us  [last_sums(): pl.pallas_call(functools.partial(last_kernel, first, padded), out_shape=o...]
  transfers between devices with their start and end apart: 16 -> 16, of which waited for: 7 -> 7; matrix products, arithmetic and copies ran while one was open for 1% -> 1% of each run, Pallas kernels for 4% -> 6%
where the time goes in v15:
time: 45.6 us; the launch traced here: 45.4 us
  starting transfers between devices  20.4 us (45%)
  waiting for transfers between devices  17.8 us (39%)
  Pallas kernels  6.17 us (14%)
  between operations  0.86 us (2%)
    ppermute x8, starting transfers between devices, along_gr(): return lax.ppermute(part, 'gr', [(i, i ^ bits) for i in range(n_gr)])  13.1 us
    ppermute x8, waiting for transfers between devices, along_gr(): return lax.ppermute(part, 'gr', [(i, i ^ bits) for i in range(n_gr)])  9.63 us
    ppermute x4, starting transfers between devices, along_gc(): return lax.ppermute(block, 'gc', [(i, i ^ bits) for i in range(n_gc)])  5.41 us
    ppermute x4, waiting for transfers between devices, along_gc(): return lax.ppermute(block, 'gc', [(i, i ^ bits) for i in range(n_gc)])  5.27 us
    ppermute x4, waiting for transfers between devices, to_side(): return lax.ppermute(block, 'gc', pairs)  2.87 us
    pallas_call x1, Pallas kernels, on_device(): pl.pallas_call(early_kernel, out_shape=[jax.ShapeDtypeStruct((count, LANE...  1.95 us
    ppermute x4, starting transfers between devices, to_side(): return lax.ppermute(block, 'gc', pairs)  1.9 us
    pallas_call x2, Pallas kernels, last_sums(): pl.pallas_call(functools.partial(last_kernel, first, padded), out_shape=o...  1.47 us
  transfers between devices with their start and end apart: 16, of which 7 were waited for; matrix products, arithmetic and copies ran while one was open for 1% of the time, Pallas kernels for 6%

profile of v15, /device:TPU:0, one launch (start us, length us, event | category | flops | bytes accessed | tf_op | source)
XLA Modules:
  0.0 45.4 jit_solution(8143384154137361979)
XLA Ops:
  0.6 1.3 %sort_rows.1 = (bf16[256,256]{1,0:T(8,128)(2,1)S(1)}, bf16[64,768]{1,0:T(8,128)(2,1)S(1)}, bf16[64,768]{1,0:T(8,128)(2,1)S(1)}, bf16[64,768]{1,0:T(8,128)(2,1)S(1)}, bf16[64,768]{1,0:T(8,128)(2,1)S(1)}) custom-call(s32[1]{0:T(128)} %bitcast.own_ref, s32[1,256]{1,0:T(1,128)} %bitcast.3, bf16[256,768]{1,0:T(8,128)(2,1)} %rows_hbm.1), custom_call_target="tpu_custom_call" | custom-call | tf_op jit(solution)/shard_map/sort_rows/pallas_call | solution.py:197
  1.9 3.1 %collective-permute-start = (bf16[64,768]{1,0:T(8,128)(2,1)S(1)}, bf16[64,768]{1,0:T(8,128)(2,1)S(1)}, u32[]{:S(2)}, u32[]{:S(2)}) collective-permute-start(bf16[64,768]{1,0:T(8,128)(2,1)S(1)} %get-tuple-element.22), channel_id=1, source_target_pairs={{0,8},{8,0},{16,24},{24,16},{1,9},{9,1},{17,25},{25,17},{2,10},{10... | collective-permute-start | bytes 294920 | tf_op jit(solution)/shard_map/ppermute | solution.py:214
  5.0 2.5 %collective-permute-start.5 = (bf16[64,768]{1,0:T(8,128)(2,1)S(1)}, bf16[64,768]{1,0:T(8,128)(2,1)S(1)}, u32[]{:S(2)}, u32[]{:S(2)}) collective-permute-start(bf16[64,768]{1,0:T(8,128)(2,1)S(1)} %get-tuple-element.24), channel_id=1, source_target_pairs={{0,24},{8,16},{16,8},{24,0},{1,25},{9,17},{17,9},{25,1},{2,26},{10... | collective-permute-start | bytes 294920 | tf_op jit(solution)/shard_map/ppermute | solution.py:214
  7.5 0.1 collective-permute-start.4
  7.6 0.2 collective-permute-done
  7.8 2.8 %collective-permute-start.1 = (bf16[128,768]{1,0:T(8,128)(2,1)S(1)}, bf16[128,768]{1,0:T(8,128)(2,1)S(1)}, u32[]{:S(2)}, u32[]{:S(2)}) collective-permute-start(bf16[128,768]{1,0:T(8,128)(2,1)S(1)} %get-tuple-element.42), channel_id=1, source_target_pairs={{0,6},{1,7},{2,4},{3,5},{4,2},{5,3},{6,0},{7,1},{8,14},{9,15},{10,... | collective-permute-start | bytes 589832 | tf_op jit(solution)/shard_map/ppermute | solution.py:217
  10.6 0.5 %collective-permute-start.2 = (bf16[128,768]{1,0:T(8,128)(2,1)S(1)}, bf16[128,768]{1,0:T(8,128)(2,1)S(1)}, u32[]{:S(2)}, u32[]{:S(2)}) collective-permute-start(bf16[128,768]{1,0:T(8,128)(2,1)S(1)} %get-tuple-element.42), channel_id=1, source_target_pairs={{0,2},{1,5},{2,0},{3,7},{4,6},{5,1},{6,4},{7,3},{8,10},{9,13},{10,... | collective-permute-start | bytes 589832 | tf_op jit(solution)/shard_map/ppermute | solution.py:237
  11.1 0.3 collective-permute-start.3
  11.4 5.1 %collective-permute-done.4 = bf16[64,768]{1,0:T(8,128)(2,1)S(1)} collective-permute-done((bf16[64,768]{1,0:T(8,128)(2,1)S(1)}, bf16[64,768]{1,0:T(8,128)(2,1)S(1)}, u32[]{:S(2)}, u32[]{:S(2)}) %collective-permute-start.4) | collective-permute-done | bytes 98336 | tf_op jit(solution)/shard_map/ppermute | solution.py:214
  16.5 0.0 collective-permute-done.5
  16.5 2.5 %collective-permute-start.7 = (bf16[128,768]{1,0:T(8,128)(2,1)S(1)}, bf16[128,768]{1,0:T(8,128)(2,1)S(1)}, u32[]{:S(2)}, u32[]{:S(2)}) collective-permute-start(bf16[128,768]{1,0:T(8,128)(2,1)S(1)} %get-tuple-element.38), channel_id=1, source_target_pairs={{0,6},{1,7},{2,4},{3,5},{4,2},{5,3},{6,0},{7,1},{8,14},{9,15},{10,... | collective-permute-start | bytes 589832 | tf_op jit(solution)/shard_map/ppermute | solution.py:217
  19.0 0.5 %collective-permute-start.8 = (bf16[128,768]{1,0:T(8,128)(2,1)S(1)}, bf16[128,768]{1,0:T(8,128)(2,1)S(1)}, u32[]{:S(2)}, u32[]{:S(2)}) collective-permute-start(bf16[128,768]{1,0:T(8,128)(2,1)S(1)} %get-tuple-element.38), channel_id=1, source_target_pairs={{0,2},{1,5},{2,0},{3,7},{4,6},{5,1},{6,4},{7,3},{8,10},{9,13},{10,... | collective-permute-start | bytes 589832 | tf_op jit(solution)/shard_map/ppermute | solution.py:237
  19.6 0.6 %collective-permute-start.9 = (bf16[128,768]{1,0:T(8,128)(2,1)S(1)}, bf16[128,768]{1,0:T(8,128)(2,1)S(1)}, u32[]{:S(2)}, u32[]{:S(2)}) collective-permute-start(bf16[128,768]{1,0:T(8,128)(2,1)S(1)} %get-tuple-element.38), channel_id=1, source_target_pairs={{0,4},{1,3},{2,6},{3,1},{4,0},{5,7},{6,2},{7,5},{8,12},{9,11},{10,... | collective-permute-start | bytes 589832 | tf_op jit(solution)/shard_map/ppermute | solution.py:237
  20.2 0.0 collective-permute-done.3
  20.2 0.1 collective-permute-start.6
  20.3 5.0 %collective-permute-done.7 = bf16[128,768]{1,0:T(8,128)(2,1)S(1)} collective-permute-done((bf16[128,768]{1,0:T(8,128)(2,1)S(1)}, bf16[128,768]{1,0:T(8,128)(2,1)S(1)}, u32[]{:S(2)}, u32[]{:S(2)}) %collective-permute-start.7) | collective-permute-done | bytes 196640 | tf_op jit(solution)/shard_map/ppermute | solution.py:217
  25.3 2.9 %collective-permute-done.8 = bf16[128,768]{1,0:T(8,128)(2,1)S(1)} collective-permute-done((bf16[128,768]{1,0:T(8,128)(2,1)S(1)}, bf16[128,768]{1,0:T(8,128)(2,1)S(1)}, u32[]{:S(2)}, u32[]{:S(2)}) %collective-permute-start.8) | collective-permute-done | bytes 196640 | tf_op jit(solution)/shard_map/ppermute | solution.py:237
  28.2 0.0 collective-permute-done.9
  28.2 0.1 collective-permute-start.10
  28.3 2.0 %early_sums.1 = (f32[256,128]{1,0:T(8,128)S(1)}, f32[256,768]{1,0:T(8,128)S(1)}, f32[256,128]{1,0:T(8,128)S(1)}) custom-call(bf16[256,768]{1,0:T(8,128)(2,1)S(1)} %pad_maximum_fusion.rows_ref, bf16[512,768]{1,0:T(8,128)(2,1)S(1)} %constant_dynamic-update-slice_fusion.2.refs_0_, bf16[512,768]{1,0:T(8,128)(2,1)S(1)} %collective-permute-done.6.refs_1_, ...), custom_call_target="tpu_custom_call" | custom-call | flops 1207959552 | tf_op jit(solution)/shard_map/early_sums/pallas_call | solution.py:249
  30.3 0.3 collective-permute-done.10.cols_ref
  30.6 0.7 %far_sums.1 = (f32[64,768]{1,0:T(8,128)S(1)}, f32[64,768]{1,0:T(8,128)S(1)}, f32[8,128]{1,0:T(8,128)S(1)}, f32[8,128]{1,0:T(8,128)S(1)}) custom-call(bf16[256,768]{1,0:T(8,128)(2,1)S(1)} %pad_maximum_fusion.rows_ref, f32[256,128]{1,0:T(8,128)S(1)} %get-tuple-element.27.scale_ref, f32[256,768]{1,0:T(8,128)S(1)} %get-tuple-element.28.total_ref, ...), custom_call_target="tpu_custom_call" | custom-call | flops 402653184 | tf_op jit(solution)/shard_map/far_sums/pallas_call | solution.py:264
  31.3 2.9 %collective-permute-start.11 = (f16[64,768]{1,0:T(8,128)(2,1)S(1)}, f16[64,768]{1,0:T(8,128)(2,1)S(1)}, u32[]{:S(2)}, u32[]{:S(2)}) collective-permute-start(f16[64,768]{1,0:T(8,128)(2,1)S(1)} %convert_element_type.24), channel_id=1, source_target_pairs={{0,24},{8,16},{16,8},{24,0},{1,25},{9,17},{17,9},{25,1},{2,26},{10... | collective-permute-start | bytes 294920 | tf_op jit(solution)/shard_map/ppermute | solution.py:214
  34.2 0.1 collective-permute-start.12
  34.3 0.7 %near_sums.1 = (f32[72,768]{1,0:T(8,128)S(1)}, f32[72,768]{1,0:T(8,128)S(1)}) custom-call(bf16[256,768]{1,0:T(8,128)(2,1)S(1)} %pad_maximum_fusion.rows_ref, f32[256,128]{1,0:T(8,128)S(1)} %get-tuple-element.27.scale_ref, f32[256,768]{1,0:T(8,128)S(1)} %get-tuple-element.28.total_ref, f32[256,128]{1,0:T(8,128)S(1)} %get-tuple-element.29.dens_ref, ...), custom_call_target="tpu_custom_call" | custom-call | flops 402653184 | tf_op jit(solution)/shard_map/near_sums/pallas_call | solution.py:264
  35.1 1.6 %collective-permute-start.13 = (f16[72,768]{1,0:T(8,128)(2,1)S(1)}, f16[72,768]{1,0:T(8,128)(2,1)S(1)}, u32[]{:S(2)}, u32[]{:S(2)}) collective-permute-start(f16[72,768]{1,0:T(8,128)(2,1)S(1)} %convert_element_type.28), channel_id=1, source_target_pairs={{0,8},{8,0},{16,24},{24,16},{1,9},{9,1},{17,25},{25,17},{2,10},{10... | collective-permute-start | bytes 331784 | tf_op jit(solution)/shard_map/ppermute | solution.py:214
  36.7 2.8 %collective-permute-start.14 = (f32[8,128]{1,0:T(8,128)S(1)}, f32[8,128]{1,0:T(8,128)S(1)}, u32[]{:S(2)}, u32[]{:S(2)}) collective-permute-start(f32[8,128]{1,0:T(8,128)S(1)} %get-tuple-element.34), channel_id=1, source_target_pairs={{0,24},{8,16},{16,8},{24,0},{1,25},{9,17},{17,9},{25,1},{2,26},{10... | collective-permute-start | bytes 12296 | tf_op jit(solution)/shard_map/ppermute | solution.py:214
  39.5 0.0 collective-permute-done.11
  39.6 3.6 %collective-permute-done.12 = f16[64,768]{1,0:T(8,128)(2,1)S(1)} collective-permute-done((f16[64,768]{1,0:T(8,128)(2,1)S(1)}, f16[64,768]{1,0:T(8,128)(2,1)S(1)}, u32[]{:S(2)}, u32[]{:S(2)}) %collective-permute-start.12) | collective-permute-done | bytes 98336 | tf_op jit(solution)/shard_map/ppermute | solution.py:214
  43.2 0.0 collective-permute-done.13
  43.2 0.8 %collective-permute-done.15.refs_5_ = f32[8,128]{1,0:T(8,128)S(1)} collective-permute-done((f32[8,128]{1,0:T(8,128)S(1)}, f32[8,128]{1,0:T(8,128)S(1)}, u32[]{:S(2)}, u32[]{:S(2)}) %collective-permute-start.15) | collective-permute-done | bytes 4128 | tf_op jit(solution)/shard_map/ppermute | solution.py:214
  44.0 1.4 %restore_rows.1 = (f32[256,768]{1,0:T(8,128)}, f32[1,256]{1,0:T(1,128)}) custom-call(bf16[256,256]{1,0:T(8,128)(2,1)S(1)} %get-tuple-element.20.chosen_ref, f32[64,768]{1,0:T(8,128)S(1)} %convert_element_type.25.refs_0_, f32[64,768]{1,0:T(8,128)S(1)} %convert_element_type.27.refs_1_, f32[72,768]{1,0:T(8,128)S(1)} %convert_element_type.29.refs_2_, ...), custom_call_target="tpu_custom_call" | custom-call | tf_op jit(solution)/shard_map/restore_rows/pallas_call | solution.py:284
  (23 shorter events, 0.3 us)
Async XLA Ops:
  1.9 5.9 %collective-permute-start = (bf16[64,768]{1,0:T(8,128)(2,1)S(1)}, bf16[64,768]{1,0:T(8,128)(2,1)S(1)}, u32[]{:S(2)}, u32[]{:S(2)}) collective-permute-start(bf16[64,768]{1,0:T(8,128)(2,1)S(1)} %get-tuple-element.22), channel_id=1, source_target_pairs={{0,8},{8,0},{16,24},{24,16},{1,9},{9,1},{17,25},{25,17},{2,10},{10... | collective-permute-start | bytes 294920 | tf_op jit(solution)/shard_map/ppermute | solution.py:214
  5.0 11.4 %collective-permute-start.5 = (bf16[64,768]{1,0:T(8,128)(2,1)S(1)}, bf16[64,768]{1,0:T(8,128)(2,1)S(1)}, u32[]{:S(2)}, u32[]{:S(2)}) collective-permute-start(bf16[64,768]{1,0:T(8,128)(2,1)S(1)} %get-tuple-element.24), channel_id=1, source_target_pairs={{0,24},{8,16},{16,8},{24,0},{1,25},{9,17},{17,9},{25,1},{2,26},{10... | collective-permute-start | bytes 294920 | tf_op jit(solution)/shard_map/ppermute | solution.py:214
  7.5 8.9 %collective-permute-start.4 = (bf16[64,768]{1,0:T(8,128)(2,1)S(1)}, bf16[64,768]{1,0:T(8,128)(2,1)S(1)}, u32[]{:S(2)}, u32[]{:S(2)}) collective-permute-start(bf16[64,768]{1,0:T(8,128)(2,1)S(1)} %get-tuple-element.23), channel_id=1, source_target_pairs={{0,16},{8,24},{16,0},{24,8},{1,17},{9,25},{17,1},{25,9},{2,18},{10... | collective-permute-start | bytes 294920 | tf_op jit(solution)/shard_map/ppermute | solution.py:214
  7.8 11.7 %collective-permute-start.1 = (bf16[128,768]{1,0:T(8,128)(2,1)S(1)}, bf16[128,768]{1,0:T(8,128)(2,1)S(1)}, u32[]{:S(2)}, u32[]{:S(2)}) collective-permute-start(bf16[128,768]{1,0:T(8,128)(2,1)S(1)} %get-tuple-element.42), channel_id=1, source_target_pairs={{0,6},{1,7},{2,4},{3,5},{4,2},{5,3},{6,0},{7,1},{8,14},{9,15},{10,... | collective-permute-start | bytes 589832 | tf_op jit(solution)/shard_map/ppermute | solution.py:217
  10.6 9.6 %collective-permute-start.2 = (bf16[128,768]{1,0:T(8,128)(2,1)S(1)}, bf16[128,768]{1,0:T(8,128)(2,1)S(1)}, u32[]{:S(2)}, u32[]{:S(2)}) collective-permute-start(bf16[128,768]{1,0:T(8,128)(2,1)S(1)} %get-tuple-element.42), channel_id=1, source_target_pairs={{0,2},{1,5},{2,0},{3,7},{4,6},{5,1},{6,4},{7,3},{8,10},{9,13},{10,... | collective-permute-start | bytes 589832 | tf_op jit(solution)/shard_map/ppermute | solution.py:237
  11.1 9.1 %collective-permute-start.3 = (bf16[128,768]{1,0:T(8,128)(2,1)S(1)}, bf16[128,768]{1,0:T(8,128)(2,1)S(1)}, u32[]{:S(2)}, u32[]{:S(2)}) collective-permute-start(bf16[128,768]{1,0:T(8,128)(2,1)S(1)} %get-tuple-element.42), channel_id=1, source_target_pairs={{0,4},{1,3},{2,6},{3,1},{4,0},{5,7},{6,2},{7,5},{8,12},{9,11},{10,... | collective-permute-start | bytes 589832 | tf_op jit(solution)/shard_map/ppermute | solution.py:237
  16.5 8.8 %collective-permute-start.7 = (bf16[128,768]{1,0:T(8,128)(2,1)S(1)}, bf16[128,768]{1,0:T(8,128)(2,1)S(1)}, u32[]{:S(2)}, u32[]{:S(2)}) collective-permute-start(bf16[128,768]{1,0:T(8,128)(2,1)S(1)} %get-tuple-element.38), channel_id=1, source_target_pairs={{0,6},{1,7},{2,4},{3,5},{4,2},{5,3},{6,0},{7,1},{8,14},{9,15},{10,... | collective-permute-start | bytes 589832 | tf_op jit(solution)/shard_map/ppermute | solution.py:217
  19.0 9.2 %collective-permute-start.8 = (bf16[128,768]{1,0:T(8,128)(2,1)S(1)}, bf16[128,768]{1,0:T(8,128)(2,1)S(1)}, u32[]{:S(2)}, u32[]{:S(2)}) collective-permute-start(bf16[128,768]{1,0:T(8,128)(2,1)S(1)} %get-tuple-element.38), channel_id=1, source_target_pairs={{0,2},{1,5},{2,0},{3,7},{4,6},{5,1},{6,4},{7,3},{8,10},{9,13},{10,... | collective-permute-start | bytes 589832 | tf_op jit(solution)/shard_map/ppermute | solution.py:237
  19.6 8.6 %collective-permute-start.9 = (bf16[128,768]{1,0:T(8,128)(2,1)S(1)}, bf16[128,768]{1,0:T(8,128)(2,1)S(1)}, u32[]{:S(2)}, u32[]{:S(2)}) collective-permute-start(bf16[128,768]{1,0:T(8,128)(2,1)S(1)} %get-tuple-element.38), channel_id=1, source_target_pairs={{0,4},{1,3},{2,6},{3,1},{4,0},{5,7},{6,2},{7,5},{8,12},{9,11},{10,... | collective-permute-start | bytes 589832 | tf_op jit(solution)/shard_map/ppermute | solution.py:237
  20.2 8.1 %collective-permute-start.6 = (bf16[512,768]{1,0:T(8,128)(2,1)S(1)}, bf16[512,768]{1,0:T(8,128)(2,1)S(1)}, u32[]{:S(2)}, u32[]{:S(2)}) collective-permute-start(bf16[512,768]{1,0:T(8,128)(2,1)S(1)} %constant_dynamic-update-slice_fusion.2.refs_0_), channel_id=1, source_target_pairs={{0,1},{1,0},{2,3},{3,2},{4,5},{5,4},{6,7},{7,6},{8,9},{9,8},{10,11... | collective-permute-start | bytes 2359304 | tf_op jit(solution)/shard_map/ppermute | solution.py:217
  28.2 2.4 %collective-permute-start.10 = (bf16[512,768]{1,0:T(8,128)(2,1)S(1)}, bf16[512,768]{1,0:T(8,128)(2,1)S(1)}, u32[]{:S(2)}, u32[]{:S(2)}) collective-permute-start(bf16[512,768]{1,0:T(8,128)(2,1)S(1)} %constant_dynamic-update-slice_fusion.9.refs_2_), channel_id=1, source_target_pairs={{0,1},{1,0},{2,3},{3,2},{4,5},{5,4},{6,7},{7,6},{8,9},{9,8},{10,11... | collective-permute-start | bytes 2359304 | tf_op jit(solution)/shard_map/ppermute | solution.py:217
  31.3 8.2 %collective-permute-start.11 = (f16[64,768]{1,0:T(8,128)(2,1)S(1)}, f16[64,768]{1,0:T(8,128)(2,1)S(1)}, u32[]{:S(2)}, u32[]{:S(2)}) collective-permute-start(f16[64,768]{1,0:T(8,128)(2,1)S(1)} %convert_element_type.24), channel_id=1, source_target_pairs={{0,24},{8,16},{16,8},{24,0},{1,25},{9,17},{17,9},{25,1},{2,26},{10... | collective-permute-start | bytes 294920 | tf_op jit(solution)/shard_map/ppermute | solution.py:214
  34.2 8.9 %collective-permute-start.12 = (f16[64,768]{1,0:T(8,128)(2,1)S(1)}, f16[64,768]{1,0:T(8,128)(2,1)S(1)}, u32[]{:S(2)}, u32[]{:S(2)}) collective-permute-start(f16[64,768]{1,0:T(8,128)(2,1)S(1)} %convert_element_type.26), channel_id=1, source_target_pairs={{0,16},{8,24},{16,0},{24,8},{1,17},{9,25},{17,1},{25,9},{2,18},{10... | collective-permute-start | bytes 294920 | tf_op jit(solution)/shard_map/ppermute | solution.py:214
  35.1 8.1 %collective-permute-start.13 = (f16[72,768]{1,0:T(8,128)(2,1)S(1)}, f16[72,768]{1,0:T(8,128)(2,1)S(1)}, u32[]{:S(2)}, u32[]{:S(2)}) collective-permute-start(f16[72,768]{1,0:T(8,128)(2,1)S(1)} %convert_element_type.28), channel_id=1, source_target_pairs={{0,8},{8,0},{16,24},{24,16},{1,9},{9,1},{17,25},{25,17},{2,10},{10... | collective-permute-start | bytes 331784 | tf_op jit(solution)/shard_map/ppermute | solution.py:214
  36.7 6.5 %collective-permute-start.14 = (f32[8,128]{1,0:T(8,128)S(1)}, f32[8,128]{1,0:T(8,128)S(1)}, u32[]{:S(2)}, u32[]{:S(2)}) collective-permute-start(f32[8,128]{1,0:T(8,128)S(1)} %get-tuple-element.34), channel_id=1, source_target_pairs={{0,24},{8,16},{16,8},{24,0},{1,25},{9,17},{17,9},{25,1},{2,26},{10... | collective-permute-start | bytes 12296 | tf_op jit(solution)/shard_map/ppermute | solution.py:214
  39.5 4.5 %collective-permute-start.15 = (f32[8,128]{1,0:T(8,128)S(1)}, f32[8,128]{1,0:T(8,128)S(1)}, u32[]{:S(2)}, u32[]{:S(2)}) collective-permute-start(f32[8,128]{1,0:T(8,128)S(1)} %get-tuple-element.35), channel_id=1, source_target_pairs={{0,16},{8,24},{16,0},{24,8},{1,17},{9,25},{17,1},{25,9},{2,18},{10... | collective-permute-start | bytes 12296 | tf_op jit(solution)/shard_map/ppermute | solution.py:214

commit v16 on v10

--- a/solution.py
+++ b/solution.py
@@ -233,10 +233,11 @@
         return lax.ppermute(block, "gc", pairs)
 
     chunks = []
-    for pieces in (held[:half], held[half:]):
+    for k, pieces in enumerate((held[:half], held[half:])):
         block = jnp.concatenate(pieces, axis=0)
-        near = [block] + [along_gc(block, k) for k in corners]
-        near += [to_side(block, step) for step in range(len(sides))]
+        side_blocks = [to_side(block, step) for step in range(len(sides))]
+        corner_blocks = [along_gc(block, bits) for bits in corners]
+        near = [block] + (corner_blocks + side_blocks if k else side_blocks + corner_blocks)
         chunks.append(jnp.concatenate(near, axis=0))
     rows = jnp.concatenate(held, axis=0)
     chunks[0], rows = lax.optimization_barrier((chunks[0], rows))

time: 45 us -> 45.4 us (level)
    ppermute x4, starting transfers between devices: 5.41 us -> 2.89 us  [along_gc(): return lax.ppermute(block, 'gc', [(i, i ^ bits) for i in range(n_gc)])]
    ppermute x4, starting transfers between devices: 1.9 us -> 4.43 us  [to_side(): return lax.ppermute(block, 'gc', pairs)]
where the time goes in v16:
time: 45.4 us; the launch traced here: 45.2 us
  starting transfers between devices  20.8 us (46%)
  waiting for transfers between devices  17.7 us (39%)
  Pallas kernels  5.56 us (12%)
  between operations  0.86 us (2%)
    ppermute x8, starting transfers between devices, along_gr(): return lax.ppermute(part, 'gr', [(i, i ^ bits) for i in range(n_gr)])  13.5 us
    ppermute x8, waiting for transfers between devices, along_gr(): return lax.ppermute(part, 'gr', [(i, i ^ bits) for i in range(n_gr)])  9.63 us
    ppermute x4, waiting for transfers between devices, along_gc(): return lax.ppermute(block, 'gc', [(i, i ^ bits) for i in range(n_gc)])  5.27 us
    ppermute x4, starting transfers between devices, to_side(): return lax.ppermute(block, 'gc', pairs)  4.43 us
    ppermute x4, starting transfers between devices, along_gc(): return lax.ppermute(block, 'gc', [(i, i ^ bits) for i in range(n_gc)])  2.89 us
    ppermute x4, waiting for transfers between devices, to_side(): return lax.ppermute(block, 'gc', pairs)  2.83 us
    pallas_call x1, Pallas kernels, on_device(): pl.pallas_call(early_kernel, out_shape=[jax.ShapeDtypeStruct((count, LANE...  1.95 us
    pallas_call x1, Pallas kernels, on_device(): pl.pallas_call(functools.partial(restore_kernel, half), out_shape=[jax.Sh...  1.44 us
  transfers between devices with their start and end apart: 16, of which 7 were waited for; matrix products, arithmetic and copies ran while one was open for 1% of the time, Pallas kernels for 4%

profile of v16, /device:TPU:0, one launch (start us, length us, event | category | flops | bytes accessed | tf_op | source)
XLA Modules:
  0.0 45.2 jit_solution(14222139148071213147)
XLA Ops:
  0.6 1.3 %sort_rows.1 = (bf16[256,256]{1,0:T(8,128)(2,1)S(1)}, bf16[64,768]{1,0:T(8,128)(2,1)S(1)}, bf16[64,768]{1,0:T(8,128)(2,1)S(1)}, bf16[64,768]{1,0:T(8,128)(2,1)S(1)}, bf16[64,768]{1,0:T(8,128)(2,1)S(1)}) custom-call(s32[1]{0:T(128)} %bitcast.own_ref, s32[1,256]{1,0:T(1,128)} %bitcast.3, bf16[256,768]{1,0:T(8,128)(2,1)} %rows_hbm.1), custom_call_target="tpu_custom_call" | custom-call | tf_op jit(solution)/shard_map/sort_rows/pallas_call | solution.py:193
  1.9 3.1 %collective-permute-start = (bf16[64,768]{1,0:T(8,128)(2,1)S(1)}, bf16[64,768]{1,0:T(8,128)(2,1)S(1)}, u32[]{:S(2)}, u32[]{:S(2)}) collective-permute-start(bf16[64,768]{1,0:T(8,128)(2,1)S(1)} %get-tuple-element.22), channel_id=1, source_target_pairs={{0,8},{8,0},{16,24},{24,16},{1,9},{9,1},{17,25},{25,17},{2,10},{10... | collective-permute-start | bytes 294920 | tf_op jit(solution)/shard_map/ppermute | solution.py:210
  5.0 2.5 %collective-permute-start.5 = (bf16[64,768]{1,0:T(8,128)(2,1)S(1)}, bf16[64,768]{1,0:T(8,128)(2,1)S(1)}, u32[]{:S(2)}, u32[]{:S(2)}) collective-permute-start(bf16[64,768]{1,0:T(8,128)(2,1)S(1)} %get-tuple-element.24), channel_id=1, source_target_pairs={{0,24},{8,16},{16,8},{24,0},{1,25},{9,17},{17,9},{25,1},{2,26},{10... | collective-permute-start | bytes 294920 | tf_op jit(solution)/shard_map/ppermute | solution.py:210
  7.5 0.1 collective-permute-start.4
  7.6 0.2 collective-permute-done
  7.8 1.8 %collective-permute-start.1 = (bf16[128,768]{1,0:T(8,128)(2,1)S(1)}, bf16[128,768]{1,0:T(8,128)(2,1)S(1)}, u32[]{:S(2)}, u32[]{:S(2)}) collective-permute-start(bf16[128,768]{1,0:T(8,128)(2,1)S(1)} %get-tuple-element.42), channel_id=1, source_target_pairs={{0,2},{1,5},{2,0},{3,7},{4,6},{5,1},{6,4},{7,3},{8,10},{9,13},{10,... | collective-permute-start | bytes 589832 | tf_op jit(solution)/shard_map/ppermute | solution.py:233
  9.6 1.5 %collective-permute-start.2 = (bf16[128,768]{1,0:T(8,128)(2,1)S(1)}, bf16[128,768]{1,0:T(8,128)(2,1)S(1)}, u32[]{:S(2)}, u32[]{:S(2)}) collective-permute-start(bf16[128,768]{1,0:T(8,128)(2,1)S(1)} %get-tuple-element.42), channel_id=1, source_target_pairs={{0,4},{1,3},{2,6},{3,1},{4,0},{5,7},{6,2},{7,5},{8,12},{9,11},{10,... | collective-permute-start | bytes 589832 | tf_op jit(solution)/shard_map/ppermute | solution.py:233
  11.2 0.2 collective-permute-start.3
  11.4 5.1 %collective-permute-done.4 = bf16[64,768]{1,0:T(8,128)(2,1)S(1)} collective-permute-done((bf16[64,768]{1,0:T(8,128)(2,1)S(1)}, bf16[64,768]{1,0:T(8,128)(2,1)S(1)}, u32[]{:S(2)}, u32[]{:S(2)}) %collective-permute-start.4) | collective-permute-done | bytes 98336 | tf_op jit(solution)/shard_map/ppermute | solution.py:210
  16.5 0.0 collective-permute-done.5
  16.5 2.5 %collective-permute-start.7 = (bf16[128,768]{1,0:T(8,128)(2,1)S(1)}, bf16[128,768]{1,0:T(8,128)(2,1)S(1)}, u32[]{:S(2)}, u32[]{:S(2)}) collective-permute-start(bf16[128,768]{1,0:T(8,128)(2,1)S(1)} %get-tuple-element.38), channel_id=1, source_target_pairs={{0,6},{1,7},{2,4},{3,5},{4,2},{5,3},{6,0},{7,1},{8,14},{9,15},{10,... | collective-permute-start | bytes 589832 | tf_op jit(solution)/shard_map/ppermute | solution.py:213
  19.0 0.5 %collective-permute-start.8 = (bf16[128,768]{1,0:T(8,128)(2,1)S(1)}, bf16[128,768]{1,0:T(8,128)(2,1)S(1)}, u32[]{:S(2)}, u32[]{:S(2)}) collective-permute-start(bf16[128,768]{1,0:T(8,128)(2,1)S(1)} %get-tuple-element.38), channel_id=1, source_target_pairs={{0,2},{1,5},{2,0},{3,7},{4,6},{5,1},{6,4},{7,3},{8,10},{9,13},{10,... | collective-permute-start | bytes 589832 | tf_op jit(solution)/shard_map/ppermute | solution.py:233
  19.6 0.6 %collective-permute-start.9 = (bf16[128,768]{1,0:T(8,128)(2,1)S(1)}, bf16[128,768]{1,0:T(8,128)(2,1)S(1)}, u32[]{:S(2)}, u32[]{:S(2)}) collective-permute-start(bf16[128,768]{1,0:T(8,128)(2,1)S(1)} %get-tuple-element.38), channel_id=1, source_target_pairs={{0,4},{1,3},{2,6},{3,1},{4,0},{5,7},{6,2},{7,5},{8,12},{9,11},{10,... | collective-permute-start | bytes 589832 | tf_op jit(solution)/shard_map/ppermute | solution.py:233
  20.2 0.0 collective-permute-done.2
  20.2 0.0 collective-permute-done.3
  20.2 0.1 collective-permute-start.6
  20.3 5.0 %collective-permute-done.7 = bf16[128,768]{1,0:T(8,128)(2,1)S(1)} collective-permute-done((bf16[128,768]{1,0:T(8,128)(2,1)S(1)}, bf16[128,768]{1,0:T(8,128)(2,1)S(1)}, u32[]{:S(2)}, u32[]{:S(2)}) %collective-permute-start.7) | collective-permute-done | bytes 196640 | tf_op jit(solution)/shard_map/ppermute | solution.py:213
  25.3 2.8 %collective-permute-done.8 = bf16[128,768]{1,0:T(8,128)(2,1)S(1)} collective-permute-done((bf16[128,768]{1,0:T(8,128)(2,1)S(1)}, bf16[128,768]{1,0:T(8,128)(2,1)S(1)}, u32[]{:S(2)}, u32[]{:S(2)}) %collective-permute-start.8) | collective-permute-done | bytes 196640 | tf_op jit(solution)/shard_map/ppermute | solution.py:233
  28.1 0.0 collective-permute-done.9
  28.2 0.1 collective-permute-start.10
  28.3 2.0 %early_sums.1 = (f32[256,128]{1,0:T(8,128)S(1)}, f32[256,768]{1,0:T(8,128)S(1)}, f32[256,128]{1,0:T(8,128)S(1)}) custom-call(bf16[256,768]{1,0:T(8,128)(2,1)S(1)} %pad_maximum_fusion.rows_ref, bf16[512,768]{1,0:T(8,128)(2,1)S(1)} %constant_dynamic-update-slice_fusion.2.refs_0_, bf16[512,768]{1,0:T(8,128)(2,1)S(1)} %collective-permute-done.6.refs_1_, ...), custom_call_target="tpu_custom_call" | custom-call | flops 1207959552 | tf_op jit(solution)/shard_map/early_sums/pallas_call | solution.py:246
  30.2 0.3 collective-permute-done.10.cols_ref
  30.5 0.9 %last_sums.1 = (f32[72,768]{1,0:T(8,128)S(1)}, f32[72,768]{1,0:T(8,128)S(1)}, f32[64,768]{1,0:T(8,128)S(1)}, f32[64,768]{1,0:T(8,128)S(1)}, f32[8,128]{1,0:T(8,128)S(1)}, /*index=5*/f32[8,128]{1,0:T(8,128)S(1)}) custom-call(bf16[256,768]{1,0:T(8,128)(2,1)S(1)} %pad_maximum_fusion.rows_ref, f32[256,128]{1,0:T(8,128)S(1)} %get-tuple-element.27.scale_ref, ...), custom_call_target="tpu_custom_call" | custom-call | flops 402653184 | tf_op jit(solution)/shard_map/last_sums/pallas_call | solution.py:260
  31.4 3.3 %collective-permute-start.11 = (f16[64,768]{1,0:T(8,128)(2,1)S(1)}, f16[64,768]{1,0:T(8,128)(2,1)S(1)}, u32[]{:S(2)}, u32[]{:S(2)}) collective-permute-start(f16[64,768]{1,0:T(8,128)(2,1)S(1)} %convert_element_type.24), channel_id=1, source_target_pairs={{0,24},{8,16},{16,8},{24,0},{1,25},{9,17},{17,9},{25,1},{2,26},{10... | collective-permute-start | bytes 294920 | tf_op jit(solution)/shard_map/ppermute | solution.py:210
  34.8 0.1 collective-permute-start.12
  34.9 1.2 %collective-permute-start.13 = (f16[72,768]{1,0:T(8,128)(2,1)S(1)}, f16[72,768]{1,0:T(8,128)(2,1)S(1)}, u32[]{:S(2)}, u32[]{:S(2)}) collective-permute-start(f16[72,768]{1,0:T(8,128)(2,1)S(1)} %convert_element_type.28), channel_id=1, source_target_pairs={{0,8},{8,0},{16,24},{24,16},{1,9},{9,1},{17,25},{25,17},{2,10},{10... | collective-permute-start | bytes 331784 | tf_op jit(solution)/shard_map/ppermute | solution.py:210
  36.0 3.2 %collective-permute-start.14 = (f32[8,128]{1,0:T(8,128)S(1)}, f32[8,128]{1,0:T(8,128)S(1)}, u32[]{:S(2)}, u32[]{:S(2)}) collective-permute-start(f32[8,128]{1,0:T(8,128)S(1)} %get-tuple-element.34), channel_id=1, source_target_pairs={{0,24},{8,16},{16,8},{24,0},{1,25},{9,17},{17,9},{25,1},{2,26},{10... | collective-permute-start | bytes 12296 | tf_op jit(solution)/shard_map/ppermute | solution.py:210
  39.3 0.0 collective-permute-start.15
  39.3 4.3 %collective-permute-done.12 = f16[64,768]{1,0:T(8,128)(2,1)S(1)} collective-permute-done((f16[64,768]{1,0:T(8,128)(2,1)S(1)}, f16[64,768]{1,0:T(8,128)(2,1)S(1)}, u32[]{:S(2)}, u32[]{:S(2)}) %collective-permute-start.12) | collective-permute-done | bytes 98336 | tf_op jit(solution)/shard_map/ppermute | solution.py:210
  43.7 0.0 collective-permute-done.13
  43.7 0.1 collective-permute-done.15.refs_5_
  43.8 1.4 %restore_rows.1 = (f32[256,768]{1,0:T(8,128)}, f32[1,256]{1,0:T(1,128)}) custom-call(bf16[256,256]{1,0:T(8,128)(2,1)S(1)} %get-tuple-element.20.chosen_ref, f32[64,768]{1,0:T(8,128)S(1)} %convert_element_type.25.refs_0_, f32[64,768]{1,0:T(8,128)S(1)} %convert_element_type.27.refs_1_, f32[72,768]{1,0:T(8,128)S(1)} %convert_element_type.29.refs_2_, ...), custom_call_target="tpu_custom_call" | custom-call | tf_op jit(solution)/shard_map/restore_rows/pallas_call | solution.py:276
  (22 shorter events, 0.3 us)
Async XLA Ops:
  1.9 5.9 %collective-permute-start = (bf16[64,768]{1,0:T(8,128)(2,1)S(1)}, bf16[64,768]{1,0:T(8,128)(2,1)S(1)}, u32[]{:S(2)}, u32[]{:S(2)}) collective-permute-start(bf16[64,768]{1,0:T(8,128)(2,1)S(1)} %get-tuple-element.22), channel_id=1, source_target_pairs={{0,8},{8,0},{16,24},{24,16},{1,9},{9,1},{17,25},{25,17},{2,10},{10... | collective-permute-start | bytes 294920 | tf_op jit(solution)/shard_map/ppermute | solution.py:210
  5.0 11.4 %collective-permute-start.5 = (bf16[64,768]{1,0:T(8,128)(2,1)S(1)}, bf16[64,768]{1,0:T(8,128)(2,1)S(1)}, u32[]{:S(2)}, u32[]{:S(2)}) collective-permute-start(bf16[64,768]{1,0:T(8,128)(2,1)S(1)} %get-tuple-element.24), channel_id=1, source_target_pairs={{0,24},{8,16},{16,8},{24,0},{1,25},{9,17},{17,9},{25,1},{2,26},{10... | collective-permute-start | bytes 294920 | tf_op jit(solution)/shard_map/ppermute | solution.py:210
  7.5 8.9 %collective-permute-start.4 = (bf16[64,768]{1,0:T(8,128)(2,1)S(1)}, bf16[64,768]{1,0:T(8,128)(2,1)S(1)}, u32[]{:S(2)}, u32[]{:S(2)}) collective-permute-start(bf16[64,768]{1,0:T(8,128)(2,1)S(1)} %get-tuple-element.23), channel_id=1, source_target_pairs={{0,16},{8,24},{16,0},{24,8},{1,17},{9,25},{17,1},{25,9},{2,18},{10... | collective-permute-start | bytes 294920 | tf_op jit(solution)/shard_map/ppermute | solution.py:210
  7.8 11.7 %collective-permute-start.1 = (bf16[128,768]{1,0:T(8,128)(2,1)S(1)}, bf16[128,768]{1,0:T(8,128)(2,1)S(1)}, u32[]{:S(2)}, u32[]{:S(2)}) collective-permute-start(bf16[128,768]{1,0:T(8,128)(2,1)S(1)} %get-tuple-element.42), channel_id=1, source_target_pairs={{0,2},{1,5},{2,0},{3,7},{4,6},{5,1},{6,4},{7,3},{8,10},{9,13},{10,... | collective-permute-start | bytes 589832 | tf_op jit(solution)/shard_map/ppermute | solution.py:233
  9.6 10.5 %collective-permute-start.2 = (bf16[128,768]{1,0:T(8,128)(2,1)S(1)}, bf16[128,768]{1,0:T(8,128)(2,1)S(1)}, u32[]{:S(2)}, u32[]{:S(2)}) collective-permute-start(bf16[128,768]{1,0:T(8,128)(2,1)S(1)} %get-tuple-element.42), channel_id=1, source_target_pairs={{0,4},{1,3},{2,6},{3,1},{4,0},{5,7},{6,2},{7,5},{8,12},{9,11},{10,... | collective-permute-start | bytes 589832 | tf_op jit(solution)/shard_map/ppermute | solution.py:233
  11.2 9.1 %collective-permute-start.3 = (bf16[128,768]{1,0:T(8,128)(2,1)S(1)}, bf16[128,768]{1,0:T(8,128)(2,1)S(1)}, u32[]{:S(2)}, u32[]{:S(2)}) collective-permute-start(bf16[128,768]{1,0:T(8,128)(2,1)S(1)} %get-tuple-element.42), channel_id=1, source_target_pairs={{0,6},{1,7},{2,4},{3,5},{4,2},{5,3},{6,0},{7,1},{8,14},{9,15},{10,... | collective-permute-start | bytes 589832 | tf_op jit(solution)/shard_map/ppermute | solution.py:213
  16.5 8.8 %collective-permute-start.7 = (bf16[128,768]{1,0:T(8,128)(2,1)S(1)}, bf16[128,768]{1,0:T(8,128)(2,1)S(1)}, u32[]{:S(2)}, u32[]{:S(2)}) collective-permute-start(bf16[128,768]{1,0:T(8,128)(2,1)S(1)} %get-tuple-element.38), channel_id=1, source_target_pairs={{0,6},{1,7},{2,4},{3,5},{4,2},{5,3},{6,0},{7,1},{8,14},{9,15},{10,... | collective-permute-start | bytes 589832 | tf_op jit(solution)/shard_map/ppermute | solution.py:213
  19.0 9.1 %collective-permute-start.8 = (bf16[128,768]{1,0:T(8,128)(2,1)S(1)}, bf16[128,768]{1,0:T(8,128)(2,1)S(1)}, u32[]{:S(2)}, u32[]{:S(2)}) collective-permute-start(bf16[128,768]{1,0:T(8,128)(2,1)S(1)} %get-tuple-element.38), channel_id=1, source_target_pairs={{0,2},{1,5},{2,0},{3,7},{4,6},{5,1},{6,4},{7,3},{8,10},{9,13},{10,... | collective-permute-start | bytes 589832 | tf_op jit(solution)/shard_map/ppermute | solution.py:233
  19.6 8.6 %collective-permute-start.9 = (bf16[128,768]{1,0:T(8,128)(2,1)S(1)}, bf16[128,768]{1,0:T(8,128)(2,1)S(1)}, u32[]{:S(2)}, u32[]{:S(2)}) collective-permute-start(bf16[128,768]{1,0:T(8,128)(2,1)S(1)} %get-tuple-element.38), channel_id=1, source_target_pairs={{0,4},{1,3},{2,6},{3,1},{4,0},{5,7},{6,2},{7,5},{8,12},{9,11},{10,... | collective-permute-start | bytes 589832 | tf_op jit(solution)/shard_map/ppermute | solution.py:233
  20.2 8.0 %collective-permute-start.6 = (bf16[512,768]{1,0:T(8,128)(2,1)S(1)}, bf16[512,768]{1,0:T(8,128)(2,1)S(1)}, u32[]{:S(2)}, u32[]{:S(2)}) collective-permute-start(bf16[512,768]{1,0:T(8,128)(2,1)S(1)} %constant_dynamic-update-slice_fusion.2.refs_0_), channel_id=1, source_target_pairs={{0,1},{1,0},{2,3},{3,2},{4,5},{5,4},{6,7},{7,6},{8,9},{9,8},{10,11... | collective-permute-start | bytes 2359304 | tf_op jit(solution)/shard_map/ppermute | solution.py:213
  28.2 2.4 %collective-permute-start.10 = (bf16[512,768]{1,0:T(8,128)(2,1)S(1)}, bf16[512,768]{1,0:T(8,128)(2,1)S(1)}, u32[]{:S(2)}, u32[]{:S(2)}) collective-permute-start(bf16[512,768]{1,0:T(8,128)(2,1)S(1)} %constant_dynamic-update-slice_fusion.9.refs_2_), channel_id=1, source_target_pairs={{0,1},{1,0},{2,3},{3,2},{4,5},{5,4},{6,7},{7,6},{8,9},{9,8},{10,11... | collective-permute-start | bytes 2359304 | tf_op jit(solution)/shard_map/ppermute | solution.py:213
  31.4 7.9 %collective-permute-start.11 = (f16[64,768]{1,0:T(8,128)(2,1)S(1)}, f16[64,768]{1,0:T(8,128)(2,1)S(1)}, u32[]{:S(2)}, u32[]{:S(2)}) collective-permute-start(f16[64,768]{1,0:T(8,128)(2,1)S(1)} %convert_element_type.24), channel_id=1, source_target_pairs={{0,24},{8,16},{16,8},{24,0},{1,25},{9,17},{17,9},{25,1},{2,26},{10... | collective-permute-start | bytes 294920 | tf_op jit(solution)/shard_map/ppermute | solution.py:210
  34.8 8.9 %collective-permute-start.12 = (f16[64,768]{1,0:T(8,128)(2,1)S(1)}, f16[64,768]{1,0:T(8,128)(2,1)S(1)}, u32[]{:S(2)}, u32[]{:S(2)}) collective-permute-start(f16[64,768]{1,0:T(8,128)(2,1)S(1)} %convert_element_type.26), channel_id=1, source_target_pairs={{0,16},{8,24},{16,0},{24,8},{1,17},{9,25},{17,1},{25,9},{2,18},{10... | collective-permute-start | bytes 294920 | tf_op jit(solution)/shard_map/ppermute | solution.py:210
  34.9 8.8 %collective-permute-start.13 = (f16[72,768]{1,0:T(8,128)(2,1)S(1)}, f16[72,768]{1,0:T(8,128)(2,1)S(1)}, u32[]{:S(2)}, u32[]{:S(2)}) collective-permute-start(f16[72,768]{1,0:T(8,128)(2,1)S(1)} %convert_element_type.28), channel_id=1, source_target_pairs={{0,8},{8,0},{16,24},{24,16},{1,9},{9,1},{17,25},{25,17},{2,10},{10... | collective-permute-start | bytes 331784 | tf_op jit(solution)/shard_map/ppermute | solution.py:210
  36.0 7.6 %collective-permute-start.14 = (f32[8,128]{1,0:T(8,128)S(1)}, f32[8,128]{1,0:T(8,128)S(1)}, u32[]{:S(2)}, u32[]{:S(2)}) collective-permute-start(f32[8,128]{1,0:T(8,128)S(1)} %get-tuple-element.34), channel_id=1, source_target_pairs={{0,24},{8,16},{16,8},{24,0},{1,25},{9,17},{17,9},{25,1},{2,26},{10... | collective-permute-start | bytes 12296 | tf_op jit(solution)/shard_map/ppermute | solution.py:210
  39.3 4.5 %collective-permute-start.15 = (f32[8,128]{1,0:T(8,128)S(1)}, f32[8,128]{1,0:T(8,128)S(1)}, u32[]{:S(2)}, u32[]{:S(2)}) collective-permute-start(f32[8,128]{1,0:T(8,128)S(1)} %get-tuple-element.35), channel_id=1, source_target_pairs={{0,16},{8,24},{16,0},{24,8},{1,17},{9,25},{17,1},{25,9},{2,18},{10... | collective-permute-start | bytes 12296 | tf_op jit(solution)/shard_map/ppermute | solution.py:210

commit v17 on v10

--- a/solution.py
+++ b/solution.py
@@ -10,7 +10,7 @@
 
 beta_scale = 16.0
 floor_weight = math.exp(-beta_scale)
-BLOCK = 512
+BLOCK = 256
 LANES = 128
 EXTRA = 8
 TOP = 14.0

time: 45 us -> 45.6 us (1.013)
  Pallas kernels: 5.55 us -> 6.18 us
  transfers between devices with their start and end apart: 16 -> 16, of which waited for: 7 -> 6; matrix products, arithmetic and copies ran while one was open for 1% -> 1% of each run, Pallas kernels for 4% -> 5%
where the time goes in v17:
time: 45.6 us; the launch traced here: 45.4 us
  starting transfers between devices  20.4 us (45%)
  waiting for transfers between devices  17.8 us (39%)
  Pallas kernels  6.18 us (14%)
  between operations  0.85 us (2%)
    ppermute x8, starting transfers between devices, along_gr(): return lax.ppermute(part, 'gr', [(i, i ^ bits) for i in range(n_gr)])  13.1 us
    ppermute x8, waiting for transfers between devices, along_gr(): return lax.ppermute(part, 'gr', [(i, i ^ bits) for i in range(n_gr)])  9.93 us
    ppermute x4, starting transfers between devices, along_gc(): return lax.ppermute(block, 'gc', [(i, i ^ bits) for i in range(n_gc)])  5.41 us
    ppermute x4, waiting for transfers between devices, along_gc(): return lax.ppermute(block, 'gc', [(i, i ^ bits) for i in range(n_gc)])  4.97 us
    ppermute x4, waiting for transfers between devices, to_side(): return lax.ppermute(block, 'gc', pairs)  2.87 us
    pallas_call x1, Pallas kernels, on_device(): pl.pallas_call(early_kernel, out_shape=[jax.ShapeDtypeStruct((count, LANE...  2.28 us
    ppermute x4, starting transfers between devices, to_side(): return lax.ppermute(block, 'gc', pairs)  1.9 us
    pallas_call x1, Pallas kernels, on_device(): pl.pallas_call(functools.partial(restore_kernel, half), out_shape=[jax.Sh...  1.45 us
  transfers between devices with their start and end apart: 16, of which 6 were waited for; matrix products, arithmetic and copies ran while one was open for 1% of the time, Pallas kernels for 5%

profile of v17, /device:TPU:0, one launch (start us, length us, event | category | flops | bytes accessed | tf_op | source)
XLA Modules:
  0.0 45.4 jit_solution(10030014461485592425)
XLA Ops:
  0.6 1.3 %sort_rows.1 = (bf16[256,256]{1,0:T(8,128)(2,1)S(1)}, bf16[64,768]{1,0:T(8,128)(2,1)S(1)}, bf16[64,768]{1,0:T(8,128)(2,1)S(1)}, bf16[64,768]{1,0:T(8,128)(2,1)S(1)}, bf16[64,768]{1,0:T(8,128)(2,1)S(1)}) custom-call(s32[1]{0:T(128)} %bitcast.own_ref, s32[1,256]{1,0:T(1,128)} %bitcast.3, bf16[256,768]{1,0:T(8,128)(2,1)} %rows_hbm.1), custom_call_target="tpu_custom_call" | custom-call | tf_op jit(solution)/shard_map/sort_rows/pallas_call | solution.py:193
  1.9 3.1 %collective-permute-start = (bf16[64,768]{1,0:T(8,128)(2,1)S(1)}, bf16[64,768]{1,0:T(8,128)(2,1)S(1)}, u32[]{:S(2)}, u32[]{:S(2)}) collective-permute-start(bf16[64,768]{1,0:T(8,128)(2,1)S(1)} %get-tuple-element.22), channel_id=1, source_target_pairs={{0,8},{8,0},{16,24},{24,16},{1,9},{9,1},{17,25},{25,17},{2,10},{10... | collective-permute-start | bytes 294920 | tf_op jit(solution)/shard_map/ppermute | solution.py:210
  5.0 2.5 %collective-permute-start.5 = (bf16[64,768]{1,0:T(8,128)(2,1)S(1)}, bf16[64,768]{1,0:T(8,128)(2,1)S(1)}, u32[]{:S(2)}, u32[]{:S(2)}) collective-permute-start(bf16[64,768]{1,0:T(8,128)(2,1)S(1)} %get-tuple-element.24), channel_id=1, source_target_pairs={{0,24},{8,16},{16,8},{24,0},{1,25},{9,17},{17,9},{25,1},{2,26},{10... | collective-permute-start | bytes 294920 | tf_op jit(solution)/shard_map/ppermute | solution.py:210
  7.5 0.1 collective-permute-start.4
  7.6 0.2 collective-permute-done
  7.8 2.8 %collective-permute-start.1 = (bf16[128,768]{1,0:T(8,128)(2,1)S(1)}, bf16[128,768]{1,0:T(8,128)(2,1)S(1)}, u32[]{:S(2)}, u32[]{:S(2)}) collective-permute-start(bf16[128,768]{1,0:T(8,128)(2,1)S(1)} %get-tuple-element.42), channel_id=1, source_target_pairs={{0,6},{1,7},{2,4},{3,5},{4,2},{5,3},{6,0},{7,1},{8,14},{9,15},{10,... | collective-permute-start | bytes 589832 | tf_op jit(solution)/shard_map/ppermute | solution.py:213
  10.6 0.5 %collective-permute-start.2 = (bf16[128,768]{1,0:T(8,128)(2,1)S(1)}, bf16[128,768]{1,0:T(8,128)(2,1)S(1)}, u32[]{:S(2)}, u32[]{:S(2)}) collective-permute-start(bf16[128,768]{1,0:T(8,128)(2,1)S(1)} %get-tuple-element.42), channel_id=1, source_target_pairs={{0,2},{1,5},{2,0},{3,7},{4,6},{5,1},{6,4},{7,3},{8,10},{9,13},{10,... | collective-permute-start | bytes 589832 | tf_op jit(solution)/shard_map/ppermute | solution.py:233
  11.1 0.3 collective-permute-start.3
  11.4 5.1 %collective-permute-done.4 = bf16[64,768]{1,0:T(8,128)(2,1)S(1)} collective-permute-done((bf16[64,768]{1,0:T(8,128)(2,1)S(1)}, bf16[64,768]{1,0:T(8,128)(2,1)S(1)}, u32[]{:S(2)}, u32[]{:S(2)}) %collective-permute-start.4) | collective-permute-done | bytes 98336 | tf_op jit(solution)/shard_map/ppermute | solution.py:210
  16.5 0.0 collective-permute-done.5
  16.5 2.5 %collective-permute-start.7 = (bf16[128,768]{1,0:T(8,128)(2,1)S(1)}, bf16[128,768]{1,0:T(8,128)(2,1)S(1)}, u32[]{:S(2)}, u32[]{:S(2)}) collective-permute-start(bf16[128,768]{1,0:T(8,128)(2,1)S(1)} %get-tuple-element.38), channel_id=1, source_target_pairs={{0,6},{1,7},{2,4},{3,5},{4,2},{5,3},{6,0},{7,1},{8,14},{9,15},{10,... | collective-permute-start | bytes 589832 | tf_op jit(solution)/shard_map/ppermute | solution.py:213
  19.0 0.5 %collective-permute-start.8 = (bf16[128,768]{1,0:T(8,128)(2,1)S(1)}, bf16[128,768]{1,0:T(8,128)(2,1)S(1)}, u32[]{:S(2)}, u32[]{:S(2)}) collective-permute-start(bf16[128,768]{1,0:T(8,128)(2,1)S(1)} %get-tuple-element.38), channel_id=1, source_target_pairs={{0,2},{1,5},{2,0},{3,7},{4,6},{5,1},{6,4},{7,3},{8,10},{9,13},{10,... | collective-permute-start | bytes 589832 | tf_op jit(solution)/shard_map/ppermute | solution.py:233
  19.6 0.6 %collective-permute-start.9 = (bf16[128,768]{1,0:T(8,128)(2,1)S(1)}, bf16[128,768]{1,0:T(8,128)(2,1)S(1)}, u32[]{:S(2)}, u32[]{:S(2)}) collective-permute-start(bf16[128,768]{1,0:T(8,128)(2,1)S(1)} %get-tuple-element.38), channel_id=1, source_target_pairs={{0,4},{1,3},{2,6},{3,1},{4,0},{5,7},{6,2},{7,5},{8,12},{9,11},{10,... | collective-permute-start | bytes 589832 | tf_op jit(solution)/shard_map/ppermute | solution.py:233
  20.2 0.0 collective-permute-done.2
  20.2 0.0 collective-permute-done.3
  20.2 0.1 collective-permute-start.6
  20.3 5.0 %collective-permute-done.7 = bf16[128,768]{1,0:T(8,128)(2,1)S(1)} collective-permute-done((bf16[128,768]{1,0:T(8,128)(2,1)S(1)}, bf16[128,768]{1,0:T(8,128)(2,1)S(1)}, u32[]{:S(2)}, u32[]{:S(2)}) %collective-permute-start.7) | collective-permute-done | bytes 196640 | tf_op jit(solution)/shard_map/ppermute | solution.py:213
  25.3 2.9 %collective-permute-done.8 = bf16[128,768]{1,0:T(8,128)(2,1)S(1)} collective-permute-done((bf16[128,768]{1,0:T(8,128)(2,1)S(1)}, bf16[128,768]{1,0:T(8,128)(2,1)S(1)}, u32[]{:S(2)}, u32[]{:S(2)}) %collective-permute-start.8) | collective-permute-done | bytes 196640 | tf_op jit(solution)/shard_map/ppermute | solution.py:233
  28.2 0.1 collective-permute-start.10
  28.3 0.0 collective-permute-done.6.refs_1_
  28.3 2.3 %early_sums.1 = (f32[256,128]{1,0:T(8,128)S(1)}, f32[256,768]{1,0:T(8,128)S(1)}, f32[256,128]{1,0:T(8,128)S(1)}) custom-call(bf16[256,768]{1,0:T(8,128)(2,1)S(1)} %pad_maximum_fusion.rows_ref, bf16[512,768]{1,0:T(8,128)(2,1)S(1)} %constant_dynamic-update-slice_fusion.2.refs_0_, bf16[512,768]{1,0:T(8,128)(2,1)S(1)} %collective-permute-done.6.refs_1_, ...), custom_call_target="tpu_custom_call" | custom-call | flops 1207959552 | tf_op jit(solution)/shard_map/early_sums/pallas_call | solution.py:245
  30.6 1.2 %last_sums.1 = (f32[72,768]{1,0:T(8,128)S(1)}, f32[72,768]{1,0:T(8,128)S(1)}, f32[64,768]{1,0:T(8,128)S(1)}, f32[64,768]{1,0:T(8,128)S(1)}, f32[8,128]{1,0:T(8,128)S(1)}, /*index=5*/f32[8,128]{1,0:T(8,128)S(1)}) custom-call(bf16[256,768]{1,0:T(8,128)(2,1)S(1)} %pad_maximum_fusion.rows_ref, f32[256,128]{1,0:T(8,128)S(1)} %get-tuple-element.27.scale_ref, ...), custom_call_target="tpu_custom_call" | custom-call | flops 402653184 | tf_op jit(solution)/shard_map/last_sums/pallas_call | solution.py:259
  31.8 2.9 %collective-permute-start.11 = (f16[64,768]{1,0:T(8,128)(2,1)S(1)}, f16[64,768]{1,0:T(8,128)(2,1)S(1)}, u32[]{:S(2)}, u32[]{:S(2)}) collective-permute-start(f16[64,768]{1,0:T(8,128)(2,1)S(1)} %convert_element_type.24), channel_id=1, source_target_pairs={{0,24},{8,16},{16,8},{24,0},{1,25},{9,17},{17,9},{25,1},{2,26},{10... | collective-permute-start | bytes 294920 | tf_op jit(solution)/shard_map/ppermute | solution.py:210
  34.7 0.1 collective-permute-start.12
  34.8 1.6 %collective-permute-start.13 = (f16[72,768]{1,0:T(8,128)(2,1)S(1)}, f16[72,768]{1,0:T(8,128)(2,1)S(1)}, u32[]{:S(2)}, u32[]{:S(2)}) collective-permute-start(f16[72,768]{1,0:T(8,128)(2,1)S(1)} %convert_element_type.28), channel_id=1, source_target_pairs={{0,8},{8,0},{16,24},{24,16},{1,9},{9,1},{17,25},{25,17},{2,10},{10... | collective-permute-start | bytes 331784 | tf_op jit(solution)/shard_map/ppermute | solution.py:210
  36.4 2.8 %collective-permute-start.14 = (f32[8,128]{1,0:T(8,128)S(1)}, f32[8,128]{1,0:T(8,128)S(1)}, u32[]{:S(2)}, u32[]{:S(2)}) collective-permute-start(f32[8,128]{1,0:T(8,128)S(1)} %get-tuple-element.34), channel_id=1, source_target_pairs={{0,24},{8,16},{16,8},{24,0},{1,25},{9,17},{17,9},{25,1},{2,26},{10... | collective-permute-start | bytes 12296 | tf_op jit(solution)/shard_map/ppermute | solution.py:210
  39.2 0.0 collective-permute-start.15
  39.2 0.1 collective-permute-done.11
  39.4 4.5 %collective-permute-done.12 = f16[64,768]{1,0:T(8,128)(2,1)S(1)} collective-permute-done((f16[64,768]{1,0:T(8,128)(2,1)S(1)}, f16[64,768]{1,0:T(8,128)(2,1)S(1)}, u32[]{:S(2)}, u32[]{:S(2)}) %collective-permute-start.12) | collective-permute-done | bytes 98336 | tf_op jit(solution)/shard_map/ppermute | solution.py:210
  44.0 0.0 collective-permute-done.14.refs_4_
  44.0 0.0 collective-permute-done.15.refs_5_
  44.0 1.4 %restore_rows.1 = (f32[256,768]{1,0:T(8,128)}, f32[1,256]{1,0:T(1,128)}) custom-call(bf16[256,256]{1,0:T(8,128)(2,1)S(1)} %get-tuple-element.20.chosen_ref, f32[64,768]{1,0:T(8,128)S(1)} %convert_element_type.25.refs_0_, f32[64,768]{1,0:T(8,128)S(1)} %convert_element_type.27.refs_1_, f32[72,768]{1,0:T(8,128)S(1)} %convert_element_type.29.refs_2_, ...), custom_call_target="tpu_custom_call" | custom-call | tf_op jit(solution)/shard_map/restore_rows/pallas_call | solution.py:275
  (22 shorter events, 0.3 us)
Async XLA Ops:
  1.9 5.9 %collective-permute-start = (bf16[64,768]{1,0:T(8,128)(2,1)S(1)}, bf16[64,768]{1,0:T(8,128)(2,1)S(1)}, u32[]{:S(2)}, u32[]{:S(2)}) collective-permute-start(bf16[64,768]{1,0:T(8,128)(2,1)S(1)} %get-tuple-element.22), channel_id=1, source_target_pairs={{0,8},{8,0},{16,24},{24,16},{1,9},{9,1},{17,25},{25,17},{2,10},{10... | collective-permute-start | bytes 294920 | tf_op jit(solution)/shard_map/ppermute | solution.py:210
  5.0 11.4 %collective-permute-start.5 = (bf16[64,768]{1,0:T(8,128)(2,1)S(1)}, bf16[64,768]{1,0:T(8,128)(2,1)S(1)}, u32[]{:S(2)}, u32[]{:S(2)}) collective-permute-start(bf16[64,768]{1,0:T(8,128)(2,1)S(1)} %get-tuple-element.24), channel_id=1, source_target_pairs={{0,24},{8,16},{16,8},{24,0},{1,25},{9,17},{17,9},{25,1},{2,26},{10... | collective-permute-start | bytes 294920 | tf_op jit(solution)/shard_map/ppermute | solution.py:210
  7.5 8.9 %collective-permute-start.4 = (bf16[64,768]{1,0:T(8,128)(2,1)S(1)}, bf16[64,768]{1,0:T(8,128)(2,1)S(1)}, u32[]{:S(2)}, u32[]{:S(2)}) collective-permute-start(bf16[64,768]{1,0:T(8,128)(2,1)S(1)} %get-tuple-element.23), channel_id=1, source_target_pairs={{0,16},{8,24},{16,0},{24,8},{1,17},{9,25},{17,1},{25,9},{2,18},{10... | collective-permute-start | bytes 294920 | tf_op jit(solution)/shard_map/ppermute | solution.py:210
  7.8 11.7 %collective-permute-start.1 = (bf16[128,768]{1,0:T(8,128)(2,1)S(1)}, bf16[128,768]{1,0:T(8,128)(2,1)S(1)}, u32[]{:S(2)}, u32[]{:S(2)}) collective-permute-start(bf16[128,768]{1,0:T(8,128)(2,1)S(1)} %get-tuple-element.42), channel_id=1, source_target_pairs={{0,6},{1,7},{2,4},{3,5},{4,2},{5,3},{6,0},{7,1},{8,14},{9,15},{10,... | collective-permute-start | bytes 589832 | tf_op jit(solution)/shard_map/ppermute | solution.py:213
  10.6 9.6 %collective-permute-start.2 = (bf16[128,768]{1,0:T(8,128)(2,1)S(1)}, bf16[128,768]{1,0:T(8,128)(2,1)S(1)}, u32[]{:S(2)}, u32[]{:S(2)}) collective-permute-start(bf16[128,768]{1,0:T(8,128)(2,1)S(1)} %get-tuple-element.42), channel_id=1, source_target_pairs={{0,2},{1,5},{2,0},{3,7},{4,6},{5,1},{6,4},{7,3},{8,10},{9,13},{10,... | collective-permute-start | bytes 589832 | tf_op jit(solution)/shard_map/ppermute | solution.py:233
  11.1 9.1 %collective-permute-start.3 = (bf16[128,768]{1,0:T(8,128)(2,1)S(1)}, bf16[128,768]{1,0:T(8,128)(2,1)S(1)}, u32[]{:S(2)}, u32[]{:S(2)}) collective-permute-start(bf16[128,768]{1,0:T(8,128)(2,1)S(1)} %get-tuple-element.42), channel_id=1, source_target_pairs={{0,4},{1,3},{2,6},{3,1},{4,0},{5,7},{6,2},{7,5},{8,12},{9,11},{10,... | collective-permute-start | bytes 589832 | tf_op jit(solution)/shard_map/ppermute | solution.py:233
  16.5 8.8 %collective-permute-start.7 = (bf16[128,768]{1,0:T(8,128)(2,1)S(1)}, bf16[128,768]{1,0:T(8,128)(2,1)S(1)}, u32[]{:S(2)}, u32[]{:S(2)}) collective-permute-start(bf16[128,768]{1,0:T(8,128)(2,1)S(1)} %get-tuple-element.38), channel_id=1, source_target_pairs={{0,6},{1,7},{2,4},{3,5},{4,2},{5,3},{6,0},{7,1},{8,14},{9,15},{10,... | collective-permute-start | bytes 589832 | tf_op jit(solution)/shard_map/ppermute | solution.py:213
  19.0 9.2 %collective-permute-start.8 = (bf16[128,768]{1,0:T(8,128)(2,1)S(1)}, bf16[128,768]{1,0:T(8,128)(2,1)S(1)}, u32[]{:S(2)}, u32[]{:S(2)}) collective-permute-start(bf16[128,768]{1,0:T(8,128)(2,1)S(1)} %get-tuple-element.38), channel_id=1, source_target_pairs={{0,2},{1,5},{2,0},{3,7},{4,6},{5,1},{6,4},{7,3},{8,10},{9,13},{10,... | collective-permute-start | bytes 589832 | tf_op jit(solution)/shard_map/ppermute | solution.py:233
  19.6 8.6 %collective-permute-start.9 = (bf16[128,768]{1,0:T(8,128)(2,1)S(1)}, bf16[128,768]{1,0:T(8,128)(2,1)S(1)}, u32[]{:S(2)}, u32[]{:S(2)}) collective-permute-start(bf16[128,768]{1,0:T(8,128)(2,1)S(1)} %get-tuple-element.38), channel_id=1, source_target_pairs={{0,4},{1,3},{2,6},{3,1},{4,0},{5,7},{6,2},{7,5},{8,12},{9,11},{10,... | collective-permute-start | bytes 589832 | tf_op jit(solution)/shard_map/ppermute | solution.py:233
  20.2 8.1 %collective-permute-start.6 = (bf16[512,768]{1,0:T(8,128)(2,1)S(1)}, bf16[512,768]{1,0:T(8,128)(2,1)S(1)}, u32[]{:S(2)}, u32[]{:S(2)}) collective-permute-start(bf16[512,768]{1,0:T(8,128)(2,1)S(1)} %constant_dynamic-update-slice_fusion.2.refs_0_), channel_id=1, source_target_pairs={{0,1},{1,0},{2,3},{3,2},{4,5},{5,4},{6,7},{7,6},{8,9},{9,8},{10,11... | collective-permute-start | bytes 2359304 | tf_op jit(solution)/shard_map/ppermute | solution.py:213
  28.2 2.4 %collective-permute-start.10 = (bf16[512,768]{1,0:T(8,128)(2,1)S(1)}, bf16[512,768]{1,0:T(8,128)(2,1)S(1)}, u32[]{:S(2)}, u32[]{:S(2)}) collective-permute-start(bf16[512,768]{1,0:T(8,128)(2,1)S(1)} %constant_dynamic-update-slice_fusion.9.refs_2_), channel_id=1, source_target_pairs={{0,1},{1,0},{2,3},{3,2},{4,5},{5,4},{6,7},{7,6},{8,9},{9,8},{10,11... | collective-permute-start | bytes 2359304 | tf_op jit(solution)/shard_map/ppermute | solution.py:213
  31.8 7.6 %collective-permute-start.11 = (f16[64,768]{1,0:T(8,128)(2,1)S(1)}, f16[64,768]{1,0:T(8,128)(2,1)S(1)}, u32[]{:S(2)}, u32[]{:S(2)}) collective-permute-start(f16[64,768]{1,0:T(8,128)(2,1)S(1)} %convert_element_type.24), channel_id=1, source_target_pairs={{0,24},{8,16},{16,8},{24,0},{1,25},{9,17},{17,9},{25,1},{2,26},{10... | collective-permute-start | bytes 294920 | tf_op jit(solution)/shard_map/ppermute | solution.py:210
  34.7 9.2 %collective-permute-start.12 = (f16[64,768]{1,0:T(8,128)(2,1)S(1)}, f16[64,768]{1,0:T(8,128)(2,1)S(1)}, u32[]{:S(2)}, u32[]{:S(2)}) collective-permute-start(f16[64,768]{1,0:T(8,128)(2,1)S(1)} %convert_element_type.26), channel_id=1, source_target_pairs={{0,16},{8,24},{16,0},{24,8},{1,17},{9,25},{17,1},{25,9},{2,18},{10... | collective-permute-start | bytes 294920 | tf_op jit(solution)/shard_map/ppermute | solution.py:210
  34.8 9.2 %collective-permute-start.13 = (f16[72,768]{1,0:T(8,128)(2,1)S(1)}, f16[72,768]{1,0:T(8,128)(2,1)S(1)}, u32[]{:S(2)}, u32[]{:S(2)}) collective-permute-start(f16[72,768]{1,0:T(8,128)(2,1)S(1)} %convert_element_type.28), channel_id=1, source_target_pairs={{0,8},{8,0},{16,24},{24,16},{1,9},{9,1},{17,25},{25,17},{2,10},{10... | collective-permute-start | bytes 331784 | tf_op jit(solution)/shard_map/ppermute | solution.py:210
  36.4 7.6 %collective-permute-start.14 = (f32[8,128]{1,0:T(8,128)S(1)}, f32[8,128]{1,0:T(8,128)S(1)}, u32[]{:S(2)}, u32[]{:S(2)}) collective-permute-start(f32[8,128]{1,0:T(8,128)S(1)} %get-tuple-element.34), channel_id=1, source_target_pairs={{0,24},{8,16},{16,8},{24,0},{1,25},{9,17},{17,9},{25,1},{2,26},{10... | collective-permute-start | bytes 12296 | tf_op jit(solution)/shard_map/ppermute | solution.py:210
  39.2 4.8 %collective-permute-start.15 = (f32[8,128]{1,0:T(8,128)S(1)}, f32[8,128]{1,0:T(8,128)S(1)}, u32[]{:S(2)}, u32[]{:S(2)}) collective-permute-start(f32[8,128]{1,0:T(8,128)S(1)} %get-tuple-element.35), channel_id=1, source_target_pairs={{0,16},{8,24},{16,0},{24,8},{1,17},{9,25},{17,1},{25,9},{2,18},{10... | collective-permute-start | bytes 12296 | tf_op jit(solution)/shard_map/ppermute | solution.py:210

commit v18 on v15

--- a/solution.py
+++ b/solution.py
@@ -161,7 +161,8 @@
 def restore_kernel(half, chosen_ref, *refs):
     refs, (total_ref, dens_ref) = refs[:-2], refs[-2:]
     groups = len(refs) - half
-    part_refs = refs[groups - 1 :: -1] + refs[: groups - 1 : -1]
+    part_refs = refs[::-1]
+    part_refs = part_refs[:half] + part_refs[groups:] + part_refs[half:groups]
     size = part_refs[half].shape[0]
     chosen = chosen_ref[...]
     sums, dens = [], []
@@ -291,7 +292,7 @@
         out_specs=[VMEM, VMEM],
         compiler_params=GRANT,
         name="restore_rows",
-    )(chosen, *back[n_gr - 1 :: -1], *back[:n_gr - 1 : -1])
+    )(chosen, *back[half:n_gr][::-1], *back[n_gr:][::-1], *back[:half][::-1])
     return (neighbour_sum, density.reshape(count))
 
 

time: 45.6 us -> 46.2 us (1.013)
  waiting for transfers between devices: 17.8 us -> 18.3 us
    ppermute x8, waiting for transfers between devices: 9.63 us -> 10.2 us  [along_gr(): return lax.ppermute(part, 'gr', [(i, i ^ bits) for i in range(n_gr)])]
where the time goes in v18:
time: 46.2 us; the launch traced here: 46.1 us
  starting transfers between devices  20.5 us (44%)
  waiting for transfers between devices  18.3 us (40%)
  Pallas kernels  6.16 us (13%)
  between operations  0.86 us (2%)
    ppermute x8, starting transfers between devices, along_gr(): return lax.ppermute(part, 'gr', [(i, i ^ bits) for i in range(n_gr)])  13.1 us
    ppermute x8, waiting for transfers between devices, along_gr(): return lax.ppermute(part, 'gr', [(i, i ^ bits) for i in range(n_gr)])  10.2 us
    ppermute x4, starting transfers between devices, along_gc(): return lax.ppermute(block, 'gc', [(i, i ^ bits) for i in range(n_gc)])  5.41 us
    ppermute x4, waiting for transfers between devices, along_gc(): return lax.ppermute(block, 'gc', [(i, i ^ bits) for i in range(n_gc)])  5.27 us
    ppermute x4, waiting for transfers between devices, to_side(): return lax.ppermute(block, 'gc', pairs)  2.87 us
    pallas_call x1, Pallas kernels, on_device(): pl.pallas_call(early_kernel, out_shape=[jax.ShapeDtypeStruct((count, LANE...  1.95 us
    ppermute x4, starting transfers between devices, to_side(): return lax.ppermute(block, 'gc', pairs)  1.9 us
    pallas_call x2, Pallas kernels, last_sums(): pl.pallas_call(functools.partial(last_kernel, first, padded), out_shape=o...  1.47 us
  transfers between devices with their start and end apart: 16, of which 7 were waited for; matrix products, arithmetic and copies ran while one was open for 1% of the time, Pallas kernels for 6%

profile of v18, /device:TPU:0, one launch (start us, length us, event | category | flops | bytes accessed | tf_op | source)
XLA Modules:
  0.0 46.1 jit_solution(4607528072330877472)
XLA Ops:
  0.6 1.3 %sort_rows.1 = (bf16[256,256]{1,0:T(8,128)(2,1)S(1)}, bf16[64,768]{1,0:T(8,128)(2,1)S(1)}, bf16[64,768]{1,0:T(8,128)(2,1)S(1)}, bf16[64,768]{1,0:T(8,128)(2,1)S(1)}, bf16[64,768]{1,0:T(8,128)(2,1)S(1)}) custom-call(s32[1]{0:T(128)} %bitcast.own_ref, s32[1,256]{1,0:T(1,128)} %bitcast.3, bf16[256,768]{1,0:T(8,128)(2,1)} %rows_hbm.1), custom_call_target="tpu_custom_call" | custom-call | tf_op jit(solution)/shard_map/sort_rows/pallas_call | solution.py:198
  1.9 3.1 %collective-permute-start = (bf16[64,768]{1,0:T(8,128)(2,1)S(1)}, bf16[64,768]{1,0:T(8,128)(2,1)S(1)}, u32[]{:S(2)}, u32[]{:S(2)}) collective-permute-start(bf16[64,768]{1,0:T(8,128)(2,1)S(1)} %get-tuple-element.22), channel_id=1, source_target_pairs={{0,8},{8,0},{16,24},{24,16},{1,9},{9,1},{17,25},{25,17},{2,10},{10... | collective-permute-start | bytes 294920 | tf_op jit(solution)/shard_map/ppermute | solution.py:215
  5.0 2.5 %collective-permute-start.5 = (bf16[64,768]{1,0:T(8,128)(2,1)S(1)}, bf16[64,768]{1,0:T(8,128)(2,1)S(1)}, u32[]{:S(2)}, u32[]{:S(2)}) collective-permute-start(bf16[64,768]{1,0:T(8,128)(2,1)S(1)} %get-tuple-element.24), channel_id=1, source_target_pairs={{0,24},{8,16},{16,8},{24,0},{1,25},{9,17},{17,9},{25,1},{2,26},{10... | collective-permute-start | bytes 294920 | tf_op jit(solution)/shard_map/ppermute | solution.py:215
  7.5 0.1 collective-permute-start.4
  7.6 0.2 collective-permute-done
  7.8 2.8 %collective-permute-start.1 = (bf16[128,768]{1,0:T(8,128)(2,1)S(1)}, bf16[128,768]{1,0:T(8,128)(2,1)S(1)}, u32[]{:S(2)}, u32[]{:S(2)}) collective-permute-start(bf16[128,768]{1,0:T(8,128)(2,1)S(1)} %get-tuple-element.42), channel_id=1, source_target_pairs={{0,6},{1,7},{2,4},{3,5},{4,2},{5,3},{6,0},{7,1},{8,14},{9,15},{10,... | collective-permute-start | bytes 589832 | tf_op jit(solution)/shard_map/ppermute | solution.py:218
  10.6 0.5 %collective-permute-start.2 = (bf16[128,768]{1,0:T(8,128)(2,1)S(1)}, bf16[128,768]{1,0:T(8,128)(2,1)S(1)}, u32[]{:S(2)}, u32[]{:S(2)}) collective-permute-start(bf16[128,768]{1,0:T(8,128)(2,1)S(1)} %get-tuple-element.42), channel_id=1, source_target_pairs={{0,2},{1,5},{2,0},{3,7},{4,6},{5,1},{6,4},{7,3},{8,10},{9,13},{10,... | collective-permute-start | bytes 589832 | tf_op jit(solution)/shard_map/ppermute | solution.py:238
  11.1 0.3 collective-permute-start.3
  11.4 5.1 %collective-permute-done.4 = bf16[64,768]{1,0:T(8,128)(2,1)S(1)} collective-permute-done((bf16[64,768]{1,0:T(8,128)(2,1)S(1)}, bf16[64,768]{1,0:T(8,128)(2,1)S(1)}, u32[]{:S(2)}, u32[]{:S(2)}) %collective-permute-start.4) | collective-permute-done | bytes 98336 | tf_op jit(solution)/shard_map/ppermute | solution.py:215
  16.5 2.5 %collective-permute-start.7 = (bf16[128,768]{1,0:T(8,128)(2,1)S(1)}, bf16[128,768]{1,0:T(8,128)(2,1)S(1)}, u32[]{:S(2)}, u32[]{:S(2)}) collective-permute-start(bf16[128,768]{1,0:T(8,128)(2,1)S(1)} %get-tuple-element.38), channel_id=1, source_target_pairs={{0,6},{1,7},{2,4},{3,5},{4,2},{5,3},{6,0},{7,1},{8,14},{9,15},{10,... | collective-permute-start | bytes 589832 | tf_op jit(solution)/shard_map/ppermute | solution.py:218
  19.0 0.5 %collective-permute-start.8 = (bf16[128,768]{1,0:T(8,128)(2,1)S(1)}, bf16[128,768]{1,0:T(8,128)(2,1)S(1)}, u32[]{:S(2)}, u32[]{:S(2)}) collective-permute-start(bf16[128,768]{1,0:T(8,128)(2,1)S(1)} %get-tuple-element.38), channel_id=1, source_target_pairs={{0,2},{1,5},{2,0},{3,7},{4,6},{5,1},{6,4},{7,3},{8,10},{9,13},{10,... | collective-permute-start | bytes 589832 | tf_op jit(solution)/shard_map/ppermute | solution.py:238
  19.6 0.6 %collective-permute-start.9 = (bf16[128,768]{1,0:T(8,128)(2,1)S(1)}, bf16[128,768]{1,0:T(8,128)(2,1)S(1)}, u32[]{:S(2)}, u32[]{:S(2)}) collective-permute-start(bf16[128,768]{1,0:T(8,128)(2,1)S(1)} %get-tuple-element.38), channel_id=1, source_target_pairs={{0,4},{1,3},{2,6},{3,1},{4,0},{5,7},{6,2},{7,5},{8,12},{9,11},{10,... | collective-permute-start | bytes 589832 | tf_op jit(solution)/shard_map/ppermute | solution.py:238
  20.2 0.0 collective-permute-done.2
  20.2 0.0 collective-permute-done.3
  20.2 0.1 collective-permute-start.6
  20.3 5.0 %collective-permute-done.7 = bf16[128,768]{1,0:T(8,128)(2,1)S(1)} collective-permute-done((bf16[128,768]{1,0:T(8,128)(2,1)S(1)}, bf16[128,768]{1,0:T(8,128)(2,1)S(1)}, u32[]{:S(2)}, u32[]{:S(2)}) %collective-permute-start.7) | collective-permute-done | bytes 196640 | tf_op jit(solution)/shard_map/ppermute | solution.py:218
  25.3 2.9 %collective-permute-done.8 = bf16[128,768]{1,0:T(8,128)(2,1)S(1)} collective-permute-done((bf16[128,768]{1,0:T(8,128)(2,1)S(1)}, bf16[128,768]{1,0:T(8,128)(2,1)S(1)}, u32[]{:S(2)}, u32[]{:S(2)}) %collective-permute-start.8) | collective-permute-done | bytes 196640 | tf_op jit(solution)/shard_map/ppermute | solution.py:238
  28.2 0.0 collective-permute-done.9
  28.2 0.1 collective-permute-start.10
  28.3 2.0 %early_sums.1 = (f32[256,128]{1,0:T(8,128)S(1)}, f32[256,768]{1,0:T(8,128)S(1)}, f32[256,128]{1,0:T(8,128)S(1)}) custom-call(bf16[256,768]{1,0:T(8,128)(2,1)S(1)} %pad_maximum_fusion.rows_ref, bf16[512,768]{1,0:T(8,128)(2,1)S(1)} %constant_dynamic-update-slice_fusion.2.refs_0_, bf16[512,768]{1,0:T(8,128)(2,1)S(1)} %collective-permute-done.6.refs_1_, ...), custom_call_target="tpu_custom_call" | custom-call | flops 1207959552 | tf_op jit(solution)/shard_map/early_sums/pallas_call | solution.py:250
  30.3 0.3 collective-permute-done.10.cols_ref
  30.6 0.7 %far_sums.1 = (f32[64,768]{1,0:T(8,128)S(1)}, f32[64,768]{1,0:T(8,128)S(1)}, f32[8,128]{1,0:T(8,128)S(1)}, f32[8,128]{1,0:T(8,128)S(1)}) custom-call(bf16[256,768]{1,0:T(8,128)(2,1)S(1)} %pad_maximum_fusion.rows_ref, f32[256,128]{1,0:T(8,128)S(1)} %get-tuple-element.27.scale_ref, f32[256,768]{1,0:T(8,128)S(1)} %get-tuple-element.28.total_ref, ...), custom_call_target="tpu_custom_call" | custom-call | flops 402653184 | tf_op jit(solution)/shard_map/far_sums/pallas_call | solution.py:265
  31.3 2.9 %collective-permute-start.11 = (f16[64,768]{1,0:T(8,128)(2,1)S(1)}, f16[64,768]{1,0:T(8,128)(2,1)S(1)}, u32[]{:S(2)}, u32[]{:S(2)}) collective-permute-start(f16[64,768]{1,0:T(8,128)(2,1)S(1)} %convert_element_type.24), channel_id=1, source_target_pairs={{0,24},{8,16},{16,8},{24,0},{1,25},{9,17},{17,9},{25,1},{2,26},{10... | collective-permute-start | bytes 294920 | tf_op jit(solution)/shard_map/ppermute | solution.py:215
  34.2 0.1 collective-permute-start.12
  34.3 2.0 %collective-permute-start.13 = (f32[8,128]{1,0:T(8,128)S(1)}, f32[8,128]{1,0:T(8,128)S(1)}, u32[]{:S(2)}, u32[]{:S(2)}) collective-permute-start(f32[8,128]{1,0:T(8,128)S(1)} %get-tuple-element.32), channel_id=1, source_target_pairs={{0,24},{8,16},{16,8},{24,0},{1,25},{9,17},{17,9},{25,1},{2,26},{10... | collective-permute-start | bytes 12296 | tf_op jit(solution)/shard_map/ppermute | solution.py:215
  36.3 1.1 %collective-permute-start.14 = (f32[8,128]{1,0:T(8,128)S(1)}, f32[8,128]{1,0:T(8,128)S(1)}, u32[]{:S(2)}, u32[]{:S(2)}) collective-permute-start(f32[8,128]{1,0:T(8,128)S(1)} %get-tuple-element.33), channel_id=1, source_target_pairs={{0,16},{8,24},{16,0},{24,8},{1,17},{9,25},{17,1},{25,9},{2,18},{10... | collective-permute-start | bytes 12296 | tf_op jit(solution)/shard_map/ppermute | solution.py:215
  37.3 0.7 %near_sums.1 = (f32[72,768]{1,0:T(8,128)S(1)}, f32[72,768]{1,0:T(8,128)S(1)}) custom-call(bf16[256,768]{1,0:T(8,128)(2,1)S(1)} %pad_maximum_fusion.rows_ref, f32[256,128]{1,0:T(8,128)S(1)} %get-tuple-element.27.scale_ref, f32[256,768]{1,0:T(8,128)S(1)} %get-tuple-element.28.total_ref, f32[256,128]{1,0:T(8,128)S(1)} %get-tuple-element.29.dens_ref, ...), custom_call_target="tpu_custom_call" | custom-call | flops 402653184 | tf_op jit(solution)/shard_map/near_sums/pallas_call | solution.py:265
  38.1 1.5 %collective-permute-start.15 = (f16[72,768]{1,0:T(8,128)(2,1)S(1)}, f16[72,768]{1,0:T(8,128)(2,1)S(1)}, u32[]{:S(2)}, u32[]{:S(2)}) collective-permute-start(f16[72,768]{1,0:T(8,128)(2,1)S(1)} %convert_element_type.28), channel_id=1, source_target_pairs={{0,8},{8,0},{16,24},{24,16},{1,9},{9,1},{17,25},{25,17},{2,10},{10... | collective-permute-start | bytes 331784 | tf_op jit(solution)/shard_map/ppermute | solution.py:215
  39.6 0.0 collective-permute-done.11
  39.6 3.6 %collective-permute-done.12 = f16[64,768]{1,0:T(8,128)(2,1)S(1)} collective-permute-done((f16[64,768]{1,0:T(8,128)(2,1)S(1)}, f16[64,768]{1,0:T(8,128)(2,1)S(1)}, u32[]{:S(2)}, u32[]{:S(2)}) %collective-permute-start.12) | collective-permute-done | bytes 98336 | tf_op jit(solution)/shard_map/ppermute | solution.py:215
  43.2 1.4 %collective-permute-done.15 = f16[72,768]{1,0:T(8,128)(2,1)S(1)} collective-permute-done((f16[72,768]{1,0:T(8,128)(2,1)S(1)}, f16[72,768]{1,0:T(8,128)(2,1)S(1)}, u32[]{:S(2)}, u32[]{:S(2)}) %collective-permute-start.15) | collective-permute-done | bytes 110624 | tf_op jit(solution)/shard_map/ppermute | solution.py:215
  44.6 1.4 %restore_rows.1 = (f32[256,768]{1,0:T(8,128)}, f32[1,256]{1,0:T(1,128)}) custom-call(bf16[256,256]{1,0:T(8,128)(2,1)S(1)} %get-tuple-element.20.chosen_ref, f32[64,768]{1,0:T(8,128)S(1)} %convert_element_type.25.refs_0_, f32[64,768]{1,0:T(8,128)S(1)} %convert_element_type.27.refs_1_, f32[8,128]{1,0:T(8,128)S(1)} %collective-permute-done.13.refs_2_, ...), custom_call_target="tpu_custom_call" | custom-call | tf_op jit(solution)/shard_map/restore_rows/pallas_call | solution.py:285
  (23 shorter events, 0.3 us)
Async XLA Ops:
  1.9 5.9 %collective-permute-start = (bf16[64,768]{1,0:T(8,128)(2,1)S(1)}, bf16[64,768]{1,0:T(8,128)(2,1)S(1)}, u32[]{:S(2)}, u32[]{:S(2)}) collective-permute-start(bf16[64,768]{1,0:T(8,128)(2,1)S(1)} %get-tuple-element.22), channel_id=1, source_target_pairs={{0,8},{8,0},{16,24},{24,16},{1,9},{9,1},{17,25},{25,17},{2,10},{10... | collective-permute-start | bytes 294920 | tf_op jit(solution)/shard_map/ppermute | solution.py:215
  5.0 11.4 %collective-permute-start.5 = (bf16[64,768]{1,0:T(8,128)(2,1)S(1)}, bf16[64,768]{1,0:T(8,128)(2,1)S(1)}, u32[]{:S(2)}, u32[]{:S(2)}) collective-permute-start(bf16[64,768]{1,0:T(8,128)(2,1)S(1)} %get-tuple-element.24), channel_id=1, source_target_pairs={{0,24},{8,16},{16,8},{24,0},{1,25},{9,17},{17,9},{25,1},{2,26},{10... | collective-permute-start | bytes 294920 | tf_op jit(solution)/shard_map/ppermute | solution.py:215
  7.5 8.9 %collective-permute-start.4 = (bf16[64,768]{1,0:T(8,128)(2,1)S(1)}, bf16[64,768]{1,0:T(8,128)(2,1)S(1)}, u32[]{:S(2)}, u32[]{:S(2)}) collective-permute-start(bf16[64,768]{1,0:T(8,128)(2,1)S(1)} %get-tuple-element.23), channel_id=1, source_target_pairs={{0,16},{8,24},{16,0},{24,8},{1,17},{9,25},{17,1},{25,9},{2,18},{10... | collective-permute-start | bytes 294920 | tf_op jit(solution)/shard_map/ppermute | solution.py:215
  7.8 11.7 %collective-permute-start.1 = (bf16[128,768]{1,0:T(8,128)(2,1)S(1)}, bf16[128,768]{1,0:T(8,128)(2,1)S(1)}, u32[]{:S(2)}, u32[]{:S(2)}) collective-permute-start(bf16[128,768]{1,0:T(8,128)(2,1)S(1)} %get-tuple-element.42), channel_id=1, source_target_pairs={{0,6},{1,7},{2,4},{3,5},{4,2},{5,3},{6,0},{7,1},{8,14},{9,15},{10,... | collective-permute-start | bytes 589832 | tf_op jit(solution)/shard_map/ppermute | solution.py:218
  10.6 9.6 %collective-permute-start.2 = (bf16[128,768]{1,0:T(8,128)(2,1)S(1)}, bf16[128,768]{1,0:T(8,128)(2,1)S(1)}, u32[]{:S(2)}, u32[]{:S(2)}) collective-permute-start(bf16[128,768]{1,0:T(8,128)(2,1)S(1)} %get-tuple-element.42), channel_id=1, source_target_pairs={{0,2},{1,5},{2,0},{3,7},{4,6},{5,1},{6,4},{7,3},{8,10},{9,13},{10,... | collective-permute-start | bytes 589832 | tf_op jit(solution)/shard_map/ppermute | solution.py:238
  11.1 9.1 %collective-permute-start.3 = (bf16[128,768]{1,0:T(8,128)(2,1)S(1)}, bf16[128,768]{1,0:T(8,128)(2,1)S(1)}, u32[]{:S(2)}, u32[]{:S(2)}) collective-permute-start(bf16[128,768]{1,0:T(8,128)(2,1)S(1)} %get-tuple-element.42), channel_id=1, source_target_pairs={{0,4},{1,3},{2,6},{3,1},{4,0},{5,7},{6,2},{7,5},{8,12},{9,11},{10,... | collective-permute-start | bytes 589832 | tf_op jit(solution)/shard_map/ppermute | solution.py:238
  16.5 8.8 %collective-permute-start.7 = (bf16[128,768]{1,0:T(8,128)(2,1)S(1)}, bf16[128,768]{1,0:T(8,128)(2,1)S(1)}, u32[]{:S(2)}, u32[]{:S(2)}) collective-permute-start(bf16[128,768]{1,0:T(8,128)(2,1)S(1)} %get-tuple-element.38), channel_id=1, source_target_pairs={{0,6},{1,7},{2,4},{3,5},{4,2},{5,3},{6,0},{7,1},{8,14},{9,15},{10,... | collective-permute-start | bytes 589832 | tf_op jit(solution)/shard_map/ppermute | solution.py:218
  19.0 9.2 %collective-permute-start.8 = (bf16[128,768]{1,0:T(8,128)(2,1)S(1)}, bf16[128,768]{1,0:T(8,128)(2,1)S(1)}, u32[]{:S(2)}, u32[]{:S(2)}) collective-permute-start(bf16[128,768]{1,0:T(8,128)(2,1)S(1)} %get-tuple-element.38), channel_id=1, source_target_pairs={{0,2},{1,5},{2,0},{3,7},{4,6},{5,1},{6,4},{7,3},{8,10},{9,13},{10,... | collective-permute-start | bytes 589832 | tf_op jit(solution)/shard_map/ppermute | solution.py:238
  19.6 8.6 %collective-permute-start.9 = (bf16[128,768]{1,0:T(8,128)(2,1)S(1)}, bf16[128,768]{1,0:T(8,128)(2,1)S(1)}, u32[]{:S(2)}, u32[]{:S(2)}) collective-permute-start(bf16[128,768]{1,0:T(8,128)(2,1)S(1)} %get-tuple-element.38), channel_id=1, source_target_pairs={{0,4},{1,3},{2,6},{3,1},{4,0},{5,7},{6,2},{7,5},{8,12},{9,11},{10,... | collective-permute-start | bytes 589832 | tf_op jit(solution)/shard_map/ppermute | solution.py:238
  20.2 8.1 %collective-permute-start.6 = (bf16[512,768]{1,0:T(8,128)(2,1)S(1)}, bf16[512,768]{1,0:T(8,128)(2,1)S(1)}, u32[]{:S(2)}, u32[]{:S(2)}) collective-permute-start(bf16[512,768]{1,0:T(8,128)(2,1)S(1)} %constant_dynamic-update-slice_fusion.2.refs_0_), channel_id=1, source_target_pairs={{0,1},{1,0},{2,3},{3,2},{4,5},{5,4},{6,7},{7,6},{8,9},{9,8},{10,11... | collective-permute-start | bytes 2359304 | tf_op jit(solution)/shard_map/ppermute | solution.py:218
  28.2 2.4 %collective-permute-start.10 = (bf16[512,768]{1,0:T(8,128)(2,1)S(1)}, bf16[512,768]{1,0:T(8,128)(2,1)S(1)}, u32[]{:S(2)}, u32[]{:S(2)}) collective-permute-start(bf16[512,768]{1,0:T(8,128)(2,1)S(1)} %constant_dynamic-update-slice_fusion.9.refs_2_), channel_id=1, source_target_pairs={{0,1},{1,0},{2,3},{3,2},{4,5},{5,4},{6,7},{7,6},{8,9},{9,8},{10,11... | collective-permute-start | bytes 2359304 | tf_op jit(solution)/shard_map/ppermute | solution.py:218
  31.3 8.3 %collective-permute-start.11 = (f16[64,768]{1,0:T(8,128)(2,1)S(1)}, f16[64,768]{1,0:T(8,128)(2,1)S(1)}, u32[]{:S(2)}, u32[]{:S(2)}) collective-permute-start(f16[64,768]{1,0:T(8,128)(2,1)S(1)} %convert_element_type.24), channel_id=1, source_target_pairs={{0,24},{8,16},{16,8},{24,0},{1,25},{9,17},{17,9},{25,1},{2,26},{10... | collective-permute-start | bytes 294920 | tf_op jit(solution)/shard_map/ppermute | solution.py:215
  34.2 9.0 %collective-permute-start.12 = (f16[64,768]{1,0:T(8,128)(2,1)S(1)}, f16[64,768]{1,0:T(8,128)(2,1)S(1)}, u32[]{:S(2)}, u32[]{:S(2)}) collective-permute-start(f16[64,768]{1,0:T(8,128)(2,1)S(1)} %convert_element_type.26), channel_id=1, source_target_pairs={{0,16},{8,24},{16,0},{24,8},{1,17},{9,25},{17,1},{25,9},{2,18},{10... | collective-permute-start | bytes 294920 | tf_op jit(solution)/shard_map/ppermute | solution.py:215
  34.3 10.3 %collective-permute-start.13 = (f32[8,128]{1,0:T(8,128)S(1)}, f32[8,128]{1,0:T(8,128)S(1)}, u32[]{:S(2)}, u32[]{:S(2)}) collective-permute-start(f32[8,128]{1,0:T(8,128)S(1)} %get-tuple-element.32), channel_id=1, source_target_pairs={{0,24},{8,16},{16,8},{24,0},{1,25},{9,17},{17,9},{25,1},{2,26},{10... | collective-permute-start | bytes 12296 | tf_op jit(solution)/shard_map/ppermute | solution.py:215
  36.3 8.4 %collective-permute-start.14 = (f32[8,128]{1,0:T(8,128)S(1)}, f32[8,128]{1,0:T(8,128)S(1)}, u32[]{:S(2)}, u32[]{:S(2)}) collective-permute-start(f32[8,128]{1,0:T(8,128)S(1)} %get-tuple-element.33), channel_id=1, source_target_pairs={{0,16},{8,24},{16,0},{24,8},{1,17},{9,25},{17,1},{25,9},{2,18},{10... | collective-permute-start | bytes 12296 | tf_op jit(solution)/shard_map/ppermute | solution.py:215
  38.1 6.5 %collective-permute-start.15 = (f16[72,768]{1,0:T(8,128)(2,1)S(1)}, f16[72,768]{1,0:T(8,128)(2,1)S(1)}, u32[]{:S(2)}, u32[]{:S(2)}) collective-permute-start(f16[72,768]{1,0:T(8,128)(2,1)S(1)} %convert_element_type.28), channel_id=1, source_target_pairs={{0,8},{8,0},{16,24},{24,16},{1,9},{9,1},{17,25},{25,17},{2,10},{10... | collective-permute-start | bytes 331784 | tf_op jit(solution)/shard_map/ppermute | solution.py:215

commit v19 on v16

--- a/solution.py
+++ b/solution.py
@@ -235,9 +235,9 @@
     chunks = []
     for k, pieces in enumerate((held[:half], held[half:])):
         block = jnp.concatenate(pieces, axis=0)
-        side_blocks = [to_side(block, step) for step in range(len(sides))]
-        corner_blocks = [along_gc(block, bits) for bits in corners]
-        near = [block] + (corner_blocks + side_blocks if k else side_blocks + corner_blocks)
+        near = [block] + [to_side(block, step) for step in range(k)]
+        near += [along_gc(block, bits) for bits in corners]
+        near += [to_side(block, step) for step in range(k, len(sides))]
         chunks.append(jnp.concatenate(near, axis=0))
     rows = jnp.concatenate(held, axis=0)
     chunks[0], rows = lax.optimization_barrier((chunks[0], rows))

time: 45.4 us -> 45.6 us (level)
  waiting for transfers between devices: 17.7 us -> 19 us
  starting transfers between devices: 20.8 us -> 19.8 us
    ppermute x4, starting transfers between devices: 4.43 us -> 2.92 us  [to_side(): return lax.ppermute(block, 'gc', pairs)]
    ppermute x4, starting transfers between devices: 2.89 us -> 4.39 us  [along_gc(): return lax.ppermute(block, 'gc', [(i, i ^ bits) for i in range(n_gc)])]
    ppermute x4, waiting for transfers between devices: 2.83 us -> 4.02 us  [to_side(): return lax.ppermute(block, 'gc', pairs)]
    ppermute x8, starting transfers between devices: 13.5 us -> 12.5 us  [along_gr(): return lax.ppermute(part, 'gr', [(i, i ^ bits) for i in range(n_gr)])]
  transfers between devices with their start and end apart: 16 -> 16, of which waited for: 7 -> 8; matrix products, arithmetic and copies ran while one was open for 1% -> 1% of each run, Pallas kernels for 4% -> 4%
where the time goes in v19:
time: 45.6 us; the launch traced here: 45.5 us
  starting transfers between devices  19.8 us (43%)
  waiting for transfers between devices  19 us (42%)
  Pallas kernels  5.56 us (12%)
  between operations  0.83 us (2%)
    ppermute x8, starting transfers between devices, along_gr(): return lax.ppermute(part, 'gr', [(i, i ^ bits) for i in range(n_gr)])  12.5 us
    ppermute x8, waiting for transfers between devices, along_gr(): return lax.ppermute(part, 'gr', [(i, i ^ bits) for i in range(n_gr)])  9.74 us
    ppermute x4, waiting for transfers between devices, along_gc(): return lax.ppermute(block, 'gc', [(i, i ^ bits) for i in range(n_gc)])  5.26 us
    ppermute x4, starting transfers between devices, along_gc(): return lax.ppermute(block, 'gc', [(i, i ^ bits) for i in range(n_gc)])  4.39 us
    ppermute x4, waiting for transfers between devices, to_side(): return lax.ppermute(block, 'gc', pairs)  4.02 us
    ppermute x4, starting transfers between devices, to_side(): return lax.ppermute(block, 'gc', pairs)  2.92 us
    pallas_call x1, Pallas kernels, on_device(): pl.pallas_call(early_kernel, out_shape=[jax.ShapeDtypeStruct((count, LANE...  1.95 us
    pallas_call x1, Pallas kernels, on_device(): pl.pallas_call(functools.partial(restore_kernel, half), out_shape=[jax.Sh...  1.44 us
  transfers between devices with their start and end apart: 16, of which 8 were waited for; matrix products, arithmetic and copies ran while one was open for 1% of the time, Pallas kernels for 4%

profile of v19, /device:TPU:0, one launch (start us, length us, event | category | flops | bytes accessed | tf_op | source)
XLA Modules:
  0.0 45.5 jit_solution(17212455967452482440)
XLA Ops:
  0.6 1.3 %sort_rows.1 = (bf16[256,256]{1,0:T(8,128)(2,1)S(1)}, bf16[64,768]{1,0:T(8,128)(2,1)S(1)}, bf16[64,768]{1,0:T(8,128)(2,1)S(1)}, bf16[64,768]{1,0:T(8,128)(2,1)S(1)}, bf16[64,768]{1,0:T(8,128)(2,1)S(1)}) custom-call(s32[1]{0:T(128)} %bitcast.own_ref, s32[1,256]{1,0:T(1,128)} %bitcast.3, bf16[256,768]{1,0:T(8,128)(2,1)} %rows_hbm.1), custom_call_target="tpu_custom_call" | custom-call | tf_op jit(solution)/shard_map/sort_rows/pallas_call | solution.py:193
  1.9 3.1 %collective-permute-start = (bf16[64,768]{1,0:T(8,128)(2,1)S(1)}, bf16[64,768]{1,0:T(8,128)(2,1)S(1)}, u32[]{:S(2)}, u32[]{:S(2)}) collective-permute-start(bf16[64,768]{1,0:T(8,128)(2,1)S(1)} %get-tuple-element.22), channel_id=1, source_target_pairs={{0,8},{8,0},{16,24},{24,16},{1,9},{9,1},{17,25},{25,17},{2,10},{10... | collective-permute-start | bytes 294920 | tf_op jit(solution)/shard_map/ppermute | solution.py:210
  5.0 2.5 %collective-permute-start.5 = (bf16[64,768]{1,0:T(8,128)(2,1)S(1)}, bf16[64,768]{1,0:T(8,128)(2,1)S(1)}, u32[]{:S(2)}, u32[]{:S(2)}) collective-permute-start(bf16[64,768]{1,0:T(8,128)(2,1)S(1)} %get-tuple-element.24), channel_id=1, source_target_pairs={{0,24},{8,16},{16,8},{24,0},{1,25},{9,17},{17,9},{25,1},{2,26},{10... | collective-permute-start | bytes 294920 | tf_op jit(solution)/shard_map/ppermute | solution.py:210
  7.5 0.1 collective-permute-start.4
  7.6 0.2 collective-permute-done
  7.8 2.8 %collective-permute-start.1 = (bf16[128,768]{1,0:T(8,128)(2,1)S(1)}, bf16[128,768]{1,0:T(8,128)(2,1)S(1)}, u32[]{:S(2)}, u32[]{:S(2)}) collective-permute-start(bf16[128,768]{1,0:T(8,128)(2,1)S(1)} %get-tuple-element.42), channel_id=1, source_target_pairs={{0,6},{1,7},{2,4},{3,5},{4,2},{5,3},{6,0},{7,1},{8,14},{9,15},{10,... | collective-permute-start | bytes 589832 | tf_op jit(solution)/shard_map/ppermute | solution.py:213
  10.6 0.5 %collective-permute-start.2 = (bf16[128,768]{1,0:T(8,128)(2,1)S(1)}, bf16[128,768]{1,0:T(8,128)(2,1)S(1)}, u32[]{:S(2)}, u32[]{:S(2)}) collective-permute-start(bf16[128,768]{1,0:T(8,128)(2,1)S(1)} %get-tuple-element.42), channel_id=1, source_target_pairs={{0,2},{1,5},{2,0},{3,7},{4,6},{5,1},{6,4},{7,3},{8,10},{9,13},{10,... | collective-permute-start | bytes 589832 | tf_op jit(solution)/shard_map/ppermute | solution.py:233
  11.1 0.3 collective-permute-start.3
  11.4 5.1 %collective-permute-done.4 = bf16[64,768]{1,0:T(8,128)(2,1)S(1)} collective-permute-done((bf16[64,768]{1,0:T(8,128)(2,1)S(1)}, bf16[64,768]{1,0:T(8,128)(2,1)S(1)}, u32[]{:S(2)}, u32[]{:S(2)}) %collective-permute-start.4) | collective-permute-done | bytes 98336 | tf_op jit(solution)/shard_map/ppermute | solution.py:210
  16.5 0.0 collective-permute-done.5
  16.5 1.6 %collective-permute-start.7 = (bf16[128,768]{1,0:T(8,128)(2,1)S(1)}, bf16[128,768]{1,0:T(8,128)(2,1)S(1)}, u32[]{:S(2)}, u32[]{:S(2)}) collective-permute-start(bf16[128,768]{1,0:T(8,128)(2,1)S(1)} %get-tuple-element.38), channel_id=1, source_target_pairs={{0,2},{1,5},{2,0},{3,7},{4,6},{5,1},{6,4},{7,3},{8,10},{9,13},{10,... | collective-permute-start | bytes 589832 | tf_op jit(solution)/shard_map/ppermute | solution.py:233
  18.1 1.5 %collective-permute-start.8 = (bf16[128,768]{1,0:T(8,128)(2,1)S(1)}, bf16[128,768]{1,0:T(8,128)(2,1)S(1)}, u32[]{:S(2)}, u32[]{:S(2)}) collective-permute-start(bf16[128,768]{1,0:T(8,128)(2,1)S(1)} %get-tuple-element.38), channel_id=1, source_target_pairs={{0,6},{1,7},{2,4},{3,5},{4,2},{5,3},{6,0},{7,1},{8,14},{9,15},{10,... | collective-permute-start | bytes 589832 | tf_op jit(solution)/shard_map/ppermute | solution.py:213
  19.6 0.0 collective-permute-done.1
  19.6 0.6 %collective-permute-start.9 = (bf16[128,768]{1,0:T(8,128)(2,1)S(1)}, bf16[128,768]{1,0:T(8,128)(2,1)S(1)}, u32[]{:S(2)}, u32[]{:S(2)}) collective-permute-start(bf16[128,768]{1,0:T(8,128)(2,1)S(1)} %get-tuple-element.38), channel_id=1, source_target_pairs={{0,4},{1,3},{2,6},{3,1},{4,0},{5,7},{6,2},{7,5},{8,12},{9,11},{10,... | collective-permute-start | bytes 589832 | tf_op jit(solution)/shard_map/ppermute | solution.py:233
  20.2 0.1 collective-permute-start.6
  20.3 4.0 %collective-permute-done.7 = bf16[128,768]{1,0:T(8,128)(2,1)S(1)} collective-permute-done((bf16[128,768]{1,0:T(8,128)(2,1)S(1)}, bf16[128,768]{1,0:T(8,128)(2,1)S(1)}, u32[]{:S(2)}, u32[]{:S(2)}) %collective-permute-start.7) | collective-permute-done | bytes 196640 | tf_op jit(solution)/shard_map/ppermute | solution.py:233
  24.4 4.9 %collective-permute-done.8 = bf16[128,768]{1,0:T(8,128)(2,1)S(1)} collective-permute-done((bf16[128,768]{1,0:T(8,128)(2,1)S(1)}, bf16[128,768]{1,0:T(8,128)(2,1)S(1)}, u32[]{:S(2)}, u32[]{:S(2)}) %collective-permute-start.8) | collective-permute-done | bytes 196640 | tf_op jit(solution)/shard_map/ppermute | solution.py:213
  29.3 0.0 collective-permute-done.9
  29.4 0.1 collective-permute-start.10
  29.4 0.0 collective-permute-done.6.refs_1_
  29.5 1.9 %early_sums.1 = (f32[256,128]{1,0:T(8,128)S(1)}, f32[256,768]{1,0:T(8,128)S(1)}, f32[256,128]{1,0:T(8,128)S(1)}) custom-call(bf16[256,768]{1,0:T(8,128)(2,1)S(1)} %pad_maximum_fusion.rows_ref, bf16[512,768]{1,0:T(8,128)(2,1)S(1)} %constant_dynamic-update-slice_fusion.2.refs_0_, bf16[512,768]{1,0:T(8,128)(2,1)S(1)} %collective-permute-done.6.refs_1_, ...), custom_call_target="tpu_custom_call" | custom-call | flops 1207959552 | tf_op jit(solution)/shard_map/early_sums/pallas_call | solution.py:246
  31.4 0.3 collective-permute-done.10.cols_ref
  31.7 0.9 %last_sums.1 = (f32[72,768]{1,0:T(8,128)S(1)}, f32[72,768]{1,0:T(8,128)S(1)}, f32[64,768]{1,0:T(8,128)S(1)}, f32[64,768]{1,0:T(8,128)S(1)}, f32[8,128]{1,0:T(8,128)S(1)}, /*index=5*/f32[8,128]{1,0:T(8,128)S(1)}) custom-call(bf16[256,768]{1,0:T(8,128)(2,1)S(1)} %pad_maximum_fusion.rows_ref, f32[256,128]{1,0:T(8,128)S(1)} %get-tuple-element.27.scale_ref, ...), custom_call_target="tpu_custom_call" | custom-call | flops 402653184 | tf_op jit(solution)/shard_map/last_sums/pallas_call | solution.py:260
  32.6 2.3 %collective-permute-start.11 = (f16[64,768]{1,0:T(8,128)(2,1)S(1)}, f16[64,768]{1,0:T(8,128)(2,1)S(1)}, u32[]{:S(2)}, u32[]{:S(2)}) collective-permute-start(f16[64,768]{1,0:T(8,128)(2,1)S(1)} %convert_element_type.24), channel_id=1, source_target_pairs={{0,24},{8,16},{16,8},{24,0},{1,25},{9,17},{17,9},{25,1},{2,26},{10... | collective-permute-start | bytes 294920 | tf_op jit(solution)/shard_map/ppermute | solution.py:210
  34.9 0.1 collective-permute-start.12
  35.0 2.2 %collective-permute-start.13 = (f16[72,768]{1,0:T(8,128)(2,1)S(1)}, f16[72,768]{1,0:T(8,128)(2,1)S(1)}, u32[]{:S(2)}, u32[]{:S(2)}) collective-permute-start(f16[72,768]{1,0:T(8,128)(2,1)S(1)} %convert_element_type.28), channel_id=1, source_target_pairs={{0,8},{8,0},{16,24},{24,16},{1,9},{9,1},{17,25},{25,17},{2,10},{10... | collective-permute-start | bytes 331784 | tf_op jit(solution)/shard_map/ppermute | solution.py:210
  37.2 2.2 %collective-permute-start.14 = (f32[8,128]{1,0:T(8,128)S(1)}, f32[8,128]{1,0:T(8,128)S(1)}, u32[]{:S(2)}, u32[]{:S(2)}) collective-permute-start(f32[8,128]{1,0:T(8,128)S(1)} %get-tuple-element.34), channel_id=1, source_target_pairs={{0,24},{8,16},{16,8},{24,0},{1,25},{9,17},{17,9},{25,1},{2,26},{10... | collective-permute-start | bytes 12296 | tf_op jit(solution)/shard_map/ppermute | solution.py:210
  39.5 0.7 %collective-permute-done.11 = f16[64,768]{1,0:T(8,128)(2,1)S(1)} collective-permute-done((f16[64,768]{1,0:T(8,128)(2,1)S(1)}, f16[64,768]{1,0:T(8,128)(2,1)S(1)}, u32[]{:S(2)}, u32[]{:S(2)}) %collective-permute-start.11) | collective-permute-done | bytes 98336 | tf_op jit(solution)/shard_map/ppermute | solution.py:210
  40.2 3.6 %collective-permute-done.12 = f16[64,768]{1,0:T(8,128)(2,1)S(1)} collective-permute-done((f16[64,768]{1,0:T(8,128)(2,1)S(1)}, f16[64,768]{1,0:T(8,128)(2,1)S(1)}, u32[]{:S(2)}, u32[]{:S(2)}) %collective-permute-start.12) | collective-permute-done | bytes 98336 | tf_op jit(solution)/shard_map/ppermute | solution.py:210
  43.8 0.2 collective-permute-done.13
  44.0 0.0 collective-permute-done.14.refs_4_
  44.0 1.4 %restore_rows.1 = (f32[256,768]{1,0:T(8,128)}, f32[1,256]{1,0:T(1,128)}) custom-call(bf16[256,256]{1,0:T(8,128)(2,1)S(1)} %get-tuple-element.20.chosen_ref, f32[64,768]{1,0:T(8,128)S(1)} %convert_element_type.25.refs_0_, f32[64,768]{1,0:T(8,128)S(1)} %convert_element_type.27.refs_1_, f32[72,768]{1,0:T(8,128)S(1)} %convert_element_type.29.refs_2_, ...), custom_call_target="tpu_custom_call" | custom-call | tf_op jit(solution)/shard_map/restore_rows/pallas_call | solution.py:276
  (22 shorter events, 0.3 us)
Async XLA Ops:
  1.9 5.9 %collective-permute-start = (bf16[64,768]{1,0:T(8,128)(2,1)S(1)}, bf16[64,768]{1,0:T(8,128)(2,1)S(1)}, u32[]{:S(2)}, u32[]{:S(2)}) collective-permute-start(bf16[64,768]{1,0:T(8,128)(2,1)S(1)} %get-tuple-element.22), channel_id=1, source_target_pairs={{0,8},{8,0},{16,24},{24,16},{1,9},{9,1},{17,25},{25,17},{2,10},{10... | collective-permute-start | bytes 294920 | tf_op jit(solution)/shard_map/ppermute | solution.py:210
  5.0 11.4 %collective-permute-start.5 = (bf16[64,768]{1,0:T(8,128)(2,1)S(1)}, bf16[64,768]{1,0:T(8,128)(2,1)S(1)}, u32[]{:S(2)}, u32[]{:S(2)}) collective-permute-start(bf16[64,768]{1,0:T(8,128)(2,1)S(1)} %get-tuple-element.24), channel_id=1, source_target_pairs={{0,24},{8,16},{16,8},{24,0},{1,25},{9,17},{17,9},{25,1},{2,26},{10... | collective-permute-start | bytes 294920 | tf_op jit(solution)/shard_map/ppermute | solution.py:210
  7.5 8.9 %collective-permute-start.4 = (bf16[64,768]{1,0:T(8,128)(2,1)S(1)}, bf16[64,768]{1,0:T(8,128)(2,1)S(1)}, u32[]{:S(2)}, u32[]{:S(2)}) collective-permute-start(bf16[64,768]{1,0:T(8,128)(2,1)S(1)} %get-tuple-element.23), channel_id=1, source_target_pairs={{0,16},{8,24},{16,0},{24,8},{1,17},{9,25},{17,1},{25,9},{2,18},{10... | collective-permute-start | bytes 294920 | tf_op jit(solution)/shard_map/ppermute | solution.py:210
  7.8 11.7 %collective-permute-start.1 = (bf16[128,768]{1,0:T(8,128)(2,1)S(1)}, bf16[128,768]{1,0:T(8,128)(2,1)S(1)}, u32[]{:S(2)}, u32[]{:S(2)}) collective-permute-start(bf16[128,768]{1,0:T(8,128)(2,1)S(1)} %get-tuple-element.42), channel_id=1, source_target_pairs={{0,6},{1,7},{2,4},{3,5},{4,2},{5,3},{6,0},{7,1},{8,14},{9,15},{10,... | collective-permute-start | bytes 589832 | tf_op jit(solution)/shard_map/ppermute | solution.py:213
  10.6 9.6 %collective-permute-start.2 = (bf16[128,768]{1,0:T(8,128)(2,1)S(1)}, bf16[128,768]{1,0:T(8,128)(2,1)S(1)}, u32[]{:S(2)}, u32[]{:S(2)}) collective-permute-start(bf16[128,768]{1,0:T(8,128)(2,1)S(1)} %get-tuple-element.42), channel_id=1, source_target_pairs={{0,2},{1,5},{2,0},{3,7},{4,6},{5,1},{6,4},{7,3},{8,10},{9,13},{10,... | collective-permute-start | bytes 589832 | tf_op jit(solution)/shard_map/ppermute | solution.py:233
  11.1 9.1 %collective-permute-start.3 = (bf16[128,768]{1,0:T(8,128)(2,1)S(1)}, bf16[128,768]{1,0:T(8,128)(2,1)S(1)}, u32[]{:S(2)}, u32[]{:S(2)}) collective-permute-start(bf16[128,768]{1,0:T(8,128)(2,1)S(1)} %get-tuple-element.42), channel_id=1, source_target_pairs={{0,4},{1,3},{2,6},{3,1},{4,0},{5,7},{6,2},{7,5},{8,12},{9,11},{10,... | collective-permute-start | bytes 589832 | tf_op jit(solution)/shard_map/ppermute | solution.py:233
  16.5 7.8 %collective-permute-start.7 = (bf16[128,768]{1,0:T(8,128)(2,1)S(1)}, bf16[128,768]{1,0:T(8,128)(2,1)S(1)}, u32[]{:S(2)}, u32[]{:S(2)}) collective-permute-start(bf16[128,768]{1,0:T(8,128)(2,1)S(1)} %get-tuple-element.38), channel_id=1, source_target_pairs={{0,2},{1,5},{2,0},{3,7},{4,6},{5,1},{6,4},{7,3},{8,10},{9,13},{10,... | collective-permute-start | bytes 589832 | tf_op jit(solution)/shard_map/ppermute | solution.py:233
  18.1 11.3 %collective-permute-start.8 = (bf16[128,768]{1,0:T(8,128)(2,1)S(1)}, bf16[128,768]{1,0:T(8,128)(2,1)S(1)}, u32[]{:S(2)}, u32[]{:S(2)}) collective-permute-start(bf16[128,768]{1,0:T(8,128)(2,1)S(1)} %get-tuple-element.38), channel_id=1, source_target_pairs={{0,6},{1,7},{2,4},{3,5},{4,2},{5,3},{6,0},{7,1},{8,14},{9,15},{10,... | collective-permute-start | bytes 589832 | tf_op jit(solution)/shard_map/ppermute | solution.py:213
  19.6 9.7 %collective-permute-start.9 = (bf16[128,768]{1,0:T(8,128)(2,1)S(1)}, bf16[128,768]{1,0:T(8,128)(2,1)S(1)}, u32[]{:S(2)}, u32[]{:S(2)}) collective-permute-start(bf16[128,768]{1,0:T(8,128)(2,1)S(1)} %get-tuple-element.38), channel_id=1, source_target_pairs={{0,4},{1,3},{2,6},{3,1},{4,0},{5,7},{6,2},{7,5},{8,12},{9,11},{10,... | collective-permute-start | bytes 589832 | tf_op jit(solution)/shard_map/ppermute | solution.py:233
  20.2 9.2 %collective-permute-start.6 = (bf16[512,768]{1,0:T(8,128)(2,1)S(1)}, bf16[512,768]{1,0:T(8,128)(2,1)S(1)}, u32[]{:S(2)}, u32[]{:S(2)}) collective-permute-start(bf16[512,768]{1,0:T(8,128)(2,1)S(1)} %constant_dynamic-update-slice_fusion.2.refs_0_), channel_id=1, source_target_pairs={{0,1},{1,0},{2,3},{3,2},{4,5},{5,4},{6,7},{7,6},{8,9},{9,8},{10,11... | collective-permute-start | bytes 2359304 | tf_op jit(solution)/shard_map/ppermute | solution.py:213
  29.4 2.4 %collective-permute-start.10 = (bf16[512,768]{1,0:T(8,128)(2,1)S(1)}, bf16[512,768]{1,0:T(8,128)(2,1)S(1)}, u32[]{:S(2)}, u32[]{:S(2)}) collective-permute-start(bf16[512,768]{1,0:T(8,128)(2,1)S(1)} %constant_dynamic-update-slice_fusion.9.refs_2_), channel_id=1, source_target_pairs={{0,1},{1,0},{2,3},{3,2},{4,5},{5,4},{6,7},{7,6},{8,9},{9,8},{10,11... | collective-permute-start | bytes 2359304 | tf_op jit(solution)/shard_map/ppermute | solution.py:213
  32.6 7.6 %collective-permute-start.11 = (f16[64,768]{1,0:T(8,128)(2,1)S(1)}, f16[64,768]{1,0:T(8,128)(2,1)S(1)}, u32[]{:S(2)}, u32[]{:S(2)}) collective-permute-start(f16[64,768]{1,0:T(8,128)(2,1)S(1)} %convert_element_type.24), channel_id=1, source_target_pairs={{0,24},{8,16},{16,8},{24,0},{1,25},{9,17},{17,9},{25,1},{2,26},{10... | collective-permute-start | bytes 294920 | tf_op jit(solution)/shard_map/ppermute | solution.py:210
  34.9 8.9 %collective-permute-start.12 = (f16[64,768]{1,0:T(8,128)(2,1)S(1)}, f16[64,768]{1,0:T(8,128)(2,1)S(1)}, u32[]{:S(2)}, u32[]{:S(2)}) collective-permute-start(f16[64,768]{1,0:T(8,128)(2,1)S(1)} %convert_element_type.26), channel_id=1, source_target_pairs={{0,16},{8,24},{16,0},{24,8},{1,17},{9,25},{17,1},{25,9},{2,18},{10... | collective-permute-start | bytes 294920 | tf_op jit(solution)/shard_map/ppermute | solution.py:210
  35.0 9.0 %collective-permute-start.13 = (f16[72,768]{1,0:T(8,128)(2,1)S(1)}, f16[72,768]{1,0:T(8,128)(2,1)S(1)}, u32[]{:S(2)}, u32[]{:S(2)}) collective-permute-start(f16[72,768]{1,0:T(8,128)(2,1)S(1)} %convert_element_type.28), channel_id=1, source_target_pairs={{0,8},{8,0},{16,24},{24,16},{1,9},{9,1},{17,25},{25,17},{2,10},{10... | collective-permute-start | bytes 331784 | tf_op jit(solution)/shard_map/ppermute | solution.py:210
  37.2 6.8 %collective-permute-start.14 = (f32[8,128]{1,0:T(8,128)S(1)}, f32[8,128]{1,0:T(8,128)S(1)}, u32[]{:S(2)}, u32[]{:S(2)}) collective-permute-start(f32[8,128]{1,0:T(8,128)S(1)} %get-tuple-element.34), channel_id=1, source_target_pairs={{0,24},{8,16},{16,8},{24,0},{1,25},{9,17},{17,9},{25,1},{2,26},{10... | collective-permute-start | bytes 12296 | tf_op jit(solution)/shard_map/ppermute | solution.py:210
  39.5 4.6 %collective-permute-start.15 = (f32[8,128]{1,0:T(8,128)S(1)}, f32[8,128]{1,0:T(8,128)S(1)}, u32[]{:S(2)}, u32[]{:S(2)}) collective-permute-start(f32[8,128]{1,0:T(8,128)S(1)} %get-tuple-element.35), channel_id=1, source_target_pairs={{0,16},{8,24},{16,0},{24,8},{1,17},{9,25},{17,1},{25,9},{2,18},{10... | collective-permute-start | bytes 12296 | tf_op jit(solution)/shard_map/ppermute | solution.py:210

commit v20 on v10

--- a/solution.py
+++ b/solution.py
@@ -61,14 +61,24 @@
     ids_ref, rows_ref, ids_sem, rows_sem = refs[-4:]
     groups = len(out_refs)
     ids_copy = pltpu.make_async_copy(ids_hbm, ids_ref, ids_sem)
-    rows_copy = pltpu.make_async_copy(rows_hbm, rows_ref, rows_sem)
+    count = rows_hbm.shape[0]
+    halves = [slice(0, count // 2), slice(count // 2, count)]
+    row_copies = [
+        pltpu.make_async_copy(rows_hbm.at[half], rows_ref.at[half], rows_sem.at[k])
+        for k, half in enumerate(halves)
+    ]
     ids_copy.start()
-    rows_copy.start()
+    for row_copy in row_copies:
+        row_copy.start()
     ids_copy.wait()
     chosen = placement(own_ref[0], ids_ref[...], groups).astype(jnp.bfloat16)
     chosen_ref[...] = chosen
-    rows_copy.wait()
-    ordered = jnp.dot(chosen, rows_ref[...], preferred_element_type=jnp.float32)
+    ordered = 0.0
+    for row_copy, half in zip(row_copies, halves):
+        row_copy.wait()
+        ordered += jnp.dot(
+            chosen[:, half], rows_ref[half, :], preferred_element_type=jnp.float32
+        )
     ordered = ordered.astype(jnp.bfloat16)
     size = ordered.shape[0] // groups
     for k, out_ref in enumerate(out_refs):
@@ -200,7 +210,7 @@
             pltpu.VMEM((1, count), jnp.int32),
             pltpu.VMEM((count, width), embeddings.dtype),
             pltpu.SemaphoreType.DMA,
-            pltpu.SemaphoreType.DMA,
+            pltpu.SemaphoreType.DMA((2,)),
         ],
         compiler_params=GRANT,
         name="sort_rows",

time: 45 us -> 45.1 us (level)
  no operation moved by 1% of the time
where the time goes in v20:
time: 45.1 us; the launch traced here: 45 us
  starting transfers between devices  20.4 us (45%)
  waiting for transfers between devices  17.8 us (39%)
  Pallas kernels  5.67 us (13%)
  between operations  0.85 us (2%)
    ppermute x8, starting transfers between devices, along_gr(): return lax.ppermute(part, 'gr', [(i, i ^ bits) for i in range(n_gr)])  13.1 us
    ppermute x8, waiting for transfers between devices, along_gr(): return lax.ppermute(part, 'gr', [(i, i ^ bits) for i in range(n_gr)])  9.65 us
    ppermute x4, starting transfers between devices, along_gc(): return lax.ppermute(block, 'gc', [(i, i ^ bits) for i in range(n_gc)])  5.41 us
    ppermute x4, waiting for transfers between devices, along_gc(): return lax.ppermute(block, 'gc', [(i, i ^ bits) for i in range(n_gc)])  5.28 us
    ppermute x4, waiting for transfers between devices, to_side(): return lax.ppermute(block, 'gc', pairs)  2.87 us
    pallas_call x1, Pallas kernels, on_device(): pl.pallas_call(early_kernel, out_shape=[jax.ShapeDtypeStruct((count, LANE...  1.95 us
    ppermute x4, starting transfers between devices, to_side(): return lax.ppermute(block, 'gc', pairs)  1.9 us
    pallas_call x1, Pallas kernels, on_device(): pl.pallas_call(functools.partial(restore_kernel, half), out_shape=[jax.Sh...  1.44 us
  transfers between devices with their start and end apart: 16, of which 7 were waited for; matrix products, arithmetic and copies ran while one was open for 1% of the time, Pallas kernels for 4%

profile of v20, /device:TPU:0, one launch (start us, length us, event | category | flops | bytes accessed | tf_op | source)
XLA Modules:
  0.0 45.0 jit_solution(4621458715984592889)
XLA Ops:
  0.6 1.4 %sort_rows.1 = (bf16[256,256]{1,0:T(8,128)(2,1)S(1)}, bf16[64,768]{1,0:T(8,128)(2,1)S(1)}, bf16[64,768]{1,0:T(8,128)(2,1)S(1)}, bf16[64,768]{1,0:T(8,128)(2,1)S(1)}, bf16[64,768]{1,0:T(8,128)(2,1)S(1)}) custom-call(s32[1]{0:T(128)} %bitcast.own_ref, s32[1,256]{1,0:T(1,128)} %bitcast.3, bf16[256,768]{1,0:T(8,128)(2,1)} %rows_hbm.1), custom_call_target="tpu_custom_call" | custom-call | tf_op jit(solution)/shard_map/sort_rows/pallas_call | solution.py:203
  2.1 3.1 %collective-permute-start = (bf16[64,768]{1,0:T(8,128)(2,1)S(1)}, bf16[64,768]{1,0:T(8,128)(2,1)S(1)}, u32[]{:S(2)}, u32[]{:S(2)}) collective-permute-start(bf16[64,768]{1,0:T(8,128)(2,1)S(1)} %get-tuple-element.22), channel_id=1, source_target_pairs={{0,8},{8,0},{16,24},{24,16},{1,9},{9,1},{17,25},{25,17},{2,10},{10... | collective-permute-start | bytes 294920 | tf_op jit(solution)/shard_map/ppermute | solution.py:220
  5.2 2.5 %collective-permute-start.5 = (bf16[64,768]{1,0:T(8,128)(2,1)S(1)}, bf16[64,768]{1,0:T(8,128)(2,1)S(1)}, u32[]{:S(2)}, u32[]{:S(2)}) collective-permute-start(bf16[64,768]{1,0:T(8,128)(2,1)S(1)} %get-tuple-element.24), channel_id=1, source_target_pairs={{0,24},{8,16},{16,8},{24,0},{1,25},{9,17},{17,9},{25,1},{2,26},{10... | collective-permute-start | bytes 294920 | tf_op jit(solution)/shard_map/ppermute | solution.py:220
  7.6 0.1 collective-permute-start.4
  7.8 0.2 collective-permute-done
  8.0 2.8 %collective-permute-start.1 = (bf16[128,768]{1,0:T(8,128)(2,1)S(1)}, bf16[128,768]{1,0:T(8,128)(2,1)S(1)}, u32[]{:S(2)}, u32[]{:S(2)}) collective-permute-start(bf16[128,768]{1,0:T(8,128)(2,1)S(1)} %get-tuple-element.42), channel_id=1, source_target_pairs={{0,6},{1,7},{2,4},{3,5},{4,2},{5,3},{6,0},{7,1},{8,14},{9,15},{10,... | collective-permute-start | bytes 589832 | tf_op jit(solution)/shard_map/ppermute | solution.py:223
  10.7 0.5 %collective-permute-start.2 = (bf16[128,768]{1,0:T(8,128)(2,1)S(1)}, bf16[128,768]{1,0:T(8,128)(2,1)S(1)}, u32[]{:S(2)}, u32[]{:S(2)}) collective-permute-start(bf16[128,768]{1,0:T(8,128)(2,1)S(1)} %get-tuple-element.42), channel_id=1, source_target_pairs={{0,2},{1,5},{2,0},{3,7},{4,6},{5,1},{6,4},{7,3},{8,10},{9,13},{10,... | collective-permute-start | bytes 589832 | tf_op jit(solution)/shard_map/ppermute | solution.py:243
  11.3 0.3 collective-permute-start.3
  11.5 5.1 %collective-permute-done.4 = bf16[64,768]{1,0:T(8,128)(2,1)S(1)} collective-permute-done((bf16[64,768]{1,0:T(8,128)(2,1)S(1)}, bf16[64,768]{1,0:T(8,128)(2,1)S(1)}, u32[]{:S(2)}, u32[]{:S(2)}) %collective-permute-start.4) | collective-permute-done | bytes 98336 | tf_op jit(solution)/shard_map/ppermute | solution.py:220
  16.6 0.0 collective-permute-done.5
  16.6 2.5 %collective-permute-start.7 = (bf16[128,768]{1,0:T(8,128)(2,1)S(1)}, bf16[128,768]{1,0:T(8,128)(2,1)S(1)}, u32[]{:S(2)}, u32[]{:S(2)}) collective-permute-start(bf16[128,768]{1,0:T(8,128)(2,1)S(1)} %get-tuple-element.38), channel_id=1, source_target_pairs={{0,6},{1,7},{2,4},{3,5},{4,2},{5,3},{6,0},{7,1},{8,14},{9,15},{10,... | collective-permute-start | bytes 589832 | tf_op jit(solution)/shard_map/ppermute | solution.py:223
  19.1 0.5 %collective-permute-start.8 = (bf16[128,768]{1,0:T(8,128)(2,1)S(1)}, bf16[128,768]{1,0:T(8,128)(2,1)S(1)}, u32[]{:S(2)}, u32[]{:S(2)}) collective-permute-start(bf16[128,768]{1,0:T(8,128)(2,1)S(1)} %get-tuple-element.38), channel_id=1, source_target_pairs={{0,2},{1,5},{2,0},{3,7},{4,6},{5,1},{6,4},{7,3},{8,10},{9,13},{10,... | collective-permute-start | bytes 589832 | tf_op jit(solution)/shard_map/ppermute | solution.py:243
  19.7 0.0 collective-permute-done.1
  19.7 0.6 %collective-permute-start.9 = (bf16[128,768]{1,0:T(8,128)(2,1)S(1)}, bf16[128,768]{1,0:T(8,128)(2,1)S(1)}, u32[]{:S(2)}, u32[]{:S(2)}) collective-permute-start(bf16[128,768]{1,0:T(8,128)(2,1)S(1)} %get-tuple-element.38), channel_id=1, source_target_pairs={{0,4},{1,3},{2,6},{3,1},{4,0},{5,7},{6,2},{7,5},{8,12},{9,11},{10,... | collective-permute-start | bytes 589832 | tf_op jit(solution)/shard_map/ppermute | solution.py:243
  20.3 0.0 collective-permute-done.2
  20.4 0.1 collective-permute-start.6
  20.4 5.0 %collective-permute-done.7 = bf16[128,768]{1,0:T(8,128)(2,1)S(1)} collective-permute-done((bf16[128,768]{1,0:T(8,128)(2,1)S(1)}, bf16[128,768]{1,0:T(8,128)(2,1)S(1)}, u32[]{:S(2)}, u32[]{:S(2)}) %collective-permute-start.7) | collective-permute-done | bytes 196640 | tf_op jit(solution)/shard_map/ppermute | solution.py:223
  25.4 2.9 %collective-permute-done.8 = bf16[128,768]{1,0:T(8,128)(2,1)S(1)} collective-permute-done((bf16[128,768]{1,0:T(8,128)(2,1)S(1)}, bf16[128,768]{1,0:T(8,128)(2,1)S(1)}, u32[]{:S(2)}, u32[]{:S(2)}) %collective-permute-start.8) | collective-permute-done | bytes 196640 | tf_op jit(solution)/shard_map/ppermute | solution.py:243
  28.3 0.0 collective-permute-done.9
  28.3 0.1 collective-permute-start.10
  28.4 1.9 %early_sums.1 = (f32[256,128]{1,0:T(8,128)S(1)}, f32[256,768]{1,0:T(8,128)S(1)}, f32[256,128]{1,0:T(8,128)S(1)}) custom-call(bf16[256,768]{1,0:T(8,128)(2,1)S(1)} %pad_maximum_fusion.rows_ref, bf16[512,768]{1,0:T(8,128)(2,1)S(1)} %constant_dynamic-update-slice_fusion.2.refs_0_, bf16[512,768]{1,0:T(8,128)(2,1)S(1)} %collective-permute-done.6.refs_1_, ...), custom_call_target="tpu_custom_call" | custom-call | flops 1207959552 | tf_op jit(solution)/shard_map/early_sums/pallas_call | solution.py:255
  30.4 0.3 collective-permute-done.10.cols_ref
  30.7 0.9 %last_sums.1 = (f32[72,768]{1,0:T(8,128)S(1)}, f32[72,768]{1,0:T(8,128)S(1)}, f32[64,768]{1,0:T(8,128)S(1)}, f32[64,768]{1,0:T(8,128)S(1)}, f32[8,128]{1,0:T(8,128)S(1)}, /*index=5*/f32[8,128]{1,0:T(8,128)S(1)}) custom-call(bf16[256,768]{1,0:T(8,128)(2,1)S(1)} %pad_maximum_fusion.rows_ref, f32[256,128]{1,0:T(8,128)S(1)} %get-tuple-element.27.scale_ref, ...), custom_call_target="tpu_custom_call" | custom-call | flops 402653184 | tf_op jit(solution)/shard_map/last_sums/pallas_call | solution.py:269
  31.6 2.9 %collective-permute-start.11 = (f16[64,768]{1,0:T(8,128)(2,1)S(1)}, f16[64,768]{1,0:T(8,128)(2,1)S(1)}, u32[]{:S(2)}, u32[]{:S(2)}) collective-permute-start(f16[64,768]{1,0:T(8,128)(2,1)S(1)} %convert_element_type.24), channel_id=1, source_target_pairs={{0,24},{8,16},{16,8},{24,0},{1,25},{9,17},{17,9},{25,1},{2,26},{10... | collective-permute-start | bytes 294920 | tf_op jit(solution)/shard_map/ppermute | solution.py:220
  34.5 0.1 collective-permute-start.12
  34.6 1.6 %collective-permute-start.13 = (f16[72,768]{1,0:T(8,128)(2,1)S(1)}, f16[72,768]{1,0:T(8,128)(2,1)S(1)}, u32[]{:S(2)}, u32[]{:S(2)}) collective-permute-start(f16[72,768]{1,0:T(8,128)(2,1)S(1)} %convert_element_type.28), channel_id=1, source_target_pairs={{0,8},{8,0},{16,24},{24,16},{1,9},{9,1},{17,25},{25,17},{2,10},{10... | collective-permute-start | bytes 331784 | tf_op jit(solution)/shard_map/ppermute | solution.py:220
  36.2 2.8 %collective-permute-start.14 = (f32[8,128]{1,0:T(8,128)S(1)}, f32[8,128]{1,0:T(8,128)S(1)}, u32[]{:S(2)}, u32[]{:S(2)}) collective-permute-start(f32[8,128]{1,0:T(8,128)S(1)} %get-tuple-element.34), channel_id=1, source_target_pairs={{0,24},{8,16},{16,8},{24,0},{1,25},{9,17},{17,9},{25,1},{2,26},{10... | collective-permute-start | bytes 12296 | tf_op jit(solution)/shard_map/ppermute | solution.py:220
  39.0 0.2 collective-permute-done.11
  39.2 4.2 %collective-permute-done.12 = f16[64,768]{1,0:T(8,128)(2,1)S(1)} collective-permute-done((f16[64,768]{1,0:T(8,128)(2,1)S(1)}, f16[64,768]{1,0:T(8,128)(2,1)S(1)}, u32[]{:S(2)}, u32[]{:S(2)}) %collective-permute-start.12) | collective-permute-done | bytes 98336 | tf_op jit(solution)/shard_map/ppermute | solution.py:220
  43.4 0.0 collective-permute-done.13
  43.5 0.0 collective-permute-done.15.refs_5_
  43.5 1.4 %restore_rows.1 = (f32[256,768]{1,0:T(8,128)}, f32[1,256]{1,0:T(1,128)}) custom-call(bf16[256,256]{1,0:T(8,128)(2,1)S(1)} %get-tuple-element.20.chosen_ref, f32[64,768]{1,0:T(8,128)S(1)} %convert_element_type.25.refs_0_, f32[64,768]{1,0:T(8,128)S(1)} %convert_element_type.27.refs_1_, f32[72,768]{1,0:T(8,128)S(1)} %convert_element_type.29.refs_2_, ...), custom_call_target="tpu_custom_call" | custom-call | tf_op jit(solution)/shard_map/restore_rows/pallas_call | solution.py:285
  (22 shorter events, 0.3 us)
Async XLA Ops:
  2.1 5.9 %collective-permute-start = (bf16[64,768]{1,0:T(8,128)(2,1)S(1)}, bf16[64,768]{1,0:T(8,128)(2,1)S(1)}, u32[]{:S(2)}, u32[]{:S(2)}) collective-permute-start(bf16[64,768]{1,0:T(8,128)(2,1)S(1)} %get-tuple-element.22), channel_id=1, source_target_pairs={{0,8},{8,0},{16,24},{24,16},{1,9},{9,1},{17,25},{25,17},{2,10},{10... | collective-permute-start | bytes 294920 | tf_op jit(solution)/shard_map/ppermute | solution.py:220
  5.2 11.4 %collective-permute-start.5 = (bf16[64,768]{1,0:T(8,128)(2,1)S(1)}, bf16[64,768]{1,0:T(8,128)(2,1)S(1)}, u32[]{:S(2)}, u32[]{:S(2)}) collective-permute-start(bf16[64,768]{1,0:T(8,128)(2,1)S(1)} %get-tuple-element.24), channel_id=1, source_target_pairs={{0,24},{8,16},{16,8},{24,0},{1,25},{9,17},{17,9},{25,1},{2,26},{10... | collective-permute-start | bytes 294920 | tf_op jit(solution)/shard_map/ppermute | solution.py:220
  7.6 8.9 %collective-permute-start.4 = (bf16[64,768]{1,0:T(8,128)(2,1)S(1)}, bf16[64,768]{1,0:T(8,128)(2,1)S(1)}, u32[]{:S(2)}, u32[]{:S(2)}) collective-permute-start(bf16[64,768]{1,0:T(8,128)(2,1)S(1)} %get-tuple-element.23), channel_id=1, source_target_pairs={{0,16},{8,24},{16,0},{24,8},{1,17},{9,25},{17,1},{25,9},{2,18},{10... | collective-permute-start | bytes 294920 | tf_op jit(solution)/shard_map/ppermute | solution.py:220
  8.0 11.7 %collective-permute-start.1 = (bf16[128,768]{1,0:T(8,128)(2,1)S(1)}, bf16[128,768]{1,0:T(8,128)(2,1)S(1)}, u32[]{:S(2)}, u32[]{:S(2)}) collective-permute-start(bf16[128,768]{1,0:T(8,128)(2,1)S(1)} %get-tuple-element.42), channel_id=1, source_target_pairs={{0,6},{1,7},{2,4},{3,5},{4,2},{5,3},{6,0},{7,1},{8,14},{9,15},{10,... | collective-permute-start | bytes 589832 | tf_op jit(solution)/shard_map/ppermute | solution.py:223
  10.7 9.6 %collective-permute-start.2 = (bf16[128,768]{1,0:T(8,128)(2,1)S(1)}, bf16[128,768]{1,0:T(8,128)(2,1)S(1)}, u32[]{:S(2)}, u32[]{:S(2)}) collective-permute-start(bf16[128,768]{1,0:T(8,128)(2,1)S(1)} %get-tuple-element.42), channel_id=1, source_target_pairs={{0,2},{1,5},{2,0},{3,7},{4,6},{5,1},{6,4},{7,3},{8,10},{9,13},{10,... | collective-permute-start | bytes 589832 | tf_op jit(solution)/shard_map/ppermute | solution.py:243
  11.3 9.1 %collective-permute-start.3 = (bf16[128,768]{1,0:T(8,128)(2,1)S(1)}, bf16[128,768]{1,0:T(8,128)(2,1)S(1)}, u32[]{:S(2)}, u32[]{:S(2)}) collective-permute-start(bf16[128,768]{1,0:T(8,128)(2,1)S(1)} %get-tuple-element.42), channel_id=1, source_target_pairs={{0,4},{1,3},{2,6},{3,1},{4,0},{5,7},{6,2},{7,5},{8,12},{9,11},{10,... | collective-permute-start | bytes 589832 | tf_op jit(solution)/shard_map/ppermute | solution.py:243
  16.6 8.8 %collective-permute-start.7 = (bf16[128,768]{1,0:T(8,128)(2,1)S(1)}, bf16[128,768]{1,0:T(8,128)(2,1)S(1)}, u32[]{:S(2)}, u32[]{:S(2)}) collective-permute-start(bf16[128,768]{1,0:T(8,128)(2,1)S(1)} %get-tuple-element.38), channel_id=1, source_target_pairs={{0,6},{1,7},{2,4},{3,5},{4,2},{5,3},{6,0},{7,1},{8,14},{9,15},{10,... | collective-permute-start | bytes 589832 | tf_op jit(solution)/shard_map/ppermute | solution.py:223
  19.1 9.2 %collective-permute-start.8 = (bf16[128,768]{1,0:T(8,128)(2,1)S(1)}, bf16[128,768]{1,0:T(8,128)(2,1)S(1)}, u32[]{:S(2)}, u32[]{:S(2)}) collective-permute-start(bf16[128,768]{1,0:T(8,128)(2,1)S(1)} %get-tuple-element.38), channel_id=1, source_target_pairs={{0,2},{1,5},{2,0},{3,7},{4,6},{5,1},{6,4},{7,3},{8,10},{9,13},{10,... | collective-permute-start | bytes 589832 | tf_op jit(solution)/shard_map/ppermute | solution.py:243
  19.7 8.6 %collective-permute-start.9 = (bf16[128,768]{1,0:T(8,128)(2,1)S(1)}, bf16[128,768]{1,0:T(8,128)(2,1)S(1)}, u32[]{:S(2)}, u32[]{:S(2)}) collective-permute-start(bf16[128,768]{1,0:T(8,128)(2,1)S(1)} %get-tuple-element.38), channel_id=1, source_target_pairs={{0,4},{1,3},{2,6},{3,1},{4,0},{5,7},{6,2},{7,5},{8,12},{9,11},{10,... | collective-permute-start | bytes 589832 | tf_op jit(solution)/shard_map/ppermute | solution.py:243
  20.4 8.1 %collective-permute-start.6 = (bf16[512,768]{1,0:T(8,128)(2,1)S(1)}, bf16[512,768]{1,0:T(8,128)(2,1)S(1)}, u32[]{:S(2)}, u32[]{:S(2)}) collective-permute-start(bf16[512,768]{1,0:T(8,128)(2,1)S(1)} %constant_dynamic-update-slice_fusion.2.refs_0_), channel_id=1, source_target_pairs={{0,1},{1,0},{2,3},{3,2},{4,5},{5,4},{6,7},{7,6},{8,9},{9,8},{10,11... | collective-permute-start | bytes 2359304 | tf_op jit(solution)/shard_map/ppermute | solution.py:223
  28.3 2.4 %collective-permute-start.10 = (bf16[512,768]{1,0:T(8,128)(2,1)S(1)}, bf16[512,768]{1,0:T(8,128)(2,1)S(1)}, u32[]{:S(2)}, u32[]{:S(2)}) collective-permute-start(bf16[512,768]{1,0:T(8,128)(2,1)S(1)} %constant_dynamic-update-slice_fusion.9.refs_2_), channel_id=1, source_target_pairs={{0,1},{1,0},{2,3},{3,2},{4,5},{5,4},{6,7},{7,6},{8,9},{9,8},{10,11... | collective-permute-start | bytes 2359304 | tf_op jit(solution)/shard_map/ppermute | solution.py:223
  31.6 7.6 %collective-permute-start.11 = (f16[64,768]{1,0:T(8,128)(2,1)S(1)}, f16[64,768]{1,0:T(8,128)(2,1)S(1)}, u32[]{:S(2)}, u32[]{:S(2)}) collective-permute-start(f16[64,768]{1,0:T(8,128)(2,1)S(1)} %convert_element_type.24), channel_id=1, source_target_pairs={{0,24},{8,16},{16,8},{24,0},{1,25},{9,17},{17,9},{25,1},{2,26},{10... | collective-permute-start | bytes 294920 | tf_op jit(solution)/shard_map/ppermute | solution.py:220
  34.5 8.9 %collective-permute-start.12 = (f16[64,768]{1,0:T(8,128)(2,1)S(1)}, f16[64,768]{1,0:T(8,128)(2,1)S(1)}, u32[]{:S(2)}, u32[]{:S(2)}) collective-permute-start(f16[64,768]{1,0:T(8,128)(2,1)S(1)} %convert_element_type.26), channel_id=1, source_target_pairs={{0,16},{8,24},{16,0},{24,8},{1,17},{9,25},{17,1},{25,9},{2,18},{10... | collective-permute-start | bytes 294920 | tf_op jit(solution)/shard_map/ppermute | solution.py:220
  34.6 8.9 %collective-permute-start.13 = (f16[72,768]{1,0:T(8,128)(2,1)S(1)}, f16[72,768]{1,0:T(8,128)(2,1)S(1)}, u32[]{:S(2)}, u32[]{:S(2)}) collective-permute-start(f16[72,768]{1,0:T(8,128)(2,1)S(1)} %convert_element_type.28), channel_id=1, source_target_pairs={{0,8},{8,0},{16,24},{24,16},{1,9},{9,1},{17,25},{25,17},{2,10},{10... | collective-permute-start | bytes 331784 | tf_op jit(solution)/shard_map/ppermute | solution.py:220
  36.2 7.3 %collective-permute-start.14 = (f32[8,128]{1,0:T(8,128)S(1)}, f32[8,128]{1,0:T(8,128)S(1)}, u32[]{:S(2)}, u32[]{:S(2)}) collective-permute-start(f32[8,128]{1,0:T(8,128)S(1)} %get-tuple-element.34), channel_id=1, source_target_pairs={{0,24},{8,16},{16,8},{24,0},{1,25},{9,17},{17,9},{25,1},{2,26},{10... | collective-permute-start | bytes 12296 | tf_op jit(solution)/shard_map/ppermute | solution.py:220
  39.0 4.5 %collective-permute-start.15 = (f32[8,128]{1,0:T(8,128)S(1)}, f32[8,128]{1,0:T(8,128)S(1)}, u32[]{:S(2)}, u32[]{:S(2)}) collective-permute-start(f32[8,128]{1,0:T(8,128)S(1)} %get-tuple-element.35), channel_id=1, source_target_pairs={{0,16},{8,24},{16,0},{24,8},{1,17},{9,25},{17,1},{25,9},{2,18},{10... | collective-permute-start | bytes 12296 | tf_op jit(solution)/shard_map/ppermute | solution.py:220
